TPU v7x, 32 devices: a whole 2x2x4 slice. The times are simulated.
32 devices in a mesh: row: 8 (over y, x, core), col: 4 (over z).
Axes of the slice: x: 2, y: 2, z: 4, core: 2. Of those that a mesh axis runs over, the one named last changes fastest.
Arguments:
- features: bfloat16 [16384, 256], P(('col', 'row')), may hold values from -6 to 6
- weight: bfloat16 [256, 256], replicated, may hold values from -0.375 to 0.375
- block_cols: int32 [8, 4, 128], P('row', 'col'), may hold values from 0 to 31, as said below
- row_starts: int32 [8, 4, 17], P('row', 'col'), may hold values from 0 to 128, as said below
- block_values: bfloat16 [8, 4, 128, 128, 128], P('row', 'col'), as said below
- cotangent: bfloat16 [16384, 256], P(('row', 'col')), may hold values from -6 to 6
Outputs:
- activations: bfloat16 [16384, 256], P(('row', 'col'))
- feature_grad: bfloat16 [16384, 256], P(('col', 'row'))
- weight_grad: float32 [256, 256], replicated
Inputs may be any that keep to these rules, and one draw needn't show every extreme that they name: `block_cols`: each slot names one of the 32 block columns of its cell's column group. `row_starts`: in each cell the entries start at 0 and never fall; the last one is the cell's count of live slots, and it equals 128 in at least one cell. `block_values`: every entry is zero or positive.
All inputs are finite; a program needn't handle non-finite values.
Results may differ from a plain program's by a relative error of at most 0.018.
Values may be sent and summed in bfloat16 or wider, within the bound.
No kernel may reach another device: no remote copies, remote signals or barrier semaphores. Data moves between devices by JAX's collectives and lax.ppermute only.
A program may use at most 128 MiB of HBM per device.

v0:
```python
import jax
import jax.numpy as jnp
from jax import lax
from jax.sharding import PartitionSpec as P


def slot_rows(starts, count):
    index = jnp.arange(count, dtype=jnp.int32)
    inner = starts[1:]
    rows = jnp.sum((inner[None, :] <= index[:, None]).astype(jnp.int32), axis=1)
    rows = jnp.minimum(rows, inner.shape[0] - 1)
    live = index < starts[-1]
    return (rows, live)


def on_device(features, weight, block_cols, row_starts, block_values, cotangent):
    values = block_values[0, 0]
    cols = block_cols[0, 0]
    starts = row_starts[0, 0]
    slots = values.shape[0]
    size = values.shape[1]
    width = features.shape[1]
    row_blocks = starts.shape[0] - 1
    rows, live = slot_rows(starts, slots)
    masked = values * live[:, None, None].astype(values.dtype)
    panel = lax.all_gather(features, "row", axis=0, tiled=True)
    col_blocks = panel.shape[0] // size
    blocks = panel.reshape(col_blocks, size, width)[cols]
    terms = jnp.einsum("kij,kjf->kif", masked, blocks, preferred_element_type=jnp.float32)
    partial_value = jax.ops.segment_sum(terms, rows, num_segments=row_blocks).reshape(
        row_blocks * size, width
    )
    aggregated = lax.psum_scatter(
        partial_value.astype(jnp.bfloat16), "col", scatter_dimension=0, tiled=True
    ).astype(jnp.float32)
    weight_wide = weight.astype(jnp.float32)
    mixed = jnp.dot(aggregated, weight_wide, precision=lax.Precision.HIGHEST)
    sigma = jax.nn.sigmoid(mixed)
    activations = (mixed * sigma).astype(jnp.bfloat16)
    mixed_grad = cotangent.astype(jnp.float32) * (sigma * (1.0 + mixed * (1.0 - sigma)))
    weight_term = jnp.dot(aggregated.T, mixed_grad, precision=lax.Precision.HIGHEST)
    mixed_whole = lax.all_gather(mixed_grad.astype(jnp.bfloat16), "col", axis=0, tiled=True).astype(
        mixed_grad.dtype
    )
    grad_panel = jnp.dot(mixed_whole, weight_wide.T, precision=lax.Precision.HIGHEST).astype(
        jnp.bfloat16
    )
    back_blocks = grad_panel.reshape(row_blocks, size, width)[rows]
    back_terms = jnp.einsum("kij,kif->kjf", masked, back_blocks, preferred_element_type=jnp.float32)
    back_partial = jax.ops.segment_sum(back_terms, cols, num_segments=col_blocks).reshape(
        col_blocks * size, width
    )
    feature_grad = lax.psum_scatter(
        back_partial.astype(jnp.bfloat16), "row", scatter_dimension=0, tiled=True
    )
    weight_grad = lax.psum(weight_term, ("row", "col"))
    return (activations, feature_grad, weight_grad)


def solution(mesh):
    placed = (
        P(("col", "row"), None),
        P(),
        P("row", "col", None),
        P("row", "col", None),
        P("row", "col", None, None, None),
        P(("row", "col"), None),
    )
    return jax.shard_map(
        on_device,
        mesh=mesh,
        in_specs=placed,
        out_specs=(P(("row", "col"), None), P(("col", "row"), None), P()),
        check_vma=False,
    )
```

profile of v0, /device:TPU:0, one launch (start us, length us, event | category | flops | bytes accessed | tf_op | source)
XLA Modules:
  0.0 327.0 jit_solution(4562466581939686061)
XLA Ops:
  7.2 0.0 copy-start
  7.2 0.0 all-gather.3.cloned.1.call-start
  7.2 0.7 all-gather.3.cloned.1.call-update
  7.9 0.0 reduce-scatter.3.cloned.1.call-start
  8.0 1.2 slice.9
  9.2 0.6 compare_convert_fusion
  9.9 0.7 fusion.4
  10.5 0.7 slice_bitcast_fusion
  11.3 0.1 convert_reduce_fusion
  11.3 29.2 %all-gather.3.cloned.1.call-done = bf16[4096,256]{1,0:T(8,128)(2,1)} async-done(((bf16[512,256]{1,0:T(8,128)(2,1)}), bf16[4096,256]{1,0:T(8,128)(2,1)}) %all-gather.3.cloned.1.call-update) | async-done | bytes 2097168 | tf_op jit(solution)/shard_map/all_gather | solution.py:26
  40.6 8.2 %gather_fusion = bf16[128,128,256]{2,1,0:T(8,128)(2,1)} fusion(bf16[32,128,256]{2,1,0:T(8,128)(2,1)} %bitcast.28, s32[1024]{0:T(1024)S(1)} %pad_clamp_fusion.1), kind=kCustom, calls=%fused_computation | custom fusion | bytes 16777728 | tf_op jit(solution)/shard_map/gather | solution.py:28
  48.8 12.8 %fusion.1 = f32[128,128,256]{2,1,0:T(8,128)} fusion(bf16[128,128,256]{2,1,0:T(8,128)(2,1)} %gather_fusion, bf16[1,1,128,128,128]{4,3,2,1,0:T(8,128)(2,1)} %param.10, bf16[128]{0:T(256)(128)(2,1)S(1)} %compare_convert_fusion), kind=kOutput, calls=%fused_computation.6 | convolution fusion | flops 1075838976 | bytes 29360384 | tf_op jit(solution)/shard_map/kij,kjf->kif/dot_general | solution.py:29
  61.5 0.2 broadcast_in_dim.4
  61.7 0.0 copy-start.3
  61.7 24.0 %scatter_fusion = f32[16,128,256]{2,1,0:T(8,128)S(1)} fusion(f32[16,128,256]{2,1,0:T(8,128)S(1)} %broadcast_in_dim.4, s32[128]{0:T(128)S(1)} %broadcast_minimum_fusion, f32[128,128,256]{2,1,0:T(8,128)} %fusion.1), kind=kCustom, calls=%fused_computation.2 | custom fusion | flops 4194304 | bytes 50332160 | tf_op jit(solution)/shard_map/scatter-add | solution.py:30
  85.8 1.1 convert_element_type.40
  86.9 0.0 reduce-scatter.3.cloned.1.call-update
  86.9 0.0 all-gather.5.cloned.1.call-start
  86.9 27.3 %reduce-scatter.3.cloned.1.call-done = bf16[512,256]{1,0:T(8,128)(2,1)} async-done(((bf16[2048,256]{1,0:T(8,128)(2,1)}), bf16[512,256]{1,0:T(8,128)(2,1)}) %reduce-scatter.3.cloned.1.call-update) | async-done | bytes 262160 | tf_op jit(solution)/shard_map/reduce_scatter | solution.py:33
  114.2 0.0 copy-done
  114.2 0.0 copy-done.3
  114.2 2.1 fusion.7
  116.3 0.0 all-gather.5.cloned.1.call-update
  116.4 0.0 all-reduce.2.cloned.1.call-start
  116.4 2.3 fusion.6
  118.8 0.0 all-reduce.2.cloned.1.call-update
  118.8 0.2 reduce-scatter.5.cloned.1.call-start
  119.0 24.1 %all-gather.5.cloned.1.call-done = bf16[2048,256]{1,0:T(8,128)(2,1)} async-done(((bf16[512,256]{1,0:T(8,128)(2,1)}), bf16[2048,256]{1,0:T(8,128)(2,1)}) %all-gather.5.cloned.1.call-update) | async-done | bytes 1048592 | tf_op jit(solution)/shard_map/all_gather | solution.py:42
  143.1 1.7 convolution_convert_fusion
  144.8 6.4 %gather_fusion.1 = bf16[128,128,256]{2,1,0:T(8,128)(2,1)} fusion(bf16[16,128,256]{2,1,0:T(8,128)(2,1)S(1)} %bitcast.27, s32[1024]{0:T(1024)S(1)} %pad_clamp_fusion), kind=kCustom, calls=%fused_computation.1 | custom fusion | bytes 16777728 | tf_op jit(solution)/shard_map/gather | solution.py:48
  151.2 0.0 copy-start.2
  151.2 13.9 %fusion = f32[128,128,256]{2,1,0:T(8,128)} fusion(bf16[128,128,256]{2,1,0:T(8,128)(2,1)} %gather_fusion.1, bf16[1,1,128,128,128]{4,3,2,1,0:T(8,128)(2,1)} %param.10, bf16[128]{0:T(256)(128)(2,1)S(1)} %compare_convert_fusion), kind=kOutput, calls=%fused_computation.5 | convolution fusion | flops 1075838976 | bytes 29360384 | tf_op jit(solution)/shard_map/kij,kif->kjf/dot_general | solution.py:49
  165.1 2.4 broadcast_in_dim.5
  167.5 0.0 copy-done.2
  167.5 0.0 copy-start.1
  167.5 37.9 %scatter_fusion.1 = f32[32,128,256]{2,1,0:T(8,128)} fusion(f32[32,128,256]{2,1,0:T(8,128)} %broadcast_in_dim.5, s32[128]{0:T(128)S(1)} %bitcast.31, f32[128,128,256]{2,1,0:T(8,128)} %fusion), kind=kCustom, calls=%fused_computation.3 | custom fusion | flops 4194304 | bytes 50332160 | tf_op jit(solution)/shard_map/scatter-add | solution.py:50
  205.4 3.8 %convert_element_type.46 = bf16[32,128,256]{2,1,0:T(8,128)(2,1)} convert(f32[32,128,256]{2,1,0:T(8,128)} %scatter_fusion.1) | non-fusion elementwise | flops 1048576 | bytes 6291456 | tf_op jit(solution)/shard_map/convert_element_type | solution.py:54
  209.3 0.0 reduce-scatter.5.cloned.1.call-update
  209.3 65.2 %all-reduce.2.cloned.1.call-done = f32[256,256]{1,0:T(8,128)} async-done(((f32[256,256]{1,0:T(8,128)}), f32[256,256]{1,0:T(8,128)}) %all-reduce.2.cloned.1.call-update) | async-done | bytes 262160 | tf_op jit(solution)/shard_map/psum | solution.py:56
  274.5 44.3 %reduce-scatter.5.cloned.1.call-done = bf16[512,256]{1,0:T(8,128)(2,1)} async-done(((bf16[4096,256]{1,0:T(8,128)(2,1)}), bf16[512,256]{1,0:T(8,128)(2,1)}) %reduce-scatter.5.cloned.1.call-update) | async-done | bytes 262160 | tf_op jit(solution)/shard_map/reduce_scatter | solution.py:53
  318.8 1.7 copy.15
  320.5 0.0 copy-done.1
  (4 shorter events, 0.0 us)
Async XLA Ops:
  7.2 107.0 %copy-start = (bf16[256,256]{1,0:T(8,128)(2,1)S(1)}, bf16[256,256]{1,0:T(8,128)(2,1)}, u32[]{:S(2)}) copy-start(bf16[256,256]{1,0:T(8,128)(2,1)} %param.7) | copy-start | bytes 393220
  7.2 33.4 %all-gather.3.cloned.1.call-start = ((), (), s32[]{:S(2)}) async-start(), calls=%async_computation.2 | async-start | bytes 2359296 | tf_op jit(solution)/shard_map/all_gather | solution.py:26
  7.9 106.3 %reduce-scatter.3.cloned.1.call-start = ((), (), s32[]{:S(2)}) async-start(), calls=%async_computation.3 | async-start | bytes 1310720 | tf_op jit(solution)/shard_map/reduce_scatter | solution.py:33
  61.7 52.5 %copy-start.3 = (bf16[512,256]{1,0:T(8,128)(2,1)S(1)}, bf16[512,256]{1,0:T(8,128)(2,1)}, u32[]{:S(2)}) copy-start(bf16[512,256]{1,0:T(8,128)(2,1)} %param.11) | copy-start | bytes 786436
  86.9 56.2 %all-gather.5.cloned.1.call-start = ((), (), s32[]{:S(2)}) async-start(), calls=%async_computation.4 | async-start | bytes 1310720 | tf_op jit(solution)/shard_map/all_gather | solution.py:42
  116.4 158.1 %all-reduce.2.cloned.1.call-start = ((), (), s32[]{:S(2)}) async-start(), calls=%async_computation.6 | async-start | bytes 524288 | tf_op jit(solution)/shard_map/psum | solution.py:56
  118.8 200.0 %reduce-scatter.5.cloned.1.call-start = ((), (), s32[]{:S(2)}) async-start(), calls=%async_computation.5 | async-start | bytes 2359296 | tf_op jit(solution)/shard_map/reduce_scatter | solution.py:53
  151.2 16.3 %copy-start.2 = (s32[1,1,128]{2,1,0:T(1,128)S(1)}, s32[1,1,128]{2,1,0:T(1,128)}, u32[]{:S(2)}) copy-start(s32[1,1,128]{2,1,0:T(1,128)} %param.8) | copy-start | bytes 1540
  167.5 153.0 %copy-start.1 = (bf16[256,256]{1,0:T(8,128)(2,1)S(1)}, bf16[256,256]{1,0:T(8,128)(2,1)}, u32[]{:S(2)}) copy-start(bf16[256,256]{1,0:T(8,128)(2,1)} %param.7) | copy-start | bytes 393220
Sparse Core Ops, SparseCore 0:
  9.9 30.6 all-gather.2
  87.0 27.1 reduce-scatter.2
  116.5 26.5 all-gather.4
  149.9 124.4 all-reduce.1
  278.5 40.2 reduce-scatter.4
where the time goes:
time: 328 us; the launch traced here: 327 us
  waiting for transfers between devices  191 us (58%)
  other arithmetic  68.3 us (21%)
  matrix products  32.8 us (10%)
  local copies, waits for them, and re-layouts  20.9 us (6%)
  between operations  13.8 us (4%)
    psum x1, waiting for transfers between devices, on_device(): weight_grad = lax.psum(weight_term, ('row', 'col'))  65.2 us
    reduce_scatter x1, waiting for transfers between devices, on_device(): lax.psum_scatter(back_partial.astype(jnp.bfloat16), 'row', scatter_dimens...  44.3 us
    scatter-add x1, other arithmetic, on_device(): jax.ops.segment_sum(back_terms, cols, num_segments=col_blocks)  37.9 us
    all_gather x1, waiting for transfers between devices, on_device(): panel = lax.all_gather(features, 'row', axis=0, tiled=True)  29.2 us
    reduce_scatter x1, waiting for transfers between devices, on_device(): lax.psum_scatter(partial_value.astype(jnp.bfloat16), 'col', scatter_dimen...  27.3 us
    all_gather x1, waiting for transfers between devices, on_device(): lax.all_gather(mixed_grad.astype(jnp.bfloat16), 'col', axis=0, tiled=True)  24.1 us
    scatter-add x1, other arithmetic, on_device(): jax.ops.segment_sum(terms, rows, num_segments=row_blocks)  24 us
    dot_general x1, matrix products, on_device(): jnp.einsum('kij,kif->kjf', masked, back_blocks, preferred_element_type=jn...  13.9 us
  transfers between devices with their start and end apart: 5, of which 5 were waited for; matrix products, arithmetic and copies ran while one was open for 22% of the time, Pallas kernels for 0%

commit v1 on v0

v1 whole, which is shorter than its diff:
```python
import functools

import jax
import jax.numpy as jnp
from jax import lax
from jax.experimental import pallas as pl
from jax.experimental.pallas import tpu as pltpu
from jax.sharding import PartitionSpec as P

F32 = jnp.float32
BF16 = jnp.bfloat16
GROUP = 8
ANY = pl.BlockSpec(memory_space=pl.ANY)
VMEM = pl.BlockSpec(memory_space=pltpu.VMEM)
SMEM = pl.BlockSpec(memory_space=pltpu.SMEM)


def params(mib):
    return pltpu.CompilerParams(vmem_limit_bytes=mib << 20)


def cost(flops, nbytes):
    return pl.CostEstimate(flops=flops, bytes_accessed=nbytes, transcendentals=0)


def sparse_kernel(parts, outs, transposed, meta, to, source, *refs):
    panel_refs = refs[:parts]
    values_ref = refs[parts]
    out_refs = refs[parts + 1 : parts + 1 + len(outs)]
    panel, values, total, panel_sem, values_sem = refs[parts + 1 + len(outs) :]
    live, here, mine = meta[0], meta[1], meta[2]
    chunk = panel_refs[0].shape[0]
    size = values.shape[1]
    groups = values.shape[0] // GROUP
    loads = []
    for m in range(parts):
        start = pl.multiple_of((here ^ m) * chunk, chunk)
        copy = pltpu.make_async_copy(
            panel_refs[m], panel.at[pl.ds(start, chunk)], panel_sem.at[m]
        )
        copy.start()
        loads.append(copy)

    def load(g):
        span = pl.ds(pl.multiple_of(g * GROUP, GROUP), GROUP)
        return pltpu.make_async_copy(values_ref.at[span], values.at[span], values_sem.at[g])

    used = (live + GROUP - 1) // GROUP

    def begin(g, carry):
        load(g).start()
        return carry

    lax.fori_loop(0, used, begin, 0)
    total[...] = jnp.zeros_like(total)
    for copy in loads:
        copy.wait()

    def step(g, carry):
        load(g).wait()
        for u in range(GROUP):
            k = g * GROUP + u
            i = pl.multiple_of(to[k] * size, size)
            j = pl.multiple_of(source[k] * size, size)
            block = values[k]
            if transposed:
                term = lax.dot_general(
                    block,
                    panel[pl.ds(j, size), :],
                    (((0,), (0,)), ((), ())),
                    preferred_element_type=F32,
                )
            else:
                term = jnp.dot(block, panel[pl.ds(j, size), :], preferred_element_type=F32)
            total[pl.ds(i, size), :] += term
        return carry

    lax.fori_loop(0, used, step, 0)
    for out_ref, members in zip(out_refs, outs):
        rows = out_ref.shape[0] // len(members)
        for at, m in enumerate(members):
            start = pl.multiple_of((mine ^ m) * rows, rows)
            out_ref[at * rows : (at + 1) * rows, :] = total[pl.ds(start, rows), :].astype(
                out_ref.dtype
            )


def sparse_product(panel_parts, values, meta, to, source, blocks, outs, transposed):
    parts = len(panel_parts)
    slots, size, _ = values.shape
    chunk, width = panel_parts[0].shape
    rows = chunk
    flops = 2 * slots * size * size * width
    return pl.pallas_call(
        functools.partial(sparse_kernel, parts, outs, transposed),
        out_shape=[jax.ShapeDtypeStruct((rows * len(members), width), BF16) for members in outs],
        in_specs=[SMEM] * 3 + [ANY] * (parts + 1),
        out_specs=[VMEM] * len(outs),
        scratch_shapes=[
            pltpu.VMEM((parts * chunk, width), BF16),
            pltpu.VMEM((slots, size, size), BF16),
            pltpu.VMEM(((blocks + 1) * size, width), F32),
            pltpu.SemaphoreType.DMA((parts,)),
            pltpu.SemaphoreType.DMA((slots // GROUP,)),
        ],
        compiler_params=params(48),
        cost_estimate=cost(flops, 2 * values.size + 2 * parts * chunk * width),
    )(meta, to, source, *panel_parts, values)


def split(value):
    high = value.astype(BF16)
    return high, (value - high.astype(F32)).astype(BF16)


def mm(a, b, dims):
    return lax.dot_general(a, b, (dims, ((), ())), preferred_element_type=F32)


def middle_kernel(count, *refs):
    terms = refs[:count]
    weight_ref, cotangent_ref, act_ref, back_ref, agg_ref, grad_ref = refs[count:]
    aggregated = terms[0][...].astype(F32)
    for term in terms[1:]:
        aggregated += term[...].astype(F32)
    agg_ref[...] = aggregated
    weight = weight_ref[...]
    high, low = split(aggregated)
    mixed = mm(high, weight, ((1,), (0,))) + mm(low, weight, ((1,), (0,)))
    sigma = jax.nn.sigmoid(mixed)
    act_ref[...] = (mixed * sigma).astype(BF16)
    mixed_grad = cotangent_ref[...].astype(F32) * (sigma * (1.0 + mixed * (1.0 - sigma)))
    grad_ref[...] = mixed_grad
    high, low = split(mixed_grad)
    back = mm(high, weight, ((1,), (1,))) + mm(low, weight, ((1,), (1,)))
    back_ref[...] = back.astype(BF16)


def middle(terms, weight, cotangent):
    rows, width = cotangent.shape
    return pl.pallas_call(
        functools.partial(middle_kernel, len(terms)),
        out_shape=[
            jax.ShapeDtypeStruct((rows, width), BF16),
            jax.ShapeDtypeStruct((rows, width), BF16),
            jax.ShapeDtypeStruct((rows, width), F32),
            jax.ShapeDtypeStruct((rows, width), F32),
        ],
        in_specs=[VMEM] * (len(terms) + 2),
        out_specs=[VMEM] * 4,
        compiler_params=params(40),
        cost_estimate=cost(8 * rows * width * width, 20 * rows * width),
    )(*terms, weight, cotangent)


def weight_kernel(chunks, me, agg_ref, grad_ref, *outs):
    high, low = split(agg_ref[...])
    grad_high, grad_low = split(grad_ref[...])
    contract = ((0,), (0,))
    term = (
        mm(high, grad_high, contract) + mm(low, grad_high, contract) + mm(high, grad_low, contract)
    )
    scratch = outs[-1]
    scratch[...] = term
    rows = term.shape[0] // chunks
    for m in range(chunks):
        start = pl.multiple_of((me[0] ^ m) * rows, rows)
        outs[m][...] = scratch[pl.ds(start, rows), :]


def weight_term(aggregated, mixed_grad, me, chunks):
    rows, width = aggregated.shape
    return pl.pallas_call(
        functools.partial(weight_kernel, chunks),
        out_shape=[jax.ShapeDtypeStruct((width // chunks, width), F32)] * chunks,
        in_specs=[SMEM, VMEM, VMEM],
        out_specs=[VMEM] * chunks,
        scratch_shapes=[pltpu.VMEM((width, width), F32)],
        compiler_params=params(40),
        cost_estimate=cost(6 * rows * width * width, 8 * rows * width),
    )(me, aggregated, mixed_grad)


def pair_kernel(count, own_ref, other_ref, *outs):
    rows = own_ref.shape[0] // count
    for m in range(count):
        span = slice(m * rows, (m + 1) * rows)
        outs[m][...] = (own_ref[span, :].astype(F32) + other_ref[span, :].astype(F32)).astype(BF16)


def pair_sum(own, other, count):
    rows, width = own.shape
    return pl.pallas_call(
        functools.partial(pair_kernel, count),
        out_shape=[jax.ShapeDtypeStruct((rows // count, width), BF16)] * count,
        in_specs=[VMEM] * 2,
        out_specs=[VMEM] * count,
        compiler_params=params(40),
        cost_estimate=cost(rows * width, 6 * rows * width),
    )(own, other)


def swap(x, axis, n, m):
    return lax.ppermute(x, axis, [(i, i ^ m) for i in range(n)])


def total_of(terms):
    result = terms[0].astype(F32)
    for term in terms[1:]:
        result = result + term.astype(F32)
    return result


def on_device(n_row, n_col, features, weight, block_cols, row_starts, block_values, cotangent):
    values = block_values[0, 0]
    starts = row_starts[0, 0]
    slots, size, _ = values.shape
    row_blocks = starts.shape[0] - 1
    col_blocks = n_row * features.shape[0] // size
    me_row = lax.axis_index("row")
    me_col = lax.axis_index("col")

    panel = [features] + [None] * (n_row - 1)
    for m in range(2, n_row, 2):
        panel[m] = swap(features, "row", n_row, m)
    for m in range(0, n_row, 2):
        panel[m + 1] = swap(panel[m], "row", n_row, 1)

    index = jnp.arange(slots, dtype=jnp.int32)
    rows = jnp.sum((starts[None, 1:] <= index[:, None]).astype(jnp.int32), axis=1)
    live = starts[-1]
    cols = block_cols[0, 0]
    cols_to = jnp.where(index < live, cols, col_blocks)
    rows_from = jnp.minimum(rows, row_blocks - 1)
    meta = jnp.stack([live, me_row, me_col]).astype(jnp.int32)
    meta_back = jnp.stack([live, me_col, me_row]).astype(jnp.int32)

    terms = sparse_product(
        panel, values, meta, rows, cols, row_blocks, [[m] for m in range(n_col)], False
    )
    terms = [terms[0]] + [swap(terms[m], "col", n_col, m) for m in range(1, n_col)]
    activations, back, aggregated, mixed_grad = middle(terms, weight, cotangent)

    back_panel = [back] + [swap(back, "col", n_col, m) for m in range(1, n_col)]

    pieces = weight_term(aggregated, mixed_grad, me_row[None].astype(jnp.int32), n_row)
    piece = total_of([pieces[0]] + [swap(pieces[m], "row", n_row, m) for m in range(1, n_row)])
    piece = total_of([piece] + [swap(piece, "col", n_col, m) for m in range(1, n_col)])

    even = list(range(0, n_row, 2))
    own, other = sparse_product(
        back_panel,
        values,
        meta_back,
        cols_to,
        rows_from,
        col_blocks,
        [even, [m + 1 for m in even]],
        True,
    )
    sums = pair_sum(own, swap(other, "row", n_row, 1), len(even))
    feature_grad = total_of(
        [sums[0]] + [swap(s, "row", n_row, m) for s, m in zip(sums[1:], even[1:])]
    ).astype(BF16)

    weight_grad = jnp.zeros(weight.shape, F32)
    depth = weight.shape[0] // n_row
    gathered = [piece] + [swap(piece, "row", n_row, m) for m in range(1, n_row)]
    for m in range(n_row):
        weight_grad = lax.dynamic_update_slice(
            weight_grad, gathered[m], ((me_row ^ m) * depth, jnp.int32(0))
        )
    return (activations, feature_grad, weight_grad)


def solution(mesh):
    placed = (
        P(("col", "row"), None),
        P(),
        P("row", "col", None),
        P("row", "col", None),
        P("row", "col", None, None, None),
        P(("row", "col"), None),
    )
    return jax.shard_map(
        functools.partial(on_device, mesh.shape["row"], mesh.shape["col"]),
        mesh=mesh,
        in_specs=placed,
        out_specs=(P(("row", "col"), None), P(("col", "row"), None), P()),
        check_vma=False,
    )
```

time: 328 us -> 130 us (0.40)
  waiting for transfers between devices: 191 us -> 68.6 us
  other arithmetic: 68.3 us -> 3.72 us
  starting transfers between devices: 0.38 us -> 41.1 us
  matrix products: 32.8 us -> 0 us
  local copies, waits for them, and re-layouts: 20.9 us -> 3.64 us
  between operations: 13.8 us -> 0.85 us
  Pallas kernels: 0 us -> 9.7 us
    reduce_scatter x2 -> x0, waiting for transfers between devices: 71.6 us -> none  [the longest x1 44.3 us: on_device(): lax.psum_scatter(back_partial.astype(jnp.bfloat16), 'row', scatter_dimens...]
    ppermute x0 -> x34, waiting for transfers between devices: none -> 68.6 us  [swap(): return lax.ppermute(x, axis, [(i, i ^ m) for i in range(n)])]
    psum x1 -> x0, waiting for transfers between devices: 65.2 us -> none  [on_device(): weight_grad = lax.psum(weight_term, ('row', 'col'))]
    scatter-add x2 -> x0, other arithmetic: 61.9 us -> none  [the longest x1 37.9 us: on_device(): jax.ops.segment_sum(back_terms, cols, num_segments=col_blocks)]
    all_gather x2 -> x0, waiting for transfers between devices: 53.3 us -> none  [the longest x1 29.2 us: on_device(): panel = lax.all_gather(features, 'row', axis=0, tiled=True)]
    ppermute x0 -> x34, starting transfers between devices: none -> 41.1 us  [swap(): return lax.ppermute(x, axis, [(i, i ^ m) for i in range(n)])]
    dot_general x5 -> x0, matrix products: 32.8 us -> none  [the longest x1 13.9 us: on_device(): jnp.einsum('kij,kif->kjf', masked, back_blocks, preferred_element_type=jn...]
    gather x2 -> x0, local copies, waits for them, and re-layouts: 14.6 us -> none  [the longest x1 8.16 us: on_device(): blocks = panel.reshape(col_blocks, size, width)[cols]]
  transfers between devices with their start and end apart: 5 -> 34, of which waited for: 5 -> 17; matrix products, arithmetic and copies ran while one was open for 22% -> 4% of each run, Pallas kernels for 0% -> 1%
where the time goes in v1:
time: 130 us; the launch traced here: 128 us
  waiting for transfers between devices  68.6 us (53%)
  starting transfers between devices  41.1 us (32%)
  Pallas kernels  9.7 us (7%)
  other arithmetic  3.72 us (3%)
  local copies, waits for them, and re-layouts  3.64 us (3%)
    ppermute x34, waiting for transfers between devices, swap(): return lax.ppermute(x, axis, [(i, i ^ m) for i in range(n)])  68.6 us
    ppermute x34, starting transfers between devices, swap(): return lax.ppermute(x, axis, [(i, i ^ m) for i in range(n)])  41.1 us
    pallas_call x2, Pallas kernels, sparse_product(): pl.pallas_call(functools.partial(sparse_kernel, parts, outs, transposed),...  7.78 us
  transfers between devices with their start and end apart: 34, of which 17 were waited for; matrix products, arithmetic and copies ran while one was open for 4% of the time, Pallas kernels for 1%

profile of v1, /device:TPU:0, one launch (start us, length us, event | category | flops | bytes accessed | tf_op | source)
XLA Modules:
  0.0 127.6 jit_solution(7486192422169195141)
XLA Ops:
  0.6 0.0 copy-start.4
  0.6 3.0 %collective-permute-start.3 = (bf16[512,256]{1,0:T(8,128)(2,1)}, bf16[512,256]{1,0:T(8,128)(2,1)S(1)}, u32[]{:S(2)}, u32[]{:S(2)}) collective-permute-start(bf16[512,256]{1,0:T(8,128)(2,1)} %refs_0_.1), channel_id=1, source_target_pairs={{0,16},{4,20},{8,24},{12,28},{16,0},{20,4},{24,8},{28,12},{1,17},{... | collective-permute-start | bytes 786440 | tf_op jit(solution)/shard_map/ppermute | solution.py:204
  3.7 1.5 %collective-permute-start.1 = (bf16[512,256]{1,0:T(8,128)(2,1)}, bf16[512,256]{1,0:T(8,128)(2,1)S(1)}, u32[]{:S(2)}, u32[]{:S(2)}) collective-permute-start(bf16[512,256]{1,0:T(8,128)(2,1)} %refs_0_.1), channel_id=1, source_target_pairs={{0,8},{4,12},{8,0},{12,4},{16,24},{20,28},{24,16},{28,20},{1,9},{5... | collective-permute-start | bytes 786440 | tf_op jit(solution)/shard_map/ppermute | solution.py:204
  5.2 0.1 collective-permute-start.5
  5.2 0.0 collective-permute-start
  5.2 5.0 %collective-permute-done.3.refs_4_ = bf16[512,256]{1,0:T(8,128)(2,1)S(1)} collective-permute-done((bf16[512,256]{1,0:T(8,128)(2,1)}, bf16[512,256]{1,0:T(8,128)(2,1)S(1)}, u32[]{:S(2)}, u32[]{:S(2)}) %collective-permute-start.3) | collective-permute-done | bytes 262176 | tf_op jit(solution)/shard_map/ppermute | solution.py:204
  10.2 0.0 collective-permute-start.4
  10.2 2.9 %collective-permute-done.1.refs_2_ = bf16[512,256]{1,0:T(8,128)(2,1)S(1)} collective-permute-done((bf16[512,256]{1,0:T(8,128)(2,1)}, bf16[512,256]{1,0:T(8,128)(2,1)S(1)}, u32[]{:S(2)}, u32[]{:S(2)}) %collective-permute-start.1) | collective-permute-done | bytes 262176 | tf_op jit(solution)/shard_map/ppermute | solution.py:204
  13.1 3.9 %collective-permute-done.5.refs_6_ = bf16[512,256]{1,0:T(8,128)(2,1)S(1)} collective-permute-done((bf16[512,256]{1,0:T(8,128)(2,1)}, bf16[512,256]{1,0:T(8,128)(2,1)S(1)}, u32[]{:S(2)}, u32[]{:S(2)}) %collective-permute-start.5) | collective-permute-done | bytes 262176 | tf_op jit(solution)/shard_map/ppermute | solution.py:204
  17.1 0.7 slice_bitcast_fusion
  17.8 1.2 slice.10
  19.0 0.7 pad_add_fusion.meta
  19.7 0.1 convert_reduce_fusion.to
  19.8 0.0 collective-permute-done.refs_1_
  19.8 0.0 collective-permute-done.4.refs_5_
  19.8 0.0 collective-permute-done.2.refs_3_
  19.8 0.0 copy-start
  19.9 0.9 copy-done
  20.8 0.7 copy-done.3
  21.5 3.8 %shard_map.85 = (bf16[512,256]{1,0:T(8,128)(2,1)S(1)}, bf16[512,256]{1,0:T(8,128)(2,1)S(1)}, bf16[512,256]{1,0:T(8,128)(2,1)S(1)}, bf16[512,256]{1,0:T(8,128)(2,1)S(1)}) custom-call(s32[3]{0:T(128)S(1)} %pad_add_fusion.meta, s32[128]{0:T(128)S(1)} %convert_reduce_fusion.to, s32[128]{0:T(128)S(1)} %bitcast.9, bf16[512,256]{1,0:T(8,128)(2,1)S(1)} %copy-done, ...), custom_call_target="tpu_custom_call" | custom-call | flops 1073741824 | bytes 6291456 | tf_op jit(solution)/shard_map/pallas_call | solution.py:94
  25.2 2.1 %collective-permute-start.7 = (bf16[512,256]{1,0:T(8,128)(2,1)S(1)}, bf16[512,256]{1,0:T(8,128)(2,1)S(1)}, u32[]{:S(2)}, u32[]{:S(2)}) collective-permute-start(bf16[512,256]{1,0:T(8,128)(2,1)S(1)} %get-tuple-element.26), channel_id=1, source_target_pairs={{0,1},{1,0},{2,3},{3,2},{4,5},{5,4},{6,7},{7,6},{8,9},{9,8},{10,11... | collective-permute-start | bytes 786440 | tf_op jit(solution)/shard_map/ppermute | solution.py:204
  27.3 3.8 %collective-permute-start.8 = (bf16[512,256]{1,0:T(8,128)(2,1)S(1)}, bf16[512,256]{1,0:T(8,128)(2,1)S(1)}, u32[]{:S(2)}, u32[]{:S(2)}) collective-permute-start(bf16[512,256]{1,0:T(8,128)(2,1)S(1)} %get-tuple-element.27), channel_id=1, source_target_pairs={{0,2},{1,3},{2,0},{3,1},{4,6},{5,7},{6,4},{7,5},{8,10},{9,11},{10,... | collective-permute-start | bytes 786440 | tf_op jit(solution)/shard_map/ppermute | solution.py:204
  31.1 1.4 %collective-permute-start.9 = (bf16[512,256]{1,0:T(8,128)(2,1)S(1)}, bf16[512,256]{1,0:T(8,128)(2,1)S(1)}, u32[]{:S(2)}, u32[]{:S(2)}) collective-permute-start(bf16[512,256]{1,0:T(8,128)(2,1)S(1)} %get-tuple-element.28), channel_id=1, source_target_pairs={{0,3},{1,2},{2,1},{3,0},{4,7},{5,6},{6,5},{7,4},{8,11},{9,10},{10,... | collective-permute-start | bytes 786440 | tf_op jit(solution)/shard_map/ppermute | solution.py:204
  32.5 5.9 %collective-permute-done.7.refs_1_ = bf16[512,256]{1,0:T(8,128)(2,1)S(1)} collective-permute-done((bf16[512,256]{1,0:T(8,128)(2,1)S(1)}, bf16[512,256]{1,0:T(8,128)(2,1)S(1)}, u32[]{:S(2)}, u32[]{:S(2)}) %collective-permute-start.7) | collective-permute-done | bytes 262176 | tf_op jit(solution)/shard_map/ppermute | solution.py:204
  38.4 11.2 %collective-permute-done.8.refs_2_ = bf16[512,256]{1,0:T(8,128)(2,1)S(1)} collective-permute-done((bf16[512,256]{1,0:T(8,128)(2,1)S(1)}, bf16[512,256]{1,0:T(8,128)(2,1)S(1)}, u32[]{:S(2)}, u32[]{:S(2)}) %collective-permute-start.8) | collective-permute-done | bytes 262176 | tf_op jit(solution)/shard_map/ppermute | solution.py:204
  49.6 1.2 shard_map.86
  50.8 3.7 %collective-permute-start.12 = (bf16[512,256]{1,0:T(8,128)(2,1)S(1)}, bf16[512,256]{1,0:T(8,128)(2,1)S(1)}, u32[]{:S(2)}, u32[]{:S(2)}) collective-permute-start(bf16[512,256]{1,0:T(8,128)(2,1)S(1)} %get-tuple-element.30.refs_0_), channel_id=1, source_target_pairs={{0,3},{1,2},{2,1},{3,0},{4,7},{5,6},{6,5},{7,4},{8,11},{9,10},{10,... | collective-permute-start | bytes 786440 | tf_op jit(solution)/shard_map/ppermute | solution.py:204
  54.5 4.9 %collective-permute-start.11 = (bf16[512,256]{1,0:T(8,128)(2,1)S(1)}, bf16[512,256]{1,0:T(8,128)(2,1)S(1)}, u32[]{:S(2)}, u32[]{:S(2)}) collective-permute-start(bf16[512,256]{1,0:T(8,128)(2,1)S(1)} %get-tuple-element.30.refs_0_), channel_id=1, source_target_pairs={{0,2},{1,3},{2,0},{3,1},{4,6},{5,7},{6,4},{7,5},{8,10},{9,11},{10,... | collective-permute-start | bytes 786440 | tf_op jit(solution)/shard_map/ppermute | solution.py:204
  59.3 0.4 collective-permute-start.10
  59.8 0.7 pad_add_fusion.1.meta
  60.5 0.6 compare_select_fusion
  61.1 14.8 %collective-permute-done.11.refs_2_ = bf16[512,256]{1,0:T(8,128)(2,1)S(1)} collective-permute-done((bf16[512,256]{1,0:T(8,128)(2,1)S(1)}, bf16[512,256]{1,0:T(8,128)(2,1)S(1)}, u32[]{:S(2)}, u32[]{:S(2)}) %collective-permute-start.11) | collective-permute-done | bytes 262176 | tf_op jit(solution)/shard_map/ppermute | solution.py:204
  75.9 4.0 %shard_map.87 = (bf16[2048,256]{1,0:T(8,128)(2,1)S(1)}, bf16[2048,256]{1,0:T(8,128)(2,1)S(1)}) custom-call(s32[3]{0:T(128)S(1)} %pad_add_fusion.1.meta, s32[128]{0:T(128)S(1)} %get-tuple-element.49.to, s32[128]{0:T(128)S(1)} %get-tuple-element.50.source, bf16[512,256]{1,0:T(8,128)(2,1)S(1)} %get-tuple-element.30.refs_0_, ...), custom_call_target="tpu_custom_call" | custom-call | flops 1073741824 | bytes 5242880 | tf_op jit(solution)/shard_map/pallas_call | solution.py:94
  79.9 0.1 collective-permute-start.13
  79.9 0.4 shard_map.89
  80.4 0.6 collective-permute-start.17
  81.0 1.8 %collective-permute-start.18 = (f32[32,256]{1,0:T(8,128)S(1)}, f32[32,256]{1,0:T(8,128)S(1)}, u32[]{:S(2)}, u32[]{:S(2)}) collective-permute-start(f32[32,256]{1,0:T(8,128)S(1)} %get-tuple-element.41), channel_id=1, source_target_pairs={{0,8},{4,12},{8,0},{12,4},{16,24},{20,28},{24,16},{28,20},{1,9},{5... | collective-permute-start | bytes 98312 | tf_op jit(solution)/shard_map/ppermute | solution.py:204
  82.7 2.1 %collective-permute-start.20 = (f32[32,256]{1,0:T(8,128)S(1)}, f32[32,256]{1,0:T(8,128)S(1)}, u32[]{:S(2)}, u32[]{:S(2)}) collective-permute-start(f32[32,256]{1,0:T(8,128)S(1)} %get-tuple-element.43), channel_id=1, source_target_pairs={{0,16},{4,20},{8,24},{12,28},{16,0},{20,4},{24,8},{28,12},{1,17},{... | collective-permute-start | bytes 98312 | tf_op jit(solution)/shard_map/ppermute | solution.py:204
  84.8 0.0 collective-permute-done.18
  84.9 3.3 %collective-permute-start.22 = (f32[32,256]{1,0:T(8,128)S(1)}, f32[32,256]{1,0:T(8,128)S(1)}, u32[]{:S(2)}, u32[]{:S(2)}) collective-permute-start(f32[32,256]{1,0:T(8,128)S(1)} %get-tuple-element.45), channel_id=1, source_target_pairs={{0,24},{4,28},{8,16},{12,20},{16,8},{20,12},{24,0},{28,4},{1,25},{... | collective-permute-start | bytes 98312 | tf_op jit(solution)/shard_map/ppermute | solution.py:204
  88.2 0.3 collective-permute-done.21
  88.5 1.6 %collective-permute-done.22 = f32[32,256]{1,0:T(8,128)S(1)} collective-permute-done((f32[32,256]{1,0:T(8,128)S(1)}, f32[32,256]{1,0:T(8,128)S(1)}, u32[]{:S(2)}, u32[]{:S(2)}) %collective-permute-start.22) | collective-permute-done | bytes 32800 | tf_op jit(solution)/shard_map/ppermute | solution.py:204
  90.1 2.4 %collective-permute-done.23 = f32[32,256]{1,0:T(8,128)S(1)} collective-permute-done((f32[32,256]{1,0:T(8,128)S(1)}, f32[32,256]{1,0:T(8,128)S(1)}, u32[]{:S(2)}, u32[]{:S(2)}) %collective-permute-start.23) | collective-permute-done | bytes 32800 | tf_op jit(solution)/shard_map/ppermute | solution.py:204
  92.4 2.2 %collective-permute-start.26 = (f32[32,256]{1,0:T(8,128)S(1)}, f32[32,256]{1,0:T(8,128)S(1)}, u32[]{:S(2)}, u32[]{:S(2)}) collective-permute-start(f32[32,256]{1,0:T(8,128)S(1)} %add_add_fusion.1), channel_id=1, source_target_pairs={{0,3},{1,2},{2,1},{3,0},{4,7},{5,6},{6,5},{7,4},{8,11},{9,10},{10,... | collective-permute-start | bytes 98312 | tf_op jit(solution)/shard_map/ppermute | solution.py:204
  94.7 2.2 %collective-permute-start.24 = (f32[32,256]{1,0:T(8,128)S(1)}, f32[32,256]{1,0:T(8,128)}, u32[]{:S(2)}, u32[]{:S(2)}) collective-permute-start(f32[32,256]{1,0:T(8,128)S(1)} %add_add_fusion.1), channel_id=1, source_target_pairs={{0,1},{1,0},{2,3},{3,2},{4,5},{5,4},{6,7},{7,6},{8,9},{9,8},{10,11... | collective-permute-start | bytes 98312 | tf_op jit(solution)/shard_map/ppermute | solution.py:204
  96.9 1.3 %collective-permute-done.26 = f32[32,256]{1,0:T(8,128)S(1)} collective-permute-done((f32[32,256]{1,0:T(8,128)S(1)}, f32[32,256]{1,0:T(8,128)S(1)}, u32[]{:S(2)}, u32[]{:S(2)}) %collective-permute-start.26) | collective-permute-done | bytes 32800 | tf_op jit(solution)/shard_map/ppermute | solution.py:204
  98.2 1.2 collective-permute-done.25
  99.5 0.8 constant_dynamic-update-slice_fusion.7
  100.3 0.1 collective-permute-start.27
  100.4 1.5 %collective-permute-start.32 = (f32[32,256]{1,0:T(8,128)S(1)}, f32[32,256]{1,0:T(8,128)S(1)}, u32[]{:S(2)}, u32[]{:S(2)}) collective-permute-start(f32[32,256]{1,0:T(8,128)S(1)} %get-tuple-element.48), channel_id=1, source_target_pairs={{0,24},{4,28},{8,16},{12,20},{16,8},{20,12},{24,0},{28,4},{1,25},{... | collective-permute-start | bytes 98312 | tf_op jit(solution)/shard_map/ppermute | solution.py:204
  101.9 1.7 %collective-permute-start.30 = (f32[32,256]{1,0:T(8,128)S(1)}, f32[32,256]{1,0:T(8,128)S(1)}, u32[]{:S(2)}, u32[]{:S(2)}) collective-permute-start(f32[32,256]{1,0:T(8,128)S(1)} %get-tuple-element.48), channel_id=1, source_target_pairs={{0,16},{4,20},{8,24},{12,28},{16,0},{20,4},{24,8},{28,12},{1,17},{... | collective-permute-start | bytes 98312 | tf_op jit(solution)/shard_map/ppermute | solution.py:204
  103.6 1.0 collective-permute-start.28
  104.5 3.0 %collective-permute-done.28 = f32[32,256]{1,0:T(8,128)S(1)} collective-permute-done((f32[32,256]{1,0:T(8,128)S(1)}, f32[32,256]{1,0:T(8,128)S(1)}, u32[]{:S(2)}, u32[]{:S(2)}) %collective-permute-start.28) | collective-permute-done | bytes 32800 | tf_op jit(solution)/shard_map/ppermute | solution.py:204
  107.5 3.3 %collective-permute-done.29 = f32[32,256]{1,0:T(8,128)S(1)} collective-permute-done((f32[32,256]{1,0:T(8,128)S(1)}, f32[32,256]{1,0:T(8,128)S(1)}, u32[]{:S(2)}, u32[]{:S(2)}) %collective-permute-start.29) | collective-permute-done | bytes 32800 | tf_op jit(solution)/shard_map/ppermute | solution.py:204
  110.8 0.3 collective-permute-start.33
  111.2 0.2 shard_map.88
  111.4 1.4 %collective-permute-start.14 = (bf16[512,256]{1,0:T(8,128)(2,1)S(1)}, bf16[512,256]{1,0:T(8,128)(2,1)S(1)}, u32[]{:S(2)}, u32[]{:S(2)}) collective-permute-start(bf16[512,256]{1,0:T(8,128)(2,1)S(1)} %get-tuple-element.34), channel_id=1, source_target_pairs={{0,8},{4,12},{8,0},{12,4},{16,24},{20,28},{24,16},{28,20},{1,9},{5... | collective-permute-start | bytes 786440 | tf_op jit(solution)/shard_map/ppermute | solution.py:204
  112.8 0.8 collective-permute-start.15
  113.6 1.4 %collective-permute-start.16 = (bf16[512,256]{1,0:T(8,128)(2,1)S(1)}, bf16[512,256]{1,0:T(8,128)(2,1)S(1)}, u32[]{:S(2)}, u32[]{:S(2)}) collective-permute-start(bf16[512,256]{1,0:T(8,128)(2,1)S(1)} %get-tuple-element.36), channel_id=1, source_target_pairs={{0,24},{4,28},{8,16},{12,20},{16,8},{20,12},{24,0},{28,4},{1,25},{... | collective-permute-start | bytes 786440 | tf_op jit(solution)/shard_map/ppermute | solution.py:204
  115.0 0.1 collective-permute-done.33
  115.1 5.3 %collective-permute-done.14 = bf16[512,256]{1,0:T(8,128)(2,1)S(1)} collective-permute-done((bf16[512,256]{1,0:T(8,128)(2,1)S(1)}, bf16[512,256]{1,0:T(8,128)(2,1)S(1)}, u32[]{:S(2)}, u32[]{:S(2)}) %collective-permute-start.14) | collective-permute-done | bytes 262176 | tf_op jit(solution)/shard_map/ppermute | solution.py:204
  120.4 5.5 %collective-permute-done.15 = bf16[512,256]{1,0:T(8,128)(2,1)S(1)} collective-permute-done((bf16[512,256]{1,0:T(8,128)(2,1)S(1)}, bf16[512,256]{1,0:T(8,128)(2,1)S(1)}, u32[]{:S(2)}, u32[]{:S(2)}) %collective-permute-start.15) | collective-permute-done | bytes 262176 | tf_op jit(solution)/shard_map/ppermute | solution.py:204
  125.9 0.9 collective-permute-done.16
  126.8 0.8 add_convert_fusion
  (38 shorter events, 0.1 us)
Async XLA Ops:
  0.6 59.8 %copy-start.4 = (s32[1,1,128]{2,1,0:T(1,128)S(1)}, s32[1,1,128]{2,1,0:T(1,128)}, u32[]{:S(2)}) copy-start(s32[1,1,128]{2,1,0:T(1,128)} %param.8) | copy-start | bytes 1540
  0.6 9.6 %collective-permute-start.3 = (bf16[512,256]{1,0:T(8,128)(2,1)}, bf16[512,256]{1,0:T(8,128)(2,1)S(1)}, u32[]{:S(2)}, u32[]{:S(2)}) collective-permute-start(bf16[512,256]{1,0:T(8,128)(2,1)} %refs_0_.1), channel_id=1, source_target_pairs={{0,16},{4,20},{8,24},{12,28},{16,0},{20,4},{24,8},{28,12},{1,17},{... | collective-permute-start | bytes 786440 | tf_op jit(solution)/shard_map/ppermute | solution.py:204
  3.7 9.4 %collective-permute-start.1 = (bf16[512,256]{1,0:T(8,128)(2,1)}, bf16[512,256]{1,0:T(8,128)(2,1)S(1)}, u32[]{:S(2)}, u32[]{:S(2)}) collective-permute-start(bf16[512,256]{1,0:T(8,128)(2,1)} %refs_0_.1), channel_id=1, source_target_pairs={{0,8},{4,12},{8,0},{12,4},{16,24},{20,28},{24,16},{28,20},{1,9},{5... | collective-permute-start | bytes 786440 | tf_op jit(solution)/shard_map/ppermute | solution.py:204
  5.2 11.9 %collective-permute-start.5 = (bf16[512,256]{1,0:T(8,128)(2,1)}, bf16[512,256]{1,0:T(8,128)(2,1)S(1)}, u32[]{:S(2)}, u32[]{:S(2)}) collective-permute-start(bf16[512,256]{1,0:T(8,128)(2,1)} %refs_0_.1), channel_id=1, source_target_pairs={{0,24},{4,28},{8,16},{12,20},{16,8},{20,12},{24,0},{28,4},{1,25},{... | collective-permute-start | bytes 786440 | tf_op jit(solution)/shard_map/ppermute | solution.py:204
  5.2 14.6 %collective-permute-start = (bf16[512,256]{1,0:T(8,128)(2,1)}, bf16[512,256]{1,0:T(8,128)(2,1)S(1)}, u32[]{:S(2)}, u32[]{:S(2)}) collective-permute-start(bf16[512,256]{1,0:T(8,128)(2,1)} %refs_0_.1), channel_id=1, source_target_pairs={{0,4},{4,0},{8,12},{12,8},{16,20},{20,16},{24,28},{28,24},{1,5},{5... | collective-permute-start | bytes 786440 | tf_op jit(solution)/shard_map/ppermute | solution.py:204
  10.2 9.6 %collective-permute-start.4 = (bf16[512,256]{1,0:T(8,128)(2,1)S(1)}, bf16[512,256]{1,0:T(8,128)(2,1)S(1)}, u32[]{:S(2)}, u32[]{:S(2)}) collective-permute-start(bf16[512,256]{1,0:T(8,128)(2,1)S(1)} %collective-permute-done.3.refs_4_), channel_id=1, source_target_pairs={{0,4},{4,0},{8,12},{12,8},{16,20},{20,16},{24,28},{28,24},{1,5},{5... | collective-permute-start | bytes 786440 | tf_op jit(solution)/shard_map/ppermute | solution.py:204
  13.1 6.7 %collective-permute-start.2 = (bf16[512,256]{1,0:T(8,128)(2,1)S(1)}, bf16[512,256]{1,0:T(8,128)(2,1)S(1)}, u32[]{:S(2)}, u32[]{:S(2)}) collective-permute-start(bf16[512,256]{1,0:T(8,128)(2,1)S(1)} %collective-permute-done.1.refs_2_), channel_id=1, source_target_pairs={{0,4},{4,0},{8,12},{12,8},{16,20},{20,16},{24,28},{28,24},{1,5},{5... | collective-permute-start | bytes 786440 | tf_op jit(solution)/shard_map/ppermute | solution.py:204
  17.1 2.8 %collective-permute-start.6 = (bf16[512,256]{1,0:T(8,128)(2,1)S(1)}, bf16[512,256]{1,0:T(8,128)(2,1)S(1)}, u32[]{:S(2)}, u32[]{:S(2)}) collective-permute-start(bf16[512,256]{1,0:T(8,128)(2,1)S(1)} %collective-permute-done.5.refs_6_), channel_id=1, source_target_pairs={{0,4},{4,0},{8,12},{12,8},{16,20},{20,16},{24,28},{28,24},{1,5},{5... | collective-permute-start | bytes 786440 | tf_op jit(solution)/shard_map/ppermute | solution.py:204
  19.8 1.0 copy-start
  20.8 0.7 copy-start.3
  21.5 28.1 %copy-start.1 = (bf16[512,256]{1,0:T(8,128)(2,1)S(1)}, bf16[512,256]{1,0:T(8,128)(2,1)}, u32[]{:S(2)}) copy-start(bf16[512,256]{1,0:T(8,128)(2,1)} %refs_5_.1) | copy-start | bytes 786436
  21.5 28.1 %copy-start.2 = (bf16[256,256]{1,0:T(8,128)(2,1)S(1)}, bf16[256,256]{1,0:T(8,128)(2,1)}, u32[]{:S(2)}) copy-start(bf16[256,256]{1,0:T(8,128)(2,1)} %refs_4_.1) | copy-start | bytes 393220
  25.2 13.1 %collective-permute-start.7 = (bf16[512,256]{1,0:T(8,128)(2,1)S(1)}, bf16[512,256]{1,0:T(8,128)(2,1)S(1)}, u32[]{:S(2)}, u32[]{:S(2)}) collective-permute-start(bf16[512,256]{1,0:T(8,128)(2,1)S(1)} %get-tuple-element.26), channel_id=1, source_target_pairs={{0,1},{1,0},{2,3},{3,2},{4,5},{5,4},{6,7},{7,6},{8,9},{9,8},{10,11... | collective-permute-start | bytes 786440 | tf_op jit(solution)/shard_map/ppermute | solution.py:204
  27.3 22.2 %collective-permute-start.8 = (bf16[512,256]{1,0:T(8,128)(2,1)S(1)}, bf16[512,256]{1,0:T(8,128)(2,1)S(1)}, u32[]{:S(2)}, u32[]{:S(2)}) collective-permute-start(bf16[512,256]{1,0:T(8,128)(2,1)S(1)} %get-tuple-element.27), channel_id=1, source_target_pairs={{0,2},{1,3},{2,0},{3,1},{4,6},{5,7},{6,4},{7,5},{8,10},{9,11},{10,... | collective-permute-start | bytes 786440 | tf_op jit(solution)/shard_map/ppermute | solution.py:204
  31.1 18.5 %collective-permute-start.9 = (bf16[512,256]{1,0:T(8,128)(2,1)S(1)}, bf16[512,256]{1,0:T(8,128)(2,1)S(1)}, u32[]{:S(2)}, u32[]{:S(2)}) collective-permute-start(bf16[512,256]{1,0:T(8,128)(2,1)S(1)} %get-tuple-element.28), channel_id=1, source_target_pairs={{0,3},{1,2},{2,1},{3,0},{4,7},{5,6},{6,5},{7,4},{8,11},{9,10},{10,... | collective-permute-start | bytes 786440 | tf_op jit(solution)/shard_map/ppermute | solution.py:204
  50.8 10.3 %collective-permute-start.12 = (bf16[512,256]{1,0:T(8,128)(2,1)S(1)}, bf16[512,256]{1,0:T(8,128)(2,1)S(1)}, u32[]{:S(2)}, u32[]{:S(2)}) collective-permute-start(bf16[512,256]{1,0:T(8,128)(2,1)S(1)} %get-tuple-element.30.refs_0_), channel_id=1, source_target_pairs={{0,3},{1,2},{2,1},{3,0},{4,7},{5,6},{6,5},{7,4},{8,11},{9,10},{10,... | collective-permute-start | bytes 786440 | tf_op jit(solution)/shard_map/ppermute | solution.py:204
  54.5 21.4 %collective-permute-start.11 = (bf16[512,256]{1,0:T(8,128)(2,1)S(1)}, bf16[512,256]{1,0:T(8,128)(2,1)S(1)}, u32[]{:S(2)}, u32[]{:S(2)}) collective-permute-start(bf16[512,256]{1,0:T(8,128)(2,1)S(1)} %get-tuple-element.30.refs_0_), channel_id=1, source_target_pairs={{0,2},{1,3},{2,0},{3,1},{4,6},{5,7},{6,4},{7,5},{8,10},{9,11},{10,... | collective-permute-start | bytes 786440 | tf_op jit(solution)/shard_map/ppermute | solution.py:204
  59.3 16.5 %collective-permute-start.10 = (bf16[512,256]{1,0:T(8,128)(2,1)S(1)}, bf16[512,256]{1,0:T(8,128)(2,1)S(1)}, u32[]{:S(2)}, u32[]{:S(2)}) collective-permute-start(bf16[512,256]{1,0:T(8,128)(2,1)S(1)} %get-tuple-element.30.refs_0_), channel_id=1, source_target_pairs={{0,1},{1,0},{2,3},{3,2},{4,5},{5,4},{6,7},{7,6},{8,9},{9,8},{10,11... | collective-permute-start | bytes 786440 | tf_op jit(solution)/shard_map/ppermute | solution.py:204
  79.9 31.3 %collective-permute-start.13 = (bf16[2048,256]{1,0:T(8,128)(2,1)S(1)}, bf16[2048,256]{1,0:T(8,128)(2,1)S(1)}, u32[]{:S(2)}, u32[]{:S(2)}) collective-permute-start(bf16[2048,256]{1,0:T(8,128)(2,1)S(1)} %get-tuple-element.32), channel_id=1, source_target_pairs={{0,4},{4,0},{8,12},{12,8},{16,20},{20,16},{24,28},{28,24},{1,5},{5... | collective-permute-start | bytes 3145736 | tf_op jit(solution)/shard_map/ppermute | solution.py:204
  80.4 4.4 %collective-permute-start.17 = (f32[32,256]{1,0:T(8,128)S(1)}, f32[32,256]{1,0:T(8,128)S(1)}, u32[]{:S(2)}, u32[]{:S(2)}) collective-permute-start(f32[32,256]{1,0:T(8,128)S(1)} %get-tuple-element.40), channel_id=1, source_target_pairs={{0,4},{4,0},{8,12},{12,8},{16,20},{20,16},{24,28},{28,24},{1,5},{5... | collective-permute-start | bytes 98312 | tf_op jit(solution)/shard_map/ppermute | solution.py:204
  81.0 3.9 %collective-permute-start.18 = (f32[32,256]{1,0:T(8,128)S(1)}, f32[32,256]{1,0:T(8,128)S(1)}, u32[]{:S(2)}, u32[]{:S(2)}) collective-permute-start(f32[32,256]{1,0:T(8,128)S(1)} %get-tuple-element.41), channel_id=1, source_target_pairs={{0,8},{4,12},{8,0},{12,4},{16,24},{20,28},{24,16},{28,20},{1,9},{5... | collective-permute-start | bytes 98312 | tf_op jit(solution)/shard_map/ppermute | solution.py:204
  82.7 5.5 %collective-permute-start.19 = (f32[32,256]{1,0:T(8,128)S(1)}, f32[32,256]{1,0:T(8,128)S(1)}, u32[]{:S(2)}, u32[]{:S(2)}) collective-permute-start(f32[32,256]{1,0:T(8,128)S(1)} %get-tuple-element.42), channel_id=1, source_target_pairs={{0,12},{4,8},{8,4},{12,0},{16,28},{20,24},{24,20},{28,16},{1,13},{... | collective-permute-start | bytes 98312 | tf_op jit(solution)/shard_map/ppermute | solution.py:204
  82.7 5.5 %collective-permute-start.20 = (f32[32,256]{1,0:T(8,128)S(1)}, f32[32,256]{1,0:T(8,128)S(1)}, u32[]{:S(2)}, u32[]{:S(2)}) collective-permute-start(f32[32,256]{1,0:T(8,128)S(1)} %get-tuple-element.43), channel_id=1, source_target_pairs={{0,16},{4,20},{8,24},{12,28},{16,0},{20,4},{24,8},{28,12},{1,17},{... | collective-permute-start | bytes 98312 | tf_op jit(solution)/shard_map/ppermute | solution.py:204
  84.8 3.6 %collective-permute-start.21 = (f32[32,256]{1,0:T(8,128)S(1)}, f32[32,256]{1,0:T(8,128)S(1)}, u32[]{:S(2)}, u32[]{:S(2)}) collective-permute-start(f32[32,256]{1,0:T(8,128)S(1)} %get-tuple-element.44), channel_id=1, source_target_pairs={{0,20},{4,16},{8,28},{12,24},{16,4},{20,0},{24,12},{28,8},{1,21},{... | collective-permute-start | bytes 98312 | tf_op jit(solution)/shard_map/ppermute | solution.py:204
  84.9 5.2 %collective-permute-start.22 = (f32[32,256]{1,0:T(8,128)S(1)}, f32[32,256]{1,0:T(8,128)S(1)}, u32[]{:S(2)}, u32[]{:S(2)}) collective-permute-start(f32[32,256]{1,0:T(8,128)S(1)} %get-tuple-element.45), channel_id=1, source_target_pairs={{0,24},{4,28},{8,16},{12,20},{16,8},{20,12},{24,0},{28,4},{1,25},{... | collective-permute-start | bytes 98312 | tf_op jit(solution)/shard_map/ppermute | solution.py:204
  88.2 4.2 %collective-permute-start.23 = (f32[32,256]{1,0:T(8,128)S(1)}, f32[32,256]{1,0:T(8,128)S(1)}, u32[]{:S(2)}, u32[]{:S(2)}) collective-permute-start(f32[32,256]{1,0:T(8,128)S(1)} %get-tuple-element.46), channel_id=1, source_target_pairs={{0,28},{4,24},{8,20},{12,16},{16,12},{20,8},{24,4},{28,0},{1,29},{... | collective-permute-start | bytes 98312 | tf_op jit(solution)/shard_map/ppermute | solution.py:204
  92.4 5.8 %collective-permute-start.26 = (f32[32,256]{1,0:T(8,128)S(1)}, f32[32,256]{1,0:T(8,128)S(1)}, u32[]{:S(2)}, u32[]{:S(2)}) collective-permute-start(f32[32,256]{1,0:T(8,128)S(1)} %add_add_fusion.1), channel_id=1, source_target_pairs={{0,3},{1,2},{2,1},{3,0},{4,7},{5,6},{6,5},{7,4},{8,11},{9,10},{10,... | collective-permute-start | bytes 98312 | tf_op jit(solution)/shard_map/ppermute | solution.py:204
  94.7 4.8 %collective-permute-start.25 = (f32[32,256]{1,0:T(8,128)S(1)}, f32[32,256]{1,0:T(8,128)S(1)}, u32[]{:S(2)}, u32[]{:S(2)}) collective-permute-start(f32[32,256]{1,0:T(8,128)S(1)} %add_add_fusion.1), channel_id=1, source_target_pairs={{0,2},{1,3},{2,0},{3,1},{4,6},{5,7},{6,4},{7,5},{8,10},{9,11},{10,... | collective-permute-start | bytes 98312 | tf_op jit(solution)/shard_map/ppermute | solution.py:204
  94.7 4.8 %collective-permute-start.24 = (f32[32,256]{1,0:T(8,128)S(1)}, f32[32,256]{1,0:T(8,128)}, u32[]{:S(2)}, u32[]{:S(2)}) collective-permute-start(f32[32,256]{1,0:T(8,128)S(1)} %add_add_fusion.1), channel_id=1, source_target_pairs={{0,1},{1,0},{2,3},{3,2},{4,5},{5,4},{6,7},{7,6},{8,9},{9,8},{10,11... | collective-permute-start | bytes 98312 | tf_op jit(solution)/shard_map/ppermute | solution.py:204
  100.3 3.3 %collective-permute-start.27 = (f32[32,256]{1,0:T(8,128)S(1)}, f32[32,256]{1,0:T(8,128)S(1)}, u32[]{:S(2)}, u32[]{:S(2)}) collective-permute-start(f32[32,256]{1,0:T(8,128)S(1)} %get-tuple-element.48), channel_id=1, source_target_pairs={{0,4},{4,0},{8,12},{12,8},{16,20},{20,16},{24,28},{28,24},{1,5},{5... | collective-permute-start | bytes 98312 | tf_op jit(solution)/shard_map/ppermute | solution.py:204
  100.4 14.6 %collective-permute-start.32 = (f32[32,256]{1,0:T(8,128)S(1)}, f32[32,256]{1,0:T(8,128)S(1)}, u32[]{:S(2)}, u32[]{:S(2)}) collective-permute-start(f32[32,256]{1,0:T(8,128)S(1)} %get-tuple-element.48), channel_id=1, source_target_pairs={{0,24},{4,28},{8,16},{12,20},{16,8},{20,12},{24,0},{28,4},{1,25},{... | collective-permute-start | bytes 98312 | tf_op jit(solution)/shard_map/ppermute | solution.py:204
  101.9 11.7 %collective-permute-start.31 = (f32[32,256]{1,0:T(8,128)S(1)}, f32[32,256]{1,0:T(8,128)S(1)}, u32[]{:S(2)}, u32[]{:S(2)}) collective-permute-start(f32[32,256]{1,0:T(8,128)S(1)} %get-tuple-element.48), channel_id=1, source_target_pairs={{0,20},{4,16},{8,28},{12,24},{16,4},{20,0},{24,12},{28,8},{1,21},{... | collective-permute-start | bytes 98312 | tf_op jit(solution)/shard_map/ppermute | solution.py:204
  101.9 9.3 %collective-permute-start.30 = (f32[32,256]{1,0:T(8,128)S(1)}, f32[32,256]{1,0:T(8,128)S(1)}, u32[]{:S(2)}, u32[]{:S(2)}) collective-permute-start(f32[32,256]{1,0:T(8,128)S(1)} %get-tuple-element.48), channel_id=1, source_target_pairs={{0,16},{4,20},{8,24},{12,28},{16,0},{20,4},{24,8},{28,12},{1,17},{... | collective-permute-start | bytes 98312 | tf_op jit(solution)/shard_map/ppermute | solution.py:204
  103.6 3.9 %collective-permute-start.28 = (f32[32,256]{1,0:T(8,128)S(1)}, f32[32,256]{1,0:T(8,128)S(1)}, u32[]{:S(2)}, u32[]{:S(2)}) collective-permute-start(f32[32,256]{1,0:T(8,128)S(1)} %get-tuple-element.48), channel_id=1, source_target_pairs={{0,8},{4,12},{8,0},{12,4},{16,24},{20,28},{24,16},{28,20},{1,9},{5... | collective-permute-start | bytes 98312 | tf_op jit(solution)/shard_map/ppermute | solution.py:204
  107.5 3.3 %collective-permute-start.29 = (f32[32,256]{1,0:T(8,128)S(1)}, f32[32,256]{1,0:T(8,128)S(1)}, u32[]{:S(2)}, u32[]{:S(2)}) collective-permute-start(f32[32,256]{1,0:T(8,128)S(1)} %get-tuple-element.48), channel_id=1, source_target_pairs={{0,12},{4,8},{8,4},{12,0},{16,28},{20,24},{24,20},{28,16},{1,13},{... | collective-permute-start | bytes 98312 | tf_op jit(solution)/shard_map/ppermute | solution.py:204
  110.8 4.2 %collective-permute-start.33 = (f32[32,256]{1,0:T(8,128)S(1)}, f32[32,256]{1,0:T(8,128)S(1)}, u32[]{:S(2)}, u32[]{:S(2)}) collective-permute-start(f32[32,256]{1,0:T(8,128)S(1)} %get-tuple-element.48), channel_id=1, source_target_pairs={{0,28},{4,24},{8,20},{12,16},{16,12},{20,8},{24,4},{28,0},{1,29},{... | collective-permute-start | bytes 98312 | tf_op jit(solution)/shard_map/ppermute | solution.py:204
  111.4 8.9 %collective-permute-start.14 = (bf16[512,256]{1,0:T(8,128)(2,1)S(1)}, bf16[512,256]{1,0:T(8,128)(2,1)S(1)}, u32[]{:S(2)}, u32[]{:S(2)}) collective-permute-start(bf16[512,256]{1,0:T(8,128)(2,1)S(1)} %get-tuple-element.34), channel_id=1, source_target_pairs={{0,8},{4,12},{8,0},{12,4},{16,24},{20,28},{24,16},{28,20},{1,9},{5... | collective-permute-start | bytes 786440 | tf_op jit(solution)/shard_map/ppermute | solution.py:204
  112.8 13.1 %collective-permute-start.15 = (bf16[512,256]{1,0:T(8,128)(2,1)S(1)}, bf16[512,256]{1,0:T(8,128)(2,1)S(1)}, u32[]{:S(2)}, u32[]{:S(2)}) collective-permute-start(bf16[512,256]{1,0:T(8,128)(2,1)S(1)} %get-tuple-element.35), channel_id=1, source_target_pairs={{0,16},{4,20},{8,24},{12,28},{16,0},{20,4},{24,8},{28,12},{1,17},{... | collective-permute-start | bytes 786440 | tf_op jit(solution)/shard_map/ppermute | solution.py:204
  113.6 13.2 %collective-permute-start.16 = (bf16[512,256]{1,0:T(8,128)(2,1)S(1)}, bf16[512,256]{1,0:T(8,128)(2,1)S(1)}, u32[]{:S(2)}, u32[]{:S(2)}) collective-permute-start(bf16[512,256]{1,0:T(8,128)(2,1)S(1)} %get-tuple-element.36), channel_id=1, source_target_pairs={{0,24},{4,28},{8,16},{12,20},{16,8},{20,12},{24,0},{28,4},{1,25},{... | collective-permute-start | bytes 786440 | tf_op jit(solution)/shard_map/ppermute | solution.py:204
  115.1 12.5 %copy-start.5 = (f32[256,256]{1,0:T(8,128)}, f32[256,256]{1,0:T(8,128)S(1)}, u32[]{:S(2)}) copy-start(f32[256,256]{1,0:T(8,128)S(1)} %constant_dynamic-update-slice_fusion) | copy-start | bytes 786436

commit v2 on v1

--- a/solution.py
+++ b/solution.py
@@ -23,15 +23,58 @@
     return pl.CostEstimate(flops=flops, bytes_accessed=nbytes, transcendentals=0)
 
 
-def sparse_kernel(parts, outs, transposed, meta, to, source, *refs):
+def prepare_kernel(starts, cols, features, row_of, col_of, own):
+    own[...] = features[...]
+    slots = cols.shape[2]
+    row_blocks = starts.shape[2] - 1
+
+    def name_row(i, carry):
+        def name_slot(k, carry):
+            row_of[k] = i
+            return carry
+
+        return lax.fori_loop(starts[0, 0, i], starts[0, 0, i + 1], name_slot, carry)
+
+    lax.fori_loop(0, row_blocks, name_row, 0)
+    live = starts[0, 0, row_blocks]
+
+    def name_dead(k, carry):
+        row_of[k] = row_blocks
+        return carry
+
+    lax.fori_loop(live, slots, name_dead, 0)
+    row_of[slots] = live
+
+    def name_col(k, carry):
+        col_of[k] = cols[0, 0, k]
+        return carry
+
+    lax.fori_loop(0, slots, name_col, 0)
+
+
+def prepare(starts, cols, features):
+    slots = cols.shape[2]
+    return pl.pallas_call(
+        prepare_kernel,
+        out_shape=[
+            jax.ShapeDtypeStruct((slots + 1,), jnp.int32),
+            jax.ShapeDtypeStruct((slots,), jnp.int32),
+            jax.ShapeDtypeStruct(features.shape, BF16),
+        ],
+        in_specs=[SMEM, SMEM, VMEM],
+        out_specs=[SMEM, SMEM, VMEM],
+        compiler_params=params(32),
+    )(starts, cols, features)
+
+
+def sparse_kernel(parts, outs, backward, row_of, col_of, here_ref, mine_ref, *refs):
     panel_refs = refs[:parts]
     values_ref = refs[parts]
     out_refs = refs[parts + 1 : parts + 1 + len(outs)]
     panel, values, total, panel_sem, values_sem = refs[parts + 1 + len(outs) :]
-    live, here, mine = meta[0], meta[1], meta[2]
+    slots, size, _ = values.shape
+    live, here, mine = row_of[slots], here_ref[0], mine_ref[0]
     chunk = panel_refs[0].shape[0]
-    size = values.shape[1]
-    groups = values.shape[0] // GROUP
     loads = []
     for m in range(parts):
         start = pl.multiple_of((here ^ m) * chunk, chunk)
@@ -45,34 +88,33 @@
         span = pl.ds(pl.multiple_of(g * GROUP, GROUP), GROUP)
         return pltpu.make_async_copy(values_ref.at[span], values.at[span], values_sem.at[g])
 
-    used = (live + GROUP - 1) // GROUP
-
     def begin(g, carry):
         load(g).start()
         return carry
 
+    used = (live + GROUP - 1) // GROUP
     lax.fori_loop(0, used, begin, 0)
     total[...] = jnp.zeros_like(total)
     for copy in loads:
         copy.wait()
+    spare = total.shape[0] // size - 1
+    last = panel.shape[0] // size - 1
 
     def step(g, carry):
         load(g).wait()
         for u in range(GROUP):
             k = g * GROUP + u
-            i = pl.multiple_of(to[k] * size, size)
-            j = pl.multiple_of(source[k] * size, size)
-            block = values[k]
-            if transposed:
-                term = lax.dot_general(
-                    block,
-                    panel[pl.ds(j, size), :],
-                    (((0,), (0,)), ((), ())),
-                    preferred_element_type=F32,
-                )
-            else:
-                term = jnp.dot(block, panel[pl.ds(j, size), :], preferred_element_type=F32)
-            total[pl.ds(i, size), :] += term
+            row, col = row_of[k], col_of[k]
+            to, source = (col, jnp.minimum(row, last)) if backward else (row, col)
+            to = pl.multiple_of(jnp.where(k < live, to, spare) * size, size)
+            source = pl.multiple_of(source * size, size)
+            term = lax.dot_general(
+                values[k],
+                panel[pl.ds(source, size), :],
+                (((0 if backward else 1,), (0,)), ((), ())),
+                preferred_element_type=F32,
+            )
+            total[pl.ds(to, size), :] += term
         return carry
 
     lax.fori_loop(0, used, step, 0)
@@ -85,16 +127,15 @@
             )
 
 
-def sparse_product(panel_parts, values, meta, to, source, blocks, outs, transposed):
+def sparse_product(panel_parts, values, row_of, col_of, here, mine, blocks, outs, backward):
     parts = len(panel_parts)
     slots, size, _ = values.shape
     chunk, width = panel_parts[0].shape
-    rows = chunk
     flops = 2 * slots * size * size * width
     return pl.pallas_call(
-        functools.partial(sparse_kernel, parts, outs, transposed),
-        out_shape=[jax.ShapeDtypeStruct((rows * len(members), width), BF16) for members in outs],
-        in_specs=[SMEM] * 3 + [ANY] * (parts + 1),
+        functools.partial(sparse_kernel, parts, outs, backward),
+        out_shape=[jax.ShapeDtypeStruct((chunk * len(members), width), BF16) for members in outs],
+        in_specs=[SMEM] * 4 + [ANY] * (parts + 1),
         out_specs=[VMEM] * len(outs),
         scratch_shapes=[
             pltpu.VMEM((parts * chunk, width), BF16),
@@ -105,7 +146,7 @@
         ],
         compiler_params=params(48),
         cost_estimate=cost(flops, 2 * values.size + 2 * parts * chunk * width),
-    )(meta, to, source, *panel_parts, values)
+    )(row_of, col_of, here, mine, *panel_parts, values)
 
 
 def split(value):
@@ -153,32 +194,45 @@
     )(*terms, weight, cotangent)
 
 
-def weight_kernel(chunks, me, agg_ref, grad_ref, *outs):
+def weight_kernel(agg_ref, grad_ref, out_ref):
     high, low = split(agg_ref[...])
     grad_high, grad_low = split(grad_ref[...])
     contract = ((0,), (0,))
-    term = (
+    out_ref[...] = (
         mm(high, grad_high, contract) + mm(low, grad_high, contract) + mm(high, grad_low, contract)
     )
-    scratch = outs[-1]
-    scratch[...] = term
-    rows = term.shape[0] // chunks
-    for m in range(chunks):
-        start = pl.multiple_of((me[0] ^ m) * rows, rows)
-        outs[m][...] = scratch[pl.ds(start, rows), :]
-
-
-def weight_term(aggregated, mixed_grad, me, chunks):
+
+
+def weight_term(aggregated, mixed_grad):
     rows, width = aggregated.shape
     return pl.pallas_call(
-        functools.partial(weight_kernel, chunks),
-        out_shape=[jax.ShapeDtypeStruct((width // chunks, width), F32)] * chunks,
-        in_specs=[SMEM, VMEM, VMEM],
-        out_specs=[VMEM] * chunks,
-        scratch_shapes=[pltpu.VMEM((width, width), F32)],
+        weight_kernel,
+        out_shape=jax.ShapeDtypeStruct((width, width), F32),
+        in_specs=[VMEM, VMEM],
+        out_specs=VMEM,
         compiler_params=params(40),
         cost_estimate=cost(6 * rows * width * width, 8 * rows * width),
-    )(me, aggregated, mixed_grad)
+    )(aggregated, mixed_grad)
+
+
+def assemble_kernel(parts, me, *refs):
+    out_ref = refs[parts]
+    depth = refs[0].shape[0] // 2
+    for p in range(parts):
+        for core in range(2):
+            start = pl.multiple_of((me[0] ^ (2 * p + core)) * depth, depth)
+            out_ref[pl.ds(start, depth), :] = refs[p][core * depth : (core + 1) * depth, :]
+
+
+def assemble(parts, me):
+    depth, width = parts[0].shape
+    return pl.pallas_call(
+        functools.partial(assemble_kernel, len(parts)),
+        out_shape=jax.ShapeDtypeStruct((depth * len(parts), width), F32),
+        in_specs=[SMEM] + [VMEM] * len(parts),
+        out_specs=VMEM,
+        compiler_params=params(32),
+    )(me, *parts)
 
 
 def pair_kernel(count, own_ref, other_ref, *outs):
@@ -211,65 +265,52 @@
     return result
 
 
+def exchange(x, axis):
+    return lax.all_to_all(x, axis, 0, 0, tiled=True)
+
+
 def on_device(n_row, n_col, features, weight, block_cols, row_starts, block_values, cotangent):
     values = block_values[0, 0]
-    starts = row_starts[0, 0]
-    slots, size, _ = values.shape
-    row_blocks = starts.shape[0] - 1
+    size = values.shape[1]
+    row_blocks = row_starts.shape[2] - 1
     col_blocks = n_row * features.shape[0] // size
-    me_row = lax.axis_index("row")
-    me_col = lax.axis_index("col")
+    me_row = lax.axis_index("row")[None].astype(jnp.int32)
+    me_col = lax.axis_index("col")[None].astype(jnp.int32)
 
     panel = [features] + [None] * (n_row - 1)
     for m in range(2, n_row, 2):
         panel[m] = swap(features, "row", n_row, m)
+    prepared = prepare(row_starts, block_cols, features)
+    panel[2], (row_of, col_of, panel[0]) = lax.optimization_barrier((panel[2], prepared))
     for m in range(0, n_row, 2):
         panel[m + 1] = swap(panel[m], "row", n_row, 1)
 
-    index = jnp.arange(slots, dtype=jnp.int32)
-    rows = jnp.sum((starts[None, 1:] <= index[:, None]).astype(jnp.int32), axis=1)
-    live = starts[-1]
-    cols = block_cols[0, 0]
-    cols_to = jnp.where(index < live, cols, col_blocks)
-    rows_from = jnp.minimum(rows, row_blocks - 1)
-    meta = jnp.stack([live, me_row, me_col]).astype(jnp.int32)
-    meta_back = jnp.stack([live, me_col, me_row]).astype(jnp.int32)
-
-    terms = sparse_product(
-        panel, values, meta, rows, cols, row_blocks, [[m] for m in range(n_col)], False
-    )
+    each = [[m] for m in range(n_col)]
+    terms = sparse_product(panel, values, row_of, col_of, me_row, me_col, row_blocks, each, False)
     terms = [terms[0]] + [swap(terms[m], "col", n_col, m) for m in range(1, n_col)]
     activations, back, aggregated, mixed_grad = middle(terms, weight, cotangent)
 
     back_panel = [back] + [swap(back, "col", n_col, m) for m in range(1, n_col)]
 
-    pieces = weight_term(aggregated, mixed_grad, me_row[None].astype(jnp.int32), n_row)
-    piece = total_of([pieces[0]] + [swap(pieces[m], "row", n_row, m) for m in range(1, n_row)])
-    piece = total_of([piece] + [swap(piece, "col", n_col, m) for m in range(1, n_col)])
+    depth = weight.shape[0] // n_row
+    piece = exchange(weight_term(aggregated, mixed_grad), "row")
+    piece = jnp.sum(piece.reshape(n_row, depth, -1), axis=0)
+    piece = exchange(jnp.tile(piece, (n_col, 1)), "col")
+    piece = jnp.sum(piece.reshape(n_col, depth, -1), axis=0)
+    piece, back_panel[0] = lax.optimization_barrier((piece, back_panel[0]))
+    piece = jnp.concatenate([piece, swap(piece, "row", n_row, 1)])
+    gathered = [piece] + [swap(piece, "row", n_row, m) for m in range(2, n_row, 2)]
 
     even = list(range(0, n_row, 2))
+    pair = [even, [m + 1 for m in even]]
     own, other = sparse_product(
-        back_panel,
-        values,
-        meta_back,
-        cols_to,
-        rows_from,
-        col_blocks,
-        [even, [m + 1 for m in even]],
-        True,
+        back_panel, values, row_of, col_of, me_col, me_row, col_blocks, pair, True
     )
     sums = pair_sum(own, swap(other, "row", n_row, 1), len(even))
     feature_grad = total_of(
         [sums[0]] + [swap(s, "row", n_row, m) for s, m in zip(sums[1:], even[1:])]
     ).astype(BF16)
-
-    weight_grad = jnp.zeros(weight.shape, F32)
-    depth = weight.shape[0] // n_row
-    gathered = [piece] + [swap(piece, "row", n_row, m) for m in range(1, n_row)]
-    for m in range(n_row):
-        weight_grad = lax.dynamic_update_slice(
-            weight_grad, gathered[m], ((me_row ^ m) * depth, jnp.int32(0))
-        )
+    weight_grad = assemble(gathered, me_row)
     return (activations, feature_grad, weight_grad)
 
 

time: 130 us -> 118 us (0.908)
  waiting for transfers between devices: 68.6 us -> 41.1 us
  blocking collectives: 0 us -> 26 us
  starting transfers between devices: 41.1 us -> 31.3 us
  Pallas kernels: 9.7 us -> 14 us
  other arithmetic: 3.72 us -> 0.88 us
  local copies, waits for them, and re-layouts: 3.64 us -> 2.33 us
    ppermute x34 -> x21, waiting for transfers between devices: 68.6 us -> 40.8 us  [swap(): return lax.ppermute(x, axis, [(i, i ^ m) for i in range(n)])]
    all_to_all x0 -> x1, blocking collectives: none -> 26 us  [exchange(): return lax.all_to_all(x, axis, 0, 0, tiled=True)]
    ppermute x34 -> x21, starting transfers between devices: 41.1 us -> 26.5 us  [swap(): return lax.ppermute(x, axis, [(i, i ^ m) for i in range(n)])]
    all_to_all x0 -> x1, starting transfers between devices: none -> 4.79 us  [exchange(): return lax.all_to_all(x, axis, 0, 0, tiled=True)]
    pallas_call x3 -> x5, Pallas kernels: 8.23 us -> 12.5 us  [the longest x2 7.79 us: sparse_product(): pl.pallas_call(functools.partial(sparse_kernel, parts, outs, backward), o...]
    another operation x2 -> x0, other arithmetic: 1.38 us -> none  [the longest x1 0.69 us: on_device(): meta = jnp.stack([live, me_row, me_col]).astype(jnp.int32)]
  transfers between devices with their start and end apart: 34 -> 22, of which waited for: 17 -> 10; matrix products, arithmetic and copies ran while one was open for 4% -> 0% of each run, Pallas kernels for 1% -> 3%
where the time goes in v2:
time: 118 us; the launch traced here: 116 us
  waiting for transfers between devices  41.1 us (35%)
  starting transfers between devices  31.3 us (27%)
  blocking collectives  26 us (22%)
  Pallas kernels  14 us (12%)
  local copies, waits for them, and re-layouts  2.33 us (2%)
    ppermute x21, waiting for transfers between devices, swap(): return lax.ppermute(x, axis, [(i, i ^ m) for i in range(n)])  40.8 us
    ppermute x21, starting transfers between devices, swap(): return lax.ppermute(x, axis, [(i, i ^ m) for i in range(n)])  26.5 us
    all_to_all x1, blocking collectives, exchange(): return lax.all_to_all(x, axis, 0, 0, tiled=True)  26 us
    pallas_call x2, Pallas kernels, sparse_product(): pl.pallas_call(functools.partial(sparse_kernel, parts, outs, backward), o...  7.79 us
    all_to_all x1, starting transfers between devices, exchange(): return lax.all_to_all(x, axis, 0, 0, tiled=True)  4.79 us
    pallas_call x1, Pallas kernels, prepare(): pl.pallas_call(prepare_kernel, out_shape=[jax.ShapeDtypeStruct((slots + 1...  2.89 us
  transfers between devices with their start and end apart: 22, of which 10 were waited for; matrix products, arithmetic and copies ran while one was open for 0% of the time, Pallas kernels for 3%

profile of v2, /device:TPU:0, one launch (start us, length us, event | category | flops | bytes accessed | tf_op | source)
XLA Modules:
  0.0 116.4 jit_solution(9465522578913851554)
XLA Ops:
  0.6 3.0 %collective-permute-start = (bf16[512,256]{1,0:T(8,128)(2,1)}, bf16[512,256]{1,0:T(8,128)(2,1)S(1)}, u32[]{:S(2)}, u32[]{:S(2)}) collective-permute-start(bf16[512,256]{1,0:T(8,128)(2,1)} %features.1), channel_id=1, source_target_pairs={{0,8},{4,12},{8,0},{12,4},{16,24},{20,28},{24,16},{28,20},{1,9},{5... | collective-permute-start | bytes 786440 | tf_op jit(solution)/shard_map/ppermute | solution.py:258
  3.6 1.5 %collective-permute-start.3 = (bf16[512,256]{1,0:T(8,128)(2,1)}, bf16[512,256]{1,0:T(8,128)(2,1)S(1)}, u32[]{:S(2)}, u32[]{:S(2)}) collective-permute-start(bf16[512,256]{1,0:T(8,128)(2,1)} %features.1), channel_id=1, source_target_pairs={{0,16},{4,20},{8,24},{12,28},{16,0},{20,4},{24,8},{28,12},{1,17},{... | collective-permute-start | bytes 786440 | tf_op jit(solution)/shard_map/ppermute | solution.py:258
  5.2 0.0 collective-permute-start.5
  5.2 0.0 copy-start
  5.2 1.0 copy-done
  6.2 0.0 copy-start.3
  6.2 0.7 copy-done.3
  6.8 0.0 copy-start.4
  6.8 0.7 copy-done.4
  7.5 0.0 copy-start.1
  7.5 0.0 copy-start.2
  7.5 2.9 %shard_map.85 = (s32[129]{0:T(256)S(1)}, s32[128]{0:T(128)S(1)}, bf16[512,256]{1,0:T(8,128)(2,1)S(1)}) custom-call(s32[1,1,17]{2,1,0:T(1,128)S(1)} %copy-done.3, s32[1,1,128]{2,1,0:T(1,128)S(1)} %copy-done.4, bf16[512,256]{1,0:T(8,128)(2,1)S(1)} %copy-done), custom_call_target="tpu_custom_call" | custom-call | tf_op jit(solution)/shard_map/pallas_call | solution.py:57
  10.4 0.6 collective-permute-done.refs_2_
  11.0 0.0 collective-permute-start.1
  11.0 0.5 collective-permute-start.2
  11.5 5.7 %collective-permute-done.3.refs_4_ = bf16[512,256]{1,0:T(8,128)(2,1)S(1)} collective-permute-done((bf16[512,256]{1,0:T(8,128)(2,1)}, bf16[512,256]{1,0:T(8,128)(2,1)S(1)}, u32[]{:S(2)}, u32[]{:S(2)}) %collective-permute-start.3) | collective-permute-done | bytes 262176 | tf_op jit(solution)/shard_map/ppermute | solution.py:258
  17.2 0.0 collective-permute-start.4
  17.2 0.0 collective-permute-done.5.refs_6_
  17.2 0.5 collective-permute-start.6
  17.7 0.0 collective-permute-done.1.refs_1_
  17.7 0.0 collective-permute-done.2.refs_3_
  17.8 1.0 collective-permute-done.4.refs_5_
  18.8 0.4 collective-permute-done.6.refs_7_
  19.1 3.8 %shard_map.86 = (bf16[512,256]{1,0:T(8,128)(2,1)S(1)}, bf16[512,256]{1,0:T(8,128)(2,1)S(1)}, bf16[512,256]{1,0:T(8,128)(2,1)S(1)}, bf16[512,256]{1,0:T(8,128)(2,1)S(1)}) custom-call(s32[129]{0:T(256)S(1)} %get-tuple-element.29.row_of, s32[128]{0:T(128)S(1)} %get-tuple-element.30.col_of, s32[1]{0:T(128)} %bitcast.here_ref.mine_ref.me, ...), custom_call_target="tpu_custom_call" | custom-call | flops 1073741824 | bytes 6291456 | tf_op jit(solution)/shard_map/pallas_call | solution.py:135
  22.9 1.3 %collective-permute-start.7 = (bf16[512,256]{1,0:T(8,128)(2,1)S(1)}, bf16[512,256]{1,0:T(8,128)(2,1)S(1)}, u32[]{:S(2)}, u32[]{:S(2)}) collective-permute-start(bf16[512,256]{1,0:T(8,128)(2,1)S(1)} %get-tuple-element.34), channel_id=1, source_target_pairs={{0,1},{1,0},{2,3},{3,2},{4,5},{5,4},{6,7},{7,6},{8,9},{9,8},{10,11... | collective-permute-start | bytes 786440 | tf_op jit(solution)/shard_map/ppermute | solution.py:258
  24.3 3.5 %collective-permute-start.8 = (bf16[512,256]{1,0:T(8,128)(2,1)S(1)}, bf16[512,256]{1,0:T(8,128)(2,1)S(1)}, u32[]{:S(2)}, u32[]{:S(2)}) collective-permute-start(bf16[512,256]{1,0:T(8,128)(2,1)S(1)} %get-tuple-element.35), channel_id=1, source_target_pairs={{0,2},{1,3},{2,0},{3,1},{4,6},{5,7},{6,4},{7,5},{8,10},{9,11},{10,... | collective-permute-start | bytes 786440 | tf_op jit(solution)/shard_map/ppermute | solution.py:258
  27.8 0.0 collective-permute-start.9
  27.8 9.2 %collective-permute-done.7.refs_1_ = bf16[512,256]{1,0:T(8,128)(2,1)S(1)} collective-permute-done((bf16[512,256]{1,0:T(8,128)(2,1)S(1)}, bf16[512,256]{1,0:T(8,128)(2,1)S(1)}, u32[]{:S(2)}, u32[]{:S(2)}) %collective-permute-start.7) | collective-permute-done | bytes 262176 | tf_op jit(solution)/shard_map/ppermute | solution.py:258
  37.0 9.2 %collective-permute-done.8.refs_2_ = bf16[512,256]{1,0:T(8,128)(2,1)S(1)} collective-permute-done((bf16[512,256]{1,0:T(8,128)(2,1)S(1)}, bf16[512,256]{1,0:T(8,128)(2,1)S(1)}, u32[]{:S(2)}, u32[]{:S(2)}) %collective-permute-start.8) | collective-permute-done | bytes 262176 | tf_op jit(solution)/shard_map/ppermute | solution.py:258
  46.2 0.0 collective-permute-done.9.refs_3_
  46.2 0.0 copy-done.1
  46.2 0.0 copy-done.2
  46.2 1.2 %shard_map.87 = (bf16[512,256]{1,0:T(8,128)(2,1)}, bf16[512,256]{1,0:T(8,128)(2,1)S(1)}, f32[512,256]{1,0:T(8,128)S(1)}, f32[512,256]{1,0:T(8,128)S(1)}) custom-call(bf16[512,256]{1,0:T(8,128)(2,1)S(1)} %get-tuple-element.33.refs_0_, bf16[512,256]{1,0:T(8,128)(2,1)S(1)} %collective-permute-done.7.refs_1_, ...), custom_call_target="tpu_custom_call" | custom-call | flops 268435456 | bytes 2621440 | tf_op jit(solution)/shard_map/pallas_call | solution.py:182
  47.4 1.1 shard_map.88
  48.5 4.8 %all-to-all-start = ((f32[8,32,256]{2,1,0:T(8,128)}), f32[8,32,256]{2,1,0:T(8,128)S(1)}, u32[]{:S(2)}, u32[]{:S(2)}) async-start(f32[8,32,256]{2,1,0:T(8,128)} %bitcast.3), calls=%async_computation | async-start | bytes 524288 | tf_op jit(solution)/shard_map/all_to_all | solution.py:269
  53.3 4.1 %collective-permute-start.10 = (bf16[512,256]{1,0:T(8,128)(2,1)S(1)}, bf16[512,256]{1,0:T(8,128)(2,1)S(1)}, u32[]{:S(2)}, u32[]{:S(2)}) collective-permute-start(bf16[512,256]{1,0:T(8,128)(2,1)S(1)} %get-tuple-element.41.refs_0_), channel_id=1, source_target_pairs={{0,1},{1,0},{2,3},{3,2},{4,5},{5,4},{6,7},{7,6},{8,9},{9,8},{10,11... | collective-permute-start | bytes 786440 | tf_op jit(solution)/shard_map/ppermute | solution.py:258
  57.5 1.1 collective-permute-start.11
  58.5 1.4 %collective-permute-start.12 = (bf16[512,256]{1,0:T(8,128)(2,1)S(1)}, bf16[512,256]{1,0:T(8,128)(2,1)S(1)}, u32[]{:S(2)}, u32[]{:S(2)}) collective-permute-start(bf16[512,256]{1,0:T(8,128)(2,1)S(1)} %get-tuple-element.41.refs_0_), channel_id=1, source_target_pairs={{0,3},{1,2},{2,1},{3,0},{4,7},{5,6},{6,5},{7,4},{8,11},{9,10},{10,... | collective-permute-start | bytes 786440 | tf_op jit(solution)/shard_map/ppermute | solution.py:258
  59.9 0.3 all-to-all-done
  60.3 26.0 %all_to_all.15 = f32[4,32,256]{2,1,0:T(8,128)S(1)} all-to-all(f32[4,32,256]{2,1,0:T(8,128)S(1)} %tile.2), channel_id=1, replica_groups=mesh['row'=8,'col'=4] {'col'}, dimensions={0} | all-to-all | bytes 262144 | tf_op jit(solution)/shard_map/all_to_all | solution.py:269
  86.3 0.0 collective-permute-done.10.refs_1_
  86.4 0.0 collective-permute-done.11.refs_2_
  86.4 0.0 collective-permute-done.12.refs_3_
  86.4 4.0 %shard_map.89 = (bf16[2048,256]{1,0:T(8,128)(2,1)S(1)}, bf16[2048,256]{1,0:T(8,128)(2,1)S(1)}) custom-call(s32[129]{0:T(256)S(1)} %get-tuple-element.29.row_of, s32[128]{0:T(128)S(1)} %get-tuple-element.30.col_of, s32[1]{0:T(128)} %bitcast.1.mine_ref.here_ref, s32[1]{0:T(128)} %bitcast.here_ref.mine_ref.me, bf16[512,256]{1,0:T(8,128)(2,1)S(1)} %get-tuple-element.41.refs_0_, ...), custom_call_target="tpu_custom_call" | custom-call | flops 1073741824 | bytes 5242880 | tf_op jit(solution)/shard_map/pallas_call | solution.py:135
  90.4 0.1 collective-permute-start.13
  90.5 0.5 collective-permute-start.17
  91.0 2.1 %collective-permute-done.13.other_ref = bf16[2048,256]{1,0:T(8,128)(2,1)S(1)} collective-permute-done((bf16[2048,256]{1,0:T(8,128)(2,1)S(1)}, bf16[2048,256]{1,0:T(8,128)(2,1)S(1)}, u32[]{:S(2)}, u32[]{:S(2)}) %collective-permute-start.13) | collective-permute-done | bytes 1048608 | tf_op jit(solution)/shard_map/ppermute | solution.py:258
  93.1 0.2 shard_map.90
  93.4 2.3 %collective-permute-start.16 = (bf16[512,256]{1,0:T(8,128)(2,1)S(1)}, bf16[512,256]{1,0:T(8,128)(2,1)S(1)}, u32[]{:S(2)}, u32[]{:S(2)}) collective-permute-start(bf16[512,256]{1,0:T(8,128)(2,1)S(1)} %get-tuple-element.47), channel_id=1, source_target_pairs={{0,24},{4,28},{8,16},{12,20},{16,8},{20,12},{24,0},{28,4},{1,25},{... | collective-permute-start | bytes 786440 | tf_op jit(solution)/shard_map/ppermute | solution.py:258
  95.7 1.5 %collective-permute-start.15 = (bf16[512,256]{1,0:T(8,128)(2,1)S(1)}, bf16[512,256]{1,0:T(8,128)(2,1)S(1)}, u32[]{:S(2)}, u32[]{:S(2)}) collective-permute-start(bf16[512,256]{1,0:T(8,128)(2,1)S(1)} %get-tuple-element.46), channel_id=1, source_target_pairs={{0,16},{4,20},{8,24},{12,28},{16,0},{20,4},{24,8},{28,12},{1,17},{... | collective-permute-start | bytes 786440 | tf_op jit(solution)/shard_map/ppermute | solution.py:258
  97.2 0.0 collective-permute-start.14
  97.2 0.0 collective-permute-done.17
  97.3 2.1 %collective-permute-start.18 = (f32[64,256]{1,0:T(8,128)S(1)}, f32[64,256]{1,0:T(8,128)S(1)}, u32[]{:S(2)}, u32[]{:S(2)}) collective-permute-start(f32[64,256]{1,0:T(8,128)S(1)} %constant_dynamic-update-slice_fusion.refs_0_), channel_id=1, source_target_pairs={{0,8},{4,12},{8,0},{12,4},{16,24},{20,28},{24,16},{28,20},{1,9},{5... | collective-permute-start | bytes 196616 | tf_op jit(solution)/shard_map/ppermute | solution.py:258
  99.3 0.5 collective-permute-start.19
  99.8 9.8 %collective-permute-done.18.refs_1_ = f32[64,256]{1,0:T(8,128)S(1)} collective-permute-done((f32[64,256]{1,0:T(8,128)S(1)}, f32[64,256]{1,0:T(8,128)S(1)}, u32[]{:S(2)}, u32[]{:S(2)}) %collective-permute-start.18) | collective-permute-done | bytes 65568 | tf_op jit(solution)/shard_map/ppermute | solution.py:258
  109.6 2.5 %collective-permute-start.20 = (f32[64,256]{1,0:T(8,128)S(1)}, f32[64,256]{1,0:T(8,128)S(1)}, u32[]{:S(2)}, u32[]{:S(2)}) collective-permute-start(f32[64,256]{1,0:T(8,128)S(1)} %constant_dynamic-update-slice_fusion.refs_0_), channel_id=1, source_target_pairs={{0,24},{4,28},{8,16},{12,20},{16,8},{20,12},{24,0},{28,4},{1,25},{... | collective-permute-start | bytes 196616 | tf_op jit(solution)/shard_map/ppermute | solution.py:258
  112.1 0.0 collective-permute-done.19.refs_2_
  112.1 2.7 %collective-permute-done.20.refs_3_ = f32[64,256]{1,0:T(8,128)S(1)} collective-permute-done((f32[64,256]{1,0:T(8,128)S(1)}, f32[64,256]{1,0:T(8,128)S(1)}, u32[]{:S(2)}, u32[]{:S(2)}) %collective-permute-start.20) | collective-permute-done | bytes 65568 | tf_op jit(solution)/shard_map/ppermute | solution.py:258
  114.8 0.7 shard_map.91
  115.5 0.0 collective-permute-done.16
  115.5 0.0 collective-permute-done.15
  115.5 0.0 collective-permute-done.14
  115.5 0.8 add_convert_fusion
  (5 shorter events, 0.0 us)
Async XLA Ops:
  0.6 10.3 %collective-permute-start = (bf16[512,256]{1,0:T(8,128)(2,1)}, bf16[512,256]{1,0:T(8,128)(2,1)S(1)}, u32[]{:S(2)}, u32[]{:S(2)}) collective-permute-start(bf16[512,256]{1,0:T(8,128)(2,1)} %features.1), channel_id=1, source_target_pairs={{0,8},{4,12},{8,0},{12,4},{16,24},{20,28},{24,16},{28,20},{1,9},{5... | collective-permute-start | bytes 786440 | tf_op jit(solution)/shard_map/ppermute | solution.py:258
  3.6 13.6 %collective-permute-start.3 = (bf16[512,256]{1,0:T(8,128)(2,1)}, bf16[512,256]{1,0:T(8,128)(2,1)S(1)}, u32[]{:S(2)}, u32[]{:S(2)}) collective-permute-start(bf16[512,256]{1,0:T(8,128)(2,1)} %features.1), channel_id=1, source_target_pairs={{0,16},{4,20},{8,24},{12,28},{16,0},{20,4},{24,8},{28,12},{1,17},{... | collective-permute-start | bytes 786440 | tf_op jit(solution)/shard_map/ppermute | solution.py:258
  5.2 12.1 %collective-permute-start.5 = (bf16[512,256]{1,0:T(8,128)(2,1)}, bf16[512,256]{1,0:T(8,128)(2,1)S(1)}, u32[]{:S(2)}, u32[]{:S(2)}) collective-permute-start(bf16[512,256]{1,0:T(8,128)(2,1)} %features.1), channel_id=1, source_target_pairs={{0,24},{4,28},{8,16},{12,20},{16,8},{20,12},{24,0},{28,4},{1,25},{... | collective-permute-start | bytes 786440 | tf_op jit(solution)/shard_map/ppermute | solution.py:258
  5.2 1.0 copy-start
  6.2 0.7 copy-start.3
  6.8 0.7 copy-start.4
  7.5 38.7 %copy-start.1 = (bf16[512,256]{1,0:T(8,128)(2,1)S(1)}, bf16[512,256]{1,0:T(8,128)(2,1)}, u32[]{:S(2)}) copy-start(bf16[512,256]{1,0:T(8,128)(2,1)} %refs_5_.1) | copy-start | bytes 786436
  7.5 38.7 %copy-start.2 = (bf16[256,256]{1,0:T(8,128)(2,1)S(1)}, bf16[256,256]{1,0:T(8,128)(2,1)}, u32[]{:S(2)}) copy-start(bf16[256,256]{1,0:T(8,128)(2,1)} %refs_4_.1) | copy-start | bytes 393220
  11.0 6.8 %collective-permute-start.1 = (bf16[512,256]{1,0:T(8,128)(2,1)S(1)}, bf16[512,256]{1,0:T(8,128)(2,1)S(1)}, u32[]{:S(2)}, u32[]{:S(2)}) collective-permute-start(bf16[512,256]{1,0:T(8,128)(2,1)S(1)} %get-tuple-element.31.refs_0_), channel_id=1, source_target_pairs={{0,4},{4,0},{8,12},{12,8},{16,20},{20,16},{24,28},{28,24},{1,5},{5... | collective-permute-start | bytes 786440 | tf_op jit(solution)/shard_map/ppermute | solution.py:258
  11.0 6.8 %collective-permute-start.2 = (bf16[512,256]{1,0:T(8,128)(2,1)S(1)}, bf16[512,256]{1,0:T(8,128)(2,1)S(1)}, u32[]{:S(2)}, u32[]{:S(2)}) collective-permute-start(bf16[512,256]{1,0:T(8,128)(2,1)S(1)} %collective-permute-done.refs_2_), channel_id=1, source_target_pairs={{0,4},{4,0},{8,12},{12,8},{16,20},{20,16},{24,28},{28,24},{1,5},{5... | collective-permute-start | bytes 786440 | tf_op jit(solution)/shard_map/ppermute | solution.py:258
  17.2 1.5 %collective-permute-start.4 = (bf16[512,256]{1,0:T(8,128)(2,1)S(1)}, bf16[512,256]{1,0:T(8,128)(2,1)S(1)}, u32[]{:S(2)}, u32[]{:S(2)}) collective-permute-start(bf16[512,256]{1,0:T(8,128)(2,1)S(1)} %collective-permute-done.3.refs_4_), channel_id=1, source_target_pairs={{0,4},{4,0},{8,12},{12,8},{16,20},{20,16},{24,28},{28,24},{1,5},{5... | collective-permute-start | bytes 786440 | tf_op jit(solution)/shard_map/ppermute | solution.py:258
  17.2 1.9 %collective-permute-start.6 = (bf16[512,256]{1,0:T(8,128)(2,1)S(1)}, bf16[512,256]{1,0:T(8,128)(2,1)S(1)}, u32[]{:S(2)}, u32[]{:S(2)}) collective-permute-start(bf16[512,256]{1,0:T(8,128)(2,1)S(1)} %collective-permute-done.5.refs_6_), channel_id=1, source_target_pairs={{0,4},{4,0},{8,12},{12,8},{16,20},{20,16},{24,28},{28,24},{1,5},{5... | collective-permute-start | bytes 786440 | tf_op jit(solution)/shard_map/ppermute | solution.py:258
  22.9 14.0 %collective-permute-start.7 = (bf16[512,256]{1,0:T(8,128)(2,1)S(1)}, bf16[512,256]{1,0:T(8,128)(2,1)S(1)}, u32[]{:S(2)}, u32[]{:S(2)}) collective-permute-start(bf16[512,256]{1,0:T(8,128)(2,1)S(1)} %get-tuple-element.34), channel_id=1, source_target_pairs={{0,1},{1,0},{2,3},{3,2},{4,5},{5,4},{6,7},{7,6},{8,9},{9,8},{10,11... | collective-permute-start | bytes 786440 | tf_op jit(solution)/shard_map/ppermute | solution.py:258
  24.3 21.9 %collective-permute-start.8 = (bf16[512,256]{1,0:T(8,128)(2,1)S(1)}, bf16[512,256]{1,0:T(8,128)(2,1)S(1)}, u32[]{:S(2)}, u32[]{:S(2)}) collective-permute-start(bf16[512,256]{1,0:T(8,128)(2,1)S(1)} %get-tuple-element.35), channel_id=1, source_target_pairs={{0,2},{1,3},{2,0},{3,1},{4,6},{5,7},{6,4},{7,5},{8,10},{9,11},{10,... | collective-permute-start | bytes 786440 | tf_op jit(solution)/shard_map/ppermute | solution.py:258
  27.8 18.4 %collective-permute-start.9 = (bf16[512,256]{1,0:T(8,128)(2,1)S(1)}, bf16[512,256]{1,0:T(8,128)(2,1)S(1)}, u32[]{:S(2)}, u32[]{:S(2)}) collective-permute-start(bf16[512,256]{1,0:T(8,128)(2,1)S(1)} %get-tuple-element.36), channel_id=1, source_target_pairs={{0,3},{1,2},{2,1},{3,0},{4,7},{5,6},{6,5},{7,4},{8,11},{9,10},{10,... | collective-permute-start | bytes 786440 | tf_op jit(solution)/shard_map/ppermute | solution.py:258
  48.5 11.7 %all-to-all-start = ((f32[8,32,256]{2,1,0:T(8,128)}), f32[8,32,256]{2,1,0:T(8,128)S(1)}, u32[]{:S(2)}, u32[]{:S(2)}) async-start(f32[8,32,256]{2,1,0:T(8,128)} %bitcast.3), calls=%async_computation | async-start | bytes 524288 | tf_op jit(solution)/shard_map/all_to_all | solution.py:269
  53.3 33.0 %collective-permute-start.10 = (bf16[512,256]{1,0:T(8,128)(2,1)S(1)}, bf16[512,256]{1,0:T(8,128)(2,1)S(1)}, u32[]{:S(2)}, u32[]{:S(2)}) collective-permute-start(bf16[512,256]{1,0:T(8,128)(2,1)S(1)} %get-tuple-element.41.refs_0_), channel_id=1, source_target_pairs={{0,1},{1,0},{2,3},{3,2},{4,5},{5,4},{6,7},{7,6},{8,9},{9,8},{10,11... | collective-permute-start | bytes 786440 | tf_op jit(solution)/shard_map/ppermute | solution.py:258
  57.5 28.9 %collective-permute-start.11 = (bf16[512,256]{1,0:T(8,128)(2,1)S(1)}, bf16[512,256]{1,0:T(8,128)(2,1)S(1)}, u32[]{:S(2)}, u32[]{:S(2)}) collective-permute-start(bf16[512,256]{1,0:T(8,128)(2,1)S(1)} %get-tuple-element.41.refs_0_), channel_id=1, source_target_pairs={{0,2},{1,3},{2,0},{3,1},{4,6},{5,7},{6,4},{7,5},{8,10},{9,11},{10,... | collective-permute-start | bytes 786440 | tf_op jit(solution)/shard_map/ppermute | solution.py:258
  58.5 27.8 %collective-permute-start.12 = (bf16[512,256]{1,0:T(8,128)(2,1)S(1)}, bf16[512,256]{1,0:T(8,128)(2,1)S(1)}, u32[]{:S(2)}, u32[]{:S(2)}) collective-permute-start(bf16[512,256]{1,0:T(8,128)(2,1)S(1)} %get-tuple-element.41.refs_0_), channel_id=1, source_target_pairs={{0,3},{1,2},{2,1},{3,0},{4,7},{5,6},{6,5},{7,4},{8,11},{9,10},{10,... | collective-permute-start | bytes 786440 | tf_op jit(solution)/shard_map/ppermute | solution.py:258
  90.4 2.7 %collective-permute-start.13 = (bf16[2048,256]{1,0:T(8,128)(2,1)S(1)}, bf16[2048,256]{1,0:T(8,128)(2,1)S(1)}, u32[]{:S(2)}, u32[]{:S(2)}) collective-permute-start(bf16[2048,256]{1,0:T(8,128)(2,1)S(1)} %get-tuple-element.43), channel_id=1, source_target_pairs={{0,4},{4,0},{8,12},{12,8},{16,20},{20,16},{24,28},{28,24},{1,5},{5... | collective-permute-start | bytes 3145736 | tf_op jit(solution)/shard_map/ppermute | solution.py:258
  90.5 6.8 %collective-permute-start.17 = (f32[32,256]{1,0:T(8,128)S(1)}, f32[32,256]{1,0:T(8,128)S(1)}, u32[]{:S(2)}, u32[]{:S(2)}) collective-permute-start(f32[32,256]{1,0:T(8,128)S(1)} %reduce_sum.19), channel_id=1, source_target_pairs={{0,4},{4,0},{8,12},{12,8},{16,20},{20,16},{24,28},{28,24},{1,5},{5... | collective-permute-start | bytes 98312 | tf_op jit(solution)/shard_map/ppermute | solution.py:258
  93.4 22.1 %collective-permute-start.16 = (bf16[512,256]{1,0:T(8,128)(2,1)S(1)}, bf16[512,256]{1,0:T(8,128)(2,1)S(1)}, u32[]{:S(2)}, u32[]{:S(2)}) collective-permute-start(bf16[512,256]{1,0:T(8,128)(2,1)S(1)} %get-tuple-element.47), channel_id=1, source_target_pairs={{0,24},{4,28},{8,16},{12,20},{16,8},{20,12},{24,0},{28,4},{1,25},{... | collective-permute-start | bytes 786440 | tf_op jit(solution)/shard_map/ppermute | solution.py:258
  95.7 19.8 %collective-permute-start.15 = (bf16[512,256]{1,0:T(8,128)(2,1)S(1)}, bf16[512,256]{1,0:T(8,128)(2,1)S(1)}, u32[]{:S(2)}, u32[]{:S(2)}) collective-permute-start(bf16[512,256]{1,0:T(8,128)(2,1)S(1)} %get-tuple-element.46), channel_id=1, source_target_pairs={{0,16},{4,20},{8,24},{12,28},{16,0},{20,4},{24,8},{28,12},{1,17},{... | collective-permute-start | bytes 786440 | tf_op jit(solution)/shard_map/ppermute | solution.py:258
  97.2 18.3 %collective-permute-start.14 = (bf16[512,256]{1,0:T(8,128)(2,1)S(1)}, bf16[512,256]{1,0:T(8,128)(2,1)S(1)}, u32[]{:S(2)}, u32[]{:S(2)}) collective-permute-start(bf16[512,256]{1,0:T(8,128)(2,1)S(1)} %get-tuple-element.45), channel_id=1, source_target_pairs={{0,8},{4,12},{8,0},{12,4},{16,24},{20,28},{24,16},{28,20},{1,9},{5... | collective-permute-start | bytes 786440 | tf_op jit(solution)/shard_map/ppermute | solution.py:258
  97.3 12.4 %collective-permute-start.18 = (f32[64,256]{1,0:T(8,128)S(1)}, f32[64,256]{1,0:T(8,128)S(1)}, u32[]{:S(2)}, u32[]{:S(2)}) collective-permute-start(f32[64,256]{1,0:T(8,128)S(1)} %constant_dynamic-update-slice_fusion.refs_0_), channel_id=1, source_target_pairs={{0,8},{4,12},{8,0},{12,4},{16,24},{20,28},{24,16},{28,20},{1,9},{5... | collective-permute-start | bytes 196616 | tf_op jit(solution)/shard_map/ppermute | solution.py:258
  99.3 12.7 %collective-permute-start.19 = (f32[64,256]{1,0:T(8,128)S(1)}, f32[64,256]{1,0:T(8,128)S(1)}, u32[]{:S(2)}, u32[]{:S(2)}) collective-permute-start(f32[64,256]{1,0:T(8,128)S(1)} %constant_dynamic-update-slice_fusion.refs_0_), channel_id=1, source_target_pairs={{0,16},{4,20},{8,24},{12,28},{16,0},{20,4},{24,8},{28,12},{1,17},{... | collective-permute-start | bytes 196616 | tf_op jit(solution)/shard_map/ppermute | solution.py:258
  109.6 5.2 %collective-permute-start.20 = (f32[64,256]{1,0:T(8,128)S(1)}, f32[64,256]{1,0:T(8,128)S(1)}, u32[]{:S(2)}, u32[]{:S(2)}) collective-permute-start(f32[64,256]{1,0:T(8,128)S(1)} %constant_dynamic-update-slice_fusion.refs_0_), channel_id=1, source_target_pairs={{0,24},{4,28},{8,16},{12,20},{16,8},{20,12},{24,0},{28,4},{1,25},{... | collective-permute-start | bytes 196616 | tf_op jit(solution)/shard_map/ppermute | solution.py:258

commit v3 on v2

--- a/solution.py
+++ b/solution.py
@@ -295,9 +295,8 @@
     depth = weight.shape[0] // n_row
     piece = exchange(weight_term(aggregated, mixed_grad), "row")
     piece = jnp.sum(piece.reshape(n_row, depth, -1), axis=0)
-    piece = exchange(jnp.tile(piece, (n_col, 1)), "col")
-    piece = jnp.sum(piece.reshape(n_col, depth, -1), axis=0)
     piece, back_panel[0] = lax.optimization_barrier((piece, back_panel[0]))
+    piece = total_of([piece] + [swap(piece, "col", n_col, m) for m in range(1, n_col)])
     piece = jnp.concatenate([piece, swap(piece, "row", n_row, 1)])
     gathered = [piece] + [swap(piece, "row", n_row, m) for m in range(2, n_row, 2)]
 

time: 118 us -> 113 us (0.958)
  blocking collectives: 26 us -> 9.89 us
  waiting for transfers between devices: 41.1 us -> 51 us
  Pallas kernels: 14 us -> 19.6 us
  starting transfers between devices: 31.3 us -> 27 us
    all_to_all x1, blocking collectives: 26 us -> 9.89 us  [exchange(): return lax.all_to_all(x, axis, 0, 0, tiled=True)]
    ppermute x21 -> x24, waiting for transfers between devices: 40.8 us -> 51 us  [swap(): return lax.ppermute(x, axis, [(i, i ^ m) for i in range(n)])]
    pallas_call x2, Pallas kernels: 7.79 us -> 14.2 us  [sparse_product(): pl.pallas_call(functools.partial(sparse_kernel, parts, outs, backward), o...]
    all_to_all x1 -> x0, starting transfers between devices: 4.79 us -> none  [exchange(): return lax.all_to_all(x, axis, 0, 0, tiled=True)]
    ppermute x21 -> x24, starting transfers between devices: 26.5 us -> 27 us  [swap(): return lax.ppermute(x, axis, [(i, i ^ m) for i in range(n)])]
  transfers between devices with their start and end apart: 22 -> 24, of which waited for: 10 -> 11; matrix products, arithmetic and copies ran while one was open for 0% -> 0% of each run, Pallas kernels for 3% -> 4%
where the time goes in v3:
time: 113 us; the launch traced here: 111 us
  waiting for transfers between devices  51 us (45%)
  starting transfers between devices  27 us (24%)
  Pallas kernels  19.6 us (17%)
  blocking collectives  9.89 us (9%)
  local copies, waits for them, and re-layouts  2.31 us (2%)
    ppermute x24, waiting for transfers between devices, swap(): return lax.ppermute(x, axis, [(i, i ^ m) for i in range(n)])  51 us
    ppermute x24, starting transfers between devices, swap(): return lax.ppermute(x, axis, [(i, i ^ m) for i in range(n)])  27 us
    pallas_call x2, Pallas kernels, sparse_product(): pl.pallas_call(functools.partial(sparse_kernel, parts, outs, backward), o...  14.2 us
    all_to_all x1, blocking collectives, exchange(): return lax.all_to_all(x, axis, 0, 0, tiled=True)  9.89 us
    pallas_call x1, Pallas kernels, prepare(): pl.pallas_call(prepare_kernel, out_shape=[jax.ShapeDtypeStruct((slots + 1...  2.8 us
    unnamed x10, local copies, waits for them, and re-layouts  2.31 us
  transfers between devices with their start and end apart: 24, of which 11 were waited for; matrix products, arithmetic and copies ran while one was open for 0% of the time, Pallas kernels for 4%

profile of v3, /device:TPU:0, one launch (start us, length us, event | category | flops | bytes accessed | tf_op | source)
XLA Modules:
  0.0 111.4 jit_solution(16014095156512889227)
XLA Ops:
  0.6 3.0 %collective-permute-start = (bf16[512,256]{1,0:T(8,128)(2,1)}, bf16[512,256]{1,0:T(8,128)(2,1)S(1)}, u32[]{:S(2)}, u32[]{:S(2)}) collective-permute-start(bf16[512,256]{1,0:T(8,128)(2,1)} %features.1), channel_id=1, source_target_pairs={{0,8},{4,12},{8,0},{12,4},{16,24},{20,28},{24,16},{28,20},{1,9},{5... | collective-permute-start | bytes 786440 | tf_op jit(solution)/shard_map/ppermute | solution.py:258
  3.6 1.5 %collective-permute-start.3 = (bf16[512,256]{1,0:T(8,128)(2,1)}, bf16[512,256]{1,0:T(8,128)(2,1)S(1)}, u32[]{:S(2)}, u32[]{:S(2)}) collective-permute-start(bf16[512,256]{1,0:T(8,128)(2,1)} %features.1), channel_id=1, source_target_pairs={{0,16},{4,20},{8,24},{12,28},{16,0},{20,4},{24,8},{28,12},{1,17},{... | collective-permute-start | bytes 786440 | tf_op jit(solution)/shard_map/ppermute | solution.py:258
  5.2 0.0 collective-permute-start.5
  5.2 0.0 copy-start
  5.2 1.0 copy-done
  6.2 0.0 copy-start.3
  6.2 0.7 copy-done.3
  6.8 0.7 copy-done.4
  7.5 2.8 %shard_map.85 = (s32[129]{0:T(256)S(1)}, s32[128]{0:T(128)S(1)}, bf16[512,256]{1,0:T(8,128)(2,1)S(1)}) custom-call(s32[1,1,17]{2,1,0:T(1,128)S(1)} %copy-done.3, s32[1,1,128]{2,1,0:T(1,128)S(1)} %copy-done.4, bf16[512,256]{1,0:T(8,128)(2,1)S(1)} %copy-done), custom_call_target="tpu_custom_call" | custom-call | tf_op jit(solution)/shard_map/pallas_call | solution.py:57
  10.3 0.7 collective-permute-done.refs_2_
  11.0 0.0 collective-permute-start.1
  11.0 0.5 collective-permute-start.2
  11.5 5.7 %collective-permute-done.3.refs_4_ = bf16[512,256]{1,0:T(8,128)(2,1)S(1)} collective-permute-done((bf16[512,256]{1,0:T(8,128)(2,1)}, bf16[512,256]{1,0:T(8,128)(2,1)S(1)}, u32[]{:S(2)}, u32[]{:S(2)}) %collective-permute-start.3) | collective-permute-done | bytes 262176 | tf_op jit(solution)/shard_map/ppermute | solution.py:258
  17.2 0.0 collective-permute-start.4
  17.2 0.0 collective-permute-done.5.refs_6_
  17.2 0.5 collective-permute-start.6
  17.7 0.0 collective-permute-done.1.refs_1_
  17.7 0.0 collective-permute-done.2.refs_3_
  17.8 1.0 collective-permute-done.4.refs_5_
  18.8 0.4 collective-permute-done.6.refs_7_
  19.1 6.8 %shard_map.86 = (bf16[512,256]{1,0:T(8,128)(2,1)S(1)}, bf16[512,256]{1,0:T(8,128)(2,1)S(1)}, bf16[512,256]{1,0:T(8,128)(2,1)S(1)}, bf16[512,256]{1,0:T(8,128)(2,1)S(1)}) custom-call(s32[129]{0:T(256)S(1)} %get-tuple-element.29.row_of, s32[128]{0:T(128)S(1)} %get-tuple-element.30.col_of, s32[1]{0:T(128)} %bitcast.here_ref.mine_ref.me, ...), custom_call_target="tpu_custom_call" | custom-call | flops 1073741824 | bytes 6291456 | tf_op jit(solution)/shard_map/pallas_call | solution.py:135
  25.9 0.1 collective-permute-start.7
  26.0 1.8 %collective-permute-start.8 = (bf16[512,256]{1,0:T(8,128)(2,1)S(1)}, bf16[512,256]{1,0:T(8,128)(2,1)S(1)}, u32[]{:S(2)}, u32[]{:S(2)}) collective-permute-start(bf16[512,256]{1,0:T(8,128)(2,1)S(1)} %get-tuple-element.35), channel_id=1, source_target_pairs={{0,2},{1,3},{2,0},{3,1},{4,6},{5,7},{6,4},{7,5},{8,10},{9,11},{10,... | collective-permute-start | bytes 786440 | tf_op jit(solution)/shard_map/ppermute | solution.py:258
  27.8 2.6 %collective-permute-start.9 = (bf16[512,256]{1,0:T(8,128)(2,1)S(1)}, bf16[512,256]{1,0:T(8,128)(2,1)S(1)}, u32[]{:S(2)}, u32[]{:S(2)}) collective-permute-start(bf16[512,256]{1,0:T(8,128)(2,1)S(1)} %get-tuple-element.36), channel_id=1, source_target_pairs={{0,3},{1,2},{2,1},{3,0},{4,7},{5,6},{6,5},{7,4},{8,11},{9,10},{10,... | collective-permute-start | bytes 786440 | tf_op jit(solution)/shard_map/ppermute | solution.py:258
  30.4 5.6 %collective-permute-done.7.refs_1_ = bf16[512,256]{1,0:T(8,128)(2,1)S(1)} collective-permute-done((bf16[512,256]{1,0:T(8,128)(2,1)S(1)}, bf16[512,256]{1,0:T(8,128)(2,1)S(1)}, u32[]{:S(2)}, u32[]{:S(2)}) %collective-permute-start.7) | collective-permute-done | bytes 262176 | tf_op jit(solution)/shard_map/ppermute | solution.py:258
  36.0 11.5 %collective-permute-done.8.refs_2_ = bf16[512,256]{1,0:T(8,128)(2,1)S(1)} collective-permute-done((bf16[512,256]{1,0:T(8,128)(2,1)S(1)}, bf16[512,256]{1,0:T(8,128)(2,1)S(1)}, u32[]{:S(2)}, u32[]{:S(2)}) %collective-permute-start.8) | collective-permute-done | bytes 262176 | tf_op jit(solution)/shard_map/ppermute | solution.py:258
  47.4 0.0 collective-permute-done.9.refs_3_
  47.5 0.0 copy-done.1
  47.5 0.0 copy-done.2
  47.5 1.2 %shard_map.87 = (bf16[512,256]{1,0:T(8,128)(2,1)}, bf16[512,256]{1,0:T(8,128)(2,1)S(1)}, f32[512,256]{1,0:T(8,128)S(1)}, f32[512,256]{1,0:T(8,128)S(1)}) custom-call(bf16[512,256]{1,0:T(8,128)(2,1)S(1)} %get-tuple-element.33.refs_0_, bf16[512,256]{1,0:T(8,128)(2,1)S(1)} %collective-permute-done.7.refs_1_, ...), custom_call_target="tpu_custom_call" | custom-call | flops 268435456 | bytes 2621440 | tf_op jit(solution)/shard_map/pallas_call | solution.py:182
  48.7 3.8 %collective-permute-start.10 = (bf16[512,256]{1,0:T(8,128)(2,1)S(1)}, bf16[512,256]{1,0:T(8,128)(2,1)S(1)}, u32[]{:S(2)}, u32[]{:S(2)}) collective-permute-start(bf16[512,256]{1,0:T(8,128)(2,1)S(1)} %get-tuple-element.41.refs_0_), channel_id=1, source_target_pairs={{0,1},{1,0},{2,3},{3,2},{4,5},{5,4},{6,7},{7,6},{8,9},{9,8},{10,11... | collective-permute-start | bytes 786440 | tf_op jit(solution)/shard_map/ppermute | solution.py:258
  52.5 0.9 collective-permute-start.11
  53.5 1.5 %collective-permute-start.12 = (bf16[512,256]{1,0:T(8,128)(2,1)S(1)}, bf16[512,256]{1,0:T(8,128)(2,1)S(1)}, u32[]{:S(2)}, u32[]{:S(2)}) collective-permute-start(bf16[512,256]{1,0:T(8,128)(2,1)S(1)} %get-tuple-element.41.refs_0_), channel_id=1, source_target_pairs={{0,3},{1,2},{2,1},{3,0},{4,7},{5,6},{6,5},{7,4},{8,11},{9,10},{10,... | collective-permute-start | bytes 786440 | tf_op jit(solution)/shard_map/ppermute | solution.py:258
  54.9 0.4 shard_map.88
  55.4 9.9 %all_to_all.9 = f32[8,32,256]{2,1,0:T(8,128)S(1)} all-to-all(f32[8,32,256]{2,1,0:T(8,128)S(1)} %bitcast.4), channel_id=1, replica_groups=mesh['row'=8,'col'=4] {'row'}, dimensions={0} | all-to-all | bytes 524288 | tf_op jit(solution)/shard_map/all_to_all | solution.py:269
  65.3 0.0 collective-permute-done.10.refs_1_
  65.3 8.0 %collective-permute-done.11.refs_2_ = bf16[512,256]{1,0:T(8,128)(2,1)S(1)} collective-permute-done((bf16[512,256]{1,0:T(8,128)(2,1)S(1)}, bf16[512,256]{1,0:T(8,128)(2,1)S(1)}, u32[]{:S(2)}, u32[]{:S(2)}) %collective-permute-start.11) | collective-permute-done | bytes 262176 | tf_op jit(solution)/shard_map/ppermute | solution.py:258
  73.3 0.0 collective-permute-done.12.refs_3_
  73.3 7.4 %shard_map.89 = (bf16[2048,256]{1,0:T(8,128)(2,1)S(1)}, bf16[2048,256]{1,0:T(8,128)(2,1)S(1)}) custom-call(s32[129]{0:T(256)S(1)} %get-tuple-element.29.row_of, s32[128]{0:T(128)S(1)} %get-tuple-element.30.col_of, s32[1]{0:T(128)} %bitcast.1.mine_ref.here_ref, s32[1]{0:T(128)} %bitcast.here_ref.mine_ref.me, bf16[512,256]{1,0:T(8,128)(2,1)S(1)} %get-tuple-element.41.refs_0_, ...), custom_call_target="tpu_custom_call" | custom-call | flops 1073741824 | bytes 5242880 | tf_op jit(solution)/shard_map/pallas_call | solution.py:135
  80.7 0.1 collective-permute-start.13
  80.7 0.1 collective-permute-start.19
  80.8 1.9 %collective-permute-start.18 = (f32[32,256]{1,0:T(8,128)S(1)}, f32[32,256]{1,0:T(8,128)S(1)}, u32[]{:S(2)}, u32[]{:S(2)}) collective-permute-start(f32[32,256]{1,0:T(8,128)S(1)} %reduce_sum.9), channel_id=1, source_target_pairs={{0,2},{1,3},{2,0},{3,1},{4,6},{5,7},{6,4},{7,5},{8,10},{9,11},{10,... | collective-permute-start | bytes 98312 | tf_op jit(solution)/shard_map/ppermute | solution.py:258
  82.7 2.5 %collective-permute-start.17 = (f32[32,256]{1,0:T(8,128)S(1)}, f32[32,256]{1,0:T(8,128)S(1)}, u32[]{:S(2)}, u32[]{:S(2)}) collective-permute-start(f32[32,256]{1,0:T(8,128)S(1)} %reduce_sum.9), channel_id=1, source_target_pairs={{0,1},{1,0},{2,3},{3,2},{4,5},{5,4},{6,7},{7,6},{8,9},{9,8},{10,11... | collective-permute-start | bytes 98312 | tf_op jit(solution)/shard_map/ppermute | solution.py:258
  85.2 1.5 %collective-permute-done.19 = f32[32,256]{1,0:T(8,128)S(1)} collective-permute-done((f32[32,256]{1,0:T(8,128)S(1)}, f32[32,256]{1,0:T(8,128)S(1)}, u32[]{:S(2)}, u32[]{:S(2)}) %collective-permute-start.19) | collective-permute-done | bytes 32800 | tf_op jit(solution)/shard_map/ppermute | solution.py:258
  86.7 0.0 collective-permute-done.18
  86.7 0.4 collective-permute-done.17
  87.1 0.1 collective-permute-start.20
  87.2 0.0 collective-permute-done.13.other_ref
  87.2 0.2 shard_map.90
  87.5 1.8 %collective-permute-start.16 = (bf16[512,256]{1,0:T(8,128)(2,1)S(1)}, bf16[512,256]{1,0:T(8,128)(2,1)S(1)}, u32[]{:S(2)}, u32[]{:S(2)}) collective-permute-start(bf16[512,256]{1,0:T(8,128)(2,1)S(1)} %get-tuple-element.47), channel_id=1, source_target_pairs={{0,24},{4,28},{8,16},{12,20},{16,8},{20,12},{24,0},{28,4},{1,25},{... | collective-permute-start | bytes 786440 | tf_op jit(solution)/shard_map/ppermute | solution.py:258
  89.3 0.3 collective-permute-start.15
  89.6 1.5 %collective-permute-start.14 = (bf16[512,256]{1,0:T(8,128)(2,1)S(1)}, bf16[512,256]{1,0:T(8,128)(2,1)S(1)}, u32[]{:S(2)}, u32[]{:S(2)}) collective-permute-start(bf16[512,256]{1,0:T(8,128)(2,1)S(1)} %get-tuple-element.45), channel_id=1, source_target_pairs={{0,8},{4,12},{8,0},{12,4},{16,24},{20,28},{24,16},{28,20},{1,9},{5... | collective-permute-start | bytes 786440 | tf_op jit(solution)/shard_map/ppermute | solution.py:258
  91.0 0.0 collective-permute-done.20
  91.0 0.6 collective-permute-start.21
  91.7 1.7 %collective-permute-start.22 = (f32[64,256]{1,0:T(8,128)S(1)}, f32[64,256]{1,0:T(8,128)S(1)}, u32[]{:S(2)}, u32[]{:S(2)}) collective-permute-start(f32[64,256]{1,0:T(8,128)S(1)} %pad_maximum_fusion.refs_0_), channel_id=1, source_target_pairs={{0,16},{4,20},{8,24},{12,28},{16,0},{20,4},{24,8},{28,12},{1,17},{... | collective-permute-start | bytes 196616 | tf_op jit(solution)/shard_map/ppermute | solution.py:258
  93.4 11.3 %collective-permute-done.21.refs_1_ = f32[64,256]{1,0:T(8,128)S(1)} collective-permute-done((f32[64,256]{1,0:T(8,128)S(1)}, f32[64,256]{1,0:T(8,128)S(1)}, u32[]{:S(2)}, u32[]{:S(2)}) %collective-permute-start.21) | collective-permute-done | bytes 65568 | tf_op jit(solution)/shard_map/ppermute | solution.py:258
  104.7 0.3 collective-permute-start.23
  105.0 0.0 collective-permute-done.22.refs_2_
  105.0 4.9 %collective-permute-done.23.refs_3_ = f32[64,256]{1,0:T(8,128)S(1)} collective-permute-done((f32[64,256]{1,0:T(8,128)S(1)}, f32[64,256]{1,0:T(8,128)S(1)}, u32[]{:S(2)}, u32[]{:S(2)}) %collective-permute-start.23) | collective-permute-done | bytes 65568 | tf_op jit(solution)/shard_map/ppermute | solution.py:258
  109.8 0.7 shard_map.91
  110.6 0.0 collective-permute-done.16
  110.6 0.0 collective-permute-done.15
  110.6 0.0 collective-permute-done.14
  110.6 0.8 add_convert_fusion
  (6 shorter events, 0.0 us)
Async XLA Ops:
  0.6 10.3 %collective-permute-start = (bf16[512,256]{1,0:T(8,128)(2,1)}, bf16[512,256]{1,0:T(8,128)(2,1)S(1)}, u32[]{:S(2)}, u32[]{:S(2)}) collective-permute-start(bf16[512,256]{1,0:T(8,128)(2,1)} %features.1), channel_id=1, source_target_pairs={{0,8},{4,12},{8,0},{12,4},{16,24},{20,28},{24,16},{28,20},{1,9},{5... | collective-permute-start | bytes 786440 | tf_op jit(solution)/shard_map/ppermute | solution.py:258
  3.6 13.6 %collective-permute-start.3 = (bf16[512,256]{1,0:T(8,128)(2,1)}, bf16[512,256]{1,0:T(8,128)(2,1)S(1)}, u32[]{:S(2)}, u32[]{:S(2)}) collective-permute-start(bf16[512,256]{1,0:T(8,128)(2,1)} %features.1), channel_id=1, source_target_pairs={{0,16},{4,20},{8,24},{12,28},{16,0},{20,4},{24,8},{28,12},{1,17},{... | collective-permute-start | bytes 786440 | tf_op jit(solution)/shard_map/ppermute | solution.py:258
  5.2 12.1 %collective-permute-start.5 = (bf16[512,256]{1,0:T(8,128)(2,1)}, bf16[512,256]{1,0:T(8,128)(2,1)S(1)}, u32[]{:S(2)}, u32[]{:S(2)}) collective-permute-start(bf16[512,256]{1,0:T(8,128)(2,1)} %features.1), channel_id=1, source_target_pairs={{0,24},{4,28},{8,16},{12,20},{16,8},{20,12},{24,0},{28,4},{1,25},{... | collective-permute-start | bytes 786440 | tf_op jit(solution)/shard_map/ppermute | solution.py:258
  5.2 1.0 copy-start
  6.2 0.7 copy-start.3
  6.8 0.7 copy-start.4
  7.5 40.0 %copy-start.1 = (bf16[512,256]{1,0:T(8,128)(2,1)S(1)}, bf16[512,256]{1,0:T(8,128)(2,1)}, u32[]{:S(2)}) copy-start(bf16[512,256]{1,0:T(8,128)(2,1)} %refs_5_.1) | copy-start | bytes 786436
  7.5 40.0 %copy-start.2 = (bf16[256,256]{1,0:T(8,128)(2,1)S(1)}, bf16[256,256]{1,0:T(8,128)(2,1)}, u32[]{:S(2)}) copy-start(bf16[256,256]{1,0:T(8,128)(2,1)} %refs_4_.1) | copy-start | bytes 393220
  11.0 6.8 %collective-permute-start.1 = (bf16[512,256]{1,0:T(8,128)(2,1)S(1)}, bf16[512,256]{1,0:T(8,128)(2,1)S(1)}, u32[]{:S(2)}, u32[]{:S(2)}) collective-permute-start(bf16[512,256]{1,0:T(8,128)(2,1)S(1)} %get-tuple-element.31.refs_0_), channel_id=1, source_target_pairs={{0,4},{4,0},{8,12},{12,8},{16,20},{20,16},{24,28},{28,24},{1,5},{5... | collective-permute-start | bytes 786440 | tf_op jit(solution)/shard_map/ppermute | solution.py:258
  11.0 6.8 %collective-permute-start.2 = (bf16[512,256]{1,0:T(8,128)(2,1)S(1)}, bf16[512,256]{1,0:T(8,128)(2,1)S(1)}, u32[]{:S(2)}, u32[]{:S(2)}) collective-permute-start(bf16[512,256]{1,0:T(8,128)(2,1)S(1)} %collective-permute-done.refs_2_), channel_id=1, source_target_pairs={{0,4},{4,0},{8,12},{12,8},{16,20},{20,16},{24,28},{28,24},{1,5},{5... | collective-permute-start | bytes 786440 | tf_op jit(solution)/shard_map/ppermute | solution.py:258
  17.2 1.5 %collective-permute-start.4 = (bf16[512,256]{1,0:T(8,128)(2,1)S(1)}, bf16[512,256]{1,0:T(8,128)(2,1)S(1)}, u32[]{:S(2)}, u32[]{:S(2)}) collective-permute-start(bf16[512,256]{1,0:T(8,128)(2,1)S(1)} %collective-permute-done.3.refs_4_), channel_id=1, source_target_pairs={{0,4},{4,0},{8,12},{12,8},{16,20},{20,16},{24,28},{28,24},{1,5},{5... | collective-permute-start | bytes 786440 | tf_op jit(solution)/shard_map/ppermute | solution.py:258
  17.2 1.9 %collective-permute-start.6 = (bf16[512,256]{1,0:T(8,128)(2,1)S(1)}, bf16[512,256]{1,0:T(8,128)(2,1)S(1)}, u32[]{:S(2)}, u32[]{:S(2)}) collective-permute-start(bf16[512,256]{1,0:T(8,128)(2,1)S(1)} %collective-permute-done.5.refs_6_), channel_id=1, source_target_pairs={{0,4},{4,0},{8,12},{12,8},{16,20},{20,16},{24,28},{28,24},{1,5},{5... | collective-permute-start | bytes 786440 | tf_op jit(solution)/shard_map/ppermute | solution.py:258
  25.9 10.0 %collective-permute-start.7 = (bf16[512,256]{1,0:T(8,128)(2,1)S(1)}, bf16[512,256]{1,0:T(8,128)(2,1)S(1)}, u32[]{:S(2)}, u32[]{:S(2)}) collective-permute-start(bf16[512,256]{1,0:T(8,128)(2,1)S(1)} %get-tuple-element.34), channel_id=1, source_target_pairs={{0,1},{1,0},{2,3},{3,2},{4,5},{5,4},{6,7},{7,6},{8,9},{9,8},{10,11... | collective-permute-start | bytes 786440 | tf_op jit(solution)/shard_map/ppermute | solution.py:258
  26.0 21.4 %collective-permute-start.8 = (bf16[512,256]{1,0:T(8,128)(2,1)S(1)}, bf16[512,256]{1,0:T(8,128)(2,1)S(1)}, u32[]{:S(2)}, u32[]{:S(2)}) collective-permute-start(bf16[512,256]{1,0:T(8,128)(2,1)S(1)} %get-tuple-element.35), channel_id=1, source_target_pairs={{0,2},{1,3},{2,0},{3,1},{4,6},{5,7},{6,4},{7,5},{8,10},{9,11},{10,... | collective-permute-start | bytes 786440 | tf_op jit(solution)/shard_map/ppermute | solution.py:258
  27.8 19.7 %collective-permute-start.9 = (bf16[512,256]{1,0:T(8,128)(2,1)S(1)}, bf16[512,256]{1,0:T(8,128)(2,1)S(1)}, u32[]{:S(2)}, u32[]{:S(2)}) collective-permute-start(bf16[512,256]{1,0:T(8,128)(2,1)S(1)} %get-tuple-element.36), channel_id=1, source_target_pairs={{0,3},{1,2},{2,1},{3,0},{4,7},{5,6},{6,5},{7,4},{8,11},{9,10},{10,... | collective-permute-start | bytes 786440 | tf_op jit(solution)/shard_map/ppermute | solution.py:258
  48.7 16.6 %collective-permute-start.10 = (bf16[512,256]{1,0:T(8,128)(2,1)S(1)}, bf16[512,256]{1,0:T(8,128)(2,1)S(1)}, u32[]{:S(2)}, u32[]{:S(2)}) collective-permute-start(bf16[512,256]{1,0:T(8,128)(2,1)S(1)} %get-tuple-element.41.refs_0_), channel_id=1, source_target_pairs={{0,1},{1,0},{2,3},{3,2},{4,5},{5,4},{6,7},{7,6},{8,9},{9,8},{10,11... | collective-permute-start | bytes 786440 | tf_op jit(solution)/shard_map/ppermute | solution.py:258
  52.5 20.7 %collective-permute-start.11 = (bf16[512,256]{1,0:T(8,128)(2,1)S(1)}, bf16[512,256]{1,0:T(8,128)(2,1)S(1)}, u32[]{:S(2)}, u32[]{:S(2)}) collective-permute-start(bf16[512,256]{1,0:T(8,128)(2,1)S(1)} %get-tuple-element.41.refs_0_), channel_id=1, source_target_pairs={{0,2},{1,3},{2,0},{3,1},{4,6},{5,7},{6,4},{7,5},{8,10},{9,11},{10,... | collective-permute-start | bytes 786440 | tf_op jit(solution)/shard_map/ppermute | solution.py:258
  53.5 19.8 %collective-permute-start.12 = (bf16[512,256]{1,0:T(8,128)(2,1)S(1)}, bf16[512,256]{1,0:T(8,128)(2,1)S(1)}, u32[]{:S(2)}, u32[]{:S(2)}) collective-permute-start(bf16[512,256]{1,0:T(8,128)(2,1)S(1)} %get-tuple-element.41.refs_0_), channel_id=1, source_target_pairs={{0,3},{1,2},{2,1},{3,0},{4,7},{5,6},{6,5},{7,4},{8,11},{9,10},{10,... | collective-permute-start | bytes 786440 | tf_op jit(solution)/shard_map/ppermute | solution.py:258
  80.7 6.5 %collective-permute-start.13 = (bf16[2048,256]{1,0:T(8,128)(2,1)S(1)}, bf16[2048,256]{1,0:T(8,128)(2,1)S(1)}, u32[]{:S(2)}, u32[]{:S(2)}) collective-permute-start(bf16[2048,256]{1,0:T(8,128)(2,1)S(1)} %get-tuple-element.43), channel_id=1, source_target_pairs={{0,4},{4,0},{8,12},{12,8},{16,20},{20,16},{24,28},{28,24},{1,5},{5... | collective-permute-start | bytes 3145736 | tf_op jit(solution)/shard_map/ppermute | solution.py:258
  80.7 6.0 %collective-permute-start.19 = (f32[32,256]{1,0:T(8,128)S(1)}, f32[32,256]{1,0:T(8,128)S(1)}, u32[]{:S(2)}, u32[]{:S(2)}) collective-permute-start(f32[32,256]{1,0:T(8,128)S(1)} %reduce_sum.9), channel_id=1, source_target_pairs={{0,3},{1,2},{2,1},{3,0},{4,7},{5,6},{6,5},{7,4},{8,11},{9,10},{10,... | collective-permute-start | bytes 98312 | tf_op jit(solution)/shard_map/ppermute | solution.py:258
  80.8 5.9 %collective-permute-start.18 = (f32[32,256]{1,0:T(8,128)S(1)}, f32[32,256]{1,0:T(8,128)S(1)}, u32[]{:S(2)}, u32[]{:S(2)}) collective-permute-start(f32[32,256]{1,0:T(8,128)S(1)} %reduce_sum.9), channel_id=1, source_target_pairs={{0,2},{1,3},{2,0},{3,1},{4,6},{5,7},{6,4},{7,5},{8,10},{9,11},{10,... | collective-permute-start | bytes 98312 | tf_op jit(solution)/shard_map/ppermute | solution.py:258
  82.7 4.4 %collective-permute-start.17 = (f32[32,256]{1,0:T(8,128)S(1)}, f32[32,256]{1,0:T(8,128)S(1)}, u32[]{:S(2)}, u32[]{:S(2)}) collective-permute-start(f32[32,256]{1,0:T(8,128)S(1)} %reduce_sum.9), channel_id=1, source_target_pairs={{0,1},{1,0},{2,3},{3,2},{4,5},{5,4},{6,7},{7,6},{8,9},{9,8},{10,11... | collective-permute-start | bytes 98312 | tf_op jit(solution)/shard_map/ppermute | solution.py:258
  87.1 3.9 %collective-permute-start.20 = (f32[32,256]{1,0:T(8,128)S(1)}, f32[32,256]{1,0:T(8,128)S(1)}, u32[]{:S(2)}, u32[]{:S(2)}) collective-permute-start(f32[32,256]{1,0:T(8,128)S(1)} %add_add_fusion), channel_id=1, source_target_pairs={{0,4},{4,0},{8,12},{12,8},{16,20},{20,16},{24,28},{28,24},{1,5},{5... | collective-permute-start | bytes 98312 | tf_op jit(solution)/shard_map/ppermute | solution.py:258
  87.5 23.1 %collective-permute-start.16 = (bf16[512,256]{1,0:T(8,128)(2,1)S(1)}, bf16[512,256]{1,0:T(8,128)(2,1)S(1)}, u32[]{:S(2)}, u32[]{:S(2)}) collective-permute-start(bf16[512,256]{1,0:T(8,128)(2,1)S(1)} %get-tuple-element.47), channel_id=1, source_target_pairs={{0,24},{4,28},{8,16},{12,20},{16,8},{20,12},{24,0},{28,4},{1,25},{... | collective-permute-start | bytes 786440 | tf_op jit(solution)/shard_map/ppermute | solution.py:258
  89.3 21.3 %collective-permute-start.15 = (bf16[512,256]{1,0:T(8,128)(2,1)S(1)}, bf16[512,256]{1,0:T(8,128)(2,1)S(1)}, u32[]{:S(2)}, u32[]{:S(2)}) collective-permute-start(bf16[512,256]{1,0:T(8,128)(2,1)S(1)} %get-tuple-element.46), channel_id=1, source_target_pairs={{0,16},{4,20},{8,24},{12,28},{16,0},{20,4},{24,8},{28,12},{1,17},{... | collective-permute-start | bytes 786440 | tf_op jit(solution)/shard_map/ppermute | solution.py:258
  89.6 21.0 %collective-permute-start.14 = (bf16[512,256]{1,0:T(8,128)(2,1)S(1)}, bf16[512,256]{1,0:T(8,128)(2,1)S(1)}, u32[]{:S(2)}, u32[]{:S(2)}) collective-permute-start(bf16[512,256]{1,0:T(8,128)(2,1)S(1)} %get-tuple-element.45), channel_id=1, source_target_pairs={{0,8},{4,12},{8,0},{12,4},{16,24},{20,28},{24,16},{28,20},{1,9},{5... | collective-permute-start | bytes 786440 | tf_op jit(solution)/shard_map/ppermute | solution.py:258
  91.0 13.7 %collective-permute-start.21 = (f32[64,256]{1,0:T(8,128)S(1)}, f32[64,256]{1,0:T(8,128)S(1)}, u32[]{:S(2)}, u32[]{:S(2)}) collective-permute-start(f32[64,256]{1,0:T(8,128)S(1)} %pad_maximum_fusion.refs_0_), channel_id=1, source_target_pairs={{0,8},{4,12},{8,0},{12,4},{16,24},{20,28},{24,16},{28,20},{1,9},{5... | collective-permute-start | bytes 196616 | tf_op jit(solution)/shard_map/ppermute | solution.py:258
  91.7 13.3 %collective-permute-start.22 = (f32[64,256]{1,0:T(8,128)S(1)}, f32[64,256]{1,0:T(8,128)S(1)}, u32[]{:S(2)}, u32[]{:S(2)}) collective-permute-start(f32[64,256]{1,0:T(8,128)S(1)} %pad_maximum_fusion.refs_0_), channel_id=1, source_target_pairs={{0,16},{4,20},{8,24},{12,28},{16,0},{20,4},{24,8},{28,12},{1,17},{... | collective-permute-start | bytes 196616 | tf_op jit(solution)/shard_map/ppermute | solution.py:258
  104.7 5.2 %collective-permute-start.23 = (f32[64,256]{1,0:T(8,128)S(1)}, f32[64,256]{1,0:T(8,128)S(1)}, u32[]{:S(2)}, u32[]{:S(2)}) collective-permute-start(f32[64,256]{1,0:T(8,128)S(1)} %pad_maximum_fusion.refs_0_), channel_id=1, source_target_pairs={{0,24},{4,28},{8,16},{12,20},{16,8},{20,12},{24,0},{28,4},{1,25},{... | collective-permute-start | bytes 196616 | tf_op jit(solution)/shard_map/ppermute | solution.py:258

commit v4 on v3

--- a/solution.py
+++ b/solution.py
@@ -194,25 +194,31 @@
     )(*terms, weight, cotangent)
 
 
-def weight_kernel(agg_ref, grad_ref, out_ref):
+def weight_kernel(chunks, me, agg_ref, grad_ref, own_ref, other_ref, scratch):
     high, low = split(agg_ref[...])
     grad_high, grad_low = split(grad_ref[...])
     contract = ((0,), (0,))
-    out_ref[...] = (
+    scratch[...] = (
         mm(high, grad_high, contract) + mm(low, grad_high, contract) + mm(high, grad_low, contract)
     )
-
-
-def weight_term(aggregated, mixed_grad):
+    depth = scratch.shape[0] // chunks
+    for c in range(chunks // 2):
+        for ref, other in ((own_ref, 0), (other_ref, 1)):
+            start = pl.multiple_of((2 * c + (me[0] % 2 ^ other)) * depth, depth)
+            ref[c * depth : (c + 1) * depth, :] = scratch[pl.ds(start, depth), :]
+
+
+def weight_term(aggregated, mixed_grad, me, chunks):
     rows, width = aggregated.shape
     return pl.pallas_call(
-        weight_kernel,
-        out_shape=jax.ShapeDtypeStruct((width, width), F32),
-        in_specs=[VMEM, VMEM],
-        out_specs=VMEM,
+        functools.partial(weight_kernel, chunks),
+        out_shape=[jax.ShapeDtypeStruct((width // 2, width), F32)] * 2,
+        in_specs=[SMEM, VMEM, VMEM],
+        out_specs=[VMEM, VMEM],
+        scratch_shapes=[pltpu.VMEM((width, width), F32)],
         compiler_params=params(40),
         cost_estimate=cost(6 * rows * width * width, 8 * rows * width),
-    )(aggregated, mixed_grad)
+    )(me, aggregated, mixed_grad)
 
 
 def assemble_kernel(parts, me, *refs):
@@ -293,12 +299,14 @@
     back_panel = [back] + [swap(back, "col", n_col, m) for m in range(1, n_col)]
 
     depth = weight.shape[0] // n_row
-    piece = exchange(weight_term(aggregated, mixed_grad), "row")
-    piece = jnp.sum(piece.reshape(n_row, depth, -1), axis=0)
+    own_term, other_term = weight_term(aggregated, mixed_grad, me_row, n_row)
+    term = own_term + swap(other_term, "row", n_row, 1)
+    cores = [list(range(0, n_row, 2)), list(range(1, n_row, 2))]
+    term = lax.all_to_all(term, "row", 0, 0, axis_index_groups=cores, tiled=True)
+    piece = jnp.sum(term.reshape(n_row // 2, depth, -1), axis=0)
+    piece = lax.all_gather(piece, "col", axis=0, tiled=True)
     piece, back_panel[0] = lax.optimization_barrier((piece, back_panel[0]))
-    piece = total_of([piece] + [swap(piece, "col", n_col, m) for m in range(1, n_col)])
-    piece = jnp.concatenate([piece, swap(piece, "row", n_row, 1)])
-    gathered = [piece] + [swap(piece, "row", n_row, m) for m in range(2, n_row, 2)]
+    piece = jnp.sum(piece.reshape(n_col, depth, -1), axis=0)
 
     even = list(range(0, n_row, 2))
     pair = [even, [m + 1 for m in even]]
@@ -309,7 +317,7 @@
     feature_grad = total_of(
         [sums[0]] + [swap(s, "row", n_row, m) for s, m in zip(sums[1:], even[1:])]
     ).astype(BF16)
-    weight_grad = assemble(gathered, me_row)
+    weight_grad = lax.all_gather(piece, 'row', axis=0, tiled=True)
     return (activations, feature_grad, weight_grad)
 
 

time: 113 us -> 115 us (1.018); the launches traced: 111 us -> 115 us
  blocking collectives: 9.89 us -> 46.5 us
  waiting for transfers between devices: 51 us -> 25.1 us
  Pallas kernels: 19.6 us -> 13.2 us
  starting transfers between devices: 27 us -> 25.7 us
    all_gather x0 -> x2, blocking collectives: none -> 38.8 us  [the longest x1 23 us: on_device(): piece = lax.all_gather(piece, 'col', axis=0, tiled=True)]
    ppermute x24 -> x18, waiting for transfers between devices: 51 us -> 25.1 us  [swap(): return lax.ppermute(x, axis, [(i, i ^ m) for i in range(n)])]
    pallas_call x2, Pallas kernels: 14.2 us -> 8.42 us  [sparse_product(): pl.pallas_call(functools.partial(sparse_kernel, parts, outs, backward), o...]
    all_to_all x1, blocking collectives: 9.89 us -> 7.72 us  [on_device(): lax.all_to_all(term, 'row', 0, 0, axis_index_groups=cores, tiled=True)]
    ppermute x24 -> x18, starting transfers between devices: 27 us -> 25.7 us  [swap(): return lax.ppermute(x, axis, [(i, i ^ m) for i in range(n)])]
    unnamed x10 -> x11, local copies, waits for them, and re-layouts: 2.31 us -> 3.02 us
  transfers between devices with their start and end apart: 24 -> 18, of which waited for: 11 -> 7; matrix products, arithmetic and copies ran while one was open for 0% -> 0% of each run, Pallas kernels for 4% -> 3%
where the time goes in v4:
time: 115 us
  blocking collectives  46.5 us (40%)
  starting transfers between devices  25.7 us (22%)
  waiting for transfers between devices  25.1 us (22%)
  Pallas kernels  13.2 us (11%)
  local copies, waits for them, and re-layouts  3.02 us (3%)
    ppermute x18, starting transfers between devices, swap(): return lax.ppermute(x, axis, [(i, i ^ m) for i in range(n)])  25.7 us
    ppermute x18, waiting for transfers between devices, swap(): return lax.ppermute(x, axis, [(i, i ^ m) for i in range(n)])  25.1 us
    all_gather x1, blocking collectives, on_device(): piece = lax.all_gather(piece, 'col', axis=0, tiled=True)  23 us
    all_gather x1, blocking collectives, on_device(): weight_grad = lax.all_gather(piece, 'row', axis=0, tiled=True)  15.8 us
    pallas_call x2, Pallas kernels, sparse_product(): pl.pallas_call(functools.partial(sparse_kernel, parts, outs, backward), o...  8.42 us
    all_to_all x1, blocking collectives, on_device(): lax.all_to_all(term, 'row', 0, 0, axis_index_groups=cores, tiled=True)  7.72 us
    unnamed x11, local copies, waits for them, and re-layouts  3.02 us
    pallas_call x1, Pallas kernels, prepare(): pl.pallas_call(prepare_kernel, out_shape=[jax.ShapeDtypeStruct((slots + 1...  2.88 us
  transfers between devices with their start and end apart: 18, of which 7 were waited for; matrix products, arithmetic and copies ran while one was open for 0% of the time, Pallas kernels for 3%

profile of v4, /device:TPU:0, one launch (start us, length us, event | category | flops | bytes accessed | tf_op | source)
XLA Modules:
  0.0 115.1 jit_solution(6328804717875496446)
XLA Ops:
  0.6 3.0 %collective-permute-start = (bf16[512,256]{1,0:T(8,128)(2,1)}, bf16[512,256]{1,0:T(8,128)(2,1)S(1)}, u32[]{:S(2)}, u32[]{:S(2)}) collective-permute-start(bf16[512,256]{1,0:T(8,128)(2,1)} %features.1), channel_id=1, source_target_pairs={{0,8},{4,12},{8,0},{12,4},{16,24},{20,28},{24,16},{28,20},{1,9},{5... | collective-permute-start | bytes 786440 | tf_op jit(solution)/shard_map/ppermute | solution.py:264
  3.6 1.5 %collective-permute-start.3 = (bf16[512,256]{1,0:T(8,128)(2,1)}, bf16[512,256]{1,0:T(8,128)(2,1)S(1)}, u32[]{:S(2)}, u32[]{:S(2)}) collective-permute-start(bf16[512,256]{1,0:T(8,128)(2,1)} %features.1), channel_id=1, source_target_pairs={{0,16},{4,20},{8,24},{12,28},{16,0},{20,4},{24,8},{28,12},{1,17},{... | collective-permute-start | bytes 786440 | tf_op jit(solution)/shard_map/ppermute | solution.py:264
  5.2 0.0 collective-permute-start.5
  5.2 0.0 copy-start
  5.2 1.0 copy-done
  6.2 0.0 copy-start.3
  6.2 0.7 copy-done.3
  6.8 0.0 copy-start.4
  6.8 0.7 copy-done.4
  7.5 0.0 copy-start.1
  7.5 0.0 copy-start.2
  7.5 2.9 %shard_map.85 = (s32[129]{0:T(256)S(1)}, s32[128]{0:T(128)S(1)}, bf16[512,256]{1,0:T(8,128)(2,1)S(1)}) custom-call(s32[1,1,17]{2,1,0:T(1,128)S(1)} %copy-done.3, s32[1,1,128]{2,1,0:T(1,128)S(1)} %copy-done.4, bf16[512,256]{1,0:T(8,128)(2,1)S(1)} %copy-done), custom_call_target="tpu_custom_call" | custom-call | tf_op jit(solution)/shard_map/pallas_call | solution.py:57
  10.4 0.6 collective-permute-done.refs_2_
  11.0 0.0 collective-permute-start.1
  11.0 0.5 collective-permute-start.2
  11.5 5.7 %collective-permute-done.3.refs_4_ = bf16[512,256]{1,0:T(8,128)(2,1)S(1)} collective-permute-done((bf16[512,256]{1,0:T(8,128)(2,1)}, bf16[512,256]{1,0:T(8,128)(2,1)S(1)}, u32[]{:S(2)}, u32[]{:S(2)}) %collective-permute-start.3) | collective-permute-done | bytes 262176 | tf_op jit(solution)/shard_map/ppermute | solution.py:264
  17.2 0.0 collective-permute-start.4
  17.2 0.0 collective-permute-done.5.refs_6_
  17.2 0.5 collective-permute-start.6
  17.7 0.0 collective-permute-done.1.refs_1_
  17.7 0.0 collective-permute-done.2.refs_3_
  17.8 1.0 collective-permute-done.4.refs_5_
  18.8 0.4 collective-permute-done.6.refs_7_
  19.1 4.1 %shard_map.86 = (bf16[512,256]{1,0:T(8,128)(2,1)S(1)}, bf16[512,256]{1,0:T(8,128)(2,1)S(1)}, bf16[512,256]{1,0:T(8,128)(2,1)S(1)}, bf16[512,256]{1,0:T(8,128)(2,1)S(1)}) custom-call(s32[129]{0:T(256)S(1)} %get-tuple-element.31.row_of, s32[128]{0:T(128)S(1)} %get-tuple-element.32.col_of, s32[1]{0:T(128)} %bitcast.here_ref.me.mine_ref, ...), custom_call_target="tpu_custom_call" | custom-call | flops 1073741824 | bytes 6291456 | tf_op jit(solution)/shard_map/pallas_call | solution.py:135
  23.2 0.7 collective-permute-start.7
  24.0 3.2 %collective-permute-start.8 = (bf16[512,256]{1,0:T(8,128)(2,1)S(1)}, bf16[512,256]{1,0:T(8,128)(2,1)S(1)}, u32[]{:S(2)}, u32[]{:S(2)}) collective-permute-start(bf16[512,256]{1,0:T(8,128)(2,1)S(1)} %get-tuple-element.37), channel_id=1, source_target_pairs={{0,2},{1,3},{2,0},{3,1},{4,6},{5,7},{6,4},{7,5},{8,10},{9,11},{10,... | collective-permute-start | bytes 786440 | tf_op jit(solution)/shard_map/ppermute | solution.py:264
  27.2 0.5 collective-permute-start.9
  27.7 8.9 %collective-permute-done.7.refs_1_ = bf16[512,256]{1,0:T(8,128)(2,1)S(1)} collective-permute-done((bf16[512,256]{1,0:T(8,128)(2,1)S(1)}, bf16[512,256]{1,0:T(8,128)(2,1)S(1)}, u32[]{:S(2)}, u32[]{:S(2)}) %collective-permute-start.7) | collective-permute-done | bytes 262176 | tf_op jit(solution)/shard_map/ppermute | solution.py:264
  36.5 0.0 collective-permute-done.8.refs_2_
  36.5 5.9 %collective-permute-done.9.refs_3_ = bf16[512,256]{1,0:T(8,128)(2,1)S(1)} collective-permute-done((bf16[512,256]{1,0:T(8,128)(2,1)S(1)}, bf16[512,256]{1,0:T(8,128)(2,1)S(1)}, u32[]{:S(2)}, u32[]{:S(2)}) %collective-permute-start.9) | collective-permute-done | bytes 262176 | tf_op jit(solution)/shard_map/ppermute | solution.py:264
  42.4 0.0 copy-done.1
  42.4 0.0 copy-done.2
  42.4 1.2 %shard_map.87 = (bf16[512,256]{1,0:T(8,128)(2,1)}, bf16[512,256]{1,0:T(8,128)(2,1)S(1)}, f32[512,256]{1,0:T(8,128)S(1)}, f32[512,256]{1,0:T(8,128)S(1)}) custom-call(bf16[512,256]{1,0:T(8,128)(2,1)S(1)} %get-tuple-element.35.refs_0_, bf16[512,256]{1,0:T(8,128)(2,1)S(1)} %collective-permute-done.7.refs_1_, ...), custom_call_target="tpu_custom_call" | custom-call | flops 268435456 | bytes 2621440 | tf_op jit(solution)/shard_map/pallas_call | solution.py:182
  43.6 0.4 shard_map.88
  44.1 4.0 %collective-permute-start.10 = (f32[128,256]{1,0:T(8,128)S(1)}, f32[128,256]{1,0:T(8,128)S(1)}, u32[]{:S(2)}, u32[]{:S(2)}) collective-permute-start(f32[128,256]{1,0:T(8,128)S(1)} %get-tuple-element.43), channel_id=1, source_target_pairs={{0,4},{4,0},{8,12},{12,8},{16,20},{20,16},{24,28},{28,24},{1,5},{5... | collective-permute-start | bytes 393224 | tf_op jit(solution)/shard_map/ppermute | solution.py:264
  48.1 5.2 %collective-permute-start.11 = (bf16[512,256]{1,0:T(8,128)(2,1)S(1)}, bf16[512,256]{1,0:T(8,128)(2,1)S(1)}, u32[]{:S(2)}, u32[]{:S(2)}) collective-permute-start(bf16[512,256]{1,0:T(8,128)(2,1)S(1)} %get-tuple-element.45.refs_0_), channel_id=1, source_target_pairs={{0,1},{1,0},{2,3},{3,2},{4,5},{5,4},{6,7},{7,6},{8,9},{9,8},{10,11... | collective-permute-start | bytes 786440 | tf_op jit(solution)/shard_map/ppermute | solution.py:264
  53.4 1.0 collective-permute-start.12
  54.3 1.5 %collective-permute-start.13 = (bf16[512,256]{1,0:T(8,128)(2,1)S(1)}, bf16[512,256]{1,0:T(8,128)(2,1)S(1)}, u32[]{:S(2)}, u32[]{:S(2)}) collective-permute-start(bf16[512,256]{1,0:T(8,128)(2,1)S(1)} %get-tuple-element.45.refs_0_), channel_id=1, source_target_pairs={{0,3},{1,2},{2,1},{3,0},{4,7},{5,6},{6,5},{7,4},{8,11},{9,10},{10,... | collective-permute-start | bytes 786440 | tf_op jit(solution)/shard_map/ppermute | solution.py:264
  55.8 0.0 collective-permute-done.10
  55.8 7.7 %all_to_all.9 = f32[4,32,256]{2,1,0:T(8,128)S(1)} all-to-all(f32[4,32,256]{2,1,0:T(8,128)S(1)} %bitcast.8), channel_id=1, replica_groups={{0,8,16,24},{4,12,20,28},{1,9,17,25},{5,13,21,29},{2,10,18,26},{6,14,22..., dimensions={0} | all-to-all | bytes 262144 | tf_op jit(solution)/shard_map/all_to_all | solution.py:305
  63.6 23.0 %all_gather.6 = f32[128,256]{1,0:T(8,128)S(1)} all-gather(f32[32,256]{1,0:T(8,128)S(1)} %reduce_sum.18), channel_id=1, replica_groups=mesh['row'=8,'col'=4] {'col'}, dimensions={0}, use_global_device_ids=true | all-gather | bytes 163840 | tf_op jit(solution)/shard_map/all_gather | solution.py:307
  86.6 0.0 collective-permute-done.11.refs_1_
  86.6 0.0 collective-permute-done.12.refs_2_
  86.6 0.0 collective-permute-done.13.refs_3_
  86.6 4.3 %shard_map.89 = (bf16[2048,256]{1,0:T(8,128)(2,1)S(1)}, bf16[2048,256]{1,0:T(8,128)(2,1)S(1)}) custom-call(s32[129]{0:T(256)S(1)} %get-tuple-element.31.row_of, s32[128]{0:T(128)S(1)} %get-tuple-element.32.col_of, s32[1]{0:T(128)} %bitcast.1.mine_ref.here_ref, s32[1]{0:T(128)} %bitcast.here_ref.me.mine_ref, bf16[512,256]{1,0:T(8,128)(2,1)S(1)} %get-tuple-element.45.refs_0_, ...), custom_call_target="tpu_custom_call" | custom-call | flops 1073741824 | bytes 5242880 | tf_op jit(solution)/shard_map/pallas_call | solution.py:135
  90.9 0.1 collective-permute-start.14
  91.0 2.6 %collective-permute-done.14.other_ref = bf16[2048,256]{1,0:T(8,128)(2,1)S(1)} collective-permute-done((bf16[2048,256]{1,0:T(8,128)(2,1)S(1)}, bf16[2048,256]{1,0:T(8,128)(2,1)S(1)}, u32[]{:S(2)}, u32[]{:S(2)}) %collective-permute-start.14) | collective-permute-done | bytes 1048608 | tf_op jit(solution)/shard_map/ppermute | solution.py:264
  93.7 0.2 shard_map.90
  93.9 1.0 collective-permute-start.17
  94.9 1.9 %collective-permute-start.16 = (bf16[512,256]{1,0:T(8,128)(2,1)S(1)}, bf16[512,256]{1,0:T(8,128)(2,1)S(1)}, u32[]{:S(2)}, u32[]{:S(2)}) collective-permute-start(bf16[512,256]{1,0:T(8,128)(2,1)S(1)} %get-tuple-element.50), channel_id=1, source_target_pairs={{0,16},{4,20},{8,24},{12,28},{16,0},{20,4},{24,8},{28,12},{1,17},{... | collective-permute-start | bytes 786440 | tf_op jit(solution)/shard_map/ppermute | solution.py:264
  96.8 1.0 collective-permute-start.15
  97.8 15.8 %all_gather.7 = f32[256,256]{1,0:T(8,128)S(1)} all-gather(f32[32,256]{1,0:T(8,128)S(1)} %reduce_sum.19), channel_id=1, replica_groups=mesh['row'=8,'col'=4] {'row'}, dimensions={0}, use_global_device_ids=true | all-gather | bytes 294912 | tf_op jit(solution)/shard_map/all_gather | solution.py:320
  113.6 0.0 collective-permute-done.17
  113.6 0.0 collective-permute-done.16
  113.6 0.0 collective-permute-done.15
  113.6 0.8 add_convert_fusion
  114.4 0.7 copy.10
  (3 shorter events, 0.0 us)
Async XLA Ops:
  0.6 10.3 %collective-permute-start = (bf16[512,256]{1,0:T(8,128)(2,1)}, bf16[512,256]{1,0:T(8,128)(2,1)S(1)}, u32[]{:S(2)}, u32[]{:S(2)}) collective-permute-start(bf16[512,256]{1,0:T(8,128)(2,1)} %features.1), channel_id=1, source_target_pairs={{0,8},{4,12},{8,0},{12,4},{16,24},{20,28},{24,16},{28,20},{1,9},{5... | collective-permute-start | bytes 786440 | tf_op jit(solution)/shard_map/ppermute | solution.py:264
  3.6 13.6 %collective-permute-start.3 = (bf16[512,256]{1,0:T(8,128)(2,1)}, bf16[512,256]{1,0:T(8,128)(2,1)S(1)}, u32[]{:S(2)}, u32[]{:S(2)}) collective-permute-start(bf16[512,256]{1,0:T(8,128)(2,1)} %features.1), channel_id=1, source_target_pairs={{0,16},{4,20},{8,24},{12,28},{16,0},{20,4},{24,8},{28,12},{1,17},{... | collective-permute-start | bytes 786440 | tf_op jit(solution)/shard_map/ppermute | solution.py:264
  5.2 12.1 %collective-permute-start.5 = (bf16[512,256]{1,0:T(8,128)(2,1)}, bf16[512,256]{1,0:T(8,128)(2,1)S(1)}, u32[]{:S(2)}, u32[]{:S(2)}) collective-permute-start(bf16[512,256]{1,0:T(8,128)(2,1)} %features.1), channel_id=1, source_target_pairs={{0,24},{4,28},{8,16},{12,20},{16,8},{20,12},{24,0},{28,4},{1,25},{... | collective-permute-start | bytes 786440 | tf_op jit(solution)/shard_map/ppermute | solution.py:264
  5.2 1.0 copy-start
  6.2 0.7 copy-start.3
  6.8 0.7 copy-start.4
  7.5 34.9 %copy-start.1 = (bf16[512,256]{1,0:T(8,128)(2,1)S(1)}, bf16[512,256]{1,0:T(8,128)(2,1)}, u32[]{:S(2)}) copy-start(bf16[512,256]{1,0:T(8,128)(2,1)} %refs_5_.1) | copy-start | bytes 786436
  7.5 34.9 %copy-start.2 = (bf16[256,256]{1,0:T(8,128)(2,1)S(1)}, bf16[256,256]{1,0:T(8,128)(2,1)}, u32[]{:S(2)}) copy-start(bf16[256,256]{1,0:T(8,128)(2,1)} %refs_4_.1) | copy-start | bytes 393220
  11.0 6.8 %collective-permute-start.1 = (bf16[512,256]{1,0:T(8,128)(2,1)S(1)}, bf16[512,256]{1,0:T(8,128)(2,1)S(1)}, u32[]{:S(2)}, u32[]{:S(2)}) collective-permute-start(bf16[512,256]{1,0:T(8,128)(2,1)S(1)} %get-tuple-element.33.refs_0_), channel_id=1, source_target_pairs={{0,4},{4,0},{8,12},{12,8},{16,20},{20,16},{24,28},{28,24},{1,5},{5... | collective-permute-start | bytes 786440 | tf_op jit(solution)/shard_map/ppermute | solution.py:264
  11.0 6.8 %collective-permute-start.2 = (bf16[512,256]{1,0:T(8,128)(2,1)S(1)}, bf16[512,256]{1,0:T(8,128)(2,1)S(1)}, u32[]{:S(2)}, u32[]{:S(2)}) collective-permute-start(bf16[512,256]{1,0:T(8,128)(2,1)S(1)} %collective-permute-done.refs_2_), channel_id=1, source_target_pairs={{0,4},{4,0},{8,12},{12,8},{16,20},{20,16},{24,28},{28,24},{1,5},{5... | collective-permute-start | bytes 786440 | tf_op jit(solution)/shard_map/ppermute | solution.py:264
  17.2 1.5 %collective-permute-start.4 = (bf16[512,256]{1,0:T(8,128)(2,1)S(1)}, bf16[512,256]{1,0:T(8,128)(2,1)S(1)}, u32[]{:S(2)}, u32[]{:S(2)}) collective-permute-start(bf16[512,256]{1,0:T(8,128)(2,1)S(1)} %collective-permute-done.3.refs_4_), channel_id=1, source_target_pairs={{0,4},{4,0},{8,12},{12,8},{16,20},{20,16},{24,28},{28,24},{1,5},{5... | collective-permute-start | bytes 786440 | tf_op jit(solution)/shard_map/ppermute | solution.py:264
  17.2 1.9 %collective-permute-start.6 = (bf16[512,256]{1,0:T(8,128)(2,1)S(1)}, bf16[512,256]{1,0:T(8,128)(2,1)S(1)}, u32[]{:S(2)}, u32[]{:S(2)}) collective-permute-start(bf16[512,256]{1,0:T(8,128)(2,1)S(1)} %collective-permute-done.5.refs_6_), channel_id=1, source_target_pairs={{0,4},{4,0},{8,12},{12,8},{16,20},{20,16},{24,28},{28,24},{1,5},{5... | collective-permute-start | bytes 786440 | tf_op jit(solution)/shard_map/ppermute | solution.py:264
  23.2 13.3 %collective-permute-start.7 = (bf16[512,256]{1,0:T(8,128)(2,1)S(1)}, bf16[512,256]{1,0:T(8,128)(2,1)S(1)}, u32[]{:S(2)}, u32[]{:S(2)}) collective-permute-start(bf16[512,256]{1,0:T(8,128)(2,1)S(1)} %get-tuple-element.36), channel_id=1, source_target_pairs={{0,1},{1,0},{2,3},{3,2},{4,5},{5,4},{6,7},{7,6},{8,9},{9,8},{10,11... | collective-permute-start | bytes 786440 | tf_op jit(solution)/shard_map/ppermute | solution.py:264
  24.0 12.6 %collective-permute-start.8 = (bf16[512,256]{1,0:T(8,128)(2,1)S(1)}, bf16[512,256]{1,0:T(8,128)(2,1)S(1)}, u32[]{:S(2)}, u32[]{:S(2)}) collective-permute-start(bf16[512,256]{1,0:T(8,128)(2,1)S(1)} %get-tuple-element.37), channel_id=1, source_target_pairs={{0,2},{1,3},{2,0},{3,1},{4,6},{5,7},{6,4},{7,5},{8,10},{9,11},{10,... | collective-permute-start | bytes 786440 | tf_op jit(solution)/shard_map/ppermute | solution.py:264
  27.2 15.3 %collective-permute-start.9 = (bf16[512,256]{1,0:T(8,128)(2,1)S(1)}, bf16[512,256]{1,0:T(8,128)(2,1)S(1)}, u32[]{:S(2)}, u32[]{:S(2)}) collective-permute-start(bf16[512,256]{1,0:T(8,128)(2,1)S(1)} %get-tuple-element.38), channel_id=1, source_target_pairs={{0,3},{1,2},{2,1},{3,0},{4,7},{5,6},{6,5},{7,4},{8,11},{9,10},{10,... | collective-permute-start | bytes 786440 | tf_op jit(solution)/shard_map/ppermute | solution.py:264
  44.1 11.7 %collective-permute-start.10 = (f32[128,256]{1,0:T(8,128)S(1)}, f32[128,256]{1,0:T(8,128)S(1)}, u32[]{:S(2)}, u32[]{:S(2)}) collective-permute-start(f32[128,256]{1,0:T(8,128)S(1)} %get-tuple-element.43), channel_id=1, source_target_pairs={{0,4},{4,0},{8,12},{12,8},{16,20},{20,16},{24,28},{28,24},{1,5},{5... | collective-permute-start | bytes 393224 | tf_op jit(solution)/shard_map/ppermute | solution.py:264
  48.1 38.4 %collective-permute-start.11 = (bf16[512,256]{1,0:T(8,128)(2,1)S(1)}, bf16[512,256]{1,0:T(8,128)(2,1)S(1)}, u32[]{:S(2)}, u32[]{:S(2)}) collective-permute-start(bf16[512,256]{1,0:T(8,128)(2,1)S(1)} %get-tuple-element.45.refs_0_), channel_id=1, source_target_pairs={{0,1},{1,0},{2,3},{3,2},{4,5},{5,4},{6,7},{7,6},{8,9},{9,8},{10,11... | collective-permute-start | bytes 786440 | tf_op jit(solution)/shard_map/ppermute | solution.py:264
  53.4 33.2 %collective-permute-start.12 = (bf16[512,256]{1,0:T(8,128)(2,1)S(1)}, bf16[512,256]{1,0:T(8,128)(2,1)S(1)}, u32[]{:S(2)}, u32[]{:S(2)}) collective-permute-start(bf16[512,256]{1,0:T(8,128)(2,1)S(1)} %get-tuple-element.45.refs_0_), channel_id=1, source_target_pairs={{0,2},{1,3},{2,0},{3,1},{4,6},{5,7},{6,4},{7,5},{8,10},{9,11},{10,... | collective-permute-start | bytes 786440 | tf_op jit(solution)/shard_map/ppermute | solution.py:264
  54.3 32.2 %collective-permute-start.13 = (bf16[512,256]{1,0:T(8,128)(2,1)S(1)}, bf16[512,256]{1,0:T(8,128)(2,1)S(1)}, u32[]{:S(2)}, u32[]{:S(2)}) collective-permute-start(bf16[512,256]{1,0:T(8,128)(2,1)S(1)} %get-tuple-element.45.refs_0_), channel_id=1, source_target_pairs={{0,3},{1,2},{2,1},{3,0},{4,7},{5,6},{6,5},{7,4},{8,11},{9,10},{10,... | collective-permute-start | bytes 786440 | tf_op jit(solution)/shard_map/ppermute | solution.py:264
  90.9 2.7 %collective-permute-start.14 = (bf16[2048,256]{1,0:T(8,128)(2,1)S(1)}, bf16[2048,256]{1,0:T(8,128)(2,1)S(1)}, u32[]{:S(2)}, u32[]{:S(2)}) collective-permute-start(bf16[2048,256]{1,0:T(8,128)(2,1)S(1)} %get-tuple-element.47), channel_id=1, source_target_pairs={{0,4},{4,0},{8,12},{12,8},{16,20},{20,16},{24,28},{28,24},{1,5},{5... | collective-permute-start | bytes 3145736 | tf_op jit(solution)/shard_map/ppermute | solution.py:264
  93.9 19.7 %collective-permute-start.17 = (bf16[512,256]{1,0:T(8,128)(2,1)S(1)}, bf16[512,256]{1,0:T(8,128)(2,1)S(1)}, u32[]{:S(2)}, u32[]{:S(2)}) collective-permute-start(bf16[512,256]{1,0:T(8,128)(2,1)S(1)} %get-tuple-element.51), channel_id=1, source_target_pairs={{0,24},{4,28},{8,16},{12,20},{16,8},{20,12},{24,0},{28,4},{1,25},{... | collective-permute-start | bytes 786440 | tf_op jit(solution)/shard_map/ppermute | solution.py:264
  94.9 18.7 %collective-permute-start.16 = (bf16[512,256]{1,0:T(8,128)(2,1)S(1)}, bf16[512,256]{1,0:T(8,128)(2,1)S(1)}, u32[]{:S(2)}, u32[]{:S(2)}) collective-permute-start(bf16[512,256]{1,0:T(8,128)(2,1)S(1)} %get-tuple-element.50), channel_id=1, source_target_pairs={{0,16},{4,20},{8,24},{12,28},{16,0},{20,4},{24,8},{28,12},{1,17},{... | collective-permute-start | bytes 786440 | tf_op jit(solution)/shard_map/ppermute | solution.py:264
  96.8 16.8 %collective-permute-start.15 = (bf16[512,256]{1,0:T(8,128)(2,1)S(1)}, bf16[512,256]{1,0:T(8,128)(2,1)S(1)}, u32[]{:S(2)}, u32[]{:S(2)}) collective-permute-start(bf16[512,256]{1,0:T(8,128)(2,1)S(1)} %get-tuple-element.49), channel_id=1, source_target_pairs={{0,8},{4,12},{8,0},{12,4},{16,24},{20,28},{24,16},{28,20},{1,9},{5... | collective-permute-start | bytes 786440 | tf_op jit(solution)/shard_map/ppermute | solution.py:264

commit v5 on v4

--- a/solution.py
+++ b/solution.py
@@ -221,24 +221,23 @@
     )(me, aggregated, mixed_grad)
 
 
-def assemble_kernel(parts, me, *refs):
-    out_ref = refs[parts]
-    depth = refs[0].shape[0] // 2
-    for p in range(parts):
-        for core in range(2):
-            start = pl.multiple_of((me[0] ^ (2 * p + core)) * depth, depth)
-            out_ref[pl.ds(start, depth), :] = refs[p][core * depth : (core + 1) * depth, :]
-
-
-def assemble(parts, me):
-    depth, width = parts[0].shape
-    return pl.pallas_call(
-        functools.partial(assemble_kernel, len(parts)),
-        out_shape=jax.ShapeDtypeStruct((depth * len(parts), width), F32),
-        in_specs=[SMEM] + [VMEM] * len(parts),
+def assemble_kernel(chunks, me, own_ref, other_ref, out_ref):
+    depth = own_ref.shape[0] // chunks
+    for c in range(chunks):
+        for ref, other in ((own_ref, 0), (other_ref, 1)):
+            start = pl.multiple_of((2 * c + (me[0] % 2 ^ other)) * depth, depth)
+            out_ref[pl.ds(start, depth), :] = ref[c * depth : (c + 1) * depth, :]
+
+
+def assemble(own, other, me, chunks):
+    depth, width = own.shape
+    return pl.pallas_call(
+        functools.partial(assemble_kernel, chunks),
+        out_shape=jax.ShapeDtypeStruct((2 * depth, width), own.dtype),
+        in_specs=[SMEM, VMEM, VMEM],
         out_specs=VMEM,
         compiler_params=params(32),
-    )(me, *parts)
+    )(me, own, other)
 
 
 def pair_kernel(count, own_ref, other_ref, *outs):
@@ -304,9 +303,8 @@
     cores = [list(range(0, n_row, 2)), list(range(1, n_row, 2))]
     term = lax.all_to_all(term, "row", 0, 0, axis_index_groups=cores, tiled=True)
     piece = jnp.sum(term.reshape(n_row // 2, depth, -1), axis=0)
-    piece = lax.all_gather(piece, "col", axis=0, tiled=True)
-    piece, back_panel[0] = lax.optimization_barrier((piece, back_panel[0]))
-    piece = jnp.sum(piece.reshape(n_col, depth, -1), axis=0)
+    half = lax.all_gather(piece, "row", axis=0, axis_index_groups=cores, tiled=True)
+    half, back_panel[0] = lax.optimization_barrier((half, back_panel[0]))
 
     even = list(range(0, n_row, 2))
     pair = [even, [m + 1 for m in even]]
@@ -317,7 +315,9 @@
     feature_grad = total_of(
         [sums[0]] + [swap(s, "row", n_row, m) for s, m in zip(sums[1:], even[1:])]
     ).astype(BF16)
-    weight_grad = lax.all_gather(piece, 'row', axis=0, tiled=True)
+    halves = lax.all_gather(half.astype(BF16), "col", axis=0, tiled=True)
+    half = jnp.sum(halves.reshape(n_col, -1, half.shape[1]).astype(F32), axis=0)
+    weight_grad = assemble(half, swap(half, "row", n_row, 1), me_row, n_row // 2)
     return (activations, feature_grad, weight_grad)
 
 

time: 115 us -> 105 us (0.913)
  blocking collectives: 46.5 us -> 32.5 us
  waiting for transfers between devices: 25.1 us -> 32.7 us
  starting transfers between devices: 25.7 us -> 22.1 us
    all_gather x2, blocking collectives: 38.8 us -> 24.9 us  [the longest x1 17.3 us: on_device(): halves = lax.all_gather(half.astype(BF16), 'col', axis=0, tiled=True)]
    ppermute x18 -> x19, waiting for transfers between devices: 25.1 us -> 32.7 us  [swap(): return lax.ppermute(x, axis, [(i, i ^ m) for i in range(n)])]
    ppermute x18 -> x19, starting transfers between devices: 25.7 us -> 22.1 us  [swap(): return lax.ppermute(x, axis, [(i, i ^ m) for i in range(n)])]
    unnamed x11 -> x10, local copies, waits for them, and re-layouts: 3.02 us -> 2.31 us
  transfers between devices with their start and end apart: 18 -> 19, of which waited for: 7 -> 10; matrix products, arithmetic and copies ran while one was open for 0% -> 0% of each run, Pallas kernels for 3% -> 4%
where the time goes in v5:
time: 105 us
  waiting for transfers between devices  32.7 us (31%)
  blocking collectives  32.5 us (31%)
  starting transfers between devices  22.1 us (21%)
  Pallas kernels  13.9 us (13%)
  local copies, waits for them, and re-layouts  2.31 us (2%)
    ppermute x19, waiting for transfers between devices, swap(): return lax.ppermute(x, axis, [(i, i ^ m) for i in range(n)])  32.7 us
    ppermute x19, starting transfers between devices, swap(): return lax.ppermute(x, axis, [(i, i ^ m) for i in range(n)])  22.1 us
    all_gather x1, blocking collectives, on_device(): halves = lax.all_gather(half.astype(BF16), 'col', axis=0, tiled=True)  17.3 us
    pallas_call x2, Pallas kernels, sparse_product(): pl.pallas_call(functools.partial(sparse_kernel, parts, outs, backward), o...  8.42 us
    all_gather x1, blocking collectives, on_device(): lax.all_gather(piece, 'row', axis=0, axis_index_groups=cores, tiled=True)  7.64 us
    all_to_all x1, blocking collectives, on_device(): lax.all_to_all(term, 'row', 0, 0, axis_index_groups=cores, tiled=True)  7.58 us
    pallas_call x1, Pallas kernels, prepare(): pl.pallas_call(prepare_kernel, out_shape=[jax.ShapeDtypeStruct((slots + 1...  2.87 us
    unnamed x10, local copies, waits for them, and re-layouts  2.31 us
  transfers between devices with their start and end apart: 19, of which 10 were waited for; matrix products, arithmetic and copies ran while one was open for 0% of the time, Pallas kernels for 4%

profile of v5, /device:TPU:0, one launch (start us, length us, event | category | flops | bytes accessed | tf_op | source)
XLA Modules:
  0.0 105.2 jit_solution(4569894312712645840)
XLA Ops:
  0.6 3.0 %collective-permute-start = (bf16[512,256]{1,0:T(8,128)(2,1)}, bf16[512,256]{1,0:T(8,128)(2,1)S(1)}, u32[]{:S(2)}, u32[]{:S(2)}) collective-permute-start(bf16[512,256]{1,0:T(8,128)(2,1)} %features.1), channel_id=1, source_target_pairs={{0,8},{4,12},{8,0},{12,4},{16,24},{20,28},{24,16},{28,20},{1,9},{5... | collective-permute-start | bytes 786440 | tf_op jit(solution)/shard_map/ppermute | solution.py:263
  3.6 1.5 %collective-permute-start.3 = (bf16[512,256]{1,0:T(8,128)(2,1)}, bf16[512,256]{1,0:T(8,128)(2,1)S(1)}, u32[]{:S(2)}, u32[]{:S(2)}) collective-permute-start(bf16[512,256]{1,0:T(8,128)(2,1)} %features.1), channel_id=1, source_target_pairs={{0,16},{4,20},{8,24},{12,28},{16,0},{20,4},{24,8},{28,12},{1,17},{... | collective-permute-start | bytes 786440 | tf_op jit(solution)/shard_map/ppermute | solution.py:263
  5.2 0.0 collective-permute-start.5
  5.2 0.0 copy-start
  5.2 1.0 copy-done
  6.2 0.0 copy-start.3
  6.2 0.7 copy-done.3
  6.8 0.0 copy-start.4
  6.8 0.7 copy-done.4
  7.5 0.0 copy-start.1
  7.5 0.0 copy-start.2
  7.5 2.9 %shard_map.85 = (s32[129]{0:T(256)S(1)}, s32[128]{0:T(128)S(1)}, bf16[512,256]{1,0:T(8,128)(2,1)S(1)}) custom-call(s32[1,1,17]{2,1,0:T(1,128)S(1)} %copy-done.3, s32[1,1,128]{2,1,0:T(1,128)S(1)} %copy-done.4, bf16[512,256]{1,0:T(8,128)(2,1)S(1)} %copy-done), custom_call_target="tpu_custom_call" | custom-call | tf_op jit(solution)/shard_map/pallas_call | solution.py:57
  10.4 0.6 collective-permute-done.refs_2_
  11.0 0.0 collective-permute-start.1
  11.0 0.5 collective-permute-start.2
  11.5 5.7 %collective-permute-done.3.refs_4_ = bf16[512,256]{1,0:T(8,128)(2,1)S(1)} collective-permute-done((bf16[512,256]{1,0:T(8,128)(2,1)}, bf16[512,256]{1,0:T(8,128)(2,1)S(1)}, u32[]{:S(2)}, u32[]{:S(2)}) %collective-permute-start.3) | collective-permute-done | bytes 262176 | tf_op jit(solution)/shard_map/ppermute | solution.py:263
  17.2 0.0 collective-permute-start.4
  17.2 0.0 collective-permute-done.5.refs_6_
  17.2 0.5 collective-permute-start.6
  17.7 0.0 collective-permute-done.1.refs_1_
  17.7 0.0 collective-permute-done.2.refs_3_
  17.8 1.0 collective-permute-done.4.refs_5_
  18.8 0.4 collective-permute-done.6.refs_7_
  19.1 4.1 %shard_map.86 = (bf16[512,256]{1,0:T(8,128)(2,1)S(1)}, bf16[512,256]{1,0:T(8,128)(2,1)S(1)}, bf16[512,256]{1,0:T(8,128)(2,1)S(1)}, bf16[512,256]{1,0:T(8,128)(2,1)S(1)}) custom-call(s32[129]{0:T(256)S(1)} %get-tuple-element.31.row_of, s32[128]{0:T(128)S(1)} %get-tuple-element.32.col_of, s32[1]{0:T(128)} %bitcast.here_ref.me.mine_ref, ...), custom_call_target="tpu_custom_call" | custom-call | flops 1073741824 | bytes 6291456 | tf_op jit(solution)/shard_map/pallas_call | solution.py:135
  23.2 1.3 %collective-permute-start.7 = (bf16[512,256]{1,0:T(8,128)(2,1)S(1)}, bf16[512,256]{1,0:T(8,128)(2,1)S(1)}, u32[]{:S(2)}, u32[]{:S(2)}) collective-permute-start(bf16[512,256]{1,0:T(8,128)(2,1)S(1)} %get-tuple-element.36), channel_id=1, source_target_pairs={{0,1},{1,0},{2,3},{3,2},{4,5},{5,4},{6,7},{7,6},{8,9},{9,8},{10,11... | collective-permute-start | bytes 786440 | tf_op jit(solution)/shard_map/ppermute | solution.py:263
  24.6 2.6 %collective-permute-start.8 = (bf16[512,256]{1,0:T(8,128)(2,1)S(1)}, bf16[512,256]{1,0:T(8,128)(2,1)S(1)}, u32[]{:S(2)}, u32[]{:S(2)}) collective-permute-start(bf16[512,256]{1,0:T(8,128)(2,1)S(1)} %get-tuple-element.37), channel_id=1, source_target_pairs={{0,2},{1,3},{2,0},{3,1},{4,6},{5,7},{6,4},{7,5},{8,10},{9,11},{10,... | collective-permute-start | bytes 786440 | tf_op jit(solution)/shard_map/ppermute | solution.py:263
  27.2 0.5 collective-permute-start.9
  27.7 8.9 %collective-permute-done.7.refs_1_ = bf16[512,256]{1,0:T(8,128)(2,1)S(1)} collective-permute-done((bf16[512,256]{1,0:T(8,128)(2,1)S(1)}, bf16[512,256]{1,0:T(8,128)(2,1)S(1)}, u32[]{:S(2)}, u32[]{:S(2)}) %collective-permute-start.7) | collective-permute-done | bytes 262176 | tf_op jit(solution)/shard_map/ppermute | solution.py:263
  36.6 9.3 %collective-permute-done.8.refs_2_ = bf16[512,256]{1,0:T(8,128)(2,1)S(1)} collective-permute-done((bf16[512,256]{1,0:T(8,128)(2,1)S(1)}, bf16[512,256]{1,0:T(8,128)(2,1)S(1)}, u32[]{:S(2)}, u32[]{:S(2)}) %collective-permute-start.8) | collective-permute-done | bytes 262176 | tf_op jit(solution)/shard_map/ppermute | solution.py:263
  45.9 0.0 collective-permute-done.9.refs_3_
  45.9 0.0 copy-done.1
  45.9 0.0 copy-done.2
  45.9 1.2 %shard_map.87 = (bf16[512,256]{1,0:T(8,128)(2,1)}, bf16[512,256]{1,0:T(8,128)(2,1)S(1)}, f32[512,256]{1,0:T(8,128)S(1)}, f32[512,256]{1,0:T(8,128)S(1)}) custom-call(bf16[512,256]{1,0:T(8,128)(2,1)S(1)} %get-tuple-element.35.refs_0_, bf16[512,256]{1,0:T(8,128)(2,1)S(1)} %collective-permute-done.7.refs_1_, ...), custom_call_target="tpu_custom_call" | custom-call | flops 268435456 | bytes 2621440 | tf_op jit(solution)/shard_map/pallas_call | solution.py:182
  47.1 5.3 %collective-permute-start.11 = (bf16[512,256]{1,0:T(8,128)(2,1)S(1)}, bf16[512,256]{1,0:T(8,128)(2,1)S(1)}, u32[]{:S(2)}, u32[]{:S(2)}) collective-permute-start(bf16[512,256]{1,0:T(8,128)(2,1)S(1)} %get-tuple-element.45.refs_0_), channel_id=1, source_target_pairs={{0,1},{1,0},{2,3},{3,2},{4,5},{5,4},{6,7},{7,6},{8,9},{9,8},{10,11... | collective-permute-start | bytes 786440 | tf_op jit(solution)/shard_map/ppermute | solution.py:263
  52.5 1.4 %collective-permute-start.12 = (bf16[512,256]{1,0:T(8,128)(2,1)S(1)}, bf16[512,256]{1,0:T(8,128)(2,1)S(1)}, u32[]{:S(2)}, u32[]{:S(2)}) collective-permute-start(bf16[512,256]{1,0:T(8,128)(2,1)S(1)} %get-tuple-element.45.refs_0_), channel_id=1, source_target_pairs={{0,2},{1,3},{2,0},{3,1},{4,6},{5,7},{6,4},{7,5},{8,10},{9,11},{10,... | collective-permute-start | bytes 786440 | tf_op jit(solution)/shard_map/ppermute | solution.py:263
  53.8 1.5 %collective-permute-start.13 = (bf16[512,256]{1,0:T(8,128)(2,1)S(1)}, bf16[512,256]{1,0:T(8,128)(2,1)S(1)}, u32[]{:S(2)}, u32[]{:S(2)}) collective-permute-start(bf16[512,256]{1,0:T(8,128)(2,1)S(1)} %get-tuple-element.45.refs_0_), channel_id=1, source_target_pairs={{0,3},{1,2},{2,1},{3,0},{4,7},{5,6},{6,5},{7,4},{8,11},{9,10},{10,... | collective-permute-start | bytes 786440 | tf_op jit(solution)/shard_map/ppermute | solution.py:263
  55.3 0.4 shard_map.88
  55.8 0.1 collective-permute-start.10
  55.8 1.3 %collective-permute-done.10 = f32[128,256]{1,0:T(8,128)S(1)} collective-permute-done((f32[128,256]{1,0:T(8,128)S(1)}, f32[128,256]{1,0:T(8,128)S(1)}, u32[]{:S(2)}, u32[]{:S(2)}) %collective-permute-start.10) | collective-permute-done | bytes 131104 | tf_op jit(solution)/shard_map/ppermute | solution.py:263
  57.2 7.6 %all_to_all.9 = f32[4,32,256]{2,1,0:T(8,128)S(1)} all-to-all(f32[4,32,256]{2,1,0:T(8,128)S(1)} %bitcast.9), channel_id=1, replica_groups={{0,8,16,24},{4,12,20,28},{1,9,17,25},{5,13,21,29},{2,10,18,26},{6,14,22..., dimensions={0} | all-to-all | bytes 262144 | tf_op jit(solution)/shard_map/all_to_all | solution.py:304
  64.8 7.6 %all_gather.6 = bf16[128,256]{1,0:T(8,128)(2,1)S(1)} all-gather(bf16[32,256]{1,0:T(8,128)(2,1)S(1)} %reduce_sum.18), channel_id=1, replica_groups={{0,8,16,24},{4,12,20,28},{1,9,17,25},{5,13,21,29},{2,10,18,26},{6,14,22..., dimensions={0}, use_global_device_ids=true | all-gather | bytes 81920 | tf_op jit(solution)/shard_map/all_gather | solution.py:306
  72.4 0.0 collective-permute-done.11.refs_1_
  72.4 1.4 %collective-permute-done.12.refs_2_ = bf16[512,256]{1,0:T(8,128)(2,1)S(1)} collective-permute-done((bf16[512,256]{1,0:T(8,128)(2,1)S(1)}, bf16[512,256]{1,0:T(8,128)(2,1)S(1)}, u32[]{:S(2)}, u32[]{:S(2)}) %collective-permute-start.12) | collective-permute-done | bytes 262176 | tf_op jit(solution)/shard_map/ppermute | solution.py:263
  73.9 0.0 collective-permute-done.13.refs_3_
  73.9 4.3 %shard_map.89 = (bf16[2048,256]{1,0:T(8,128)(2,1)S(1)}, bf16[2048,256]{1,0:T(8,128)(2,1)S(1)}) custom-call(s32[129]{0:T(256)S(1)} %get-tuple-element.31.row_of, s32[128]{0:T(128)S(1)} %get-tuple-element.32.col_of, s32[1]{0:T(128)} %bitcast.1.mine_ref.here_ref, s32[1]{0:T(128)} %bitcast.here_ref.me.mine_ref, bf16[512,256]{1,0:T(8,128)(2,1)S(1)} %get-tuple-element.45.refs_0_, ...), custom_call_target="tpu_custom_call" | custom-call | flops 1073741824 | bytes 5242880 | tf_op jit(solution)/shard_map/pallas_call | solution.py:135
  78.2 0.1 collective-permute-start.14
  78.3 2.6 %collective-permute-done.14.other_ref = bf16[2048,256]{1,0:T(8,128)(2,1)S(1)} collective-permute-done((bf16[2048,256]{1,0:T(8,128)(2,1)S(1)}, bf16[2048,256]{1,0:T(8,128)(2,1)S(1)}, u32[]{:S(2)}, u32[]{:S(2)}) %collective-permute-start.14) | collective-permute-done | bytes 1048608 | tf_op jit(solution)/shard_map/ppermute | solution.py:263
  80.9 0.2 shard_map.90
  81.2 0.2 collective-permute-start.17
  81.4 2.2 %collective-permute-start.16 = (bf16[512,256]{1,0:T(8,128)(2,1)S(1)}, bf16[512,256]{1,0:T(8,128)(2,1)S(1)}, u32[]{:S(2)}, u32[]{:S(2)}) collective-permute-start(bf16[512,256]{1,0:T(8,128)(2,1)S(1)} %get-tuple-element.50), channel_id=1, source_target_pairs={{0,16},{4,20},{8,24},{12,28},{16,0},{20,4},{24,8},{28,12},{1,17},{... | collective-permute-start | bytes 786440 | tf_op jit(solution)/shard_map/ppermute | solution.py:263
  83.5 1.4 %collective-permute-start.15 = (bf16[512,256]{1,0:T(8,128)(2,1)S(1)}, bf16[512,256]{1,0:T(8,128)(2,1)S(1)}, u32[]{:S(2)}, u32[]{:S(2)}) collective-permute-start(bf16[512,256]{1,0:T(8,128)(2,1)S(1)} %get-tuple-element.49), channel_id=1, source_target_pairs={{0,8},{4,12},{8,0},{12,4},{16,24},{20,28},{24,16},{28,20},{1,9},{5... | collective-permute-start | bytes 786440 | tf_op jit(solution)/shard_map/ppermute | solution.py:263
  84.9 17.3 %all_gather.7 = bf16[512,256]{1,0:T(8,128)(2,1)S(1)} all-gather(bf16[128,256]{1,0:T(8,128)(2,1)S(1)} %all_gather.6), channel_id=1, replica_groups=mesh['row'=8,'col'=4] {'col'}, dimensions={0}, use_global_device_ids=true | all-gather | bytes 327680 | tf_op jit(solution)/shard_map/all_gather | solution.py:318
  102.2 0.1 collective-permute-start.18
  102.3 1.3 %collective-permute-done.18.other_ref = f32[128,256]{1,0:T(8,128)S(1)} collective-permute-done((f32[128,256]{1,0:T(8,128)S(1)}, f32[128,256]{1,0:T(8,128)S(1)}, u32[]{:S(2)}, u32[]{:S(2)}) %collective-permute-start.18) | collective-permute-done | bytes 131104 | tf_op jit(solution)/shard_map/ppermute | solution.py:263
  103.6 0.7 shard_map.91
  104.4 0.0 collective-permute-done.17
  104.4 0.0 collective-permute-done.16
  104.4 0.0 collective-permute-done.15
  104.4 0.8 add_convert_fusion
  (3 shorter events, 0.1 us)
Async XLA Ops:
  0.6 10.3 %collective-permute-start = (bf16[512,256]{1,0:T(8,128)(2,1)}, bf16[512,256]{1,0:T(8,128)(2,1)S(1)}, u32[]{:S(2)}, u32[]{:S(2)}) collective-permute-start(bf16[512,256]{1,0:T(8,128)(2,1)} %features.1), channel_id=1, source_target_pairs={{0,8},{4,12},{8,0},{12,4},{16,24},{20,28},{24,16},{28,20},{1,9},{5... | collective-permute-start | bytes 786440 | tf_op jit(solution)/shard_map/ppermute | solution.py:263
  3.6 13.6 %collective-permute-start.3 = (bf16[512,256]{1,0:T(8,128)(2,1)}, bf16[512,256]{1,0:T(8,128)(2,1)S(1)}, u32[]{:S(2)}, u32[]{:S(2)}) collective-permute-start(bf16[512,256]{1,0:T(8,128)(2,1)} %features.1), channel_id=1, source_target_pairs={{0,16},{4,20},{8,24},{12,28},{16,0},{20,4},{24,8},{28,12},{1,17},{... | collective-permute-start | bytes 786440 | tf_op jit(solution)/shard_map/ppermute | solution.py:263
  5.2 12.1 %collective-permute-start.5 = (bf16[512,256]{1,0:T(8,128)(2,1)}, bf16[512,256]{1,0:T(8,128)(2,1)S(1)}, u32[]{:S(2)}, u32[]{:S(2)}) collective-permute-start(bf16[512,256]{1,0:T(8,128)(2,1)} %features.1), channel_id=1, source_target_pairs={{0,24},{4,28},{8,16},{12,20},{16,8},{20,12},{24,0},{28,4},{1,25},{... | collective-permute-start | bytes 786440 | tf_op jit(solution)/shard_map/ppermute | solution.py:263
  5.2 1.0 copy-start
  6.2 0.7 copy-start.3
  6.8 0.7 copy-start.4
  7.5 38.4 %copy-start.1 = (bf16[512,256]{1,0:T(8,128)(2,1)S(1)}, bf16[512,256]{1,0:T(8,128)(2,1)}, u32[]{:S(2)}) copy-start(bf16[512,256]{1,0:T(8,128)(2,1)} %refs_5_.1) | copy-start | bytes 786436
  7.5 38.4 %copy-start.2 = (bf16[256,256]{1,0:T(8,128)(2,1)S(1)}, bf16[256,256]{1,0:T(8,128)(2,1)}, u32[]{:S(2)}) copy-start(bf16[256,256]{1,0:T(8,128)(2,1)} %refs_4_.1) | copy-start | bytes 393220
  11.0 6.8 %collective-permute-start.1 = (bf16[512,256]{1,0:T(8,128)(2,1)S(1)}, bf16[512,256]{1,0:T(8,128)(2,1)S(1)}, u32[]{:S(2)}, u32[]{:S(2)}) collective-permute-start(bf16[512,256]{1,0:T(8,128)(2,1)S(1)} %get-tuple-element.33.refs_0_), channel_id=1, source_target_pairs={{0,4},{4,0},{8,12},{12,8},{16,20},{20,16},{24,28},{28,24},{1,5},{5... | collective-permute-start | bytes 786440 | tf_op jit(solution)/shard_map/ppermute | solution.py:263
  11.0 6.8 %collective-permute-start.2 = (bf16[512,256]{1,0:T(8,128)(2,1)S(1)}, bf16[512,256]{1,0:T(8,128)(2,1)S(1)}, u32[]{:S(2)}, u32[]{:S(2)}) collective-permute-start(bf16[512,256]{1,0:T(8,128)(2,1)S(1)} %collective-permute-done.refs_2_), channel_id=1, source_target_pairs={{0,4},{4,0},{8,12},{12,8},{16,20},{20,16},{24,28},{28,24},{1,5},{5... | collective-permute-start | bytes 786440 | tf_op jit(solution)/shard_map/ppermute | solution.py:263
  17.2 1.5 %collective-permute-start.4 = (bf16[512,256]{1,0:T(8,128)(2,1)S(1)}, bf16[512,256]{1,0:T(8,128)(2,1)S(1)}, u32[]{:S(2)}, u32[]{:S(2)}) collective-permute-start(bf16[512,256]{1,0:T(8,128)(2,1)S(1)} %collective-permute-done.3.refs_4_), channel_id=1, source_target_pairs={{0,4},{4,0},{8,12},{12,8},{16,20},{20,16},{24,28},{28,24},{1,5},{5... | collective-permute-start | bytes 786440 | tf_op jit(solution)/shard_map/ppermute | solution.py:263
  17.2 1.9 %collective-permute-start.6 = (bf16[512,256]{1,0:T(8,128)(2,1)S(1)}, bf16[512,256]{1,0:T(8,128)(2,1)S(1)}, u32[]{:S(2)}, u32[]{:S(2)}) collective-permute-start(bf16[512,256]{1,0:T(8,128)(2,1)S(1)} %collective-permute-done.5.refs_6_), channel_id=1, source_target_pairs={{0,4},{4,0},{8,12},{12,8},{16,20},{20,16},{24,28},{28,24},{1,5},{5... | collective-permute-start | bytes 786440 | tf_op jit(solution)/shard_map/ppermute | solution.py:263
  23.2 13.4 %collective-permute-start.7 = (bf16[512,256]{1,0:T(8,128)(2,1)S(1)}, bf16[512,256]{1,0:T(8,128)(2,1)S(1)}, u32[]{:S(2)}, u32[]{:S(2)}) collective-permute-start(bf16[512,256]{1,0:T(8,128)(2,1)S(1)} %get-tuple-element.36), channel_id=1, source_target_pairs={{0,1},{1,0},{2,3},{3,2},{4,5},{5,4},{6,7},{7,6},{8,9},{9,8},{10,11... | collective-permute-start | bytes 786440 | tf_op jit(solution)/shard_map/ppermute | solution.py:263
  24.6 21.3 %collective-permute-start.8 = (bf16[512,256]{1,0:T(8,128)(2,1)S(1)}, bf16[512,256]{1,0:T(8,128)(2,1)S(1)}, u32[]{:S(2)}, u32[]{:S(2)}) collective-permute-start(bf16[512,256]{1,0:T(8,128)(2,1)S(1)} %get-tuple-element.37), channel_id=1, source_target_pairs={{0,2},{1,3},{2,0},{3,1},{4,6},{5,7},{6,4},{7,5},{8,10},{9,11},{10,... | collective-permute-start | bytes 786440 | tf_op jit(solution)/shard_map/ppermute | solution.py:263
  27.2 18.7 %collective-permute-start.9 = (bf16[512,256]{1,0:T(8,128)(2,1)S(1)}, bf16[512,256]{1,0:T(8,128)(2,1)S(1)}, u32[]{:S(2)}, u32[]{:S(2)}) collective-permute-start(bf16[512,256]{1,0:T(8,128)(2,1)S(1)} %get-tuple-element.38), channel_id=1, source_target_pairs={{0,3},{1,2},{2,1},{3,0},{4,7},{5,6},{6,5},{7,4},{8,11},{9,10},{10,... | collective-permute-start | bytes 786440 | tf_op jit(solution)/shard_map/ppermute | solution.py:263
  47.1 25.3 %collective-permute-start.11 = (bf16[512,256]{1,0:T(8,128)(2,1)S(1)}, bf16[512,256]{1,0:T(8,128)(2,1)S(1)}, u32[]{:S(2)}, u32[]{:S(2)}) collective-permute-start(bf16[512,256]{1,0:T(8,128)(2,1)S(1)} %get-tuple-element.45.refs_0_), channel_id=1, source_target_pairs={{0,1},{1,0},{2,3},{3,2},{4,5},{5,4},{6,7},{7,6},{8,9},{9,8},{10,11... | collective-permute-start | bytes 786440 | tf_op jit(solution)/shard_map/ppermute | solution.py:263
  52.5 21.4 %collective-permute-start.12 = (bf16[512,256]{1,0:T(8,128)(2,1)S(1)}, bf16[512,256]{1,0:T(8,128)(2,1)S(1)}, u32[]{:S(2)}, u32[]{:S(2)}) collective-permute-start(bf16[512,256]{1,0:T(8,128)(2,1)S(1)} %get-tuple-element.45.refs_0_), channel_id=1, source_target_pairs={{0,2},{1,3},{2,0},{3,1},{4,6},{5,7},{6,4},{7,5},{8,10},{9,11},{10,... | collective-permute-start | bytes 786440 | tf_op jit(solution)/shard_map/ppermute | solution.py:263
  53.8 20.0 %collective-permute-start.13 = (bf16[512,256]{1,0:T(8,128)(2,1)S(1)}, bf16[512,256]{1,0:T(8,128)(2,1)S(1)}, u32[]{:S(2)}, u32[]{:S(2)}) collective-permute-start(bf16[512,256]{1,0:T(8,128)(2,1)S(1)} %get-tuple-element.45.refs_0_), channel_id=1, source_target_pairs={{0,3},{1,2},{2,1},{3,0},{4,7},{5,6},{6,5},{7,4},{8,11},{9,10},{10,... | collective-permute-start | bytes 786440 | tf_op jit(solution)/shard_map/ppermute | solution.py:263
  55.8 1.4 %collective-permute-start.10 = (f32[128,256]{1,0:T(8,128)S(1)}, f32[128,256]{1,0:T(8,128)S(1)}, u32[]{:S(2)}, u32[]{:S(2)}) collective-permute-start(f32[128,256]{1,0:T(8,128)S(1)} %get-tuple-element.43), channel_id=1, source_target_pairs={{0,4},{4,0},{8,12},{12,8},{16,20},{20,16},{24,28},{28,24},{1,5},{5... | collective-permute-start | bytes 393224 | tf_op jit(solution)/shard_map/ppermute | solution.py:263
  78.2 2.7 %collective-permute-start.14 = (bf16[2048,256]{1,0:T(8,128)(2,1)S(1)}, bf16[2048,256]{1,0:T(8,128)(2,1)S(1)}, u32[]{:S(2)}, u32[]{:S(2)}) collective-permute-start(bf16[2048,256]{1,0:T(8,128)(2,1)S(1)} %get-tuple-element.47), channel_id=1, source_target_pairs={{0,4},{4,0},{8,12},{12,8},{16,20},{20,16},{24,28},{28,24},{1,5},{5... | collective-permute-start | bytes 3145736 | tf_op jit(solution)/shard_map/ppermute | solution.py:263
  81.2 23.2 %collective-permute-start.17 = (bf16[512,256]{1,0:T(8,128)(2,1)S(1)}, bf16[512,256]{1,0:T(8,128)(2,1)S(1)}, u32[]{:S(2)}, u32[]{:S(2)}) collective-permute-start(bf16[512,256]{1,0:T(8,128)(2,1)S(1)} %get-tuple-element.51), channel_id=1, source_target_pairs={{0,24},{4,28},{8,16},{12,20},{16,8},{20,12},{24,0},{28,4},{1,25},{... | collective-permute-start | bytes 786440 | tf_op jit(solution)/shard_map/ppermute | solution.py:263
  81.4 23.0 %collective-permute-start.16 = (bf16[512,256]{1,0:T(8,128)(2,1)S(1)}, bf16[512,256]{1,0:T(8,128)(2,1)S(1)}, u32[]{:S(2)}, u32[]{:S(2)}) collective-permute-start(bf16[512,256]{1,0:T(8,128)(2,1)S(1)} %get-tuple-element.50), channel_id=1, source_target_pairs={{0,16},{4,20},{8,24},{12,28},{16,0},{20,4},{24,8},{28,12},{1,17},{... | collective-permute-start | bytes 786440 | tf_op jit(solution)/shard_map/ppermute | solution.py:263
  83.5 20.8 %collective-permute-start.15 = (bf16[512,256]{1,0:T(8,128)(2,1)S(1)}, bf16[512,256]{1,0:T(8,128)(2,1)S(1)}, u32[]{:S(2)}, u32[]{:S(2)}) collective-permute-start(bf16[512,256]{1,0:T(8,128)(2,1)S(1)} %get-tuple-element.49), channel_id=1, source_target_pairs={{0,8},{4,12},{8,0},{12,4},{16,24},{20,28},{24,16},{28,20},{1,9},{5... | collective-permute-start | bytes 786440 | tf_op jit(solution)/shard_map/ppermute | solution.py:263
  102.2 1.4 %collective-permute-start.18 = (f32[128,256]{1,0:T(8,128)S(1)}, f32[128,256]{1,0:T(8,128)S(1)}, u32[]{:S(2)}, u32[]{:S(2)}) collective-permute-start(f32[128,256]{1,0:T(8,128)S(1)} %convert_reduce_fusion.own_ref), channel_id=1, source_target_pairs={{0,4},{4,0},{8,12},{12,8},{16,20},{20,16},{24,28},{28,24},{1,5},{5... | collective-permute-start | bytes 393224 | tf_op jit(solution)/shard_map/ppermute | solution.py:263

commit v6 on v5

--- a/solution.py
+++ b/solution.py
@@ -10,6 +10,7 @@
 F32 = jnp.float32
 BF16 = jnp.bfloat16
 GROUP = 8
+LONG = 32
 ANY = pl.BlockSpec(memory_space=pl.ANY)
 VMEM = pl.BlockSpec(memory_space=pltpu.VMEM)
 SMEM = pl.BlockSpec(memory_space=pltpu.SMEM)
@@ -71,19 +72,10 @@
     panel_refs = refs[:parts]
     values_ref = refs[parts]
     out_refs = refs[parts + 1 : parts + 1 + len(outs)]
-    panel, values, total, panel_sem, values_sem = refs[parts + 1 + len(outs) :]
+    panel, values, total, values_sem = refs[parts + 1 + len(outs) :]
     slots, size, _ = values.shape
     live, here, mine = row_of[slots], here_ref[0], mine_ref[0]
     chunk = panel_refs[0].shape[0]
-    loads = []
-    for m in range(parts):
-        start = pl.multiple_of((here ^ m) * chunk, chunk)
-        copy = pltpu.make_async_copy(
-            panel_refs[m], panel.at[pl.ds(start, chunk)], panel_sem.at[m]
-        )
-        copy.start()
-        loads.append(copy)
-
     def load(g):
         span = pl.ds(pl.multiple_of(g * GROUP, GROUP), GROUP)
         return pltpu.make_async_copy(values_ref.at[span], values.at[span], values_sem.at[g])
@@ -95,29 +87,38 @@
     used = (live + GROUP - 1) // GROUP
     lax.fori_loop(0, used, begin, 0)
     total[...] = jnp.zeros_like(total)
-    for copy in loads:
-        copy.wait()
+    for m in range(parts):
+        start = pl.multiple_of((here ^ m) * chunk, chunk)
+        panel[pl.ds(start, chunk), :] = panel_refs[m][...]
     spare = total.shape[0] // size - 1
     last = panel.shape[0] // size - 1
 
-    def step(g, carry):
-        load(g).wait()
-        for u in range(GROUP):
-            k = g * GROUP + u
-            row, col = row_of[k], col_of[k]
-            to, source = (col, jnp.minimum(row, last)) if backward else (row, col)
-            to = pl.multiple_of(jnp.where(k < live, to, spare) * size, size)
-            source = pl.multiple_of(source * size, size)
-            term = lax.dot_general(
-                values[k],
-                panel[pl.ds(source, size), :],
-                (((0 if backward else 1,), (0,)), ((), ())),
-                preferred_element_type=F32,
-            )
-            total[pl.ds(to, size), :] += term
-        return carry
-
-    lax.fori_loop(0, used, step, 0)
+    def add_slot(k):
+        row, col = row_of[k], col_of[k]
+        to, source = (col, jnp.minimum(row, last)) if backward else (row, col)
+        to = pl.multiple_of(jnp.where(k < live, to, spare) * size, size)
+        source = pl.multiple_of(source * size, size)
+        term = lax.dot_general(
+            values[k],
+            panel[pl.ds(source, size), :],
+            (((0 if backward else 1,), (0,)), ((), ())),
+            preferred_element_type=F32,
+        )
+        total[pl.ds(to, size), :] += term
+
+    def steps(count):
+        def step(g, carry):
+            for part in range(count // GROUP):
+                load(g * (count // GROUP) + part).wait()
+            for u in range(count):
+                add_slot(g * count + u)
+            return carry
+
+        return step
+
+    long = live // LONG
+    lax.fori_loop(0, long, steps(LONG), 0)
+    lax.fori_loop(long * (LONG // GROUP), used, steps(GROUP), 0)
     for out_ref, members in zip(out_refs, outs):
         rows = out_ref.shape[0] // len(members)
         for at, m in enumerate(members):
@@ -135,13 +136,12 @@
     return pl.pallas_call(
         functools.partial(sparse_kernel, parts, outs, backward),
         out_shape=[jax.ShapeDtypeStruct((chunk * len(members), width), BF16) for members in outs],
-        in_specs=[SMEM] * 4 + [ANY] * (parts + 1),
+        in_specs=[SMEM] * 4 + [VMEM] * parts + [ANY],
         out_specs=[VMEM] * len(outs),
         scratch_shapes=[
             pltpu.VMEM((parts * chunk, width), BF16),
             pltpu.VMEM((slots, size, size), BF16),
             pltpu.VMEM(((blocks + 1) * size, width), F32),
-            pltpu.SemaphoreType.DMA((parts,)),
             pltpu.SemaphoreType.DMA((slots // GROUP,)),
         ],
         compiler_params=params(48),

time: 105 us -> 104 us (level)
  no operation moved by 1% of the time
where the time goes in v6:
time: 104 us
  blocking collectives  33.2 us (32%)
  waiting for transfers between devices  32.5 us (31%)
  starting transfers between devices  21.4 us (21%)
  Pallas kernels  13 us (12%)
  local copies, waits for them, and re-layouts  2.31 us (2%)
    ppermute x19, waiting for transfers between devices, swap(): return lax.ppermute(x, axis, [(i, i ^ m) for i in range(n)])  32.5 us
    ppermute x19, starting transfers between devices, swap(): return lax.ppermute(x, axis, [(i, i ^ m) for i in range(n)])  21.4 us
    all_gather x1, blocking collectives, on_device(): halves = lax.all_gather(half.astype(BF16), 'col', axis=0, tiled=True)  17.3 us
    all_to_all x1, blocking collectives, on_device(): lax.all_to_all(term, 'row', 0, 0, axis_index_groups=cores, tiled=True)  8.21 us
    all_gather x1, blocking collectives, on_device(): lax.all_gather(piece, 'row', axis=0, axis_index_groups=cores, tiled=True)  7.64 us
    pallas_call x2, Pallas kernels, sparse_product(): pl.pallas_call(functools.partial(sparse_kernel, parts, outs, backward), o...  7.47 us
    pallas_call x1, Pallas kernels, prepare(): pl.pallas_call(prepare_kernel, out_shape=[jax.ShapeDtypeStruct((slots + 1...  2.88 us
    unnamed x10, local copies, waits for them, and re-layouts  2.31 us
  transfers between devices with their start and end apart: 19, of which 10 were waited for; matrix products, arithmetic and copies ran while one was open for 0% of the time, Pallas kernels for 4%

profile of v6, /device:TPU:0, one launch (start us, length us, event | category | flops | bytes accessed | tf_op | source)
XLA Modules:
  0.0 104.1 jit_solution(2454958640904794891)
XLA Ops:
  0.6 3.0 %collective-permute-start = (bf16[512,256]{1,0:T(8,128)(2,1)}, bf16[512,256]{1,0:T(8,128)(2,1)S(1)}, u32[]{:S(2)}, u32[]{:S(2)}) collective-permute-start(bf16[512,256]{1,0:T(8,128)(2,1)} %features.1), channel_id=1, source_target_pairs={{0,8},{4,12},{8,0},{12,4},{16,24},{20,28},{24,16},{28,20},{1,9},{5... | collective-permute-start | bytes 786440 | tf_op jit(solution)/shard_map/ppermute | solution.py:263
  3.6 1.5 %collective-permute-start.3 = (bf16[512,256]{1,0:T(8,128)(2,1)}, bf16[512,256]{1,0:T(8,128)(2,1)S(1)}, u32[]{:S(2)}, u32[]{:S(2)}) collective-permute-start(bf16[512,256]{1,0:T(8,128)(2,1)} %features.1), channel_id=1, source_target_pairs={{0,16},{4,20},{8,24},{12,28},{16,0},{20,4},{24,8},{28,12},{1,17},{... | collective-permute-start | bytes 786440 | tf_op jit(solution)/shard_map/ppermute | solution.py:263
  5.2 0.0 collective-permute-start.5
  5.2 0.0 copy-start
  5.2 1.0 copy-done
  6.2 0.0 copy-start.3
  6.2 0.7 copy-done.3
  6.8 0.0 copy-start.4
  6.8 0.7 copy-done.4
  7.5 0.0 copy-start.1
  7.5 0.0 copy-start.2
  7.5 2.9 %shard_map.85 = (s32[129]{0:T(256)S(1)}, s32[128]{0:T(128)S(1)}, bf16[512,256]{1,0:T(8,128)(2,1)S(1)}) custom-call(s32[1,1,17]{2,1,0:T(1,128)S(1)} %copy-done.3, s32[1,1,128]{2,1,0:T(1,128)S(1)} %copy-done.4, bf16[512,256]{1,0:T(8,128)(2,1)S(1)} %copy-done), custom_call_target="tpu_custom_call" | custom-call | tf_op jit(solution)/shard_map/pallas_call | solution.py:58
  10.4 0.6 collective-permute-done.refs_2_
  11.0 0.0 collective-permute-start.1
  11.0 0.5 collective-permute-start.2
  11.5 5.7 %collective-permute-done.3.refs_4_ = bf16[512,256]{1,0:T(8,128)(2,1)S(1)} collective-permute-done((bf16[512,256]{1,0:T(8,128)(2,1)}, bf16[512,256]{1,0:T(8,128)(2,1)S(1)}, u32[]{:S(2)}, u32[]{:S(2)}) %collective-permute-start.3) | collective-permute-done | bytes 262176 | tf_op jit(solution)/shard_map/ppermute | solution.py:263
  17.2 0.0 collective-permute-start.4
  17.2 0.0 collective-permute-done.5.refs_6_
  17.2 0.5 collective-permute-start.6
  17.7 0.0 collective-permute-done.1.refs_1_
  17.7 0.0 collective-permute-done.2.refs_3_
  17.8 1.0 collective-permute-done.4.refs_5_
  18.8 0.4 collective-permute-done.6.refs_7_
  19.1 3.6 %shard_map.86 = (bf16[512,256]{1,0:T(8,128)(2,1)S(1)}, bf16[512,256]{1,0:T(8,128)(2,1)S(1)}, bf16[512,256]{1,0:T(8,128)(2,1)S(1)}, bf16[512,256]{1,0:T(8,128)(2,1)S(1)}) custom-call(s32[129]{0:T(256)S(1)} %get-tuple-element.31.row_of, s32[128]{0:T(128)S(1)} %get-tuple-element.32.col_of, s32[1]{0:T(128)} %bitcast.here_ref.me.mine_ref, ...), custom_call_target="tpu_custom_call" | custom-call | flops 1073741824 | bytes 6291456 | tf_op jit(solution)/shard_map/pallas_call | solution.py:136
  22.8 1.5 %collective-permute-start.7 = (bf16[512,256]{1,0:T(8,128)(2,1)S(1)}, bf16[512,256]{1,0:T(8,128)(2,1)S(1)}, u32[]{:S(2)}, u32[]{:S(2)}) collective-permute-start(bf16[512,256]{1,0:T(8,128)(2,1)S(1)} %get-tuple-element.36), channel_id=1, source_target_pairs={{0,1},{1,0},{2,3},{3,2},{4,5},{5,4},{6,7},{7,6},{8,9},{9,8},{10,11... | collective-permute-start | bytes 786440 | tf_op jit(solution)/shard_map/ppermute | solution.py:263
  24.2 2.8 %collective-permute-start.8 = (bf16[512,256]{1,0:T(8,128)(2,1)S(1)}, bf16[512,256]{1,0:T(8,128)(2,1)S(1)}, u32[]{:S(2)}, u32[]{:S(2)}) collective-permute-start(bf16[512,256]{1,0:T(8,128)(2,1)S(1)} %get-tuple-element.37), channel_id=1, source_target_pairs={{0,2},{1,3},{2,0},{3,1},{4,6},{5,7},{6,4},{7,5},{8,10},{9,11},{10,... | collective-permute-start | bytes 786440 | tf_op jit(solution)/shard_map/ppermute | solution.py:263
  27.0 0.2 collective-permute-start.9
  27.2 8.3 %collective-permute-done.7.refs_1_ = bf16[512,256]{1,0:T(8,128)(2,1)S(1)} collective-permute-done((bf16[512,256]{1,0:T(8,128)(2,1)S(1)}, bf16[512,256]{1,0:T(8,128)(2,1)S(1)}, u32[]{:S(2)}, u32[]{:S(2)}) %collective-permute-start.7) | collective-permute-done | bytes 262176 | tf_op jit(solution)/shard_map/ppermute | solution.py:263
  35.5 10.0 %collective-permute-done.8.refs_2_ = bf16[512,256]{1,0:T(8,128)(2,1)S(1)} collective-permute-done((bf16[512,256]{1,0:T(8,128)(2,1)S(1)}, bf16[512,256]{1,0:T(8,128)(2,1)S(1)}, u32[]{:S(2)}, u32[]{:S(2)}) %collective-permute-start.8) | collective-permute-done | bytes 262176 | tf_op jit(solution)/shard_map/ppermute | solution.py:263
  45.6 0.0 collective-permute-done.9.refs_3_
  45.6 0.0 copy-done.1
  45.6 0.0 copy-done.2
  45.6 1.2 %shard_map.87 = (bf16[512,256]{1,0:T(8,128)(2,1)}, bf16[512,256]{1,0:T(8,128)(2,1)S(1)}, f32[512,256]{1,0:T(8,128)S(1)}, f32[512,256]{1,0:T(8,128)S(1)}) custom-call(bf16[512,256]{1,0:T(8,128)(2,1)S(1)} %get-tuple-element.35.refs_0_, bf16[512,256]{1,0:T(8,128)(2,1)S(1)} %collective-permute-done.7.refs_1_, ...), custom_call_target="tpu_custom_call" | custom-call | flops 268435456 | bytes 2621440 | tf_op jit(solution)/shard_map/pallas_call | solution.py:182
  46.8 4.9 %collective-permute-start.11 = (bf16[512,256]{1,0:T(8,128)(2,1)S(1)}, bf16[512,256]{1,0:T(8,128)(2,1)S(1)}, u32[]{:S(2)}, u32[]{:S(2)}) collective-permute-start(bf16[512,256]{1,0:T(8,128)(2,1)S(1)} %get-tuple-element.45.refs_0_), channel_id=1, source_target_pairs={{0,1},{1,0},{2,3},{3,2},{4,5},{5,4},{6,7},{7,6},{8,9},{9,8},{10,11... | collective-permute-start | bytes 786440 | tf_op jit(solution)/shard_map/ppermute | solution.py:263
  51.7 1.1 %collective-permute-start.12 = (bf16[512,256]{1,0:T(8,128)(2,1)S(1)}, bf16[512,256]{1,0:T(8,128)(2,1)S(1)}, u32[]{:S(2)}, u32[]{:S(2)}) collective-permute-start(bf16[512,256]{1,0:T(8,128)(2,1)S(1)} %get-tuple-element.45.refs_0_), channel_id=1, source_target_pairs={{0,2},{1,3},{2,0},{3,1},{4,6},{5,7},{6,4},{7,5},{8,10},{9,11},{10,... | collective-permute-start | bytes 786440 | tf_op jit(solution)/shard_map/ppermute | solution.py:263
  52.8 1.5 %collective-permute-start.13 = (bf16[512,256]{1,0:T(8,128)(2,1)S(1)}, bf16[512,256]{1,0:T(8,128)(2,1)S(1)}, u32[]{:S(2)}, u32[]{:S(2)}) collective-permute-start(bf16[512,256]{1,0:T(8,128)(2,1)S(1)} %get-tuple-element.45.refs_0_), channel_id=1, source_target_pairs={{0,3},{1,2},{2,1},{3,0},{4,7},{5,6},{6,5},{7,4},{8,11},{9,10},{10,... | collective-permute-start | bytes 786440 | tf_op jit(solution)/shard_map/ppermute | solution.py:263
  54.2 0.5 shard_map.88
  54.7 0.1 collective-permute-start.10
  54.8 1.3 %collective-permute-done.10 = f32[128,256]{1,0:T(8,128)S(1)} collective-permute-done((f32[128,256]{1,0:T(8,128)S(1)}, f32[128,256]{1,0:T(8,128)S(1)}, u32[]{:S(2)}, u32[]{:S(2)}) %collective-permute-start.10) | collective-permute-done | bytes 131104 | tf_op jit(solution)/shard_map/ppermute | solution.py:263
  56.1 8.2 %all_to_all.9 = f32[4,32,256]{2,1,0:T(8,128)S(1)} all-to-all(f32[4,32,256]{2,1,0:T(8,128)S(1)} %bitcast.9), channel_id=1, replica_groups={{0,8,16,24},{4,12,20,28},{1,9,17,25},{5,13,21,29},{2,10,18,26},{6,14,22..., dimensions={0} | all-to-all | bytes 262144 | tf_op jit(solution)/shard_map/all_to_all | solution.py:304
  64.4 7.6 %all_gather.6 = bf16[128,256]{1,0:T(8,128)(2,1)S(1)} all-gather(bf16[32,256]{1,0:T(8,128)(2,1)S(1)} %reduce_sum.18), channel_id=1, replica_groups={{0,8,16,24},{4,12,20,28},{1,9,17,25},{5,13,21,29},{2,10,18,26},{6,14,22..., dimensions={0}, use_global_device_ids=true | all-gather | bytes 81920 | tf_op jit(solution)/shard_map/all_gather | solution.py:306
  72.0 0.0 collective-permute-done.11.refs_1_
  72.0 1.1 %collective-permute-done.12.refs_2_ = bf16[512,256]{1,0:T(8,128)(2,1)S(1)} collective-permute-done((bf16[512,256]{1,0:T(8,128)(2,1)S(1)}, bf16[512,256]{1,0:T(8,128)(2,1)S(1)}, u32[]{:S(2)}, u32[]{:S(2)}) %collective-permute-start.12) | collective-permute-done | bytes 262176 | tf_op jit(solution)/shard_map/ppermute | solution.py:263
  73.1 0.0 collective-permute-done.13.refs_3_
  73.1 3.9 %shard_map.89 = (bf16[2048,256]{1,0:T(8,128)(2,1)S(1)}, bf16[2048,256]{1,0:T(8,128)(2,1)S(1)}) custom-call(s32[129]{0:T(256)S(1)} %get-tuple-element.31.row_of, s32[128]{0:T(128)S(1)} %get-tuple-element.32.col_of, s32[1]{0:T(128)} %bitcast.1.mine_ref.here_ref, s32[1]{0:T(128)} %bitcast.here_ref.me.mine_ref, bf16[512,256]{1,0:T(8,128)(2,1)S(1)} %get-tuple-element.45.refs_0_, ...), custom_call_target="tpu_custom_call" | custom-call | flops 1073741824 | bytes 5242880 | tf_op jit(solution)/shard_map/pallas_call | solution.py:136
  77.0 0.1 collective-permute-start.14
  77.0 2.6 %collective-permute-done.14.other_ref = bf16[2048,256]{1,0:T(8,128)(2,1)S(1)} collective-permute-done((bf16[2048,256]{1,0:T(8,128)(2,1)S(1)}, bf16[2048,256]{1,0:T(8,128)(2,1)S(1)}, u32[]{:S(2)}, u32[]{:S(2)}) %collective-permute-start.14) | collective-permute-done | bytes 1048608 | tf_op jit(solution)/shard_map/ppermute | solution.py:263
  79.7 0.2 shard_map.90
  79.9 2.2 %collective-permute-start.17 = (bf16[512,256]{1,0:T(8,128)(2,1)S(1)}, bf16[512,256]{1,0:T(8,128)(2,1)S(1)}, u32[]{:S(2)}, u32[]{:S(2)}) collective-permute-start(bf16[512,256]{1,0:T(8,128)(2,1)S(1)} %get-tuple-element.51), channel_id=1, source_target_pairs={{0,24},{4,28},{8,16},{12,20},{16,8},{20,12},{24,0},{28,4},{1,25},{... | collective-permute-start | bytes 786440 | tf_op jit(solution)/shard_map/ppermute | solution.py:263
  82.2 0.1 collective-permute-start.16
  82.3 1.4 %collective-permute-start.15 = (bf16[512,256]{1,0:T(8,128)(2,1)S(1)}, bf16[512,256]{1,0:T(8,128)(2,1)S(1)}, u32[]{:S(2)}, u32[]{:S(2)}) collective-permute-start(bf16[512,256]{1,0:T(8,128)(2,1)S(1)} %get-tuple-element.49), channel_id=1, source_target_pairs={{0,8},{4,12},{8,0},{12,4},{16,24},{20,28},{24,16},{28,20},{1,9},{5... | collective-permute-start | bytes 786440 | tf_op jit(solution)/shard_map/ppermute | solution.py:263
  83.7 17.3 %all_gather.7 = bf16[512,256]{1,0:T(8,128)(2,1)S(1)} all-gather(bf16[128,256]{1,0:T(8,128)(2,1)S(1)} %all_gather.6), channel_id=1, replica_groups=mesh['row'=8,'col'=4] {'col'}, dimensions={0}, use_global_device_ids=true | all-gather | bytes 327680 | tf_op jit(solution)/shard_map/all_gather | solution.py:318
  101.1 0.1 collective-permute-start.18
  101.1 1.3 %collective-permute-done.18.other_ref = f32[128,256]{1,0:T(8,128)S(1)} collective-permute-done((f32[128,256]{1,0:T(8,128)S(1)}, f32[128,256]{1,0:T(8,128)S(1)}, u32[]{:S(2)}, u32[]{:S(2)}) %collective-permute-start.18) | collective-permute-done | bytes 131104 | tf_op jit(solution)/shard_map/ppermute | solution.py:263
  102.5 0.7 shard_map.91
  103.2 0.0 collective-permute-done.17
  103.2 0.0 collective-permute-done.16
  103.2 0.0 collective-permute-done.15
  103.2 0.8 add_convert_fusion
  (3 shorter events, 0.1 us)
Async XLA Ops:
  0.6 10.3 %collective-permute-start = (bf16[512,256]{1,0:T(8,128)(2,1)}, bf16[512,256]{1,0:T(8,128)(2,1)S(1)}, u32[]{:S(2)}, u32[]{:S(2)}) collective-permute-start(bf16[512,256]{1,0:T(8,128)(2,1)} %features.1), channel_id=1, source_target_pairs={{0,8},{4,12},{8,0},{12,4},{16,24},{20,28},{24,16},{28,20},{1,9},{5... | collective-permute-start | bytes 786440 | tf_op jit(solution)/shard_map/ppermute | solution.py:263
  3.6 13.6 %collective-permute-start.3 = (bf16[512,256]{1,0:T(8,128)(2,1)}, bf16[512,256]{1,0:T(8,128)(2,1)S(1)}, u32[]{:S(2)}, u32[]{:S(2)}) collective-permute-start(bf16[512,256]{1,0:T(8,128)(2,1)} %features.1), channel_id=1, source_target_pairs={{0,16},{4,20},{8,24},{12,28},{16,0},{20,4},{24,8},{28,12},{1,17},{... | collective-permute-start | bytes 786440 | tf_op jit(solution)/shard_map/ppermute | solution.py:263
  5.2 12.1 %collective-permute-start.5 = (bf16[512,256]{1,0:T(8,128)(2,1)}, bf16[512,256]{1,0:T(8,128)(2,1)S(1)}, u32[]{:S(2)}, u32[]{:S(2)}) collective-permute-start(bf16[512,256]{1,0:T(8,128)(2,1)} %features.1), channel_id=1, source_target_pairs={{0,24},{4,28},{8,16},{12,20},{16,8},{20,12},{24,0},{28,4},{1,25},{... | collective-permute-start | bytes 786440 | tf_op jit(solution)/shard_map/ppermute | solution.py:263
  5.2 1.0 copy-start
  6.2 0.7 copy-start.3
  6.8 0.7 copy-start.4
  7.5 38.1 %copy-start.1 = (bf16[512,256]{1,0:T(8,128)(2,1)S(1)}, bf16[512,256]{1,0:T(8,128)(2,1)}, u32[]{:S(2)}) copy-start(bf16[512,256]{1,0:T(8,128)(2,1)} %refs_5_.1) | copy-start | bytes 786436
  7.5 38.1 %copy-start.2 = (bf16[256,256]{1,0:T(8,128)(2,1)S(1)}, bf16[256,256]{1,0:T(8,128)(2,1)}, u32[]{:S(2)}) copy-start(bf16[256,256]{1,0:T(8,128)(2,1)} %refs_4_.1) | copy-start | bytes 393220
  11.0 6.8 %collective-permute-start.1 = (bf16[512,256]{1,0:T(8,128)(2,1)S(1)}, bf16[512,256]{1,0:T(8,128)(2,1)S(1)}, u32[]{:S(2)}, u32[]{:S(2)}) collective-permute-start(bf16[512,256]{1,0:T(8,128)(2,1)S(1)} %get-tuple-element.33.refs_0_), channel_id=1, source_target_pairs={{0,4},{4,0},{8,12},{12,8},{16,20},{20,16},{24,28},{28,24},{1,5},{5... | collective-permute-start | bytes 786440 | tf_op jit(solution)/shard_map/ppermute | solution.py:263
  11.0 6.8 %collective-permute-start.2 = (bf16[512,256]{1,0:T(8,128)(2,1)S(1)}, bf16[512,256]{1,0:T(8,128)(2,1)S(1)}, u32[]{:S(2)}, u32[]{:S(2)}) collective-permute-start(bf16[512,256]{1,0:T(8,128)(2,1)S(1)} %collective-permute-done.refs_2_), channel_id=1, source_target_pairs={{0,4},{4,0},{8,12},{12,8},{16,20},{20,16},{24,28},{28,24},{1,5},{5... | collective-permute-start | bytes 786440 | tf_op jit(solution)/shard_map/ppermute | solution.py:263
  17.2 1.5 %collective-permute-start.4 = (bf16[512,256]{1,0:T(8,128)(2,1)S(1)}, bf16[512,256]{1,0:T(8,128)(2,1)S(1)}, u32[]{:S(2)}, u32[]{:S(2)}) collective-permute-start(bf16[512,256]{1,0:T(8,128)(2,1)S(1)} %collective-permute-done.3.refs_4_), channel_id=1, source_target_pairs={{0,4},{4,0},{8,12},{12,8},{16,20},{20,16},{24,28},{28,24},{1,5},{5... | collective-permute-start | bytes 786440 | tf_op jit(solution)/shard_map/ppermute | solution.py:263
  17.2 1.9 %collective-permute-start.6 = (bf16[512,256]{1,0:T(8,128)(2,1)S(1)}, bf16[512,256]{1,0:T(8,128)(2,1)S(1)}, u32[]{:S(2)}, u32[]{:S(2)}) collective-permute-start(bf16[512,256]{1,0:T(8,128)(2,1)S(1)} %collective-permute-done.5.refs_6_), channel_id=1, source_target_pairs={{0,4},{4,0},{8,12},{12,8},{16,20},{20,16},{24,28},{28,24},{1,5},{5... | collective-permute-start | bytes 786440 | tf_op jit(solution)/shard_map/ppermute | solution.py:263
  22.8 12.8 %collective-permute-start.7 = (bf16[512,256]{1,0:T(8,128)(2,1)S(1)}, bf16[512,256]{1,0:T(8,128)(2,1)S(1)}, u32[]{:S(2)}, u32[]{:S(2)}) collective-permute-start(bf16[512,256]{1,0:T(8,128)(2,1)S(1)} %get-tuple-element.36), channel_id=1, source_target_pairs={{0,1},{1,0},{2,3},{3,2},{4,5},{5,4},{6,7},{7,6},{8,9},{9,8},{10,11... | collective-permute-start | bytes 786440 | tf_op jit(solution)/shard_map/ppermute | solution.py:263
  24.2 21.4 %collective-permute-start.8 = (bf16[512,256]{1,0:T(8,128)(2,1)S(1)}, bf16[512,256]{1,0:T(8,128)(2,1)S(1)}, u32[]{:S(2)}, u32[]{:S(2)}) collective-permute-start(bf16[512,256]{1,0:T(8,128)(2,1)S(1)} %get-tuple-element.37), channel_id=1, source_target_pairs={{0,2},{1,3},{2,0},{3,1},{4,6},{5,7},{6,4},{7,5},{8,10},{9,11},{10,... | collective-permute-start | bytes 786440 | tf_op jit(solution)/shard_map/ppermute | solution.py:263
  27.0 18.6 %collective-permute-start.9 = (bf16[512,256]{1,0:T(8,128)(2,1)S(1)}, bf16[512,256]{1,0:T(8,128)(2,1)S(1)}, u32[]{:S(2)}, u32[]{:S(2)}) collective-permute-start(bf16[512,256]{1,0:T(8,128)(2,1)S(1)} %get-tuple-element.38), channel_id=1, source_target_pairs={{0,3},{1,2},{2,1},{3,0},{4,7},{5,6},{6,5},{7,4},{8,11},{9,10},{10,... | collective-permute-start | bytes 786440 | tf_op jit(solution)/shard_map/ppermute | solution.py:263
  46.8 25.2 %collective-permute-start.11 = (bf16[512,256]{1,0:T(8,128)(2,1)S(1)}, bf16[512,256]{1,0:T(8,128)(2,1)S(1)}, u32[]{:S(2)}, u32[]{:S(2)}) collective-permute-start(bf16[512,256]{1,0:T(8,128)(2,1)S(1)} %get-tuple-element.45.refs_0_), channel_id=1, source_target_pairs={{0,1},{1,0},{2,3},{3,2},{4,5},{5,4},{6,7},{7,6},{8,9},{9,8},{10,11... | collective-permute-start | bytes 786440 | tf_op jit(solution)/shard_map/ppermute | solution.py:263
  51.7 21.4 %collective-permute-start.12 = (bf16[512,256]{1,0:T(8,128)(2,1)S(1)}, bf16[512,256]{1,0:T(8,128)(2,1)S(1)}, u32[]{:S(2)}, u32[]{:S(2)}) collective-permute-start(bf16[512,256]{1,0:T(8,128)(2,1)S(1)} %get-tuple-element.45.refs_0_), channel_id=1, source_target_pairs={{0,2},{1,3},{2,0},{3,1},{4,6},{5,7},{6,4},{7,5},{8,10},{9,11},{10,... | collective-permute-start | bytes 786440 | tf_op jit(solution)/shard_map/ppermute | solution.py:263
  52.8 20.3 %collective-permute-start.13 = (bf16[512,256]{1,0:T(8,128)(2,1)S(1)}, bf16[512,256]{1,0:T(8,128)(2,1)S(1)}, u32[]{:S(2)}, u32[]{:S(2)}) collective-permute-start(bf16[512,256]{1,0:T(8,128)(2,1)S(1)} %get-tuple-element.45.refs_0_), channel_id=1, source_target_pairs={{0,3},{1,2},{2,1},{3,0},{4,7},{5,6},{6,5},{7,4},{8,11},{9,10},{10,... | collective-permute-start | bytes 786440 | tf_op jit(solution)/shard_map/ppermute | solution.py:263
  54.7 1.4 %collective-permute-start.10 = (f32[128,256]{1,0:T(8,128)S(1)}, f32[128,256]{1,0:T(8,128)S(1)}, u32[]{:S(2)}, u32[]{:S(2)}) collective-permute-start(f32[128,256]{1,0:T(8,128)S(1)} %get-tuple-element.43), channel_id=1, source_target_pairs={{0,4},{4,0},{8,12},{12,8},{16,20},{20,16},{24,28},{28,24},{1,5},{5... | collective-permute-start | bytes 393224 | tf_op jit(solution)/shard_map/ppermute | solution.py:263
  77.0 2.7 %collective-permute-start.14 = (bf16[2048,256]{1,0:T(8,128)(2,1)S(1)}, bf16[2048,256]{1,0:T(8,128)(2,1)S(1)}, u32[]{:S(2)}, u32[]{:S(2)}) collective-permute-start(bf16[2048,256]{1,0:T(8,128)(2,1)S(1)} %get-tuple-element.47), channel_id=1, source_target_pairs={{0,4},{4,0},{8,12},{12,8},{16,20},{20,16},{24,28},{28,24},{1,5},{5... | collective-permute-start | bytes 3145736 | tf_op jit(solution)/shard_map/ppermute | solution.py:263
  79.9 23.3 %collective-permute-start.17 = (bf16[512,256]{1,0:T(8,128)(2,1)S(1)}, bf16[512,256]{1,0:T(8,128)(2,1)S(1)}, u32[]{:S(2)}, u32[]{:S(2)}) collective-permute-start(bf16[512,256]{1,0:T(8,128)(2,1)S(1)} %get-tuple-element.51), channel_id=1, source_target_pairs={{0,24},{4,28},{8,16},{12,20},{16,8},{20,12},{24,0},{28,4},{1,25},{... | collective-permute-start | bytes 786440 | tf_op jit(solution)/shard_map/ppermute | solution.py:263
  82.2 21.0 %collective-permute-start.16 = (bf16[512,256]{1,0:T(8,128)(2,1)S(1)}, bf16[512,256]{1,0:T(8,128)(2,1)S(1)}, u32[]{:S(2)}, u32[]{:S(2)}) collective-permute-start(bf16[512,256]{1,0:T(8,128)(2,1)S(1)} %get-tuple-element.50), channel_id=1, source_target_pairs={{0,16},{4,20},{8,24},{12,28},{16,0},{20,4},{24,8},{28,12},{1,17},{... | collective-permute-start | bytes 786440 | tf_op jit(solution)/shard_map/ppermute | solution.py:263
  82.3 20.9 %collective-permute-start.15 = (bf16[512,256]{1,0:T(8,128)(2,1)S(1)}, bf16[512,256]{1,0:T(8,128)(2,1)S(1)}, u32[]{:S(2)}, u32[]{:S(2)}) collective-permute-start(bf16[512,256]{1,0:T(8,128)(2,1)S(1)} %get-tuple-element.49), channel_id=1, source_target_pairs={{0,8},{4,12},{8,0},{12,4},{16,24},{20,28},{24,16},{28,20},{1,9},{5... | collective-permute-start | bytes 786440 | tf_op jit(solution)/shard_map/ppermute | solution.py:263
  101.1 1.4 %collective-permute-start.18 = (f32[128,256]{1,0:T(8,128)S(1)}, f32[128,256]{1,0:T(8,128)S(1)}, u32[]{:S(2)}, u32[]{:S(2)}) collective-permute-start(f32[128,256]{1,0:T(8,128)S(1)} %convert_reduce_fusion.own_ref), channel_id=1, source_target_pairs={{0,4},{4,0},{8,12},{12,8},{16,20},{20,16},{24,28},{28,24},{1,5},{5... | collective-permute-start | bytes 393224 | tf_op jit(solution)/shard_map/ppermute | solution.py:263

commit v7 on v6

--- a/solution.py
+++ b/solution.py
@@ -89,7 +89,7 @@
     total[...] = jnp.zeros_like(total)
     for m in range(parts):
         start = pl.multiple_of((here ^ m) * chunk, chunk)
-        panel[pl.ds(start, chunk), :] = panel_refs[m][...]
+        panel[pl.ds(start, chunk), :] = panel_refs[parts - 1 - m][...]
     spare = total.shape[0] // size - 1
     last = panel.shape[0] // size - 1
 
@@ -146,7 +146,7 @@
         ],
         compiler_params=params(48),
         cost_estimate=cost(flops, 2 * values.size + 2 * parts * chunk * width),
-    )(row_of, col_of, here, mine, *panel_parts, values)
+    )(row_of, col_of, here, mine, *panel_parts[::-1], values)
 
 
 def split(value):
@@ -283,19 +283,21 @@
     me_col = lax.axis_index("col")[None].astype(jnp.int32)
 
     panel = [features] + [None] * (n_row - 1)
-    for m in range(2, n_row, 2):
+    for m in range(n_row - 2, 0, -2):
         panel[m] = swap(features, "row", n_row, m)
     prepared = prepare(row_starts, block_cols, features)
-    panel[2], (row_of, col_of, panel[0]) = lax.optimization_barrier((panel[2], prepared))
+    panel[n_row - 2], (row_of, col_of, panel[0]) = lax.optimization_barrier(
+        (panel[n_row - 2], prepared)
+    )
     for m in range(0, n_row, 2):
         panel[m + 1] = swap(panel[m], "row", n_row, 1)
 
     each = [[m] for m in range(n_col)]
     terms = sparse_product(panel, values, row_of, col_of, me_row, me_col, row_blocks, each, False)
-    terms = [terms[0]] + [swap(terms[m], "col", n_col, m) for m in range(1, n_col)]
+    terms = [terms[0]] + [swap(terms[m], "col", n_col, m) for m in range(n_col - 1, 0, -1)]
     activations, back, aggregated, mixed_grad = middle(terms, weight, cotangent)
 
-    back_panel = [back] + [swap(back, "col", n_col, m) for m in range(1, n_col)]
+    back_panel = [back] + [swap(back, "col", n_col, m) for m in range(n_col - 1, 0, -1)][::-1]
 
     depth = weight.shape[0] // n_row
     own_term, other_term = weight_term(aggregated, mixed_grad, me_row, n_row)
@@ -313,11 +315,13 @@
     )
     sums = pair_sum(own, swap(other, "row", n_row, 1), len(even))
     feature_grad = total_of(
-        [sums[0]] + [swap(s, "row", n_row, m) for s, m in zip(sums[1:], even[1:])]
+        [swap(s, "row", n_row, m) for s, m in zip(sums[:0:-1], even[:0:-1])] + [sums[0]]
     ).astype(BF16)
     halves = lax.all_gather(half.astype(BF16), "col", axis=0, tiled=True)
     half = jnp.sum(halves.reshape(n_col, -1, half.shape[1]).astype(F32), axis=0)
-    weight_grad = assemble(half, swap(half, "row", n_row, 1), me_row, n_row // 2)
+    other = swap(half, "row", n_row, 1)
+    other, feature_grad = lax.optimization_barrier((other, feature_grad))
+    weight_grad = assemble(half, other, me_row, n_row // 2)
     return (activations, feature_grad, weight_grad)
 
 

time: 104 us -> 101 us (0.971)
  blocking collectives: 33.2 us -> 29.8 us
  waiting for transfers between devices: 32.5 us -> 35.5 us
  starting transfers between devices: 21.4 us -> 19.4 us
    ppermute x19, waiting for transfers between devices: 32.5 us -> 35.5 us  [swap(): return lax.ppermute(x, axis, [(i, i ^ m) for i in range(n)])]
    all_gather x1, blocking collectives: 17.3 us -> 14.5 us  [on_device(): halves = lax.all_gather(half.astype(BF16), 'col', axis=0, tiled=True)]
    ppermute x19, starting transfers between devices: 21.4 us -> 19.4 us  [swap(): return lax.ppermute(x, axis, [(i, i ^ m) for i in range(n)])]
  transfers between devices with their start and end apart: 19 -> 19, of which waited for: 10 -> 11; matrix products, arithmetic and copies ran while one was open for 0% -> 1% of each run, Pallas kernels for 4% -> 3%
where the time goes in v7:
time: 101 us; the launch traced here: 102 us
  waiting for transfers between devices  35.5 us (35%)
  blocking collectives  29.8 us (30%)
  starting transfers between devices  19.4 us (19%)
  Pallas kernels  13 us (13%)
  local copies, waits for them, and re-layouts  2.3 us (2%)
    ppermute x19, waiting for transfers between devices, swap(): return lax.ppermute(x, axis, [(i, i ^ m) for i in range(n)])  35.5 us
    ppermute x19, starting transfers between devices, swap(): return lax.ppermute(x, axis, [(i, i ^ m) for i in range(n)])  19.4 us
    all_gather x1, blocking collectives, on_device(): halves = lax.all_gather(half.astype(BF16), 'col', axis=0, tiled=True)  14.5 us
    all_to_all x1, blocking collectives, on_device(): lax.all_to_all(term, 'row', 0, 0, axis_index_groups=cores, tiled=True)  7.69 us
    all_gather x1, blocking collectives, on_device(): lax.all_gather(piece, 'row', axis=0, axis_index_groups=cores, tiled=True)  7.64 us
    pallas_call x2, Pallas kernels, sparse_product(): pl.pallas_call(functools.partial(sparse_kernel, parts, outs, backward), o...  7.47 us
    pallas_call x1, Pallas kernels, prepare(): pl.pallas_call(prepare_kernel, out_shape=[jax.ShapeDtypeStruct((slots + 1...  2.88 us
    unnamed x10, local copies, waits for them, and re-layouts  2.3 us
  transfers between devices with their start and end apart: 19, of which 11 were waited for; matrix products, arithmetic and copies ran while one was open for 1% of the time, Pallas kernels for 3%

profile of v7, /device:TPU:0, one launch (start us, length us, event | category | flops | bytes accessed | tf_op | source)
XLA Modules:
  0.0 101.6 jit_solution(10492692726926659868)
XLA Ops:
  0.6 4.0 %collective-permute-start = (bf16[512,256]{1,0:T(8,128)(2,1)}, bf16[512,256]{1,0:T(8,128)(2,1)S(1)}, u32[]{:S(2)}, u32[]{:S(2)}) collective-permute-start(bf16[512,256]{1,0:T(8,128)(2,1)} %features.1), channel_id=1, source_target_pairs={{0,24},{4,28},{8,16},{12,20},{16,8},{20,12},{24,0},{28,4},{1,25},{... | collective-permute-start | bytes 786440 | tf_op jit(solution)/shard_map/ppermute | solution.py:263
  4.6 0.5 collective-permute-start.2
  5.1 0.1 collective-permute-start.4
  5.2 0.0 copy-start
  5.2 1.0 copy-done
  6.2 0.0 copy-start.3
  6.2 0.7 copy-done.3
  6.9 0.0 copy-start.4
  6.9 0.7 copy-done.4
  7.5 0.0 copy-start.1
  7.5 0.0 copy-start.2
  7.5 2.9 %shard_map.85 = (s32[129]{0:T(256)S(1)}, s32[128]{0:T(128)S(1)}, bf16[512,256]{1,0:T(8,128)(2,1)S(1)}) custom-call(s32[1,1,17]{2,1,0:T(1,128)S(1)} %copy-done.3, s32[1,1,128]{2,1,0:T(1,128)S(1)} %copy-done.4, bf16[512,256]{1,0:T(8,128)(2,1)S(1)} %copy-done), custom_call_target="tpu_custom_call" | custom-call | tf_op jit(solution)/shard_map/pallas_call | solution.py:58
  10.4 1.6 %collective-permute-done.refs_1_ = bf16[512,256]{1,0:T(8,128)(2,1)S(1)} collective-permute-done((bf16[512,256]{1,0:T(8,128)(2,1)}, bf16[512,256]{1,0:T(8,128)(2,1)S(1)}, u32[]{:S(2)}, u32[]{:S(2)}) %collective-permute-start) | collective-permute-done | bytes 262176 | tf_op jit(solution)/shard_map/ppermute | solution.py:263
  12.0 0.0 collective-permute-start.1
  12.0 0.5 collective-permute-start.6
  12.5 4.2 %collective-permute-done.2.refs_3_ = bf16[512,256]{1,0:T(8,128)(2,1)S(1)} collective-permute-done((bf16[512,256]{1,0:T(8,128)(2,1)}, bf16[512,256]{1,0:T(8,128)(2,1)S(1)}, u32[]{:S(2)}, u32[]{:S(2)}) %collective-permute-start.2) | collective-permute-done | bytes 262176 | tf_op jit(solution)/shard_map/ppermute | solution.py:263
  16.7 0.0 collective-permute-start.3
  16.7 0.3 collective-permute-done.4.refs_5_
  17.0 0.2 collective-permute-start.5
  17.2 0.0 collective-permute-done.1.refs_0_
  17.2 0.0 collective-permute-done.6.refs_6_
  17.2 1.0 collective-permute-done.3.refs_2_
  18.3 0.4 collective-permute-done.5.refs_4_
  18.6 3.6 %shard_map.86 = (bf16[512,256]{1,0:T(8,128)(2,1)S(1)}, bf16[512,256]{1,0:T(8,128)(2,1)S(1)}, bf16[512,256]{1,0:T(8,128)(2,1)S(1)}, bf16[512,256]{1,0:T(8,128)(2,1)S(1)}) custom-call(s32[129]{0:T(256)S(1)} %get-tuple-element.33.row_of, s32[128]{0:T(128)S(1)} %get-tuple-element.34.col_of, s32[1]{0:T(128)} %bitcast.here_ref.me.mine_ref, ...), custom_call_target="tpu_custom_call" | custom-call | flops 1073741824 | bytes 6291456 | tf_op jit(solution)/shard_map/pallas_call | solution.py:136
  22.3 3.3 %collective-permute-start.7 = (bf16[512,256]{1,0:T(8,128)(2,1)S(1)}, bf16[512,256]{1,0:T(8,128)(2,1)S(1)}, u32[]{:S(2)}, u32[]{:S(2)}) collective-permute-start(bf16[512,256]{1,0:T(8,128)(2,1)S(1)} %get-tuple-element.38), channel_id=1, source_target_pairs={{0,3},{1,2},{2,1},{3,0},{4,7},{5,6},{6,5},{7,4},{8,11},{9,10},{10,... | collective-permute-start | bytes 786440 | tf_op jit(solution)/shard_map/ppermute | solution.py:263
  25.5 0.3 collective-permute-start.8
  25.9 0.9 collective-permute-start.9
  26.7 6.7 %collective-permute-done.7.refs_1_ = bf16[512,256]{1,0:T(8,128)(2,1)S(1)} collective-permute-done((bf16[512,256]{1,0:T(8,128)(2,1)S(1)}, bf16[512,256]{1,0:T(8,128)(2,1)S(1)}, u32[]{:S(2)}, u32[]{:S(2)}) %collective-permute-start.7) | collective-permute-done | bytes 262176 | tf_op jit(solution)/shard_map/ppermute | solution.py:263
  33.4 15.7 %collective-permute-done.8.refs_2_ = bf16[512,256]{1,0:T(8,128)(2,1)S(1)} collective-permute-done((bf16[512,256]{1,0:T(8,128)(2,1)S(1)}, bf16[512,256]{1,0:T(8,128)(2,1)S(1)}, u32[]{:S(2)}, u32[]{:S(2)}) %collective-permute-start.8) | collective-permute-done | bytes 262176 | tf_op jit(solution)/shard_map/ppermute | solution.py:263
  49.0 0.0 collective-permute-done.9.refs_3_
  49.0 0.0 copy-done.1
  49.0 0.0 copy-done.2
  49.0 1.2 %shard_map.87 = (bf16[512,256]{1,0:T(8,128)(2,1)}, bf16[512,256]{1,0:T(8,128)(2,1)S(1)}, f32[512,256]{1,0:T(8,128)S(1)}, f32[512,256]{1,0:T(8,128)S(1)}) custom-call(bf16[512,256]{1,0:T(8,128)(2,1)S(1)} %get-tuple-element.37.refs_0_, bf16[512,256]{1,0:T(8,128)(2,1)S(1)} %collective-permute-done.7.refs_1_, ...), custom_call_target="tpu_custom_call" | custom-call | flops 268435456 | bytes 2621440 | tf_op jit(solution)/shard_map/pallas_call | solution.py:182
  50.3 1.9 %collective-permute-start.12 = (bf16[512,256]{1,0:T(8,128)(2,1)S(1)}, bf16[512,256]{1,0:T(8,128)(2,1)S(1)}, u32[]{:S(2)}, u32[]{:S(2)}) collective-permute-start(bf16[512,256]{1,0:T(8,128)(2,1)S(1)} %get-tuple-element.48.refs_3_), channel_id=1, source_target_pairs={{0,3},{1,2},{2,1},{3,0},{4,7},{5,6},{6,5},{7,4},{8,11},{9,10},{10,... | collective-permute-start | bytes 786440 | tf_op jit(solution)/shard_map/ppermute | solution.py:263
  52.1 0.0 collective-permute-start.13
  52.1 2.5 %collective-permute-start.14 = (bf16[512,256]{1,0:T(8,128)(2,1)S(1)}, bf16[512,256]{1,0:T(8,128)(2,1)S(1)}, u32[]{:S(2)}, u32[]{:S(2)}) collective-permute-start(bf16[512,256]{1,0:T(8,128)(2,1)S(1)} %get-tuple-element.48.refs_3_), channel_id=1, source_target_pairs={{0,1},{1,0},{2,3},{3,2},{4,5},{5,4},{6,7},{7,6},{8,9},{9,8},{10,11... | collective-permute-start | bytes 786440 | tf_op jit(solution)/shard_map/ppermute | solution.py:263
  54.7 0.5 shard_map.88
  55.1 0.1 collective-permute-start.10
  55.2 1.3 %collective-permute-done.10 = f32[128,256]{1,0:T(8,128)S(1)} collective-permute-done((f32[128,256]{1,0:T(8,128)S(1)}, f32[128,256]{1,0:T(8,128)S(1)}, u32[]{:S(2)}, u32[]{:S(2)}) %collective-permute-start.10) | collective-permute-done | bytes 131104 | tf_op jit(solution)/shard_map/ppermute | solution.py:263
  56.6 7.7 %all_to_all.9 = f32[4,32,256]{2,1,0:T(8,128)S(1)} all-to-all(f32[4,32,256]{2,1,0:T(8,128)S(1)} %bitcast.9), channel_id=1, replica_groups={{0,8,16,24},{4,12,20,28},{1,9,17,25},{5,13,21,29},{2,10,18,26},{6,14,22..., dimensions={0} | all-to-all | bytes 262144 | tf_op jit(solution)/shard_map/all_to_all | solution.py:306
  64.3 7.6 %all_gather.6 = bf16[128,256]{1,0:T(8,128)(2,1)S(1)} all-gather(bf16[32,256]{1,0:T(8,128)(2,1)S(1)} %reduce_sum.18), channel_id=1, replica_groups={{0,8,16,24},{4,12,20,28},{1,9,17,25},{5,13,21,29},{2,10,18,26},{6,14,22..., dimensions={0}, use_global_device_ids=true | all-gather | bytes 81920 | tf_op jit(solution)/shard_map/all_gather | solution.py:308
  71.9 0.0 collective-permute-done.12.refs_0_
  71.9 1.2 %collective-permute-done.13.refs_1_ = bf16[512,256]{1,0:T(8,128)(2,1)S(1)} collective-permute-done((bf16[512,256]{1,0:T(8,128)(2,1)S(1)}, bf16[512,256]{1,0:T(8,128)(2,1)S(1)}, u32[]{:S(2)}, u32[]{:S(2)}) %collective-permute-start.13) | collective-permute-done | bytes 262176 | tf_op jit(solution)/shard_map/ppermute | solution.py:263
  73.1 0.0 collective-permute-done.14.refs_2_
  73.1 3.9 %shard_map.89 = (bf16[2048,256]{1,0:T(8,128)(2,1)S(1)}, bf16[2048,256]{1,0:T(8,128)(2,1)S(1)}) custom-call(s32[129]{0:T(256)S(1)} %get-tuple-element.33.row_of, s32[128]{0:T(128)S(1)} %get-tuple-element.34.col_of, s32[1]{0:T(128)} %bitcast.1.mine_ref.here_ref, s32[1]{0:T(128)} %bitcast.here_ref.me.mine_ref, ...), custom_call_target="tpu_custom_call" | custom-call | flops 1073741824 | bytes 5242880 | tf_op jit(solution)/shard_map/pallas_call | solution.py:136
  77.0 0.1 collective-permute-start.15
  77.1 2.6 %collective-permute-done.15.other_ref = bf16[2048,256]{1,0:T(8,128)(2,1)S(1)} collective-permute-done((bf16[2048,256]{1,0:T(8,128)(2,1)S(1)}, bf16[2048,256]{1,0:T(8,128)(2,1)S(1)}, u32[]{:S(2)}, u32[]{:S(2)}) %collective-permute-start.15) | collective-permute-done | bytes 1048608 | tf_op jit(solution)/shard_map/ppermute | solution.py:263
  79.7 0.2 shard_map.90
  80.0 2.4 %collective-permute-start.16 = (bf16[512,256]{1,0:T(8,128)(2,1)S(1)}, bf16[512,256]{1,0:T(8,128)(2,1)S(1)}, u32[]{:S(2)}, u32[]{:S(2)}) collective-permute-start(bf16[512,256]{1,0:T(8,128)(2,1)S(1)} %get-tuple-element.51), channel_id=1, source_target_pairs={{0,24},{4,28},{8,16},{12,20},{16,8},{20,12},{24,0},{28,4},{1,25},{... | collective-permute-start | bytes 786440 | tf_op jit(solution)/shard_map/ppermute | solution.py:263
  82.4 2.6 %collective-permute-start.17 = (bf16[512,256]{1,0:T(8,128)(2,1)S(1)}, bf16[512,256]{1,0:T(8,128)(2,1)S(1)}, u32[]{:S(2)}, u32[]{:S(2)}) collective-permute-start(bf16[512,256]{1,0:T(8,128)(2,1)S(1)} %get-tuple-element.52), channel_id=1, source_target_pairs={{0,16},{4,20},{8,24},{12,28},{16,0},{20,4},{24,8},{28,12},{1,17},{... | collective-permute-start | bytes 786440 | tf_op jit(solution)/shard_map/ppermute | solution.py:263
  85.0 0.0 collective-permute-start.18
  85.0 14.5 %all_gather.7 = bf16[512,256]{1,0:T(8,128)(2,1)S(1)} all-gather(bf16[128,256]{1,0:T(8,128)(2,1)S(1)} %all_gather.6), channel_id=1, replica_groups=mesh['row'=8,'col'=4] {'col'}, dimensions={0}, use_global_device_ids=true | all-gather | bytes 327680 | tf_op jit(solution)/shard_map/all_gather | solution.py:320
  99.5 0.1 collective-permute-start.11
  99.6 0.0 collective-permute-done.16
  99.6 0.0 collective-permute-done.17
  99.6 0.0 collective-permute-done.18
  99.6 0.9 add_convert_fusion
  100.5 0.4 collective-permute-done.11.other_ref
  100.9 0.7 shard_map.91
  (3 shorter events, 0.1 us)
Async XLA Ops:
  0.6 11.3 %collective-permute-start = (bf16[512,256]{1,0:T(8,128)(2,1)}, bf16[512,256]{1,0:T(8,128)(2,1)S(1)}, u32[]{:S(2)}, u32[]{:S(2)}) collective-permute-start(bf16[512,256]{1,0:T(8,128)(2,1)} %features.1), channel_id=1, source_target_pairs={{0,24},{4,28},{8,16},{12,20},{16,8},{20,12},{24,0},{28,4},{1,25},{... | collective-permute-start | bytes 786440 | tf_op jit(solution)/shard_map/ppermute | solution.py:263
  4.6 12.1 %collective-permute-start.2 = (bf16[512,256]{1,0:T(8,128)(2,1)}, bf16[512,256]{1,0:T(8,128)(2,1)S(1)}, u32[]{:S(2)}, u32[]{:S(2)}) collective-permute-start(bf16[512,256]{1,0:T(8,128)(2,1)} %features.1), channel_id=1, source_target_pairs={{0,16},{4,20},{8,24},{12,28},{16,0},{20,4},{24,8},{28,12},{1,17},{... | collective-permute-start | bytes 786440 | tf_op jit(solution)/shard_map/ppermute | solution.py:263
  5.1 11.9 %collective-permute-start.4 = (bf16[512,256]{1,0:T(8,128)(2,1)}, bf16[512,256]{1,0:T(8,128)(2,1)S(1)}, u32[]{:S(2)}, u32[]{:S(2)}) collective-permute-start(bf16[512,256]{1,0:T(8,128)(2,1)} %features.1), channel_id=1, source_target_pairs={{0,8},{4,12},{8,0},{12,4},{16,24},{20,28},{24,16},{28,20},{1,9},{5... | collective-permute-start | bytes 786440 | tf_op jit(solution)/shard_map/ppermute | solution.py:263
  5.2 1.0 copy-start
  6.2 0.7 copy-start.3
  6.9 0.7 copy-start.4
  7.5 41.5 %copy-start.1 = (bf16[512,256]{1,0:T(8,128)(2,1)S(1)}, bf16[512,256]{1,0:T(8,128)(2,1)}, u32[]{:S(2)}) copy-start(bf16[512,256]{1,0:T(8,128)(2,1)} %refs_5_.1) | copy-start | bytes 786436
  7.5 41.5 %copy-start.2 = (bf16[256,256]{1,0:T(8,128)(2,1)S(1)}, bf16[256,256]{1,0:T(8,128)(2,1)}, u32[]{:S(2)}) copy-start(bf16[256,256]{1,0:T(8,128)(2,1)} %refs_4_.1) | copy-start | bytes 393220
  12.0 5.3 %collective-permute-start.1 = (bf16[512,256]{1,0:T(8,128)(2,1)S(1)}, bf16[512,256]{1,0:T(8,128)(2,1)S(1)}, u32[]{:S(2)}, u32[]{:S(2)}) collective-permute-start(bf16[512,256]{1,0:T(8,128)(2,1)S(1)} %collective-permute-done.refs_1_), channel_id=1, source_target_pairs={{0,4},{4,0},{8,12},{12,8},{16,20},{20,16},{24,28},{28,24},{1,5},{5... | collective-permute-start | bytes 786440 | tf_op jit(solution)/shard_map/ppermute | solution.py:263
  12.0 5.3 %collective-permute-start.6 = (bf16[512,256]{1,0:T(8,128)(2,1)S(1)}, bf16[512,256]{1,0:T(8,128)(2,1)S(1)}, u32[]{:S(2)}, u32[]{:S(2)}) collective-permute-start(bf16[512,256]{1,0:T(8,128)(2,1)S(1)} %get-tuple-element.36.refs_7_), channel_id=1, source_target_pairs={{0,4},{4,0},{8,12},{12,8},{16,20},{20,16},{24,28},{28,24},{1,5},{5... | collective-permute-start | bytes 786440 | tf_op jit(solution)/shard_map/ppermute | solution.py:263
  16.7 1.5 %collective-permute-start.3 = (bf16[512,256]{1,0:T(8,128)(2,1)S(1)}, bf16[512,256]{1,0:T(8,128)(2,1)S(1)}, u32[]{:S(2)}, u32[]{:S(2)}) collective-permute-start(bf16[512,256]{1,0:T(8,128)(2,1)S(1)} %collective-permute-done.2.refs_3_), channel_id=1, source_target_pairs={{0,4},{4,0},{8,12},{12,8},{16,20},{20,16},{24,28},{28,24},{1,5},{5... | collective-permute-start | bytes 786440 | tf_op jit(solution)/shard_map/ppermute | solution.py:263
  17.0 1.6 %collective-permute-start.5 = (bf16[512,256]{1,0:T(8,128)(2,1)S(1)}, bf16[512,256]{1,0:T(8,128)(2,1)S(1)}, u32[]{:S(2)}, u32[]{:S(2)}) collective-permute-start(bf16[512,256]{1,0:T(8,128)(2,1)S(1)} %collective-permute-done.4.refs_5_), channel_id=1, source_target_pairs={{0,4},{4,0},{8,12},{12,8},{16,20},{20,16},{24,28},{28,24},{1,5},{5... | collective-permute-start | bytes 786440 | tf_op jit(solution)/shard_map/ppermute | solution.py:263
  22.3 11.1 %collective-permute-start.7 = (bf16[512,256]{1,0:T(8,128)(2,1)S(1)}, bf16[512,256]{1,0:T(8,128)(2,1)S(1)}, u32[]{:S(2)}, u32[]{:S(2)}) collective-permute-start(bf16[512,256]{1,0:T(8,128)(2,1)S(1)} %get-tuple-element.38), channel_id=1, source_target_pairs={{0,3},{1,2},{2,1},{3,0},{4,7},{5,6},{6,5},{7,4},{8,11},{9,10},{10,... | collective-permute-start | bytes 786440 | tf_op jit(solution)/shard_map/ppermute | solution.py:263
  25.5 23.5 %collective-permute-start.8 = (bf16[512,256]{1,0:T(8,128)(2,1)S(1)}, bf16[512,256]{1,0:T(8,128)(2,1)S(1)}, u32[]{:S(2)}, u32[]{:S(2)}) collective-permute-start(bf16[512,256]{1,0:T(8,128)(2,1)S(1)} %get-tuple-element.39), channel_id=1, source_target_pairs={{0,2},{1,3},{2,0},{3,1},{4,6},{5,7},{6,4},{7,5},{8,10},{9,11},{10,... | collective-permute-start | bytes 786440 | tf_op jit(solution)/shard_map/ppermute | solution.py:263
  25.9 23.2 %collective-permute-start.9 = (bf16[512,256]{1,0:T(8,128)(2,1)S(1)}, bf16[512,256]{1,0:T(8,128)(2,1)S(1)}, u32[]{:S(2)}, u32[]{:S(2)}) collective-permute-start(bf16[512,256]{1,0:T(8,128)(2,1)S(1)} %get-tuple-element.40), channel_id=1, source_target_pairs={{0,1},{1,0},{2,3},{3,2},{4,5},{5,4},{6,7},{7,6},{8,9},{9,8},{10,11... | collective-permute-start | bytes 786440 | tf_op jit(solution)/shard_map/ppermute | solution.py:263
  50.3 21.6 %collective-permute-start.12 = (bf16[512,256]{1,0:T(8,128)(2,1)S(1)}, bf16[512,256]{1,0:T(8,128)(2,1)S(1)}, u32[]{:S(2)}, u32[]{:S(2)}) collective-permute-start(bf16[512,256]{1,0:T(8,128)(2,1)S(1)} %get-tuple-element.48.refs_3_), channel_id=1, source_target_pairs={{0,3},{1,2},{2,1},{3,0},{4,7},{5,6},{6,5},{7,4},{8,11},{9,10},{10,... | collective-permute-start | bytes 786440 | tf_op jit(solution)/shard_map/ppermute | solution.py:263
  52.1 21.0 %collective-permute-start.13 = (bf16[512,256]{1,0:T(8,128)(2,1)S(1)}, bf16[512,256]{1,0:T(8,128)(2,1)S(1)}, u32[]{:S(2)}, u32[]{:S(2)}) collective-permute-start(bf16[512,256]{1,0:T(8,128)(2,1)S(1)} %get-tuple-element.48.refs_3_), channel_id=1, source_target_pairs={{0,2},{1,3},{2,0},{3,1},{4,6},{5,7},{6,4},{7,5},{8,10},{9,11},{10,... | collective-permute-start | bytes 786440 | tf_op jit(solution)/shard_map/ppermute | solution.py:263
  52.1 21.0 %collective-permute-start.14 = (bf16[512,256]{1,0:T(8,128)(2,1)S(1)}, bf16[512,256]{1,0:T(8,128)(2,1)S(1)}, u32[]{:S(2)}, u32[]{:S(2)}) collective-permute-start(bf16[512,256]{1,0:T(8,128)(2,1)S(1)} %get-tuple-element.48.refs_3_), channel_id=1, source_target_pairs={{0,1},{1,0},{2,3},{3,2},{4,5},{5,4},{6,7},{7,6},{8,9},{9,8},{10,11... | collective-permute-start | bytes 786440 | tf_op jit(solution)/shard_map/ppermute | solution.py:263
  55.1 1.4 %collective-permute-start.10 = (f32[128,256]{1,0:T(8,128)S(1)}, f32[128,256]{1,0:T(8,128)S(1)}, u32[]{:S(2)}, u32[]{:S(2)}) collective-permute-start(f32[128,256]{1,0:T(8,128)S(1)} %get-tuple-element.45), channel_id=1, source_target_pairs={{0,4},{4,0},{8,12},{12,8},{16,20},{20,16},{24,28},{28,24},{1,5},{5... | collective-permute-start | bytes 393224 | tf_op jit(solution)/shard_map/ppermute | solution.py:263
  77.0 2.7 %collective-permute-start.15 = (bf16[2048,256]{1,0:T(8,128)(2,1)S(1)}, bf16[2048,256]{1,0:T(8,128)(2,1)S(1)}, u32[]{:S(2)}, u32[]{:S(2)}) collective-permute-start(bf16[2048,256]{1,0:T(8,128)(2,1)S(1)} %get-tuple-element.50), channel_id=1, source_target_pairs={{0,4},{4,0},{8,12},{12,8},{16,20},{20,16},{24,28},{28,24},{1,5},{5... | collective-permute-start | bytes 3145736 | tf_op jit(solution)/shard_map/ppermute | solution.py:263
  80.0 19.6 %collective-permute-start.16 = (bf16[512,256]{1,0:T(8,128)(2,1)S(1)}, bf16[512,256]{1,0:T(8,128)(2,1)S(1)}, u32[]{:S(2)}, u32[]{:S(2)}) collective-permute-start(bf16[512,256]{1,0:T(8,128)(2,1)S(1)} %get-tuple-element.51), channel_id=1, source_target_pairs={{0,24},{4,28},{8,16},{12,20},{16,8},{20,12},{24,0},{28,4},{1,25},{... | collective-permute-start | bytes 786440 | tf_op jit(solution)/shard_map/ppermute | solution.py:263
  82.4 17.2 %collective-permute-start.17 = (bf16[512,256]{1,0:T(8,128)(2,1)S(1)}, bf16[512,256]{1,0:T(8,128)(2,1)S(1)}, u32[]{:S(2)}, u32[]{:S(2)}) collective-permute-start(bf16[512,256]{1,0:T(8,128)(2,1)S(1)} %get-tuple-element.52), channel_id=1, source_target_pairs={{0,16},{4,20},{8,24},{12,28},{16,0},{20,4},{24,8},{28,12},{1,17},{... | collective-permute-start | bytes 786440 | tf_op jit(solution)/shard_map/ppermute | solution.py:263
  85.0 14.6 %collective-permute-start.18 = (bf16[512,256]{1,0:T(8,128)(2,1)S(1)}, bf16[512,256]{1,0:T(8,128)(2,1)S(1)}, u32[]{:S(2)}, u32[]{:S(2)}) collective-permute-start(bf16[512,256]{1,0:T(8,128)(2,1)S(1)} %get-tuple-element.53), channel_id=1, source_target_pairs={{0,8},{4,12},{8,0},{12,4},{16,24},{20,28},{24,16},{28,20},{1,9},{5... | collective-permute-start | bytes 786440 | tf_op jit(solution)/shard_map/ppermute | solution.py:263
  99.5 1.4 %collective-permute-start.11 = (f32[128,256]{1,0:T(8,128)S(1)}, f32[128,256]{1,0:T(8,128)S(1)}, u32[]{:S(2)}, u32[]{:S(2)}) collective-permute-start(f32[128,256]{1,0:T(8,128)S(1)} %convert_reduce_fusion.own_ref), channel_id=1, source_target_pairs={{0,4},{4,0},{8,12},{12,8},{16,20},{20,16},{24,28},{28,24},{1,5},{5... | collective-permute-start | bytes 393224 | tf_op jit(solution)/shard_map/ppermute | solution.py:263

commit v8 on v7

--- a/solution.py
+++ b/solution.py
@@ -317,7 +317,7 @@
     feature_grad = total_of(
         [swap(s, "row", n_row, m) for s, m in zip(sums[:0:-1], even[:0:-1])] + [sums[0]]
     ).astype(BF16)
-    halves = lax.all_gather(half.astype(BF16), "col", axis=0, tiled=True)
+    halves = exchange(jnp.tile(half.astype(BF16), (n_col, 1)), "col")
     half = jnp.sum(halves.reshape(n_col, -1, half.shape[1]).astype(F32), axis=0)
     other = swap(half, "row", n_row, 1)
     other, feature_grad = lax.optimization_barrier((other, feature_grad))

time: 101 us -> 99.9 us (0.989)
  blocking collectives: 29.8 us -> 15.5 us
  waiting for transfers between devices: 35.5 us -> 42.8 us
  starting transfers between devices: 19.4 us -> 22 us
    all_gather x1 -> x0, blocking collectives: 14.5 us -> none  [on_device(): halves = lax.all_gather(half.astype(BF16), 'col', axis=0, tiled=True)]
    all_to_all x0 -> x1, waiting for transfers between devices: none -> 6.06 us  [exchange(): return lax.all_to_all(x, axis, 0, 0, tiled=True)]
    all_to_all x0 -> x1, starting transfers between devices: none -> 4.05 us  [exchange(): return lax.all_to_all(x, axis, 0, 0, tiled=True)]
    ppermute x19, starting transfers between devices: 19.4 us -> 18 us  [swap(): return lax.ppermute(x, axis, [(i, i ^ m) for i in range(n)])]
    ppermute x19, waiting for transfers between devices: 35.5 us -> 36.7 us  [swap(): return lax.ppermute(x, axis, [(i, i ^ m) for i in range(n)])]
  transfers between devices with their start and end apart: 19 -> 20, of which waited for: 11 -> 11; matrix products, arithmetic and copies ran while one was open for 1% -> 3% of each run, Pallas kernels for 3% -> 4%
where the time goes in v8:
time: 99.9 us; the launch traced here: 99.5 us
  waiting for transfers between devices  42.8 us (43%)
  starting transfers between devices  22 us (22%)
  blocking collectives  15.5 us (16%)
  Pallas kernels  13.6 us (14%)
  local copies, waits for them, and re-layouts  3.02 us (3%)
  other arithmetic  1.86 us (2%)
    ppermute x19, waiting for transfers between devices, swap(): return lax.ppermute(x, axis, [(i, i ^ m) for i in range(n)])  36.7 us
    ppermute x19, starting transfers between devices, swap(): return lax.ppermute(x, axis, [(i, i ^ m) for i in range(n)])  18 us
    pallas_call x2, Pallas kernels, sparse_product(): pl.pallas_call(functools.partial(sparse_kernel, parts, outs, backward), o...  8.11 us
    all_to_all x1, blocking collectives, on_device(): lax.all_to_all(term, 'row', 0, 0, axis_index_groups=cores, tiled=True)  7.88 us
    all_gather x1, blocking collectives, on_device(): lax.all_gather(piece, 'row', axis=0, axis_index_groups=cores, tiled=True)  7.64 us
    all_to_all x1, waiting for transfers between devices, exchange(): return lax.all_to_all(x, axis, 0, 0, tiled=True)  6.06 us
    all_to_all x1, starting transfers between devices, exchange(): return lax.all_to_all(x, axis, 0, 0, tiled=True)  4.05 us
    pallas_call x1, Pallas kernels, prepare(): pl.pallas_call(prepare_kernel, out_shape=[jax.ShapeDtypeStruct((slots + 1...  2.86 us
  transfers between devices with their start and end apart: 20, of which 11 were waited for; matrix products, arithmetic and copies ran while one was open for 3% of the time, Pallas kernels for 4%

profile of v8, /device:TPU:0, one launch (start us, length us, event | category | flops | bytes accessed | tf_op | source)
XLA Modules:
  0.0 99.5 jit_solution(1153425768667933760)
XLA Ops:
  0.6 4.0 %collective-permute-start = (bf16[512,256]{1,0:T(8,128)(2,1)}, bf16[512,256]{1,0:T(8,128)(2,1)S(1)}, u32[]{:S(2)}, u32[]{:S(2)}) collective-permute-start(bf16[512,256]{1,0:T(8,128)(2,1)} %features.1), channel_id=1, source_target_pairs={{0,24},{4,28},{8,16},{12,20},{16,8},{20,12},{24,0},{28,4},{1,25},{... | collective-permute-start | bytes 786440 | tf_op jit(solution)/shard_map/ppermute | solution.py:263
  4.6 0.5 collective-permute-start.2
  5.1 0.1 collective-permute-start.4
  5.2 0.0 copy-start
  5.2 1.0 copy-done
  6.2 0.0 copy-start.3
  6.2 0.7 copy-done.3
  6.9 0.0 copy-start.4
  6.9 0.7 copy-done.4
  7.5 0.0 copy-start.1
  7.5 0.0 copy-start.2
  7.5 2.9 %shard_map.85 = (s32[129]{0:T(256)S(1)}, s32[128]{0:T(128)S(1)}, bf16[512,256]{1,0:T(8,128)(2,1)S(1)}) custom-call(s32[1,1,17]{2,1,0:T(1,128)S(1)} %copy-done.3, s32[1,1,128]{2,1,0:T(1,128)S(1)} %copy-done.4, bf16[512,256]{1,0:T(8,128)(2,1)S(1)} %copy-done), custom_call_target="tpu_custom_call" | custom-call | tf_op jit(solution)/shard_map/pallas_call | solution.py:58
  10.4 1.6 %collective-permute-done.refs_1_ = bf16[512,256]{1,0:T(8,128)(2,1)S(1)} collective-permute-done((bf16[512,256]{1,0:T(8,128)(2,1)}, bf16[512,256]{1,0:T(8,128)(2,1)S(1)}, u32[]{:S(2)}, u32[]{:S(2)}) %collective-permute-start) | collective-permute-done | bytes 262176 | tf_op jit(solution)/shard_map/ppermute | solution.py:263
  12.0 0.0 collective-permute-start.1
  12.0 0.5 collective-permute-start.6
  12.5 4.2 %collective-permute-done.2.refs_3_ = bf16[512,256]{1,0:T(8,128)(2,1)S(1)} collective-permute-done((bf16[512,256]{1,0:T(8,128)(2,1)}, bf16[512,256]{1,0:T(8,128)(2,1)S(1)}, u32[]{:S(2)}, u32[]{:S(2)}) %collective-permute-start.2) | collective-permute-done | bytes 262176 | tf_op jit(solution)/shard_map/ppermute | solution.py:263
  16.7 0.0 collective-permute-start.3
  16.7 0.3 collective-permute-done.4.refs_5_
  17.0 0.2 collective-permute-start.5
  17.2 0.0 collective-permute-done.1.refs_0_
  17.2 0.0 collective-permute-done.6.refs_6_
  17.2 1.0 %collective-permute-done.3.refs_2_ = bf16[512,256]{1,0:T(8,128)(2,1)S(1)} collective-permute-done((bf16[512,256]{1,0:T(8,128)(2,1)S(1)}, bf16[512,256]{1,0:T(8,128)(2,1)S(1)}, u32[]{:S(2)}, u32[]{:S(2)}) %collective-permute-start.3) | collective-permute-done | bytes 262176 | tf_op jit(solution)/shard_map/ppermute | solution.py:263
  18.3 0.4 collective-permute-done.5.refs_4_
  18.6 3.9 %shard_map.86 = (bf16[512,256]{1,0:T(8,128)(2,1)S(1)}, bf16[512,256]{1,0:T(8,128)(2,1)S(1)}, bf16[512,256]{1,0:T(8,128)(2,1)S(1)}, bf16[512,256]{1,0:T(8,128)(2,1)S(1)}) custom-call(s32[129]{0:T(256)S(1)} %get-tuple-element.33.row_of, s32[128]{0:T(128)S(1)} %get-tuple-element.34.col_of, s32[1]{0:T(128)} %bitcast.here_ref.me.mine_ref, ...), custom_call_target="tpu_custom_call" | custom-call | flops 1073741824 | bytes 6291456 | tf_op jit(solution)/shard_map/pallas_call | solution.py:136
  22.6 3.6 %collective-permute-start.7 = (bf16[512,256]{1,0:T(8,128)(2,1)S(1)}, bf16[512,256]{1,0:T(8,128)(2,1)S(1)}, u32[]{:S(2)}, u32[]{:S(2)}) collective-permute-start(bf16[512,256]{1,0:T(8,128)(2,1)S(1)} %get-tuple-element.38), channel_id=1, source_target_pairs={{0,3},{1,2},{2,1},{3,0},{4,7},{5,6},{6,5},{7,4},{8,11},{9,10},{10,... | collective-permute-start | bytes 786440 | tf_op jit(solution)/shard_map/ppermute | solution.py:263
  26.1 0.0 collective-permute-start.8
  26.1 0.9 collective-permute-start.9
  27.0 6.7 %collective-permute-done.7.refs_1_ = bf16[512,256]{1,0:T(8,128)(2,1)S(1)} collective-permute-done((bf16[512,256]{1,0:T(8,128)(2,1)S(1)}, bf16[512,256]{1,0:T(8,128)(2,1)S(1)}, u32[]{:S(2)}, u32[]{:S(2)}) %collective-permute-start.7) | collective-permute-done | bytes 262176 | tf_op jit(solution)/shard_map/ppermute | solution.py:263
  33.7 14.7 %collective-permute-done.8.refs_2_ = bf16[512,256]{1,0:T(8,128)(2,1)S(1)} collective-permute-done((bf16[512,256]{1,0:T(8,128)(2,1)S(1)}, bf16[512,256]{1,0:T(8,128)(2,1)S(1)}, u32[]{:S(2)}, u32[]{:S(2)}) %collective-permute-start.8) | collective-permute-done | bytes 262176 | tf_op jit(solution)/shard_map/ppermute | solution.py:263
  48.4 0.0 collective-permute-done.9.refs_3_
  48.4 0.0 copy-done.1
  48.4 0.0 copy-done.2
  48.4 1.2 %shard_map.87 = (bf16[512,256]{1,0:T(8,128)(2,1)}, bf16[512,256]{1,0:T(8,128)(2,1)S(1)}, f32[512,256]{1,0:T(8,128)S(1)}, f32[512,256]{1,0:T(8,128)S(1)}) custom-call(bf16[512,256]{1,0:T(8,128)(2,1)S(1)} %get-tuple-element.37.refs_0_, bf16[512,256]{1,0:T(8,128)(2,1)S(1)} %collective-permute-done.7.refs_1_, ...), custom_call_target="tpu_custom_call" | custom-call | flops 268435456 | bytes 2621440 | tf_op jit(solution)/shard_map/pallas_call | solution.py:182
  49.6 2.6 %collective-permute-start.12 = (bf16[512,256]{1,0:T(8,128)(2,1)S(1)}, bf16[512,256]{1,0:T(8,128)(2,1)S(1)}, u32[]{:S(2)}, u32[]{:S(2)}) collective-permute-start(bf16[512,256]{1,0:T(8,128)(2,1)S(1)} %get-tuple-element.48.refs_3_), channel_id=1, source_target_pairs={{0,3},{1,2},{2,1},{3,0},{4,7},{5,6},{6,5},{7,4},{8,11},{9,10},{10,... | collective-permute-start | bytes 786440 | tf_op jit(solution)/shard_map/ppermute | solution.py:263
  52.3 0.0 collective-permute-start.13
  52.3 1.7 %collective-permute-start.14 = (bf16[512,256]{1,0:T(8,128)(2,1)S(1)}, bf16[512,256]{1,0:T(8,128)(2,1)S(1)}, u32[]{:S(2)}, u32[]{:S(2)}) collective-permute-start(bf16[512,256]{1,0:T(8,128)(2,1)S(1)} %get-tuple-element.48.refs_3_), channel_id=1, source_target_pairs={{0,1},{1,0},{2,3},{3,2},{4,5},{5,4},{6,7},{7,6},{8,9},{9,8},{10,11... | collective-permute-start | bytes 786440 | tf_op jit(solution)/shard_map/ppermute | solution.py:263
  54.0 0.5 shard_map.88
  54.5 0.1 collective-permute-start.10
  54.6 1.3 %collective-permute-done.10 = f32[128,256]{1,0:T(8,128)S(1)} collective-permute-done((f32[128,256]{1,0:T(8,128)S(1)}, f32[128,256]{1,0:T(8,128)S(1)}, u32[]{:S(2)}, u32[]{:S(2)}) %collective-permute-start.10) | collective-permute-done | bytes 131104 | tf_op jit(solution)/shard_map/ppermute | solution.py:263
  55.9 7.9 %all_to_all.15 = f32[4,32,256]{2,1,0:T(8,128)S(1)} all-to-all(f32[4,32,256]{2,1,0:T(8,128)S(1)} %bitcast.6), channel_id=1, replica_groups={{0,8,16,24},{4,12,20,28},{1,9,17,25},{5,13,21,29},{2,10,18,26},{6,14,22..., dimensions={0} | all-to-all | bytes 262144 | tf_op jit(solution)/shard_map/all_to_all | solution.py:306
  63.8 7.6 %all_gather.3 = bf16[128,256]{1,0:T(8,128)(2,1)S(1)} all-gather(bf16[32,256]{1,0:T(8,128)(2,1)S(1)} %reduce_sum.18), channel_id=1, replica_groups={{0,8,16,24},{4,12,20,28},{1,9,17,25},{5,13,21,29},{2,10,18,26},{6,14,22..., dimensions={0}, use_global_device_ids=true | all-gather | bytes 81920 | tf_op jit(solution)/shard_map/all_gather | solution.py:308
  71.4 0.0 collective-permute-done.12.refs_0_
  71.5 1.9 %collective-permute-done.13.refs_1_ = bf16[512,256]{1,0:T(8,128)(2,1)S(1)} collective-permute-done((bf16[512,256]{1,0:T(8,128)(2,1)S(1)}, bf16[512,256]{1,0:T(8,128)(2,1)S(1)}, u32[]{:S(2)}, u32[]{:S(2)}) %collective-permute-start.13) | collective-permute-done | bytes 262176 | tf_op jit(solution)/shard_map/ppermute | solution.py:263
  73.4 0.0 collective-permute-done.14.refs_2_
  73.4 4.2 %shard_map.89 = (bf16[2048,256]{1,0:T(8,128)(2,1)S(1)}, bf16[2048,256]{1,0:T(8,128)(2,1)S(1)}) custom-call(s32[129]{0:T(256)S(1)} %get-tuple-element.33.row_of, s32[128]{0:T(128)S(1)} %get-tuple-element.34.col_of, s32[1]{0:T(128)} %bitcast.1.mine_ref.here_ref, s32[1]{0:T(128)} %bitcast.here_ref.me.mine_ref, ...), custom_call_target="tpu_custom_call" | custom-call | flops 1073741824 | bytes 5242880 | tf_op jit(solution)/shard_map/pallas_call | solution.py:136
  77.6 0.1 collective-permute-start.15
  77.7 0.7 tile.2
  78.4 4.1 %all-to-all-start.1 = ((bf16[4,128,256]{2,1,0:T(8,128)(2,1)}), bf16[4,128,256]{2,1,0:T(8,128)(2,1)}, u32[]{:S(2)}, u32[]{:S(2)}) async-start(bf16[4,128,256]{2,1,0:T(8,128)(2,1)} %tile.2), calls=%async_computation.1 | async-start | bytes 524288 | tf_op jit(solution)/shard_map/all_to_all | solution.py:274
  82.5 0.0 collective-permute-done.15.other_ref
  82.5 0.2 shard_map.90
  82.7 1.2 %collective-permute-start.16 = (bf16[512,256]{1,0:T(8,128)(2,1)S(1)}, bf16[512,256]{1,0:T(8,128)(2,1)S(1)}, u32[]{:S(2)}, u32[]{:S(2)}) collective-permute-start(bf16[512,256]{1,0:T(8,128)(2,1)S(1)} %get-tuple-element.51), channel_id=1, source_target_pairs={{0,24},{4,28},{8,16},{12,20},{16,8},{20,12},{24,0},{28,4},{1,25},{... | collective-permute-start | bytes 786440 | tf_op jit(solution)/shard_map/ppermute | solution.py:263
  83.9 0.4 collective-permute-start.17
  84.3 1.9 %collective-permute-start.18 = (bf16[512,256]{1,0:T(8,128)(2,1)S(1)}, bf16[512,256]{1,0:T(8,128)(2,1)S(1)}, u32[]{:S(2)}, u32[]{:S(2)}) collective-permute-start(bf16[512,256]{1,0:T(8,128)(2,1)S(1)} %get-tuple-element.53), channel_id=1, source_target_pairs={{0,8},{4,12},{8,0},{12,4},{16,24},{20,28},{24,16},{28,20},{1,9},{5... | collective-permute-start | bytes 786440 | tf_op jit(solution)/shard_map/ppermute | solution.py:263
  86.3 6.1 %all-to-all-done.1 = bf16[4,128,256]{2,1,0:T(8,128)(2,1)} async-done(((bf16[4,128,256]{2,1,0:T(8,128)(2,1)}), bf16[4,128,256]{2,1,0:T(8,128)(2,1)}, u32[]{:S(2)}, u32[]{:S(2)}) %all-to-all-start.1) | async-done | bytes 262176 | tf_op jit(solution)/shard_map/all_to_all | solution.py:274
  92.3 1.0 %convert_reduce_fusion.own_ref = f32[128,256]{1,0:T(8,128)S(1)} fusion(bf16[4,128,256]{2,1,0:T(8,128)(2,1)} %all-to-all-done.1), kind=kLoop, calls=%fused_computation.1 | loop fusion | flops 229376 | bytes 393216 | tf_op jit(solution)/shard_map/reduce_sum | solution.py:321
  93.3 0.1 collective-permute-start.11
  93.4 0.0 collective-permute-done.16
  93.4 4.5 %collective-permute-done.17 = bf16[512,256]{1,0:T(8,128)(2,1)S(1)} collective-permute-done((bf16[512,256]{1,0:T(8,128)(2,1)S(1)}, bf16[512,256]{1,0:T(8,128)(2,1)S(1)}, u32[]{:S(2)}, u32[]{:S(2)}) %collective-permute-start.17) | collective-permute-done | bytes 262176 | tf_op jit(solution)/shard_map/ppermute | solution.py:263
  98.0 0.0 collective-permute-done.18
  98.0 0.8 add_convert_fusion
  98.8 0.0 collective-permute-done.11.other_ref
  98.8 0.7 shard_map.91
  (2 shorter events, 0.0 us)
Async XLA Ops:
  0.6 11.3 %collective-permute-start = (bf16[512,256]{1,0:T(8,128)(2,1)}, bf16[512,256]{1,0:T(8,128)(2,1)S(1)}, u32[]{:S(2)}, u32[]{:S(2)}) collective-permute-start(bf16[512,256]{1,0:T(8,128)(2,1)} %features.1), channel_id=1, source_target_pairs={{0,24},{4,28},{8,16},{12,20},{16,8},{20,12},{24,0},{28,4},{1,25},{... | collective-permute-start | bytes 786440 | tf_op jit(solution)/shard_map/ppermute | solution.py:263
  4.6 12.1 %collective-permute-start.2 = (bf16[512,256]{1,0:T(8,128)(2,1)}, bf16[512,256]{1,0:T(8,128)(2,1)S(1)}, u32[]{:S(2)}, u32[]{:S(2)}) collective-permute-start(bf16[512,256]{1,0:T(8,128)(2,1)} %features.1), channel_id=1, source_target_pairs={{0,16},{4,20},{8,24},{12,28},{16,0},{20,4},{24,8},{28,12},{1,17},{... | collective-permute-start | bytes 786440 | tf_op jit(solution)/shard_map/ppermute | solution.py:263
  5.1 11.9 %collective-permute-start.4 = (bf16[512,256]{1,0:T(8,128)(2,1)}, bf16[512,256]{1,0:T(8,128)(2,1)S(1)}, u32[]{:S(2)}, u32[]{:S(2)}) collective-permute-start(bf16[512,256]{1,0:T(8,128)(2,1)} %features.1), channel_id=1, source_target_pairs={{0,8},{4,12},{8,0},{12,4},{16,24},{20,28},{24,16},{28,20},{1,9},{5... | collective-permute-start | bytes 786440 | tf_op jit(solution)/shard_map/ppermute | solution.py:263
  5.2 1.0 copy-start
  6.2 0.7 copy-start.3
  6.9 0.7 copy-start.4
  7.5 40.9 %copy-start.1 = (bf16[512,256]{1,0:T(8,128)(2,1)S(1)}, bf16[512,256]{1,0:T(8,128)(2,1)}, u32[]{:S(2)}) copy-start(bf16[512,256]{1,0:T(8,128)(2,1)} %refs_5_.1) | copy-start | bytes 786436
  7.5 40.9 %copy-start.2 = (bf16[256,256]{1,0:T(8,128)(2,1)S(1)}, bf16[256,256]{1,0:T(8,128)(2,1)}, u32[]{:S(2)}) copy-start(bf16[256,256]{1,0:T(8,128)(2,1)} %refs_4_.1) | copy-start | bytes 393220
  12.0 5.3 %collective-permute-start.1 = (bf16[512,256]{1,0:T(8,128)(2,1)S(1)}, bf16[512,256]{1,0:T(8,128)(2,1)S(1)}, u32[]{:S(2)}, u32[]{:S(2)}) collective-permute-start(bf16[512,256]{1,0:T(8,128)(2,1)S(1)} %collective-permute-done.refs_1_), channel_id=1, source_target_pairs={{0,4},{4,0},{8,12},{12,8},{16,20},{20,16},{24,28},{28,24},{1,5},{5... | collective-permute-start | bytes 786440 | tf_op jit(solution)/shard_map/ppermute | solution.py:263
  12.0 5.3 %collective-permute-start.6 = (bf16[512,256]{1,0:T(8,128)(2,1)S(1)}, bf16[512,256]{1,0:T(8,128)(2,1)S(1)}, u32[]{:S(2)}, u32[]{:S(2)}) collective-permute-start(bf16[512,256]{1,0:T(8,128)(2,1)S(1)} %get-tuple-element.36.refs_7_), channel_id=1, source_target_pairs={{0,4},{4,0},{8,12},{12,8},{16,20},{20,16},{24,28},{28,24},{1,5},{5... | collective-permute-start | bytes 786440 | tf_op jit(solution)/shard_map/ppermute | solution.py:263
  16.7 1.5 %collective-permute-start.3 = (bf16[512,256]{1,0:T(8,128)(2,1)S(1)}, bf16[512,256]{1,0:T(8,128)(2,1)S(1)}, u32[]{:S(2)}, u32[]{:S(2)}) collective-permute-start(bf16[512,256]{1,0:T(8,128)(2,1)S(1)} %collective-permute-done.2.refs_3_), channel_id=1, source_target_pairs={{0,4},{4,0},{8,12},{12,8},{16,20},{20,16},{24,28},{28,24},{1,5},{5... | collective-permute-start | bytes 786440 | tf_op jit(solution)/shard_map/ppermute | solution.py:263
  17.0 1.6 %collective-permute-start.5 = (bf16[512,256]{1,0:T(8,128)(2,1)S(1)}, bf16[512,256]{1,0:T(8,128)(2,1)S(1)}, u32[]{:S(2)}, u32[]{:S(2)}) collective-permute-start(bf16[512,256]{1,0:T(8,128)(2,1)S(1)} %collective-permute-done.4.refs_5_), channel_id=1, source_target_pairs={{0,4},{4,0},{8,12},{12,8},{16,20},{20,16},{24,28},{28,24},{1,5},{5... | collective-permute-start | bytes 786440 | tf_op jit(solution)/shard_map/ppermute | solution.py:263
  22.6 11.1 %collective-permute-start.7 = (bf16[512,256]{1,0:T(8,128)(2,1)S(1)}, bf16[512,256]{1,0:T(8,128)(2,1)S(1)}, u32[]{:S(2)}, u32[]{:S(2)}) collective-permute-start(bf16[512,256]{1,0:T(8,128)(2,1)S(1)} %get-tuple-element.38), channel_id=1, source_target_pairs={{0,3},{1,2},{2,1},{3,0},{4,7},{5,6},{6,5},{7,4},{8,11},{9,10},{10,... | collective-permute-start | bytes 786440 | tf_op jit(solution)/shard_map/ppermute | solution.py:263
  26.1 22.3 %collective-permute-start.8 = (bf16[512,256]{1,0:T(8,128)(2,1)S(1)}, bf16[512,256]{1,0:T(8,128)(2,1)S(1)}, u32[]{:S(2)}, u32[]{:S(2)}) collective-permute-start(bf16[512,256]{1,0:T(8,128)(2,1)S(1)} %get-tuple-element.39), channel_id=1, source_target_pairs={{0,2},{1,3},{2,0},{3,1},{4,6},{5,7},{6,4},{7,5},{8,10},{9,11},{10,... | collective-permute-start | bytes 786440 | tf_op jit(solution)/shard_map/ppermute | solution.py:263
  26.1 22.3 %collective-permute-start.9 = (bf16[512,256]{1,0:T(8,128)(2,1)S(1)}, bf16[512,256]{1,0:T(8,128)(2,1)S(1)}, u32[]{:S(2)}, u32[]{:S(2)}) collective-permute-start(bf16[512,256]{1,0:T(8,128)(2,1)S(1)} %get-tuple-element.40), channel_id=1, source_target_pairs={{0,1},{1,0},{2,3},{3,2},{4,5},{5,4},{6,7},{7,6},{8,9},{9,8},{10,11... | collective-permute-start | bytes 786440 | tf_op jit(solution)/shard_map/ppermute | solution.py:263
  49.6 21.8 %collective-permute-start.12 = (bf16[512,256]{1,0:T(8,128)(2,1)S(1)}, bf16[512,256]{1,0:T(8,128)(2,1)S(1)}, u32[]{:S(2)}, u32[]{:S(2)}) collective-permute-start(bf16[512,256]{1,0:T(8,128)(2,1)S(1)} %get-tuple-element.48.refs_3_), channel_id=1, source_target_pairs={{0,3},{1,2},{2,1},{3,0},{4,7},{5,6},{6,5},{7,4},{8,11},{9,10},{10,... | collective-permute-start | bytes 786440 | tf_op jit(solution)/shard_map/ppermute | solution.py:263
  52.3 21.1 %collective-permute-start.13 = (bf16[512,256]{1,0:T(8,128)(2,1)S(1)}, bf16[512,256]{1,0:T(8,128)(2,1)S(1)}, u32[]{:S(2)}, u32[]{:S(2)}) collective-permute-start(bf16[512,256]{1,0:T(8,128)(2,1)S(1)} %get-tuple-element.48.refs_3_), channel_id=1, source_target_pairs={{0,2},{1,3},{2,0},{3,1},{4,6},{5,7},{6,4},{7,5},{8,10},{9,11},{10,... | collective-permute-start | bytes 786440 | tf_op jit(solution)/shard_map/ppermute | solution.py:263
  52.3 21.1 %collective-permute-start.14 = (bf16[512,256]{1,0:T(8,128)(2,1)S(1)}, bf16[512,256]{1,0:T(8,128)(2,1)S(1)}, u32[]{:S(2)}, u32[]{:S(2)}) collective-permute-start(bf16[512,256]{1,0:T(8,128)(2,1)S(1)} %get-tuple-element.48.refs_3_), channel_id=1, source_target_pairs={{0,1},{1,0},{2,3},{3,2},{4,5},{5,4},{6,7},{7,6},{8,9},{9,8},{10,11... | collective-permute-start | bytes 786440 | tf_op jit(solution)/shard_map/ppermute | solution.py:263
  54.5 1.4 %collective-permute-start.10 = (f32[128,256]{1,0:T(8,128)S(1)}, f32[128,256]{1,0:T(8,128)S(1)}, u32[]{:S(2)}, u32[]{:S(2)}) collective-permute-start(f32[128,256]{1,0:T(8,128)S(1)} %get-tuple-element.45), channel_id=1, source_target_pairs={{0,4},{4,0},{8,12},{12,8},{16,20},{20,16},{24,28},{28,24},{1,5},{5... | collective-permute-start | bytes 393224 | tf_op jit(solution)/shard_map/ppermute | solution.py:263
  77.6 4.9 %collective-permute-start.15 = (bf16[2048,256]{1,0:T(8,128)(2,1)S(1)}, bf16[2048,256]{1,0:T(8,128)(2,1)S(1)}, u32[]{:S(2)}, u32[]{:S(2)}) collective-permute-start(bf16[2048,256]{1,0:T(8,128)(2,1)S(1)} %get-tuple-element.50), channel_id=1, source_target_pairs={{0,4},{4,0},{8,12},{12,8},{16,20},{20,16},{24,28},{28,24},{1,5},{5... | collective-permute-start | bytes 3145736 | tf_op jit(solution)/shard_map/ppermute | solution.py:263
  78.4 13.9 %all-to-all-start.1 = ((bf16[4,128,256]{2,1,0:T(8,128)(2,1)}), bf16[4,128,256]{2,1,0:T(8,128)(2,1)}, u32[]{:S(2)}, u32[]{:S(2)}) async-start(bf16[4,128,256]{2,1,0:T(8,128)(2,1)} %tile.2), calls=%async_computation.1 | async-start | bytes 524288 | tf_op jit(solution)/shard_map/all_to_all | solution.py:274
  82.7 10.7 %collective-permute-start.16 = (bf16[512,256]{1,0:T(8,128)(2,1)S(1)}, bf16[512,256]{1,0:T(8,128)(2,1)S(1)}, u32[]{:S(2)}, u32[]{:S(2)}) collective-permute-start(bf16[512,256]{1,0:T(8,128)(2,1)S(1)} %get-tuple-element.51), channel_id=1, source_target_pairs={{0,24},{4,28},{8,16},{12,20},{16,8},{20,12},{24,0},{28,4},{1,25},{... | collective-permute-start | bytes 786440 | tf_op jit(solution)/shard_map/ppermute | solution.py:263
  83.9 14.0 %collective-permute-start.17 = (bf16[512,256]{1,0:T(8,128)(2,1)S(1)}, bf16[512,256]{1,0:T(8,128)(2,1)S(1)}, u32[]{:S(2)}, u32[]{:S(2)}) collective-permute-start(bf16[512,256]{1,0:T(8,128)(2,1)S(1)} %get-tuple-element.52), channel_id=1, source_target_pairs={{0,16},{4,20},{8,24},{12,28},{16,0},{20,4},{24,8},{28,12},{1,17},{... | collective-permute-start | bytes 786440 | tf_op jit(solution)/shard_map/ppermute | solution.py:263
  84.3 13.6 %collective-permute-start.18 = (bf16[512,256]{1,0:T(8,128)(2,1)S(1)}, bf16[512,256]{1,0:T(8,128)(2,1)S(1)}, u32[]{:S(2)}, u32[]{:S(2)}) collective-permute-start(bf16[512,256]{1,0:T(8,128)(2,1)S(1)} %get-tuple-element.53), channel_id=1, source_target_pairs={{0,8},{4,12},{8,0},{12,4},{16,24},{20,28},{24,16},{28,20},{1,9},{5... | collective-permute-start | bytes 786440 | tf_op jit(solution)/shard_map/ppermute | solution.py:263
  93.3 5.5 %collective-permute-start.11 = (f32[128,256]{1,0:T(8,128)S(1)}, f32[128,256]{1,0:T(8,128)S(1)}, u32[]{:S(2)}, u32[]{:S(2)}) collective-permute-start(f32[128,256]{1,0:T(8,128)S(1)} %convert_reduce_fusion.own_ref), channel_id=1, source_target_pairs={{0,4},{4,0},{8,12},{12,8},{16,20},{20,16},{24,28},{28,24},{1,5},{5... | collective-permute-start | bytes 393224 | tf_op jit(solution)/shard_map/ppermute | solution.py:263

commit v9 on v8

--- a/solution.py
+++ b/solution.py
@@ -263,6 +263,36 @@
     return lax.ppermute(x, axis, [(i, i ^ m) for i in range(n)])
 
 
+def add_kernel(*refs):
+    result = refs[0][...].astype(F32)
+    for ref in refs[1:-1]:
+        result += ref[...].astype(F32)
+    refs[-1][...] = result
+
+
+def add_up(terms):
+    return pl.pallas_call(
+        add_kernel,
+        out_shape=jax.ShapeDtypeStruct(terms[0].shape, F32),
+        in_specs=[VMEM] * len(terms),
+        out_specs=VMEM,
+        compiler_params=params(32),
+        cost_estimate=cost(0, 64 * terms[0].size),
+    )(*terms)
+
+
+def exchange_terms(terms, n):
+    if n != 4:
+        return [terms[0]] + [swap(terms[m], "col", n, m) for m in range(n - 1, 0, -1)]
+    far = lax.ppermute(terms[3], "col", [(0, 1), (3, 2)])
+    cross = lax.ppermute(terms[3], "col", [(1, 2), (2, 1)])
+    inward = lax.ppermute(terms[2], "col", [(0, 2), (3, 1)])
+    near = swap(terms[1], "col", n, 1)
+    relay = total_of([terms[2], far]).astype(BF16)
+    outward = lax.ppermute(relay, "col", [(1, 3), (2, 0)])
+    return [add_up([cross, inward, near, terms[0]]), outward]
+
+
 def total_of(terms):
     result = terms[0].astype(F32)
     for term in terms[1:]:
@@ -294,7 +324,7 @@
 
     each = [[m] for m in range(n_col)]
     terms = sparse_product(panel, values, row_of, col_of, me_row, me_col, row_blocks, each, False)
-    terms = [terms[0]] + [swap(terms[m], "col", n_col, m) for m in range(n_col - 1, 0, -1)]
+    terms = exchange_terms(terms, n_col)
     activations, back, aggregated, mixed_grad = middle(terms, weight, cotangent)
 
     back_panel = [back] + [swap(back, "col", n_col, m) for m in range(n_col - 1, 0, -1)][::-1]

time: 99.9 us -> 98.2 us (0.983)
  starting transfers between devices: 22 us -> 28.5 us
  waiting for transfers between devices: 42.8 us -> 36.5 us
  Pallas kernels: 13.6 us -> 11.8 us
    ppermute x19 -> x17, waiting for transfers between devices: 36.7 us -> 22.3 us  [swap(): return lax.ppermute(x, axis, [(i, i ^ m) for i in range(n)])]
    ppermute x0 -> x4, starting transfers between devices: none -> 10.5 us  [the longest x1 4.59 us: exchange_terms(): far = lax.ppermute(terms[3], 'col', [(0, 1), (3, 2)])]
    ppermute x0 -> x4, waiting for transfers between devices: none -> 9.22 us  [the longest x1 4.28 us: exchange_terms(): inward = lax.ppermute(terms[2], 'col', [(0, 2), (3, 1)])]
    ppermute x19 -> x17, starting transfers between devices: 18 us -> 14.4 us  [swap(): return lax.ppermute(x, axis, [(i, i ^ m) for i in range(n)])]
    pallas_call x2, Pallas kernels: 8.11 us -> 6.19 us  [sparse_product(): pl.pallas_call(functools.partial(sparse_kernel, parts, outs, backward), o...]
    all_to_all x1, waiting for transfers between devices: 6.06 us -> 5.03 us  [exchange(): return lax.all_to_all(x, axis, 0, 0, tiled=True)]
  transfers between devices with their start and end apart: 20 -> 22, of which waited for: 11 -> 15; matrix products, arithmetic and copies ran while one was open for 3% -> 2% of each run, Pallas kernels for 4% -> 4%
where the time goes in v9:
time: 98.2 us; the launch traced here: 97.9 us
  waiting for transfers between devices  36.5 us (37%)
  starting transfers between devices  28.5 us (29%)
  blocking collectives  16.2 us (16%)
  Pallas kernels  11.8 us (12%)
  local copies, waits for them, and re-layouts  3.02 us (3%)
    ppermute x17, waiting for transfers between devices, swap(): return lax.ppermute(x, axis, [(i, i ^ m) for i in range(n)])  22.3 us
    ppermute x17, starting transfers between devices, swap(): return lax.ppermute(x, axis, [(i, i ^ m) for i in range(n)])  14.4 us
    all_to_all x1, blocking collectives, on_device(): lax.all_to_all(term, 'row', 0, 0, axis_index_groups=cores, tiled=True)  8.6 us
    all_gather x1, blocking collectives, on_device(): lax.all_gather(piece, 'row', axis=0, axis_index_groups=cores, tiled=True)  7.64 us
    pallas_call x2, Pallas kernels, sparse_product(): pl.pallas_call(functools.partial(sparse_kernel, parts, outs, backward), o...  6.19 us
    all_to_all x1, waiting for transfers between devices, exchange(): return lax.all_to_all(x, axis, 0, 0, tiled=True)  5.03 us
    ppermute x1, starting transfers between devices, exchange_terms(): far = lax.ppermute(terms[3], 'col', [(0, 1), (3, 2)])  4.59 us
    ppermute x1, waiting for transfers between devices, exchange_terms(): inward = lax.ppermute(terms[2], 'col', [(0, 2), (3, 1)])  4.28 us
  transfers between devices with their start and end apart: 22, of which 15 were waited for; matrix products, arithmetic and copies ran while one was open for 2% of the time, Pallas kernels for 4%

profile of v9, /device:TPU:0, one launch (start us, length us, event | category | flops | bytes accessed | tf_op | source)
XLA Modules:
  0.0 97.9 jit_solution(12901699137281243791)
XLA Ops:
  0.6 4.0 %collective-permute-start = (bf16[512,256]{1,0:T(8,128)(2,1)}, bf16[512,256]{1,0:T(8,128)(2,1)S(1)}, u32[]{:S(2)}, u32[]{:S(2)}) collective-permute-start(bf16[512,256]{1,0:T(8,128)(2,1)} %features.1), channel_id=1, source_target_pairs={{0,24},{4,28},{8,16},{12,20},{16,8},{20,12},{24,0},{28,4},{1,25},{... | collective-permute-start | bytes 786440 | tf_op jit(solution)/shard_map/ppermute | solution.py:263
  4.6 0.5 collective-permute-start.2
  5.1 0.1 collective-permute-start.4
  5.2 0.0 copy-start
  5.2 1.0 %copy-done = bf16[512,256]{1,0:T(8,128)(2,1)S(1)} copy-done((bf16[512,256]{1,0:T(8,128)(2,1)S(1)}, bf16[512,256]{1,0:T(8,128)(2,1)}, u32[]{:S(2)}) %copy-start) | copy-done | bytes 262168
  6.2 0.0 copy-start.3
  6.2 0.7 copy-done.3
  6.9 0.7 copy-done.4
  7.5 2.9 %shard_map.85 = (s32[129]{0:T(256)S(1)}, s32[128]{0:T(128)S(1)}, bf16[512,256]{1,0:T(8,128)(2,1)S(1)}) custom-call(s32[1,1,17]{2,1,0:T(1,128)S(1)} %copy-done.3, s32[1,1,128]{2,1,0:T(1,128)S(1)} %copy-done.4, bf16[512,256]{1,0:T(8,128)(2,1)S(1)} %copy-done), custom_call_target="tpu_custom_call" | custom-call | tf_op jit(solution)/shard_map/pallas_call | solution.py:58
  10.4 1.5 %collective-permute-done.refs_1_ = bf16[512,256]{1,0:T(8,128)(2,1)S(1)} collective-permute-done((bf16[512,256]{1,0:T(8,128)(2,1)}, bf16[512,256]{1,0:T(8,128)(2,1)S(1)}, u32[]{:S(2)}, u32[]{:S(2)}) %collective-permute-start) | collective-permute-done | bytes 262176 | tf_op jit(solution)/shard_map/ppermute | solution.py:263
  12.0 0.0 collective-permute-start.1
  12.0 0.5 collective-permute-start.6
  12.5 4.2 %collective-permute-done.2.refs_3_ = bf16[512,256]{1,0:T(8,128)(2,1)S(1)} collective-permute-done((bf16[512,256]{1,0:T(8,128)(2,1)}, bf16[512,256]{1,0:T(8,128)(2,1)S(1)}, u32[]{:S(2)}, u32[]{:S(2)}) %collective-permute-start.2) | collective-permute-done | bytes 262176 | tf_op jit(solution)/shard_map/ppermute | solution.py:263
  16.7 0.0 collective-permute-start.3
  16.7 0.3 collective-permute-done.4.refs_5_
  17.0 0.2 collective-permute-start.5
  17.2 0.0 collective-permute-done.1.refs_0_
  17.2 0.0 collective-permute-done.6.refs_6_
  17.2 1.0 %collective-permute-done.3.refs_2_ = bf16[512,256]{1,0:T(8,128)(2,1)S(1)} collective-permute-done((bf16[512,256]{1,0:T(8,128)(2,1)S(1)}, bf16[512,256]{1,0:T(8,128)(2,1)S(1)}, u32[]{:S(2)}, u32[]{:S(2)}) %collective-permute-start.3) | collective-permute-done | bytes 262176 | tf_op jit(solution)/shard_map/ppermute | solution.py:263
  18.3 0.4 collective-permute-done.5.refs_4_
  18.6 3.0 %shard_map.86 = (bf16[512,256]{1,0:T(8,128)(2,1)S(1)}, bf16[512,256]{1,0:T(8,128)(2,1)S(1)}, bf16[512,256]{1,0:T(8,128)(2,1)S(1)}, bf16[512,256]{1,0:T(8,128)(2,1)S(1)}) custom-call(s32[129]{0:T(256)S(1)} %get-tuple-element.33.row_of, s32[128]{0:T(128)S(1)} %get-tuple-element.34.col_of, s32[1]{0:T(128)} %bitcast.here_ref.me.mine_ref, ...), custom_call_target="tpu_custom_call" | custom-call | flops 1073741824 | bytes 6291456 | tf_op jit(solution)/shard_map/pallas_call | solution.py:136
  21.7 4.6 %collective-permute-start.10 = (bf16[512,256]{1,0:T(8,128)(2,1)S(1)}, bf16[512,256]{1,0:T(8,128)(2,1)S(1)}, u32[]{:S(2)}, u32[]{:S(2)}) collective-permute-start(bf16[512,256]{1,0:T(8,128)(2,1)S(1)} %get-tuple-element.37), channel_id=1, source_target_pairs={{0,1},{3,2},{4,5},{7,6},{8,9},{11,10},{12,13},{15,14},{16,17},{19,... | collective-permute-start | bytes 786440 | tf_op jit(solution)/shard_map/ppermute | solution.py:287
  26.3 0.7 collective-permute-start.7
  26.9 4.0 %collective-permute-start.8 = (bf16[512,256]{1,0:T(8,128)(2,1)S(1)}, bf16[512,256]{1,0:T(8,128)(2,1)S(1)}, u32[]{:S(2)}, u32[]{:S(2)}) collective-permute-start(bf16[512,256]{1,0:T(8,128)(2,1)S(1)} %get-tuple-element.38), channel_id=1, source_target_pairs={{0,2},{3,1},{4,6},{7,5},{8,10},{11,9},{12,14},{15,13},{16,18},{19,... | collective-permute-start | bytes 786440 | tf_op jit(solution)/shard_map/ppermute | solution.py:289
  30.9 0.1 collective-permute-start.9
  31.0 1.8 %collective-permute-done.10 = bf16[512,256]{1,0:T(8,128)(2,1)S(1)} collective-permute-done((bf16[512,256]{1,0:T(8,128)(2,1)S(1)}, bf16[512,256]{1,0:T(8,128)(2,1)S(1)}, u32[]{:S(2)}, u32[]{:S(2)}) %collective-permute-start.10) | collective-permute-done | bytes 262176 | tf_op jit(solution)/shard_map/ppermute | solution.py:287
  32.8 0.1 add_convert_fusion.1
  32.9 1.3 %collective-permute-start.11 = (bf16[512,256]{1,0:T(8,128)(2,1)S(1)}, bf16[512,256]{1,0:T(8,128)(2,1)S(1)}, u32[]{:S(2)}, u32[]{:S(2)}) collective-permute-start(bf16[512,256]{1,0:T(8,128)(2,1)S(1)} %add_convert_fusion.1), channel_id=1, source_target_pairs={{1,3},{2,0},{5,7},{6,4},{9,11},{10,8},{13,15},{14,12},{17,19},{18,... | collective-permute-start | bytes 786440 | tf_op jit(solution)/shard_map/ppermute | solution.py:292
  34.2 0.0 collective-permute-done.7.refs_0_
  34.2 4.3 %collective-permute-done.8.refs_1_ = bf16[512,256]{1,0:T(8,128)(2,1)S(1)} collective-permute-done((bf16[512,256]{1,0:T(8,128)(2,1)S(1)}, bf16[512,256]{1,0:T(8,128)(2,1)S(1)}, u32[]{:S(2)}, u32[]{:S(2)}) %collective-permute-start.8) | collective-permute-done | bytes 262176 | tf_op jit(solution)/shard_map/ppermute | solution.py:289
  38.5 4.6 %collective-permute-done.9.refs_2_ = bf16[512,256]{1,0:T(8,128)(2,1)S(1)} collective-permute-done((bf16[512,256]{1,0:T(8,128)(2,1)S(1)}, bf16[512,256]{1,0:T(8,128)(2,1)S(1)}, u32[]{:S(2)}, u32[]{:S(2)}) %collective-permute-start.9) | collective-permute-done | bytes 262176 | tf_op jit(solution)/shard_map/ppermute | solution.py:263
  43.1 0.1 shard_map.87.refs_0_
  43.2 3.2 %collective-permute-done.11.refs_1_ = bf16[512,256]{1,0:T(8,128)(2,1)S(1)} collective-permute-done((bf16[512,256]{1,0:T(8,128)(2,1)S(1)}, bf16[512,256]{1,0:T(8,128)(2,1)S(1)}, u32[]{:S(2)}, u32[]{:S(2)}) %collective-permute-start.11) | collective-permute-done | bytes 262176 | tf_op jit(solution)/shard_map/ppermute | solution.py:292
  46.3 0.0 copy-done.1
  46.4 0.0 copy-done.2
  46.4 1.2 %shard_map.88 = (bf16[512,256]{1,0:T(8,128)(2,1)}, bf16[512,256]{1,0:T(8,128)(2,1)S(1)}, f32[512,256]{1,0:T(8,128)S(1)}, f32[512,256]{1,0:T(8,128)S(1)}) custom-call(f32[512,256]{1,0:T(8,128)S(1)} %shard_map.87.refs_0_, bf16[512,256]{1,0:T(8,128)(2,1)S(1)} %collective-permute-done.11.refs_1_, bf16[256,256]{1,0:T(8,128)(2,1)S(1)} %copy-done.2, ...), custom_call_target="tpu_custom_call" | custom-call | flops 268435456 | bytes 2621440 | tf_op jit(solution)/shard_map/pallas_call | solution.py:182
  47.6 2.7 %collective-permute-start.14 = (bf16[512,256]{1,0:T(8,128)(2,1)S(1)}, bf16[512,256]{1,0:T(8,128)(2,1)S(1)}, u32[]{:S(2)}, u32[]{:S(2)}) collective-permute-start(bf16[512,256]{1,0:T(8,128)(2,1)S(1)} %get-tuple-element.48.refs_3_), channel_id=1, source_target_pairs={{0,3},{1,2},{2,1},{3,0},{4,7},{5,6},{6,5},{7,4},{8,11},{9,10},{10,... | collective-permute-start | bytes 786440 | tf_op jit(solution)/shard_map/ppermute | solution.py:263
  50.2 0.0 collective-permute-start.15
  50.2 1.7 %collective-permute-start.16 = (bf16[512,256]{1,0:T(8,128)(2,1)S(1)}, bf16[512,256]{1,0:T(8,128)(2,1)S(1)}, u32[]{:S(2)}, u32[]{:S(2)}) collective-permute-start(bf16[512,256]{1,0:T(8,128)(2,1)S(1)} %get-tuple-element.48.refs_3_), channel_id=1, source_target_pairs={{0,1},{1,0},{2,3},{3,2},{4,5},{5,4},{6,7},{7,6},{8,9},{9,8},{10,11... | collective-permute-start | bytes 786440 | tf_op jit(solution)/shard_map/ppermute | solution.py:263
  51.9 0.5 shard_map.89
  52.4 0.1 collective-permute-start.12
  52.5 1.3 %collective-permute-done.12 = f32[128,256]{1,0:T(8,128)S(1)} collective-permute-done((f32[128,256]{1,0:T(8,128)S(1)}, f32[128,256]{1,0:T(8,128)S(1)}, u32[]{:S(2)}, u32[]{:S(2)}) %collective-permute-start.12) | collective-permute-done | bytes 131104 | tf_op jit(solution)/shard_map/ppermute | solution.py:263
  53.8 8.6 %all_to_all.15 = f32[4,32,256]{2,1,0:T(8,128)S(1)} all-to-all(f32[4,32,256]{2,1,0:T(8,128)S(1)} %bitcast.6), channel_id=1, replica_groups={{0,8,16,24},{4,12,20,28},{1,9,17,25},{5,13,21,29},{2,10,18,26},{6,14,22..., dimensions={0} | all-to-all | bytes 262144 | tf_op jit(solution)/shard_map/all_to_all | solution.py:336
  62.5 7.6 %all_gather.3 = bf16[128,256]{1,0:T(8,128)(2,1)S(1)} all-gather(bf16[32,256]{1,0:T(8,128)(2,1)S(1)} %reduce_sum.18), channel_id=1, replica_groups={{0,8,16,24},{4,12,20,28},{1,9,17,25},{5,13,21,29},{2,10,18,26},{6,14,22..., dimensions={0}, use_global_device_ids=true | all-gather | bytes 81920 | tf_op jit(solution)/shard_map/all_gather | solution.py:338
  70.1 0.0 collective-permute-done.14.refs_0_
  70.1 1.7 %collective-permute-done.15.refs_1_ = bf16[512,256]{1,0:T(8,128)(2,1)S(1)} collective-permute-done((bf16[512,256]{1,0:T(8,128)(2,1)S(1)}, bf16[512,256]{1,0:T(8,128)(2,1)S(1)}, u32[]{:S(2)}, u32[]{:S(2)}) %collective-permute-start.15) | collective-permute-done | bytes 262176 | tf_op jit(solution)/shard_map/ppermute | solution.py:263
  71.8 0.0 collective-permute-done.16.refs_2_
  71.8 3.2 %shard_map.90 = (bf16[2048,256]{1,0:T(8,128)(2,1)S(1)}, bf16[2048,256]{1,0:T(8,128)(2,1)S(1)}) custom-call(s32[129]{0:T(256)S(1)} %get-tuple-element.33.row_of, s32[128]{0:T(128)S(1)} %get-tuple-element.34.col_of, s32[1]{0:T(128)} %bitcast.1.mine_ref.here_ref, s32[1]{0:T(128)} %bitcast.here_ref.me.mine_ref, ...), custom_call_target="tpu_custom_call" | custom-call | flops 1073741824 | bytes 5242880 | tf_op jit(solution)/shard_map/pallas_call | solution.py:136
  75.0 0.1 collective-permute-start.17
  75.1 0.7 tile.2
  75.8 3.5 %all-to-all-start.1 = ((bf16[4,128,256]{2,1,0:T(8,128)(2,1)}), bf16[4,128,256]{2,1,0:T(8,128)(2,1)S(1)}, u32[]{:S(2)}, u32[]{:S(2)}) async-start(bf16[4,128,256]{2,1,0:T(8,128)(2,1)} %tile.2), calls=%async_computation.1 | async-start | bytes 524288 | tf_op jit(solution)/shard_map/all_to_all | solution.py:304
  79.3 0.0 collective-permute-done.17.other_ref
  79.3 0.2 shard_map.91
  79.6 1.1 %collective-permute-start.18 = (bf16[512,256]{1,0:T(8,128)(2,1)S(1)}, bf16[512,256]{1,0:T(8,128)(2,1)S(1)}, u32[]{:S(2)}, u32[]{:S(2)}) collective-permute-start(bf16[512,256]{1,0:T(8,128)(2,1)S(1)} %get-tuple-element.51), channel_id=1, source_target_pairs={{0,24},{4,28},{8,16},{12,20},{16,8},{20,12},{24,0},{28,4},{1,25},{... | collective-permute-start | bytes 786440 | tf_op jit(solution)/shard_map/ppermute | solution.py:263
  80.7 1.9 %collective-permute-start.19 = (bf16[512,256]{1,0:T(8,128)(2,1)S(1)}, bf16[512,256]{1,0:T(8,128)(2,1)S(1)}, u32[]{:S(2)}, u32[]{:S(2)}) collective-permute-start(bf16[512,256]{1,0:T(8,128)(2,1)S(1)} %get-tuple-element.52), channel_id=1, source_target_pairs={{0,16},{4,20},{8,24},{12,28},{16,0},{20,4},{24,8},{28,12},{1,17},{... | collective-permute-start | bytes 786440 | tf_op jit(solution)/shard_map/ppermute | solution.py:263
  82.6 1.4 %collective-permute-start.20 = (bf16[512,256]{1,0:T(8,128)(2,1)S(1)}, bf16[512,256]{1,0:T(8,128)(2,1)S(1)}, u32[]{:S(2)}, u32[]{:S(2)}) collective-permute-start(bf16[512,256]{1,0:T(8,128)(2,1)S(1)} %get-tuple-element.53), channel_id=1, source_target_pairs={{0,8},{4,12},{8,0},{12,4},{16,24},{20,28},{24,16},{28,20},{1,9},{5... | collective-permute-start | bytes 786440 | tf_op jit(solution)/shard_map/ppermute | solution.py:263
  84.0 5.0 %all-to-all-done.1 = bf16[4,128,256]{2,1,0:T(8,128)(2,1)S(1)} async-done(((bf16[4,128,256]{2,1,0:T(8,128)(2,1)}), bf16[4,128,256]{2,1,0:T(8,128)(2,1)S(1)}, u32[]{:S(2)}, u32[]{:S(2)}) %all-to-all-start.1) | async-done | bytes 262176 | tf_op jit(solution)/shard_map/all_to_all | solution.py:304
  89.0 0.1 collective-permute-start.13
  89.1 0.6 collective-permute-done.18
  89.7 5.0 %collective-permute-done.19 = bf16[512,256]{1,0:T(8,128)(2,1)S(1)} collective-permute-done((bf16[512,256]{1,0:T(8,128)(2,1)S(1)}, bf16[512,256]{1,0:T(8,128)(2,1)S(1)}, u32[]{:S(2)}, u32[]{:S(2)}) %collective-permute-start.19) | collective-permute-done | bytes 262176 | tf_op jit(solution)/shard_map/ppermute | solution.py:263
  94.8 1.5 %collective-permute-done.20 = bf16[512,256]{1,0:T(8,128)(2,1)S(1)} collective-permute-done((bf16[512,256]{1,0:T(8,128)(2,1)S(1)}, bf16[512,256]{1,0:T(8,128)(2,1)S(1)}, u32[]{:S(2)}, u32[]{:S(2)}) %collective-permute-start.20) | collective-permute-done | bytes 262176 | tf_op jit(solution)/shard_map/ppermute | solution.py:263
  96.3 0.8 add_convert_fusion
  97.1 0.0 collective-permute-done.13.other_ref
  97.1 0.7 shard_map.92
  (6 shorter events, 0.1 us)
Async XLA Ops:
  0.6 11.3 %collective-permute-start = (bf16[512,256]{1,0:T(8,128)(2,1)}, bf16[512,256]{1,0:T(8,128)(2,1)S(1)}, u32[]{:S(2)}, u32[]{:S(2)}) collective-permute-start(bf16[512,256]{1,0:T(8,128)(2,1)} %features.1), channel_id=1, source_target_pairs={{0,24},{4,28},{8,16},{12,20},{16,8},{20,12},{24,0},{28,4},{1,25},{... | collective-permute-start | bytes 786440 | tf_op jit(solution)/shard_map/ppermute | solution.py:263
  4.6 12.1 %collective-permute-start.2 = (bf16[512,256]{1,0:T(8,128)(2,1)}, bf16[512,256]{1,0:T(8,128)(2,1)S(1)}, u32[]{:S(2)}, u32[]{:S(2)}) collective-permute-start(bf16[512,256]{1,0:T(8,128)(2,1)} %features.1), channel_id=1, source_target_pairs={{0,16},{4,20},{8,24},{12,28},{16,0},{20,4},{24,8},{28,12},{1,17},{... | collective-permute-start | bytes 786440 | tf_op jit(solution)/shard_map/ppermute | solution.py:263
  5.1 11.9 %collective-permute-start.4 = (bf16[512,256]{1,0:T(8,128)(2,1)}, bf16[512,256]{1,0:T(8,128)(2,1)S(1)}, u32[]{:S(2)}, u32[]{:S(2)}) collective-permute-start(bf16[512,256]{1,0:T(8,128)(2,1)} %features.1), channel_id=1, source_target_pairs={{0,8},{4,12},{8,0},{12,4},{16,24},{20,28},{24,16},{28,20},{1,9},{5... | collective-permute-start | bytes 786440 | tf_op jit(solution)/shard_map/ppermute | solution.py:263
  5.2 1.0 %copy-start = (bf16[512,256]{1,0:T(8,128)(2,1)S(1)}, bf16[512,256]{1,0:T(8,128)(2,1)}, u32[]{:S(2)}) copy-start(bf16[512,256]{1,0:T(8,128)(2,1)} %features.1) | copy-start | bytes 786436
  6.2 0.7 copy-start.3
  6.9 0.7 copy-start.4
  12.0 5.3 %collective-permute-start.1 = (bf16[512,256]{1,0:T(8,128)(2,1)S(1)}, bf16[512,256]{1,0:T(8,128)(2,1)S(1)}, u32[]{:S(2)}, u32[]{:S(2)}) collective-permute-start(bf16[512,256]{1,0:T(8,128)(2,1)S(1)} %collective-permute-done.refs_1_), channel_id=1, source_target_pairs={{0,4},{4,0},{8,12},{12,8},{16,20},{20,16},{24,28},{28,24},{1,5},{5... | collective-permute-start | bytes 786440 | tf_op jit(solution)/shard_map/ppermute | solution.py:263
  12.0 5.3 %collective-permute-start.6 = (bf16[512,256]{1,0:T(8,128)(2,1)S(1)}, bf16[512,256]{1,0:T(8,128)(2,1)S(1)}, u32[]{:S(2)}, u32[]{:S(2)}) collective-permute-start(bf16[512,256]{1,0:T(8,128)(2,1)S(1)} %get-tuple-element.36.refs_7_), channel_id=1, source_target_pairs={{0,4},{4,0},{8,12},{12,8},{16,20},{20,16},{24,28},{28,24},{1,5},{5... | collective-permute-start | bytes 786440 | tf_op jit(solution)/shard_map/ppermute | solution.py:263
  16.7 1.5 %collective-permute-start.3 = (bf16[512,256]{1,0:T(8,128)(2,1)S(1)}, bf16[512,256]{1,0:T(8,128)(2,1)S(1)}, u32[]{:S(2)}, u32[]{:S(2)}) collective-permute-start(bf16[512,256]{1,0:T(8,128)(2,1)S(1)} %collective-permute-done.2.refs_3_), channel_id=1, source_target_pairs={{0,4},{4,0},{8,12},{12,8},{16,20},{20,16},{24,28},{28,24},{1,5},{5... | collective-permute-start | bytes 786440 | tf_op jit(solution)/shard_map/ppermute | solution.py:263
  17.0 1.6 %collective-permute-start.5 = (bf16[512,256]{1,0:T(8,128)(2,1)S(1)}, bf16[512,256]{1,0:T(8,128)(2,1)S(1)}, u32[]{:S(2)}, u32[]{:S(2)}) collective-permute-start(bf16[512,256]{1,0:T(8,128)(2,1)S(1)} %collective-permute-done.4.refs_5_), channel_id=1, source_target_pairs={{0,4},{4,0},{8,12},{12,8},{16,20},{20,16},{24,28},{28,24},{1,5},{5... | collective-permute-start | bytes 786440 | tf_op jit(solution)/shard_map/ppermute | solution.py:263
  18.6 27.7 %copy-start.1 = (bf16[512,256]{1,0:T(8,128)(2,1)S(1)}, bf16[512,256]{1,0:T(8,128)(2,1)}, u32[]{:S(2)}) copy-start(bf16[512,256]{1,0:T(8,128)(2,1)} %refs_3_.1) | copy-start | bytes 786436
  18.6 27.7 %copy-start.2 = (bf16[256,256]{1,0:T(8,128)(2,1)S(1)}, bf16[256,256]{1,0:T(8,128)(2,1)}, u32[]{:S(2)}) copy-start(bf16[256,256]{1,0:T(8,128)(2,1)} %refs_2_.1) | copy-start | bytes 393220
  21.7 11.1 %collective-permute-start.10 = (bf16[512,256]{1,0:T(8,128)(2,1)S(1)}, bf16[512,256]{1,0:T(8,128)(2,1)S(1)}, u32[]{:S(2)}, u32[]{:S(2)}) collective-permute-start(bf16[512,256]{1,0:T(8,128)(2,1)S(1)} %get-tuple-element.37), channel_id=1, source_target_pairs={{0,1},{3,2},{4,5},{7,6},{8,9},{11,10},{12,13},{15,14},{16,17},{19,... | collective-permute-start | bytes 786440 | tf_op jit(solution)/shard_map/ppermute | solution.py:287
  26.3 7.9 %collective-permute-start.7 = (bf16[512,256]{1,0:T(8,128)(2,1)S(1)}, bf16[512,256]{1,0:T(8,128)(2,1)S(1)}, u32[]{:S(2)}, u32[]{:S(2)}) collective-permute-start(bf16[512,256]{1,0:T(8,128)(2,1)S(1)} %get-tuple-element.37), channel_id=1, source_target_pairs={{1,2},{2,1},{5,6},{6,5},{9,10},{10,9},{13,14},{14,13},{17,18},{18,... | collective-permute-start | bytes 786440 | tf_op jit(solution)/shard_map/ppermute | solution.py:288
  26.9 11.5 %collective-permute-start.8 = (bf16[512,256]{1,0:T(8,128)(2,1)S(1)}, bf16[512,256]{1,0:T(8,128)(2,1)S(1)}, u32[]{:S(2)}, u32[]{:S(2)}) collective-permute-start(bf16[512,256]{1,0:T(8,128)(2,1)S(1)} %get-tuple-element.38), channel_id=1, source_target_pairs={{0,2},{3,1},{4,6},{7,5},{8,10},{11,9},{12,14},{15,13},{16,18},{19,... | collective-permute-start | bytes 786440 | tf_op jit(solution)/shard_map/ppermute | solution.py:289
  30.9 12.1 %collective-permute-start.9 = (bf16[512,256]{1,0:T(8,128)(2,1)S(1)}, bf16[512,256]{1,0:T(8,128)(2,1)S(1)}, u32[]{:S(2)}, u32[]{:S(2)}) collective-permute-start(bf16[512,256]{1,0:T(8,128)(2,1)S(1)} %get-tuple-element.39), channel_id=1, source_target_pairs={{0,1},{1,0},{2,3},{3,2},{4,5},{5,4},{6,7},{7,6},{8,9},{9,8},{10,11... | collective-permute-start | bytes 786440 | tf_op jit(solution)/shard_map/ppermute | solution.py:263
  32.9 13.5 %collective-permute-start.11 = (bf16[512,256]{1,0:T(8,128)(2,1)S(1)}, bf16[512,256]{1,0:T(8,128)(2,1)S(1)}, u32[]{:S(2)}, u32[]{:S(2)}) collective-permute-start(bf16[512,256]{1,0:T(8,128)(2,1)S(1)} %add_convert_fusion.1), channel_id=1, source_target_pairs={{1,3},{2,0},{5,7},{6,4},{9,11},{10,8},{13,15},{14,12},{17,19},{18,... | collective-permute-start | bytes 786440 | tf_op jit(solution)/shard_map/ppermute | solution.py:292
  47.6 22.5 %collective-permute-start.14 = (bf16[512,256]{1,0:T(8,128)(2,1)S(1)}, bf16[512,256]{1,0:T(8,128)(2,1)S(1)}, u32[]{:S(2)}, u32[]{:S(2)}) collective-permute-start(bf16[512,256]{1,0:T(8,128)(2,1)S(1)} %get-tuple-element.48.refs_3_), channel_id=1, source_target_pairs={{0,3},{1,2},{2,1},{3,0},{4,7},{5,6},{6,5},{7,4},{8,11},{9,10},{10,... | collective-permute-start | bytes 786440 | tf_op jit(solution)/shard_map/ppermute | solution.py:263
  50.2 21.6 %collective-permute-start.15 = (bf16[512,256]{1,0:T(8,128)(2,1)S(1)}, bf16[512,256]{1,0:T(8,128)(2,1)S(1)}, u32[]{:S(2)}, u32[]{:S(2)}) collective-permute-start(bf16[512,256]{1,0:T(8,128)(2,1)S(1)} %get-tuple-element.48.refs_3_), channel_id=1, source_target_pairs={{0,2},{1,3},{2,0},{3,1},{4,6},{5,7},{6,4},{7,5},{8,10},{9,11},{10,... | collective-permute-start | bytes 786440 | tf_op jit(solution)/shard_map/ppermute | solution.py:263
  50.2 21.6 %collective-permute-start.16 = (bf16[512,256]{1,0:T(8,128)(2,1)S(1)}, bf16[512,256]{1,0:T(8,128)(2,1)S(1)}, u32[]{:S(2)}, u32[]{:S(2)}) collective-permute-start(bf16[512,256]{1,0:T(8,128)(2,1)S(1)} %get-tuple-element.48.refs_3_), channel_id=1, source_target_pairs={{0,1},{1,0},{2,3},{3,2},{4,5},{5,4},{6,7},{7,6},{8,9},{9,8},{10,11... | collective-permute-start | bytes 786440 | tf_op jit(solution)/shard_map/ppermute | solution.py:263
  52.4 1.4 %collective-permute-start.12 = (f32[128,256]{1,0:T(8,128)S(1)}, f32[128,256]{1,0:T(8,128)S(1)}, u32[]{:S(2)}, u32[]{:S(2)}) collective-permute-start(f32[128,256]{1,0:T(8,128)S(1)} %get-tuple-element.45), channel_id=1, source_target_pairs={{0,4},{4,0},{8,12},{12,8},{16,20},{20,16},{24,28},{28,24},{1,5},{5... | collective-permute-start | bytes 393224 | tf_op jit(solution)/shard_map/ppermute | solution.py:263
  75.0 4.4 %collective-permute-start.17 = (bf16[2048,256]{1,0:T(8,128)(2,1)S(1)}, bf16[2048,256]{1,0:T(8,128)(2,1)S(1)}, u32[]{:S(2)}, u32[]{:S(2)}) collective-permute-start(bf16[2048,256]{1,0:T(8,128)(2,1)S(1)} %get-tuple-element.50), channel_id=1, source_target_pairs={{0,4},{4,0},{8,12},{12,8},{16,20},{20,16},{24,28},{28,24},{1,5},{5... | collective-permute-start | bytes 3145736 | tf_op jit(solution)/shard_map/ppermute | solution.py:263
  75.8 13.2 %all-to-all-start.1 = ((bf16[4,128,256]{2,1,0:T(8,128)(2,1)}), bf16[4,128,256]{2,1,0:T(8,128)(2,1)S(1)}, u32[]{:S(2)}, u32[]{:S(2)}) async-start(bf16[4,128,256]{2,1,0:T(8,128)(2,1)} %tile.2), calls=%async_computation.1 | async-start | bytes 524288 | tf_op jit(solution)/shard_map/all_to_all | solution.py:304
  79.6 10.1 %collective-permute-start.18 = (bf16[512,256]{1,0:T(8,128)(2,1)S(1)}, bf16[512,256]{1,0:T(8,128)(2,1)S(1)}, u32[]{:S(2)}, u32[]{:S(2)}) collective-permute-start(bf16[512,256]{1,0:T(8,128)(2,1)S(1)} %get-tuple-element.51), channel_id=1, source_target_pairs={{0,24},{4,28},{8,16},{12,20},{16,8},{20,12},{24,0},{28,4},{1,25},{... | collective-permute-start | bytes 786440 | tf_op jit(solution)/shard_map/ppermute | solution.py:263
  80.7 14.1 %collective-permute-start.19 = (bf16[512,256]{1,0:T(8,128)(2,1)S(1)}, bf16[512,256]{1,0:T(8,128)(2,1)S(1)}, u32[]{:S(2)}, u32[]{:S(2)}) collective-permute-start(bf16[512,256]{1,0:T(8,128)(2,1)S(1)} %get-tuple-element.52), channel_id=1, source_target_pairs={{0,16},{4,20},{8,24},{12,28},{16,0},{20,4},{24,8},{28,12},{1,17},{... | collective-permute-start | bytes 786440 | tf_op jit(solution)/shard_map/ppermute | solution.py:263
  82.6 13.7 %collective-permute-start.20 = (bf16[512,256]{1,0:T(8,128)(2,1)S(1)}, bf16[512,256]{1,0:T(8,128)(2,1)S(1)}, u32[]{:S(2)}, u32[]{:S(2)}) collective-permute-start(bf16[512,256]{1,0:T(8,128)(2,1)S(1)} %get-tuple-element.53), channel_id=1, source_target_pairs={{0,8},{4,12},{8,0},{12,4},{16,24},{20,28},{24,16},{28,20},{1,9},{5... | collective-permute-start | bytes 786440 | tf_op jit(solution)/shard_map/ppermute | solution.py:263
  89.0 8.1 %collective-permute-start.13 = (f32[128,256]{1,0:T(8,128)S(1)}, f32[128,256]{1,0:T(8,128)S(1)}, u32[]{:S(2)}, u32[]{:S(2)}) collective-permute-start(f32[128,256]{1,0:T(8,128)S(1)} %convert_reduce_fusion.own_ref), channel_id=1, source_target_pairs={{0,4},{4,0},{8,12},{12,8},{16,20},{20,16},{24,28},{28,24},{1,5},{5... | collective-permute-start | bytes 393224 | tf_op jit(solution)/shard_map/ppermute | solution.py:263

commit v10 on v9

--- a/solution.py
+++ b/solution.py
@@ -68,7 +68,8 @@
     )(starts, cols, features)
 
 
-def sparse_kernel(parts, outs, backward, row_of, col_of, here_ref, mine_ref, *refs):
+def sparse_kernel(counts, outs, backward, row_of, col_of, here_ref, mine_ref, *refs):
+    parts = sum(counts)
     panel_refs = refs[:parts]
     values_ref = refs[parts]
     out_refs = refs[parts + 1 : parts + 1 + len(outs)]
@@ -87,9 +88,14 @@
     used = (live + GROUP - 1) // GROUP
     lax.fori_loop(0, used, begin, 0)
     total[...] = jnp.zeros_like(total)
-    for m in range(parts):
+    at = parts
+    for m, count in enumerate(counts):
         start = pl.multiple_of((here ^ m) * chunk, chunk)
-        panel[pl.ds(start, chunk), :] = panel_refs[parts - 1 - m][...]
+        part = panel_refs[at - 1][...]
+        for ref in panel_refs[at - count : at - 1]:
+            part += ref[...]
+        panel[pl.ds(start, chunk), :] = part
+        at -= count
     spare = total.shape[0] // size - 1
     last = panel.shape[0] // size - 1
 
@@ -129,14 +135,16 @@
 
 
 def sparse_product(panel_parts, values, row_of, col_of, here, mine, blocks, outs, backward):
-    parts = len(panel_parts)
+    counts = [len(part) for part in panel_parts]
+    operands = [operand for part in panel_parts for operand in part]
+    parts = len(counts)
     slots, size, _ = values.shape
-    chunk, width = panel_parts[0].shape
+    chunk, width = operands[0].shape
     flops = 2 * slots * size * size * width
     return pl.pallas_call(
-        functools.partial(sparse_kernel, parts, outs, backward),
+        functools.partial(sparse_kernel, counts, outs, backward),
         out_shape=[jax.ShapeDtypeStruct((chunk * len(members), width), BF16) for members in outs],
-        in_specs=[SMEM] * 4 + [VMEM] * parts + [ANY],
+        in_specs=[SMEM] * 4 + [VMEM] * len(operands) + [ANY],
         out_specs=[VMEM] * len(outs),
         scratch_shapes=[
             pltpu.VMEM((parts * chunk, width), BF16),
@@ -146,7 +154,7 @@
         ],
         compiler_params=params(48),
         cost_estimate=cost(flops, 2 * values.size + 2 * parts * chunk * width),
-    )(row_of, col_of, here, mine, *panel_parts[::-1], values)
+    )(row_of, col_of, here, mine, *operands[::-1], values)
 
 
 def split(value):
@@ -293,6 +301,18 @@
     return [add_up([cross, inward, near, terms[0]]), outward]
 
 
+def gather_parts(own, n, first):
+    if n != 4:
+        return [[own]] + [[swap(own, "col", n, m)] for m in range(n - 1, 0, -1)][::-1], first
+    inward = lax.ppermute(own, "col", [(0, 2), (3, 1)])
+    cross = lax.ppermute(own, "col", [(1, 2), (2, 1)])
+    outward = lax.ppermute(own, "col", [(1, 3), (2, 0)])
+    near = swap(own, "col", n, 1)
+    inward, first = lax.optimization_barrier((inward, first))
+    far = lax.ppermute(inward, "col", [(2, 3), (1, 0)])
+    return [[own], [near], [inward, outward], [cross, far]], first
+
+
 def total_of(terms):
     result = terms[0].astype(F32)
     for term in terms[1:]:
@@ -323,20 +343,19 @@
         panel[m + 1] = swap(panel[m], "row", n_row, 1)
 
     each = [[m] for m in range(n_col)]
-    terms = sparse_product(panel, values, row_of, col_of, me_row, me_col, row_blocks, each, False)
+    terms = sparse_product(
+        [[part] for part in panel], values, row_of, col_of, me_row, me_col, row_blocks, each, False
+    )
     terms = exchange_terms(terms, n_col)
     activations, back, aggregated, mixed_grad = middle(terms, weight, cotangent)
 
-    back_panel = [back] + [swap(back, "col", n_col, m) for m in range(n_col - 1, 0, -1)][::-1]
-
-    depth = weight.shape[0] // n_row
     own_term, other_term = weight_term(aggregated, mixed_grad, me_row, n_row)
     term = own_term + swap(other_term, "row", n_row, 1)
+    back_panel, term = gather_parts(back, n_col, term)
     cores = [list(range(0, n_row, 2)), list(range(1, n_row, 2))]
-    term = lax.all_to_all(term, "row", 0, 0, axis_index_groups=cores, tiled=True)
-    piece = jnp.sum(term.reshape(n_row // 2, depth, -1), axis=0)
-    half = lax.all_gather(piece, "row", axis=0, axis_index_groups=cores, tiled=True)
+    half = lax.all_gather(term, "row", axis=0, axis_index_groups=cores, tiled=True)
     half, back_panel[0] = lax.optimization_barrier((half, back_panel[0]))
+    half = jnp.sum(half.reshape(n_row // 2, -1, half.shape[1]), axis=0)
 
     even = list(range(0, n_row, 2))
     pair = [even, [m + 1 for m in even]]

time: 98.2 us -> 98.9 us (level)
  blocking collectives: 16.2 us -> 12.3 us
  starting transfers between devices: 28.5 us -> 30.5 us
  other arithmetic: 0.97 us -> 2.04 us
    all_to_all x1 -> x0, blocking collectives: 8.6 us -> none  [on_device(): lax.all_to_all(term, 'row', 0, 0, axis_index_groups=cores, tiled=True)]
    ppermute x0 -> x4, starting transfers between devices: none -> 4.7 us  [the longest x1 1.45 us: gather_parts(): inward = lax.ppermute(own, 'col', [(0, 2), (3, 1)])]
    all_gather x1, blocking collectives: 7.64 us -> 12.3 us  [on_device(): lax.all_gather(term, 'row', axis=0, axis_index_groups=cores, tiled=True)]
    ppermute x17 -> x15, waiting for transfers between devices: 22.3 us -> 17.7 us  [swap(): return lax.ppermute(x, axis, [(i, i ^ m) for i in range(n)])]
    ppermute x0 -> x4, waiting for transfers between devices: none -> 4.29 us  [the longest x1 3.73 us: gather_parts(): inward = lax.ppermute(own, 'col', [(0, 2), (3, 1)])]
    ppermute x1, waiting for transfers between devices: 3.15 us -> 5.1 us  [exchange_terms(): outward = lax.ppermute(relay, 'col', [(1, 3), (2, 0)])]
    ppermute x17 -> x15, starting transfers between devices: 14.4 us -> 12.5 us  [swap(): return lax.ppermute(x, axis, [(i, i ^ m) for i in range(n)])]
    all_to_all x1, starting transfers between devices: 3.55 us -> 4.87 us  [exchange(): return lax.all_to_all(x, axis, 0, 0, tiled=True)]
  transfers between devices with their start and end apart: 22 -> 24, of which waited for: 15 -> 14; matrix products, arithmetic and copies ran while one was open for 2% -> 3% of each run, Pallas kernels for 4% -> 4%
where the time goes in v10:
time: 98.9 us; the launch traced here: 98.5 us
  waiting for transfers between devices  37.2 us (38%)
  starting transfers between devices  30.5 us (31%)
  Pallas kernels  12.6 us (13%)
  blocking collectives  12.3 us (12%)
  local copies, waits for them, and re-layouts  3.02 us (3%)
  other arithmetic  2.04 us (2%)
    ppermute x15, waiting for transfers between devices, swap(): return lax.ppermute(x, axis, [(i, i ^ m) for i in range(n)])  17.7 us
    ppermute x15, starting transfers between devices, swap(): return lax.ppermute(x, axis, [(i, i ^ m) for i in range(n)])  12.5 us
    all_gather x1, blocking collectives, on_device(): lax.all_gather(term, 'row', axis=0, axis_index_groups=cores, tiled=True)  12.3 us
    pallas_call x2, Pallas kernels, sparse_product(): pl.pallas_call(functools.partial(sparse_kernel, counts, outs, backward),...  7.03 us
    all_to_all x1, waiting for transfers between devices, exchange(): return lax.all_to_all(x, axis, 0, 0, tiled=True)  5.26 us
    ppermute x1, waiting for transfers between devices, exchange_terms(): outward = lax.ppermute(relay, 'col', [(1, 3), (2, 0)])  5.1 us
    all_to_all x1, starting transfers between devices, exchange(): return lax.all_to_all(x, axis, 0, 0, tiled=True)  4.87 us
    ppermute x1, waiting for transfers between devices, exchange_terms(): inward = lax.ppermute(terms[2], 'col', [(0, 2), (3, 1)])  4.17 us
  transfers between devices with their start and end apart: 24, of which 14 were waited for; matrix products, arithmetic and copies ran while one was open for 3% of the time, Pallas kernels for 4%

profile of v10, /device:TPU:0, one launch (start us, length us, event | category | flops | bytes accessed | tf_op | source)
XLA Modules:
  0.0 98.5 jit_solution(10102206386926220682)
XLA Ops:
  0.6 4.0 %collective-permute-start = (bf16[512,256]{1,0:T(8,128)(2,1)}, bf16[512,256]{1,0:T(8,128)(2,1)S(1)}, u32[]{:S(2)}, u32[]{:S(2)}) collective-permute-start(bf16[512,256]{1,0:T(8,128)(2,1)} %features.1), channel_id=1, source_target_pairs={{0,24},{4,28},{8,16},{12,20},{16,8},{20,12},{24,0},{28,4},{1,25},{... | collective-permute-start | bytes 786440 | tf_op jit(solution)/shard_map/ppermute | solution.py:271
  4.6 0.5 collective-permute-start.4
  5.1 0.1 collective-permute-start.2
  5.2 1.0 copy-done
  6.2 0.7 copy-done.3
  6.9 0.7 copy-done.4
  7.5 2.9 %shard_map.85 = (s32[129]{0:T(256)S(1)}, s32[128]{0:T(128)S(1)}, bf16[512,256]{1,0:T(8,128)(2,1)S(1)}) custom-call(s32[1,1,17]{2,1,0:T(1,128)S(1)} %copy-done.3, s32[1,1,128]{2,1,0:T(1,128)S(1)} %copy-done.4, bf16[512,256]{1,0:T(8,128)(2,1)S(1)} %copy-done), custom_call_target="tpu_custom_call" | custom-call | tf_op jit(solution)/shard_map/pallas_call | solution.py:58
  10.4 1.6 %collective-permute-done.refs_1_ = bf16[512,256]{1,0:T(8,128)(2,1)S(1)} collective-permute-done((bf16[512,256]{1,0:T(8,128)(2,1)}, bf16[512,256]{1,0:T(8,128)(2,1)S(1)}, u32[]{:S(2)}, u32[]{:S(2)}) %collective-permute-start) | collective-permute-done | bytes 262176 | tf_op jit(solution)/shard_map/ppermute | solution.py:271
  12.0 0.0 collective-permute-start.1
  12.0 0.5 collective-permute-start.6
  12.5 4.5 %collective-permute-done.4.refs_5_ = bf16[512,256]{1,0:T(8,128)(2,1)S(1)} collective-permute-done((bf16[512,256]{1,0:T(8,128)(2,1)}, bf16[512,256]{1,0:T(8,128)(2,1)S(1)}, u32[]{:S(2)}, u32[]{:S(2)}) %collective-permute-start.4) | collective-permute-done | bytes 262176 | tf_op jit(solution)/shard_map/ppermute | solution.py:271
  17.0 0.0 collective-permute-start.5
  17.0 0.0 collective-permute-done.2.refs_3_
  17.0 0.5 collective-permute-start.3
  17.5 0.0 collective-permute-done.1.refs_0_
  17.5 0.0 collective-permute-done.6.refs_6_
  17.5 1.0 %collective-permute-done.5.refs_4_ = bf16[512,256]{1,0:T(8,128)(2,1)S(1)} collective-permute-done((bf16[512,256]{1,0:T(8,128)(2,1)S(1)}, bf16[512,256]{1,0:T(8,128)(2,1)S(1)}, u32[]{:S(2)}, u32[]{:S(2)}) %collective-permute-start.5) | collective-permute-done | bytes 262176 | tf_op jit(solution)/shard_map/ppermute | solution.py:271
  18.6 0.4 collective-permute-done.3.refs_2_
  18.9 3.4 %shard_map.86 = (bf16[512,256]{1,0:T(8,128)(2,1)S(1)}, bf16[512,256]{1,0:T(8,128)(2,1)S(1)}, bf16[512,256]{1,0:T(8,128)(2,1)S(1)}, bf16[512,256]{1,0:T(8,128)(2,1)S(1)}) custom-call(s32[129]{0:T(256)S(1)} %get-tuple-element.35.row_of, s32[128]{0:T(128)S(1)} %get-tuple-element.36.col_of, s32[1]{0:T(128)} %bitcast.here_ref.me.mine_ref, ...), custom_call_target="tpu_custom_call" | custom-call | flops 1073741824 | bytes 6291456 | tf_op jit(solution)/shard_map/pallas_call | solution.py:144
  22.4 3.7 %collective-permute-start.10 = (bf16[512,256]{1,0:T(8,128)(2,1)S(1)}, bf16[512,256]{1,0:T(8,128)(2,1)S(1)}, u32[]{:S(2)}, u32[]{:S(2)}) collective-permute-start(bf16[512,256]{1,0:T(8,128)(2,1)S(1)} %get-tuple-element.39), channel_id=1, source_target_pairs={{0,1},{3,2},{4,5},{7,6},{8,9},{11,10},{12,13},{15,14},{16,17},{19,... | collective-permute-start | bytes 786440 | tf_op jit(solution)/shard_map/ppermute | solution.py:295
  26.1 0.7 collective-permute-start.7
  26.7 2.5 %collective-permute-start.9 = (bf16[512,256]{1,0:T(8,128)(2,1)S(1)}, bf16[512,256]{1,0:T(8,128)(2,1)S(1)}, u32[]{:S(2)}, u32[]{:S(2)}) collective-permute-start(bf16[512,256]{1,0:T(8,128)(2,1)S(1)} %get-tuple-element.41), channel_id=1, source_target_pairs={{0,1},{1,0},{2,3},{3,2},{4,5},{5,4},{6,7},{7,6},{8,9},{9,8},{10,11... | collective-permute-start | bytes 786440 | tf_op jit(solution)/shard_map/ppermute | solution.py:271
  29.3 2.8 %collective-permute-start.8 = (bf16[512,256]{1,0:T(8,128)(2,1)S(1)}, bf16[512,256]{1,0:T(8,128)(2,1)S(1)}, u32[]{:S(2)}, u32[]{:S(2)}) collective-permute-start(bf16[512,256]{1,0:T(8,128)(2,1)S(1)} %get-tuple-element.40), channel_id=1, source_target_pairs={{0,2},{3,1},{4,6},{7,5},{8,10},{11,9},{12,14},{15,13},{16,18},{19,... | collective-permute-start | bytes 786440 | tf_op jit(solution)/shard_map/ppermute | solution.py:297
  32.1 0.7 collective-permute-done.10
  32.8 0.1 add_convert_fusion.1
  32.9 1.3 %collective-permute-start.11 = (bf16[512,256]{1,0:T(8,128)(2,1)S(1)}, bf16[512,256]{1,0:T(8,128)(2,1)S(1)}, u32[]{:S(2)}, u32[]{:S(2)}) collective-permute-start(bf16[512,256]{1,0:T(8,128)(2,1)S(1)} %add_convert_fusion.1), channel_id=1, source_target_pairs={{1,3},{2,0},{5,7},{6,4},{9,11},{10,8},{13,15},{14,12},{17,19},{18,... | collective-permute-start | bytes 786440 | tf_op jit(solution)/shard_map/ppermute | solution.py:300
  34.2 4.2 %collective-permute-done.9.refs_2_ = bf16[512,256]{1,0:T(8,128)(2,1)S(1)} collective-permute-done((bf16[512,256]{1,0:T(8,128)(2,1)S(1)}, bf16[512,256]{1,0:T(8,128)(2,1)S(1)}, u32[]{:S(2)}, u32[]{:S(2)}) %collective-permute-start.9) | collective-permute-done | bytes 262176 | tf_op jit(solution)/shard_map/ppermute | solution.py:271
  38.4 0.0 collective-permute-done.7.refs_0_
  38.4 4.2 %collective-permute-done.8.refs_1_ = bf16[512,256]{1,0:T(8,128)(2,1)S(1)} collective-permute-done((bf16[512,256]{1,0:T(8,128)(2,1)S(1)}, bf16[512,256]{1,0:T(8,128)(2,1)S(1)}, u32[]{:S(2)}, u32[]{:S(2)}) %collective-permute-start.8) | collective-permute-done | bytes 262176 | tf_op jit(solution)/shard_map/ppermute | solution.py:297
  42.6 0.1 shard_map.87.refs_0_
  42.7 5.1 %collective-permute-done.11.refs_1_ = bf16[512,256]{1,0:T(8,128)(2,1)S(1)} collective-permute-done((bf16[512,256]{1,0:T(8,128)(2,1)S(1)}, bf16[512,256]{1,0:T(8,128)(2,1)S(1)}, u32[]{:S(2)}, u32[]{:S(2)}) %collective-permute-start.11) | collective-permute-done | bytes 262176 | tf_op jit(solution)/shard_map/ppermute | solution.py:300
  47.8 1.2 %shard_map.88 = (bf16[512,256]{1,0:T(8,128)(2,1)}, bf16[512,256]{1,0:T(8,128)(2,1)S(1)}, f32[512,256]{1,0:T(8,128)S(1)}, f32[512,256]{1,0:T(8,128)S(1)}) custom-call(f32[512,256]{1,0:T(8,128)S(1)} %shard_map.87.refs_0_, bf16[512,256]{1,0:T(8,128)(2,1)S(1)} %collective-permute-done.11.refs_1_, bf16[256,256]{1,0:T(8,128)(2,1)S(1)} %copy-done.2, ...), custom_call_target="tpu_custom_call" | custom-call | flops 268435456 | bytes 2621440 | tf_op jit(solution)/shard_map/pallas_call | solution.py:190
  49.0 1.5 %collective-permute-start.12 = (bf16[512,256]{1,0:T(8,128)(2,1)S(1)}, bf16[512,256]{1,0:T(8,128)(2,1)S(1)}, u32[]{:S(2)}, u32[]{:S(2)}) collective-permute-start(bf16[512,256]{1,0:T(8,128)(2,1)S(1)} %get-tuple-element.52.refs_5_), channel_id=1, source_target_pairs={{0,2},{3,1},{4,6},{7,5},{8,10},{11,9},{12,14},{15,13},{16,18},{19,... | collective-permute-start | bytes 786440 | tf_op jit(solution)/shard_map/ppermute | solution.py:307
  50.5 0.5 shard_map.89
  50.9 0.1 collective-permute-start.13
  51.0 0.1 collective-permute-start.18
  51.1 1.3 %collective-permute-start.17 = (bf16[512,256]{1,0:T(8,128)(2,1)S(1)}, bf16[512,256]{1,0:T(8,128)(2,1)S(1)}, u32[]{:S(2)}, u32[]{:S(2)}) collective-permute-start(bf16[512,256]{1,0:T(8,128)(2,1)S(1)} %get-tuple-element.52.refs_5_), channel_id=1, source_target_pairs={{1,3},{2,0},{5,7},{6,4},{9,11},{10,8},{13,15},{14,12},{17,19},{18,... | collective-permute-start | bytes 786440 | tf_op jit(solution)/shard_map/ppermute | solution.py:309
  52.4 0.7 collective-permute-start.16
  53.1 0.0 collective-permute-done.13
  53.1 3.7 %collective-permute-done.12.refs_3_ = bf16[512,256]{1,0:T(8,128)(2,1)S(1)} collective-permute-done((bf16[512,256]{1,0:T(8,128)(2,1)S(1)}, bf16[512,256]{1,0:T(8,128)(2,1)S(1)}, u32[]{:S(2)}, u32[]{:S(2)}) %collective-permute-start.12) | collective-permute-done | bytes 262176 | tf_op jit(solution)/shard_map/ppermute | solution.py:307
  56.8 1.3 %collective-permute-start.15 = (bf16[512,256]{1,0:T(8,128)(2,1)S(1)}, bf16[512,256]{1,0:T(8,128)(2,1)S(1)}, u32[]{:S(2)}, u32[]{:S(2)}) collective-permute-start(bf16[512,256]{1,0:T(8,128)(2,1)S(1)} %collective-permute-done.12.refs_3_), channel_id=1, source_target_pairs={{2,3},{1,0},{6,7},{5,4},{10,11},{9,8},{14,15},{13,12},{18,19},{17,... | collective-permute-start | bytes 786440 | tf_op jit(solution)/shard_map/ppermute | solution.py:312
  58.1 12.3 %all_gather.3 = f32[512,256]{1,0:T(8,128)} all-gather(f32[128,256]{1,0:T(8,128)S(1)} %add.16), channel_id=1, replica_groups={{0,8,16,24},{4,12,20,28},{1,9,17,25},{5,13,21,29},{2,10,18,26},{6,14,22..., dimensions={0}, use_global_device_ids=true | all-gather | bytes 655360 | tf_op jit(solution)/shard_map/all_gather | solution.py:356
  70.4 0.0 collective-permute-done.18.refs_4_
  70.4 0.0 collective-permute-done.17.refs_2_
  70.4 0.0 collective-permute-done.16.refs_1_
  70.4 0.6 collective-permute-done.15.refs_0_
  71.0 3.6 %shard_map.90 = (bf16[2048,256]{1,0:T(8,128)(2,1)S(1)}, bf16[2048,256]{1,0:T(8,128)(2,1)S(1)}) custom-call(s32[129]{0:T(256)S(1)} %get-tuple-element.35.row_of, s32[128]{0:T(128)S(1)} %get-tuple-element.36.col_of, s32[1]{0:T(128)} %bitcast.1.mine_ref.here_ref, s32[1]{0:T(128)} %bitcast.here_ref.me.mine_ref, ...), custom_call_target="tpu_custom_call" | custom-call | flops 1073741824 | bytes 5242880 | tf_op jit(solution)/shard_map/pallas_call | solution.py:144
  74.6 0.1 collective-permute-start.19
  74.7 1.1 %reduce_sum.18 = bf16[128,256]{1,0:T(8,128)(2,1)S(1)} reduce(f32[4,128,256]{2,1,0:T(8,128)} %bitcast.6, f32[]{:T(128)} %constant.10.clone.1), dimensions={0}, to_apply=%region_0.0 | reduce | flops 98304 | bytes 589828 | tf_op jit(solution)/shard_map/reduce_sum | solution.py:358
  75.7 0.7 tile.2
  76.5 4.9 %all-to-all-start = ((bf16[4,128,256]{2,1,0:T(8,128)(2,1)}), bf16[4,128,256]{2,1,0:T(8,128)(2,1)S(1)}, u32[]{:S(2)}, u32[]{:S(2)}) async-start(bf16[4,128,256]{2,1,0:T(8,128)(2,1)} %tile.2), calls=%async_computation | async-start | bytes 524288 | tf_op jit(solution)/shard_map/all_to_all | solution.py:324
  81.3 0.0 collective-permute-done.19.other_ref
  81.3 0.2 shard_map.91
  81.6 3.4 %collective-permute-start.20 = (bf16[512,256]{1,0:T(8,128)(2,1)S(1)}, bf16[512,256]{1,0:T(8,128)(2,1)S(1)}, u32[]{:S(2)}, u32[]{:S(2)}) collective-permute-start(bf16[512,256]{1,0:T(8,128)(2,1)S(1)} %get-tuple-element.55), channel_id=1, source_target_pairs={{0,24},{4,28},{8,16},{12,20},{16,8},{20,12},{24,0},{28,4},{1,25},{... | collective-permute-start | bytes 786440 | tf_op jit(solution)/shard_map/ppermute | solution.py:271
  85.0 0.0 collective-permute-start.21
  85.0 0.6 collective-permute-start.22
  85.6 5.3 %all-to-all-done = bf16[4,128,256]{2,1,0:T(8,128)(2,1)S(1)} async-done(((bf16[4,128,256]{2,1,0:T(8,128)(2,1)}), bf16[4,128,256]{2,1,0:T(8,128)(2,1)S(1)}, u32[]{:S(2)}, u32[]{:S(2)}) %all-to-all-start) | async-done | bytes 262176 | tf_op jit(solution)/shard_map/all_to_all | solution.py:324
  90.9 0.1 collective-permute-start.14
  91.0 1.2 %collective-permute-done.20 = bf16[512,256]{1,0:T(8,128)(2,1)S(1)} collective-permute-done((bf16[512,256]{1,0:T(8,128)(2,1)S(1)}, bf16[512,256]{1,0:T(8,128)(2,1)S(1)}, u32[]{:S(2)}, u32[]{:S(2)}) %collective-permute-start.20) | collective-permute-done | bytes 262176 | tf_op jit(solution)/shard_map/ppermute | solution.py:271
  92.1 4.6 %collective-permute-done.21 = bf16[512,256]{1,0:T(8,128)(2,1)S(1)} collective-permute-done((bf16[512,256]{1,0:T(8,128)(2,1)S(1)}, bf16[512,256]{1,0:T(8,128)(2,1)S(1)}, u32[]{:S(2)}, u32[]{:S(2)}) %collective-permute-start.21) | collective-permute-done | bytes 262176 | tf_op jit(solution)/shard_map/ppermute | solution.py:271
  96.8 0.1 collective-permute-done.22
  96.9 0.8 add_convert_fusion
  97.8 0.0 collective-permute-done.14.other_ref
  97.8 0.7 shard_map.92
  (9 shorter events, 0.1 us)
Async XLA Ops:
  0.6 11.3 %collective-permute-start = (bf16[512,256]{1,0:T(8,128)(2,1)}, bf16[512,256]{1,0:T(8,128)(2,1)S(1)}, u32[]{:S(2)}, u32[]{:S(2)}) collective-permute-start(bf16[512,256]{1,0:T(8,128)(2,1)} %features.1), channel_id=1, source_target_pairs={{0,24},{4,28},{8,16},{12,20},{16,8},{20,12},{24,0},{28,4},{1,25},{... | collective-permute-start | bytes 786440 | tf_op jit(solution)/shard_map/ppermute | solution.py:271
  4.6 12.4 %collective-permute-start.4 = (bf16[512,256]{1,0:T(8,128)(2,1)}, bf16[512,256]{1,0:T(8,128)(2,1)S(1)}, u32[]{:S(2)}, u32[]{:S(2)}) collective-permute-start(bf16[512,256]{1,0:T(8,128)(2,1)} %features.1), channel_id=1, source_target_pairs={{0,8},{4,12},{8,0},{12,4},{16,24},{20,28},{24,16},{28,20},{1,9},{5... | collective-permute-start | bytes 786440 | tf_op jit(solution)/shard_map/ppermute | solution.py:271
  5.1 11.9 %collective-permute-start.2 = (bf16[512,256]{1,0:T(8,128)(2,1)}, bf16[512,256]{1,0:T(8,128)(2,1)S(1)}, u32[]{:S(2)}, u32[]{:S(2)}) collective-permute-start(bf16[512,256]{1,0:T(8,128)(2,1)} %features.1), channel_id=1, source_target_pairs={{0,16},{4,20},{8,24},{12,28},{16,0},{20,4},{24,8},{28,12},{1,17},{... | collective-permute-start | bytes 786440 | tf_op jit(solution)/shard_map/ppermute | solution.py:271
  5.2 1.0 copy-start
  6.2 0.7 copy-start.3
  6.9 0.7 copy-start.4
  12.0 5.6 %collective-permute-start.1 = (bf16[512,256]{1,0:T(8,128)(2,1)S(1)}, bf16[512,256]{1,0:T(8,128)(2,1)S(1)}, u32[]{:S(2)}, u32[]{:S(2)}) collective-permute-start(bf16[512,256]{1,0:T(8,128)(2,1)S(1)} %collective-permute-done.refs_1_), channel_id=1, source_target_pairs={{0,4},{4,0},{8,12},{12,8},{16,20},{20,16},{24,28},{28,24},{1,5},{5... | collective-permute-start | bytes 786440 | tf_op jit(solution)/shard_map/ppermute | solution.py:271
  12.0 5.6 %collective-permute-start.6 = (bf16[512,256]{1,0:T(8,128)(2,1)S(1)}, bf16[512,256]{1,0:T(8,128)(2,1)S(1)}, u32[]{:S(2)}, u32[]{:S(2)}) collective-permute-start(bf16[512,256]{1,0:T(8,128)(2,1)S(1)} %get-tuple-element.38.refs_7_), channel_id=1, source_target_pairs={{0,4},{4,0},{8,12},{12,8},{16,20},{20,16},{24,28},{28,24},{1,5},{5... | collective-permute-start | bytes 786440 | tf_op jit(solution)/shard_map/ppermute | solution.py:271
  17.0 1.5 %collective-permute-start.5 = (bf16[512,256]{1,0:T(8,128)(2,1)S(1)}, bf16[512,256]{1,0:T(8,128)(2,1)S(1)}, u32[]{:S(2)}, u32[]{:S(2)}) collective-permute-start(bf16[512,256]{1,0:T(8,128)(2,1)S(1)} %collective-permute-done.4.refs_5_), channel_id=1, source_target_pairs={{0,4},{4,0},{8,12},{12,8},{16,20},{20,16},{24,28},{28,24},{1,5},{5... | collective-permute-start | bytes 786440 | tf_op jit(solution)/shard_map/ppermute | solution.py:271
  17.0 1.9 %collective-permute-start.3 = (bf16[512,256]{1,0:T(8,128)(2,1)S(1)}, bf16[512,256]{1,0:T(8,128)(2,1)S(1)}, u32[]{:S(2)}, u32[]{:S(2)}) collective-permute-start(bf16[512,256]{1,0:T(8,128)(2,1)S(1)} %collective-permute-done.2.refs_3_), channel_id=1, source_target_pairs={{0,4},{4,0},{8,12},{12,8},{16,20},{20,16},{24,28},{28,24},{1,5},{5... | collective-permute-start | bytes 786440 | tf_op jit(solution)/shard_map/ppermute | solution.py:271
  18.9 28.9 %copy-start.1 = (bf16[512,256]{1,0:T(8,128)(2,1)S(1)}, bf16[512,256]{1,0:T(8,128)(2,1)}, u32[]{:S(2)}) copy-start(bf16[512,256]{1,0:T(8,128)(2,1)} %refs_3_.1) | copy-start | bytes 786436
  18.9 28.9 %copy-start.2 = (bf16[256,256]{1,0:T(8,128)(2,1)S(1)}, bf16[256,256]{1,0:T(8,128)(2,1)}, u32[]{:S(2)}) copy-start(bf16[256,256]{1,0:T(8,128)(2,1)} %refs_2_.1) | copy-start | bytes 393220
  22.4 10.4 %collective-permute-start.10 = (bf16[512,256]{1,0:T(8,128)(2,1)S(1)}, bf16[512,256]{1,0:T(8,128)(2,1)S(1)}, u32[]{:S(2)}, u32[]{:S(2)}) collective-permute-start(bf16[512,256]{1,0:T(8,128)(2,1)S(1)} %get-tuple-element.39), channel_id=1, source_target_pairs={{0,1},{3,2},{4,5},{7,6},{8,9},{11,10},{12,13},{15,14},{16,17},{19,... | collective-permute-start | bytes 786440 | tf_op jit(solution)/shard_map/ppermute | solution.py:295
  26.1 12.3 %collective-permute-start.7 = (bf16[512,256]{1,0:T(8,128)(2,1)S(1)}, bf16[512,256]{1,0:T(8,128)(2,1)S(1)}, u32[]{:S(2)}, u32[]{:S(2)}) collective-permute-start(bf16[512,256]{1,0:T(8,128)(2,1)S(1)} %get-tuple-element.39), channel_id=1, source_target_pairs={{1,2},{2,1},{5,6},{6,5},{9,10},{10,9},{13,14},{14,13},{17,18},{18,... | collective-permute-start | bytes 786440 | tf_op jit(solution)/shard_map/ppermute | solution.py:296
  26.7 11.7 %collective-permute-start.9 = (bf16[512,256]{1,0:T(8,128)(2,1)S(1)}, bf16[512,256]{1,0:T(8,128)(2,1)S(1)}, u32[]{:S(2)}, u32[]{:S(2)}) collective-permute-start(bf16[512,256]{1,0:T(8,128)(2,1)S(1)} %get-tuple-element.41), channel_id=1, source_target_pairs={{0,1},{1,0},{2,3},{3,2},{4,5},{5,4},{6,7},{7,6},{8,9},{9,8},{10,11... | collective-permute-start | bytes 786440 | tf_op jit(solution)/shard_map/ppermute | solution.py:271
  29.3 13.3 %collective-permute-start.8 = (bf16[512,256]{1,0:T(8,128)(2,1)S(1)}, bf16[512,256]{1,0:T(8,128)(2,1)S(1)}, u32[]{:S(2)}, u32[]{:S(2)}) collective-permute-start(bf16[512,256]{1,0:T(8,128)(2,1)S(1)} %get-tuple-element.40), channel_id=1, source_target_pairs={{0,2},{3,1},{4,6},{7,5},{8,10},{11,9},{12,14},{15,13},{16,18},{19,... | collective-permute-start | bytes 786440 | tf_op jit(solution)/shard_map/ppermute | solution.py:297
  32.9 14.9 %collective-permute-start.11 = (bf16[512,256]{1,0:T(8,128)(2,1)S(1)}, bf16[512,256]{1,0:T(8,128)(2,1)S(1)}, u32[]{:S(2)}, u32[]{:S(2)}) collective-permute-start(bf16[512,256]{1,0:T(8,128)(2,1)S(1)} %add_convert_fusion.1), channel_id=1, source_target_pairs={{1,3},{2,0},{5,7},{6,4},{9,11},{10,8},{13,15},{14,12},{17,19},{18,... | collective-permute-start | bytes 786440 | tf_op jit(solution)/shard_map/ppermute | solution.py:300
  49.0 7.8 %collective-permute-start.12 = (bf16[512,256]{1,0:T(8,128)(2,1)S(1)}, bf16[512,256]{1,0:T(8,128)(2,1)S(1)}, u32[]{:S(2)}, u32[]{:S(2)}) collective-permute-start(bf16[512,256]{1,0:T(8,128)(2,1)S(1)} %get-tuple-element.52.refs_5_), channel_id=1, source_target_pairs={{0,2},{3,1},{4,6},{7,5},{8,10},{11,9},{12,14},{15,13},{16,18},{19,... | collective-permute-start | bytes 786440 | tf_op jit(solution)/shard_map/ppermute | solution.py:307
  50.9 2.1 %collective-permute-start.13 = (f32[128,256]{1,0:T(8,128)S(1)}, f32[128,256]{1,0:T(8,128)S(1)}, u32[]{:S(2)}, u32[]{:S(2)}) collective-permute-start(f32[128,256]{1,0:T(8,128)S(1)} %get-tuple-element.48), channel_id=1, source_target_pairs={{0,4},{4,0},{8,12},{12,8},{16,20},{20,16},{24,28},{28,24},{1,5},{5... | collective-permute-start | bytes 393224 | tf_op jit(solution)/shard_map/ppermute | solution.py:271
  51.0 19.4 %collective-permute-start.18 = (bf16[512,256]{1,0:T(8,128)(2,1)S(1)}, bf16[512,256]{1,0:T(8,128)(2,1)S(1)}, u32[]{:S(2)}, u32[]{:S(2)}) collective-permute-start(bf16[512,256]{1,0:T(8,128)(2,1)S(1)} %get-tuple-element.52.refs_5_), channel_id=1, source_target_pairs={{0,1},{1,0},{2,3},{3,2},{4,5},{5,4},{6,7},{7,6},{8,9},{9,8},{10,11... | collective-permute-start | bytes 786440 | tf_op jit(solution)/shard_map/ppermute | solution.py:271
  51.1 19.3 %collective-permute-start.17 = (bf16[512,256]{1,0:T(8,128)(2,1)S(1)}, bf16[512,256]{1,0:T(8,128)(2,1)S(1)}, u32[]{:S(2)}, u32[]{:S(2)}) collective-permute-start(bf16[512,256]{1,0:T(8,128)(2,1)S(1)} %get-tuple-element.52.refs_5_), channel_id=1, source_target_pairs={{1,3},{2,0},{5,7},{6,4},{9,11},{10,8},{13,15},{14,12},{17,19},{18,... | collective-permute-start | bytes 786440 | tf_op jit(solution)/shard_map/ppermute | solution.py:309
  52.4 18.0 %collective-permute-start.16 = (bf16[512,256]{1,0:T(8,128)(2,1)S(1)}, bf16[512,256]{1,0:T(8,128)(2,1)S(1)}, u32[]{:S(2)}, u32[]{:S(2)}) collective-permute-start(bf16[512,256]{1,0:T(8,128)(2,1)S(1)} %get-tuple-element.52.refs_5_), channel_id=1, source_target_pairs={{1,2},{2,1},{5,6},{6,5},{9,10},{10,9},{13,14},{14,13},{17,18},{18,... | collective-permute-start | bytes 786440 | tf_op jit(solution)/shard_map/ppermute | solution.py:308
  56.8 14.1 %collective-permute-start.15 = (bf16[512,256]{1,0:T(8,128)(2,1)S(1)}, bf16[512,256]{1,0:T(8,128)(2,1)S(1)}, u32[]{:S(2)}, u32[]{:S(2)}) collective-permute-start(bf16[512,256]{1,0:T(8,128)(2,1)S(1)} %collective-permute-done.12.refs_3_), channel_id=1, source_target_pairs={{2,3},{1,0},{6,7},{5,4},{10,11},{9,8},{14,15},{13,12},{18,19},{17,... | collective-permute-start | bytes 786440 | tf_op jit(solution)/shard_map/ppermute | solution.py:312
  74.6 6.8 %collective-permute-start.19 = (bf16[2048,256]{1,0:T(8,128)(2,1)S(1)}, bf16[2048,256]{1,0:T(8,128)(2,1)S(1)}, u32[]{:S(2)}, u32[]{:S(2)}) collective-permute-start(bf16[2048,256]{1,0:T(8,128)(2,1)S(1)} %get-tuple-element.54), channel_id=1, source_target_pairs={{0,4},{4,0},{8,12},{12,8},{16,20},{20,16},{24,28},{28,24},{1,5},{5... | collective-permute-start | bytes 3145736 | tf_op jit(solution)/shard_map/ppermute | solution.py:271
  76.5 14.4 %all-to-all-start = ((bf16[4,128,256]{2,1,0:T(8,128)(2,1)}), bf16[4,128,256]{2,1,0:T(8,128)(2,1)S(1)}, u32[]{:S(2)}, u32[]{:S(2)}) async-start(bf16[4,128,256]{2,1,0:T(8,128)(2,1)} %tile.2), calls=%async_computation | async-start | bytes 524288 | tf_op jit(solution)/shard_map/all_to_all | solution.py:324
  81.6 10.6 %collective-permute-start.20 = (bf16[512,256]{1,0:T(8,128)(2,1)S(1)}, bf16[512,256]{1,0:T(8,128)(2,1)S(1)}, u32[]{:S(2)}, u32[]{:S(2)}) collective-permute-start(bf16[512,256]{1,0:T(8,128)(2,1)S(1)} %get-tuple-element.55), channel_id=1, source_target_pairs={{0,24},{4,28},{8,16},{12,20},{16,8},{20,12},{24,0},{28,4},{1,25},{... | collective-permute-start | bytes 786440 | tf_op jit(solution)/shard_map/ppermute | solution.py:271
  85.0 11.8 %collective-permute-start.21 = (bf16[512,256]{1,0:T(8,128)(2,1)S(1)}, bf16[512,256]{1,0:T(8,128)(2,1)S(1)}, u32[]{:S(2)}, u32[]{:S(2)}) collective-permute-start(bf16[512,256]{1,0:T(8,128)(2,1)S(1)} %get-tuple-element.56), channel_id=1, source_target_pairs={{0,16},{4,20},{8,24},{12,28},{16,0},{20,4},{24,8},{28,12},{1,17},{... | collective-permute-start | bytes 786440 | tf_op jit(solution)/shard_map/ppermute | solution.py:271
  85.0 12.0 %collective-permute-start.22 = (bf16[512,256]{1,0:T(8,128)(2,1)S(1)}, bf16[512,256]{1,0:T(8,128)(2,1)S(1)}, u32[]{:S(2)}, u32[]{:S(2)}) collective-permute-start(bf16[512,256]{1,0:T(8,128)(2,1)S(1)} %get-tuple-element.57), channel_id=1, source_target_pairs={{0,8},{4,12},{8,0},{12,4},{16,24},{20,28},{24,16},{28,20},{1,9},{5... | collective-permute-start | bytes 786440 | tf_op jit(solution)/shard_map/ppermute | solution.py:271
  90.9 6.9 %collective-permute-start.14 = (f32[128,256]{1,0:T(8,128)S(1)}, f32[128,256]{1,0:T(8,128)S(1)}, u32[]{:S(2)}, u32[]{:S(2)}) collective-permute-start(f32[128,256]{1,0:T(8,128)S(1)} %convert_reduce_fusion.own_ref), channel_id=1, source_target_pairs={{0,4},{4,0},{8,12},{12,8},{16,20},{20,16},{24,28},{28,24},{1,5},{5... | collective-permute-start | bytes 393224 | tf_op jit(solution)/shard_map/ppermute | solution.py:271

commit v11 on v10

--- a/solution.py
+++ b/solution.py
@@ -271,6 +271,28 @@
     return lax.ppermute(x, axis, [(i, i ^ m) for i in range(n)])
 
 
+def copies_kernel(parts, copies, in_ref, out_ref):
+    rows = in_ref.shape[0] // parts
+    result = in_ref[:rows, :]
+    for p in range(1, parts):
+        result += in_ref[p * rows : (p + 1) * rows, :]
+    result = result.astype(BF16)
+    for c in range(copies):
+        out_ref[c * rows : (c + 1) * rows, :] = result
+
+
+def sum_copies(stacked, parts, copies):
+    rows, width = stacked.shape
+    return pl.pallas_call(
+        functools.partial(copies_kernel, parts, copies),
+        out_shape=jax.ShapeDtypeStruct((rows // parts * copies, width), BF16),
+        in_specs=[VMEM],
+        out_specs=VMEM,
+        compiler_params=params(32),
+        cost_estimate=cost(0, 0),
+    )(stacked)
+
+
 def add_kernel(*refs):
     result = refs[0][...].astype(F32)
     for ref in refs[1:-1]:
@@ -354,8 +376,8 @@
     back_panel, term = gather_parts(back, n_col, term)
     cores = [list(range(0, n_row, 2)), list(range(1, n_row, 2))]
     half = lax.all_gather(term, "row", axis=0, axis_index_groups=cores, tiled=True)
-    half, back_panel[0] = lax.optimization_barrier((half, back_panel[0]))
-    half = jnp.sum(half.reshape(n_row // 2, -1, half.shape[1]), axis=0)
+    copies = sum_copies(half, n_row // 2, n_col)
+    copies, back_panel[0] = lax.optimization_barrier((copies, back_panel[0]))
 
     even = list(range(0, n_row, 2))
     pair = [even, [m + 1 for m in even]]
@@ -366,8 +388,8 @@
     feature_grad = total_of(
         [swap(s, "row", n_row, m) for s, m in zip(sums[:0:-1], even[:0:-1])] + [sums[0]]
     ).astype(BF16)
-    halves = exchange(jnp.tile(half.astype(BF16), (n_col, 1)), "col")
-    half = jnp.sum(halves.reshape(n_col, -1, half.shape[1]).astype(F32), axis=0)
+    halves = exchange(copies, "col")
+    half = jnp.sum(halves.reshape(n_col, -1, halves.shape[1]).astype(F32), axis=0)
     other = swap(half, "row", n_row, 1)
     other, feature_grad = lax.optimization_barrier((other, feature_grad))
     weight_grad = assemble(half, other, me_row, n_row // 2)

time: 98.9 us -> 96.9 us (0.980)
  Pallas kernels: 12.6 us -> 14.5 us
  blocking collectives: 12.3 us -> 10.5 us
  starting transfers between devices: 30.5 us -> 28.8 us
  waiting for transfers between devices: 37.2 us -> 38.8 us
  other arithmetic: 2.04 us -> 0.96 us
    all_gather x1, blocking collectives: 12.3 us -> 10.5 us  [on_device(): lax.all_gather(term, 'row', axis=0, axis_index_groups=cores, tiled=True)]
    reduce_sum x2 -> x1, other arithmetic: 1.12 us -> 0.03 us  [on_device(): jnp.sum(halves.reshape(n_col, -1, halves.shape[1]).astype(F32), axis=0)]
    pallas_call x2, Pallas kernels: 7.03 us -> 8.11 us  [sparse_product(): pl.pallas_call(functools.partial(sparse_kernel, counts, outs, backward),...]
    ppermute x1, waiting for transfers between devices: 4.17 us -> 5.2 us  [exchange_terms(): inward = lax.ppermute(terms[2], 'col', [(0, 2), (3, 1)])]
  transfers between devices with their start and end apart: 24 -> 24, of which waited for: 14 -> 13; matrix products, arithmetic and copies ran while one was open for 3% -> 1% of each run, Pallas kernels for 4% -> 5%
where the time goes in v11:
time: 96.9 us; the launch traced here: 96.7 us
  waiting for transfers between devices  38.8 us (40%)
  starting transfers between devices  28.8 us (30%)
  Pallas kernels  14.5 us (15%)
  blocking collectives  10.5 us (11%)
  local copies, waits for them, and re-layouts  2.3 us (2%)
    ppermute x15, waiting for transfers between devices, swap(): return lax.ppermute(x, axis, [(i, i ^ m) for i in range(n)])  17.3 us
    ppermute x15, starting transfers between devices, swap(): return lax.ppermute(x, axis, [(i, i ^ m) for i in range(n)])  12.3 us
    all_gather x1, blocking collectives, on_device(): lax.all_gather(term, 'row', axis=0, axis_index_groups=cores, tiled=True)  10.5 us
    pallas_call x2, Pallas kernels, sparse_product(): pl.pallas_call(functools.partial(sparse_kernel, counts, outs, backward),...  8.11 us
    all_to_all x1, waiting for transfers between devices, exchange(): return lax.all_to_all(x, axis, 0, 0, tiled=True)  5.72 us
    ppermute x1, waiting for transfers between devices, exchange_terms(): inward = lax.ppermute(terms[2], 'col', [(0, 2), (3, 1)])  5.2 us
    ppermute x1, waiting for transfers between devices, exchange_terms(): outward = lax.ppermute(relay, 'col', [(1, 3), (2, 0)])  4.94 us
    all_to_all x1, starting transfers between devices, exchange(): return lax.all_to_all(x, axis, 0, 0, tiled=True)  4.18 us
  transfers between devices with their start and end apart: 24, of which 13 were waited for; matrix products, arithmetic and copies ran while one was open for 1% of the time, Pallas kernels for 5%

profile of v11, /device:TPU:0, one launch (start us, length us, event | category | flops | bytes accessed | tf_op | source)
XLA Modules:
  0.0 96.7 jit_solution(17728159418777504519)
XLA Ops:
  0.6 4.0 %collective-permute-start = (bf16[512,256]{1,0:T(8,128)(2,1)}, bf16[512,256]{1,0:T(8,128)(2,1)S(1)}, u32[]{:S(2)}, u32[]{:S(2)}) collective-permute-start(bf16[512,256]{1,0:T(8,128)(2,1)} %features.1), channel_id=1, source_target_pairs={{0,24},{4,28},{8,16},{12,20},{16,8},{20,12},{24,0},{28,4},{1,25},{... | collective-permute-start | bytes 786440 | tf_op jit(solution)/shard_map/ppermute | solution.py:271
  4.6 0.5 collective-permute-start.4
  5.1 0.1 collective-permute-start.2
  5.2 1.0 %copy-done = bf16[512,256]{1,0:T(8,128)(2,1)S(1)} copy-done((bf16[512,256]{1,0:T(8,128)(2,1)S(1)}, bf16[512,256]{1,0:T(8,128)(2,1)}, u32[]{:S(2)}) %copy-start) | copy-done | bytes 262168
  6.2 0.7 copy-done.3
  6.9 0.7 copy-done.4
  7.5 2.9 %shard_map.85 = (s32[129]{0:T(256)S(1)}, s32[128]{0:T(128)S(1)}, bf16[512,256]{1,0:T(8,128)(2,1)S(1)}) custom-call(s32[1,1,17]{2,1,0:T(1,128)S(1)} %copy-done.3, s32[1,1,128]{2,1,0:T(1,128)S(1)} %copy-done.4, bf16[512,256]{1,0:T(8,128)(2,1)S(1)} %copy-done), custom_call_target="tpu_custom_call" | custom-call | tf_op jit(solution)/shard_map/pallas_call | solution.py:58
  10.4 1.6 %collective-permute-done.refs_1_ = bf16[512,256]{1,0:T(8,128)(2,1)S(1)} collective-permute-done((bf16[512,256]{1,0:T(8,128)(2,1)}, bf16[512,256]{1,0:T(8,128)(2,1)S(1)}, u32[]{:S(2)}, u32[]{:S(2)}) %collective-permute-start) | collective-permute-done | bytes 262176 | tf_op jit(solution)/shard_map/ppermute | solution.py:271
  12.0 0.0 collective-permute-start.1
  12.0 0.5 collective-permute-start.6
  12.5 4.5 %collective-permute-done.4.refs_5_ = bf16[512,256]{1,0:T(8,128)(2,1)S(1)} collective-permute-done((bf16[512,256]{1,0:T(8,128)(2,1)}, bf16[512,256]{1,0:T(8,128)(2,1)S(1)}, u32[]{:S(2)}, u32[]{:S(2)}) %collective-permute-start.4) | collective-permute-done | bytes 262176 | tf_op jit(solution)/shard_map/ppermute | solution.py:271
  17.0 0.0 collective-permute-start.5
  17.0 0.0 collective-permute-done.2.refs_3_
  17.0 0.5 collective-permute-start.3
  17.5 0.0 collective-permute-done.1.refs_0_
  17.5 0.0 collective-permute-done.6.refs_6_
  17.5 1.0 %collective-permute-done.5.refs_4_ = bf16[512,256]{1,0:T(8,128)(2,1)S(1)} collective-permute-done((bf16[512,256]{1,0:T(8,128)(2,1)S(1)}, bf16[512,256]{1,0:T(8,128)(2,1)S(1)}, u32[]{:S(2)}, u32[]{:S(2)}) %collective-permute-start.5) | collective-permute-done | bytes 262176 | tf_op jit(solution)/shard_map/ppermute | solution.py:271
  18.6 0.4 collective-permute-done.3.refs_2_
  18.9 3.9 %shard_map.86 = (bf16[512,256]{1,0:T(8,128)(2,1)S(1)}, bf16[512,256]{1,0:T(8,128)(2,1)S(1)}, bf16[512,256]{1,0:T(8,128)(2,1)S(1)}, bf16[512,256]{1,0:T(8,128)(2,1)S(1)}) custom-call(s32[129]{0:T(256)S(1)} %get-tuple-element.35.row_of, s32[128]{0:T(128)S(1)} %get-tuple-element.36.col_of, s32[1]{0:T(128)} %bitcast.here_ref.me.mine_ref, ...), custom_call_target="tpu_custom_call" | custom-call | flops 1073741824 | bytes 6291456 | tf_op jit(solution)/shard_map/pallas_call | solution.py:144
  22.9 2.9 %collective-permute-start.10 = (bf16[512,256]{1,0:T(8,128)(2,1)S(1)}, bf16[512,256]{1,0:T(8,128)(2,1)S(1)}, u32[]{:S(2)}, u32[]{:S(2)}) collective-permute-start(bf16[512,256]{1,0:T(8,128)(2,1)S(1)} %get-tuple-element.39), channel_id=1, source_target_pairs={{0,1},{3,2},{4,5},{7,6},{8,9},{11,10},{12,13},{15,14},{16,17},{19,... | collective-permute-start | bytes 786440 | tf_op jit(solution)/shard_map/ppermute | solution.py:317
  25.8 0.7 collective-permute-start.7
  26.4 2.8 %collective-permute-start.9 = (bf16[512,256]{1,0:T(8,128)(2,1)S(1)}, bf16[512,256]{1,0:T(8,128)(2,1)S(1)}, u32[]{:S(2)}, u32[]{:S(2)}) collective-permute-start(bf16[512,256]{1,0:T(8,128)(2,1)S(1)} %get-tuple-element.41), channel_id=1, source_target_pairs={{0,1},{1,0},{2,3},{3,2},{4,5},{5,4},{6,7},{7,6},{8,9},{9,8},{10,11... | collective-permute-start | bytes 786440 | tf_op jit(solution)/shard_map/ppermute | solution.py:271
  29.3 2.8 %collective-permute-start.8 = (bf16[512,256]{1,0:T(8,128)(2,1)S(1)}, bf16[512,256]{1,0:T(8,128)(2,1)S(1)}, u32[]{:S(2)}, u32[]{:S(2)}) collective-permute-start(bf16[512,256]{1,0:T(8,128)(2,1)S(1)} %get-tuple-element.40), channel_id=1, source_target_pairs={{0,2},{3,1},{4,6},{7,5},{8,10},{11,9},{12,14},{15,13},{16,18},{19,... | collective-permute-start | bytes 786440 | tf_op jit(solution)/shard_map/ppermute | solution.py:319
  32.1 0.3 collective-permute-done.10
  32.4 0.1 add_convert_fusion.1
  32.4 1.3 %collective-permute-start.11 = (bf16[512,256]{1,0:T(8,128)(2,1)S(1)}, bf16[512,256]{1,0:T(8,128)(2,1)S(1)}, u32[]{:S(2)}, u32[]{:S(2)}) collective-permute-start(bf16[512,256]{1,0:T(8,128)(2,1)S(1)} %add_convert_fusion.1), channel_id=1, source_target_pairs={{1,3},{2,0},{5,7},{6,4},{9,11},{10,8},{13,15},{14,12},{17,19},{18,... | collective-permute-start | bytes 786440 | tf_op jit(solution)/shard_map/ppermute | solution.py:322
  33.7 4.2 %collective-permute-done.9.refs_2_ = bf16[512,256]{1,0:T(8,128)(2,1)S(1)} collective-permute-done((bf16[512,256]{1,0:T(8,128)(2,1)S(1)}, bf16[512,256]{1,0:T(8,128)(2,1)S(1)}, u32[]{:S(2)}, u32[]{:S(2)}) %collective-permute-start.9) | collective-permute-done | bytes 262176 | tf_op jit(solution)/shard_map/ppermute | solution.py:271
  38.0 0.0 collective-permute-done.7.refs_0_
  38.0 5.2 %collective-permute-done.8.refs_1_ = bf16[512,256]{1,0:T(8,128)(2,1)S(1)} collective-permute-done((bf16[512,256]{1,0:T(8,128)(2,1)S(1)}, bf16[512,256]{1,0:T(8,128)(2,1)S(1)}, u32[]{:S(2)}, u32[]{:S(2)}) %collective-permute-start.8) | collective-permute-done | bytes 262176 | tf_op jit(solution)/shard_map/ppermute | solution.py:319
  43.2 0.1 shard_map.87.refs_0_
  43.3 4.9 %collective-permute-done.11.refs_1_ = bf16[512,256]{1,0:T(8,128)(2,1)S(1)} collective-permute-done((bf16[512,256]{1,0:T(8,128)(2,1)S(1)}, bf16[512,256]{1,0:T(8,128)(2,1)S(1)}, u32[]{:S(2)}, u32[]{:S(2)}) %collective-permute-start.11) | collective-permute-done | bytes 262176 | tf_op jit(solution)/shard_map/ppermute | solution.py:322
  48.2 0.0 copy-done.1
  48.2 1.2 %shard_map.88 = (bf16[512,256]{1,0:T(8,128)(2,1)}, bf16[512,256]{1,0:T(8,128)(2,1)S(1)}, f32[512,256]{1,0:T(8,128)S(1)}, f32[512,256]{1,0:T(8,128)S(1)}) custom-call(f32[512,256]{1,0:T(8,128)S(1)} %shard_map.87.refs_0_, bf16[512,256]{1,0:T(8,128)(2,1)S(1)} %collective-permute-done.11.refs_1_, bf16[256,256]{1,0:T(8,128)(2,1)S(1)} %copy-done.2, ...), custom_call_target="tpu_custom_call" | custom-call | flops 268435456 | bytes 2621440 | tf_op jit(solution)/shard_map/pallas_call | solution.py:190
  49.5 1.5 %collective-permute-start.12 = (bf16[512,256]{1,0:T(8,128)(2,1)S(1)}, bf16[512,256]{1,0:T(8,128)(2,1)S(1)}, u32[]{:S(2)}, u32[]{:S(2)}) collective-permute-start(bf16[512,256]{1,0:T(8,128)(2,1)S(1)} %get-tuple-element.52.refs_5_), channel_id=1, source_target_pairs={{0,2},{3,1},{4,6},{7,5},{8,10},{11,9},{12,14},{15,13},{16,18},{19,... | collective-permute-start | bytes 786440 | tf_op jit(solution)/shard_map/ppermute | solution.py:329
  50.9 0.5 shard_map.89
  51.4 0.1 collective-permute-start.13
  51.5 0.1 collective-permute-start.18
  51.5 1.3 %collective-permute-start.17 = (bf16[512,256]{1,0:T(8,128)(2,1)S(1)}, bf16[512,256]{1,0:T(8,128)(2,1)S(1)}, u32[]{:S(2)}, u32[]{:S(2)}) collective-permute-start(bf16[512,256]{1,0:T(8,128)(2,1)S(1)} %get-tuple-element.52.refs_5_), channel_id=1, source_target_pairs={{1,3},{2,0},{5,7},{6,4},{9,11},{10,8},{13,15},{14,12},{17,19},{18,... | collective-permute-start | bytes 786440 | tf_op jit(solution)/shard_map/ppermute | solution.py:331
  52.8 0.7 collective-permute-start.16
  53.5 0.0 collective-permute-done.13
  53.6 4.1 %collective-permute-done.12.refs_3_ = bf16[512,256]{1,0:T(8,128)(2,1)S(1)} collective-permute-done((bf16[512,256]{1,0:T(8,128)(2,1)S(1)}, bf16[512,256]{1,0:T(8,128)(2,1)S(1)}, u32[]{:S(2)}, u32[]{:S(2)}) %collective-permute-start.12) | collective-permute-done | bytes 262176 | tf_op jit(solution)/shard_map/ppermute | solution.py:329
  57.6 1.3 %collective-permute-start.15 = (bf16[512,256]{1,0:T(8,128)(2,1)S(1)}, bf16[512,256]{1,0:T(8,128)(2,1)S(1)}, u32[]{:S(2)}, u32[]{:S(2)}) collective-permute-start(bf16[512,256]{1,0:T(8,128)(2,1)S(1)} %collective-permute-done.12.refs_3_), channel_id=1, source_target_pairs={{2,3},{1,0},{6,7},{5,4},{10,11},{9,8},{14,15},{13,12},{18,19},{17,... | collective-permute-start | bytes 786440 | tf_op jit(solution)/shard_map/ppermute | solution.py:334
  58.9 10.5 %all_gather.3.in_ref = f32[512,256]{1,0:T(8,128)S(1)} all-gather(f32[128,256]{1,0:T(8,128)S(1)} %add.16), channel_id=1, replica_groups={{0,8,16,24},{4,12,20,28},{1,9,17,25},{5,13,21,29},{2,10,18,26},{6,14,22..., dimensions={0}, use_global_device_ids=true | all-gather | bytes 655360 | tf_op jit(solution)/shard_map/all_gather | solution.py:378
  69.4 0.7 shard_map.90
  70.2 0.0 collective-permute-done.18.refs_4_
  70.2 0.0 collective-permute-done.17.refs_2_
  70.2 0.0 collective-permute-done.16.refs_1_
  70.2 1.2 %collective-permute-done.15.refs_0_ = bf16[512,256]{1,0:T(8,128)(2,1)S(1)} collective-permute-done((bf16[512,256]{1,0:T(8,128)(2,1)S(1)}, bf16[512,256]{1,0:T(8,128)(2,1)S(1)}, u32[]{:S(2)}, u32[]{:S(2)}) %collective-permute-start.15) | collective-permute-done | bytes 262176 | tf_op jit(solution)/shard_map/ppermute | solution.py:334
  71.4 4.2 %shard_map.91 = (bf16[2048,256]{1,0:T(8,128)(2,1)S(1)}, bf16[2048,256]{1,0:T(8,128)(2,1)S(1)}) custom-call(s32[129]{0:T(256)S(1)} %get-tuple-element.35.row_of, s32[128]{0:T(128)S(1)} %get-tuple-element.36.col_of, s32[1]{0:T(128)} %bitcast.1.mine_ref.here_ref, s32[1]{0:T(128)} %bitcast.here_ref.me.mine_ref, ...), custom_call_target="tpu_custom_call" | custom-call | flops 1073741824 | bytes 5242880 | tf_op jit(solution)/shard_map/pallas_call | solution.py:144
  75.6 0.1 collective-permute-start.19
  75.7 4.2 %all-to-all-start = ((bf16[4,128,256]{2,1,0:T(8,128)(2,1)}), bf16[4,128,256]{2,1,0:T(8,128)(2,1)S(1)}, u32[]{:S(2)}, u32[]{:S(2)}) async-start(bf16[4,128,256]{2,1,0:T(8,128)(2,1)} %bitcast.3), calls=%async_computation | async-start | bytes 524288 | tf_op jit(solution)/shard_map/all_to_all | solution.py:346
  79.9 0.0 collective-permute-done.19.other_ref
  79.9 0.2 shard_map.92
  80.1 1.8 %collective-permute-start.20 = (bf16[512,256]{1,0:T(8,128)(2,1)S(1)}, bf16[512,256]{1,0:T(8,128)(2,1)S(1)}, u32[]{:S(2)}, u32[]{:S(2)}) collective-permute-start(bf16[512,256]{1,0:T(8,128)(2,1)S(1)} %get-tuple-element.55), channel_id=1, source_target_pairs={{0,24},{4,28},{8,16},{12,20},{16,8},{20,12},{24,0},{28,4},{1,25},{... | collective-permute-start | bytes 786440 | tf_op jit(solution)/shard_map/ppermute | solution.py:271
  82.0 0.9 collective-permute-start.21
  82.9 0.8 collective-permute-start.22
  83.7 5.7 %all-to-all-done = bf16[4,128,256]{2,1,0:T(8,128)(2,1)S(1)} async-done(((bf16[4,128,256]{2,1,0:T(8,128)(2,1)}), bf16[4,128,256]{2,1,0:T(8,128)(2,1)S(1)}, u32[]{:S(2)}, u32[]{:S(2)}) %all-to-all-start) | async-done | bytes 262176 | tf_op jit(solution)/shard_map/all_to_all | solution.py:346
  89.4 0.1 collective-permute-start.14
  89.5 0.8 collective-permute-done.20
  90.3 4.8 %collective-permute-done.21 = bf16[512,256]{1,0:T(8,128)(2,1)S(1)} collective-permute-done((bf16[512,256]{1,0:T(8,128)(2,1)S(1)}, bf16[512,256]{1,0:T(8,128)(2,1)S(1)}, u32[]{:S(2)}, u32[]{:S(2)}) %collective-permute-start.21) | collective-permute-done | bytes 262176 | tf_op jit(solution)/shard_map/ppermute | solution.py:271
  95.1 0.0 collective-permute-done.22
  95.1 0.8 add_convert_fusion
  96.0 0.0 collective-permute-done.14.other_ref
  96.0 0.7 shard_map.93
  (8 shorter events, 0.1 us)
Async XLA Ops:
  0.6 11.3 %collective-permute-start = (bf16[512,256]{1,0:T(8,128)(2,1)}, bf16[512,256]{1,0:T(8,128)(2,1)S(1)}, u32[]{:S(2)}, u32[]{:S(2)}) collective-permute-start(bf16[512,256]{1,0:T(8,128)(2,1)} %features.1), channel_id=1, source_target_pairs={{0,24},{4,28},{8,16},{12,20},{16,8},{20,12},{24,0},{28,4},{1,25},{... | collective-permute-start | bytes 786440 | tf_op jit(solution)/shard_map/ppermute | solution.py:271
  4.6 12.4 %collective-permute-start.4 = (bf16[512,256]{1,0:T(8,128)(2,1)}, bf16[512,256]{1,0:T(8,128)(2,1)S(1)}, u32[]{:S(2)}, u32[]{:S(2)}) collective-permute-start(bf16[512,256]{1,0:T(8,128)(2,1)} %features.1), channel_id=1, source_target_pairs={{0,8},{4,12},{8,0},{12,4},{16,24},{20,28},{24,16},{28,20},{1,9},{5... | collective-permute-start | bytes 786440 | tf_op jit(solution)/shard_map/ppermute | solution.py:271
  5.1 11.9 %collective-permute-start.2 = (bf16[512,256]{1,0:T(8,128)(2,1)}, bf16[512,256]{1,0:T(8,128)(2,1)S(1)}, u32[]{:S(2)}, u32[]{:S(2)}) collective-permute-start(bf16[512,256]{1,0:T(8,128)(2,1)} %features.1), channel_id=1, source_target_pairs={{0,16},{4,20},{8,24},{12,28},{16,0},{20,4},{24,8},{28,12},{1,17},{... | collective-permute-start | bytes 786440 | tf_op jit(solution)/shard_map/ppermute | solution.py:271
  5.2 1.0 %copy-start = (bf16[512,256]{1,0:T(8,128)(2,1)S(1)}, bf16[512,256]{1,0:T(8,128)(2,1)}, u32[]{:S(2)}) copy-start(bf16[512,256]{1,0:T(8,128)(2,1)} %features.1) | copy-start | bytes 786436
  6.2 0.7 copy-start.3
  6.9 0.7 copy-start.4
  12.0 5.6 %collective-permute-start.1 = (bf16[512,256]{1,0:T(8,128)(2,1)S(1)}, bf16[512,256]{1,0:T(8,128)(2,1)S(1)}, u32[]{:S(2)}, u32[]{:S(2)}) collective-permute-start(bf16[512,256]{1,0:T(8,128)(2,1)S(1)} %collective-permute-done.refs_1_), channel_id=1, source_target_pairs={{0,4},{4,0},{8,12},{12,8},{16,20},{20,16},{24,28},{28,24},{1,5},{5... | collective-permute-start | bytes 786440 | tf_op jit(solution)/shard_map/ppermute | solution.py:271
  12.0 5.6 %collective-permute-start.6 = (bf16[512,256]{1,0:T(8,128)(2,1)S(1)}, bf16[512,256]{1,0:T(8,128)(2,1)S(1)}, u32[]{:S(2)}, u32[]{:S(2)}) collective-permute-start(bf16[512,256]{1,0:T(8,128)(2,1)S(1)} %get-tuple-element.38.refs_7_), channel_id=1, source_target_pairs={{0,4},{4,0},{8,12},{12,8},{16,20},{20,16},{24,28},{28,24},{1,5},{5... | collective-permute-start | bytes 786440 | tf_op jit(solution)/shard_map/ppermute | solution.py:271
  17.0 1.5 %collective-permute-start.5 = (bf16[512,256]{1,0:T(8,128)(2,1)S(1)}, bf16[512,256]{1,0:T(8,128)(2,1)S(1)}, u32[]{:S(2)}, u32[]{:S(2)}) collective-permute-start(bf16[512,256]{1,0:T(8,128)(2,1)S(1)} %collective-permute-done.4.refs_5_), channel_id=1, source_target_pairs={{0,4},{4,0},{8,12},{12,8},{16,20},{20,16},{24,28},{28,24},{1,5},{5... | collective-permute-start | bytes 786440 | tf_op jit(solution)/shard_map/ppermute | solution.py:271
  17.0 1.9 %collective-permute-start.3 = (bf16[512,256]{1,0:T(8,128)(2,1)S(1)}, bf16[512,256]{1,0:T(8,128)(2,1)S(1)}, u32[]{:S(2)}, u32[]{:S(2)}) collective-permute-start(bf16[512,256]{1,0:T(8,128)(2,1)S(1)} %collective-permute-done.2.refs_3_), channel_id=1, source_target_pairs={{0,4},{4,0},{8,12},{12,8},{16,20},{20,16},{24,28},{28,24},{1,5},{5... | collective-permute-start | bytes 786440 | tf_op jit(solution)/shard_map/ppermute | solution.py:271
  18.9 29.3 %copy-start.1 = (bf16[512,256]{1,0:T(8,128)(2,1)S(1)}, bf16[512,256]{1,0:T(8,128)(2,1)}, u32[]{:S(2)}) copy-start(bf16[512,256]{1,0:T(8,128)(2,1)} %refs_3_.1) | copy-start | bytes 786436
  18.9 29.3 %copy-start.2 = (bf16[256,256]{1,0:T(8,128)(2,1)S(1)}, bf16[256,256]{1,0:T(8,128)(2,1)}, u32[]{:S(2)}) copy-start(bf16[256,256]{1,0:T(8,128)(2,1)} %refs_2_.1) | copy-start | bytes 393220
  22.9 9.5 %collective-permute-start.10 = (bf16[512,256]{1,0:T(8,128)(2,1)S(1)}, bf16[512,256]{1,0:T(8,128)(2,1)S(1)}, u32[]{:S(2)}, u32[]{:S(2)}) collective-permute-start(bf16[512,256]{1,0:T(8,128)(2,1)S(1)} %get-tuple-element.39), channel_id=1, source_target_pairs={{0,1},{3,2},{4,5},{7,6},{8,9},{11,10},{12,13},{15,14},{16,17},{19,... | collective-permute-start | bytes 786440 | tf_op jit(solution)/shard_map/ppermute | solution.py:317
  25.8 12.2 %collective-permute-start.7 = (bf16[512,256]{1,0:T(8,128)(2,1)S(1)}, bf16[512,256]{1,0:T(8,128)(2,1)S(1)}, u32[]{:S(2)}, u32[]{:S(2)}) collective-permute-start(bf16[512,256]{1,0:T(8,128)(2,1)S(1)} %get-tuple-element.39), channel_id=1, source_target_pairs={{1,2},{2,1},{5,6},{6,5},{9,10},{10,9},{13,14},{14,13},{17,18},{18,... | collective-permute-start | bytes 786440 | tf_op jit(solution)/shard_map/ppermute | solution.py:318
  26.4 11.5 %collective-permute-start.9 = (bf16[512,256]{1,0:T(8,128)(2,1)S(1)}, bf16[512,256]{1,0:T(8,128)(2,1)S(1)}, u32[]{:S(2)}, u32[]{:S(2)}) collective-permute-start(bf16[512,256]{1,0:T(8,128)(2,1)S(1)} %get-tuple-element.41), channel_id=1, source_target_pairs={{0,1},{1,0},{2,3},{3,2},{4,5},{5,4},{6,7},{7,6},{8,9},{9,8},{10,11... | collective-permute-start | bytes 786440 | tf_op jit(solution)/shard_map/ppermute | solution.py:271
  29.3 13.9 %collective-permute-start.8 = (bf16[512,256]{1,0:T(8,128)(2,1)S(1)}, bf16[512,256]{1,0:T(8,128)(2,1)S(1)}, u32[]{:S(2)}, u32[]{:S(2)}) collective-permute-start(bf16[512,256]{1,0:T(8,128)(2,1)S(1)} %get-tuple-element.40), channel_id=1, source_target_pairs={{0,2},{3,1},{4,6},{7,5},{8,10},{11,9},{12,14},{15,13},{16,18},{19,... | collective-permute-start | bytes 786440 | tf_op jit(solution)/shard_map/ppermute | solution.py:319
  32.4 15.8 %collective-permute-start.11 = (bf16[512,256]{1,0:T(8,128)(2,1)S(1)}, bf16[512,256]{1,0:T(8,128)(2,1)S(1)}, u32[]{:S(2)}, u32[]{:S(2)}) collective-permute-start(bf16[512,256]{1,0:T(8,128)(2,1)S(1)} %add_convert_fusion.1), channel_id=1, source_target_pairs={{1,3},{2,0},{5,7},{6,4},{9,11},{10,8},{13,15},{14,12},{17,19},{18,... | collective-permute-start | bytes 786440 | tf_op jit(solution)/shard_map/ppermute | solution.py:322
  49.5 8.2 %collective-permute-start.12 = (bf16[512,256]{1,0:T(8,128)(2,1)S(1)}, bf16[512,256]{1,0:T(8,128)(2,1)S(1)}, u32[]{:S(2)}, u32[]{:S(2)}) collective-permute-start(bf16[512,256]{1,0:T(8,128)(2,1)S(1)} %get-tuple-element.52.refs_5_), channel_id=1, source_target_pairs={{0,2},{3,1},{4,6},{7,5},{8,10},{11,9},{12,14},{15,13},{16,18},{19,... | collective-permute-start | bytes 786440 | tf_op jit(solution)/shard_map/ppermute | solution.py:329
  51.4 2.1 %collective-permute-start.13 = (f32[128,256]{1,0:T(8,128)S(1)}, f32[128,256]{1,0:T(8,128)S(1)}, u32[]{:S(2)}, u32[]{:S(2)}) collective-permute-start(f32[128,256]{1,0:T(8,128)S(1)} %get-tuple-element.48), channel_id=1, source_target_pairs={{0,4},{4,0},{8,12},{12,8},{16,20},{20,16},{24,28},{28,24},{1,5},{5... | collective-permute-start | bytes 393224 | tf_op jit(solution)/shard_map/ppermute | solution.py:271
  51.5 18.7 %collective-permute-start.18 = (bf16[512,256]{1,0:T(8,128)(2,1)S(1)}, bf16[512,256]{1,0:T(8,128)(2,1)S(1)}, u32[]{:S(2)}, u32[]{:S(2)}) collective-permute-start(bf16[512,256]{1,0:T(8,128)(2,1)S(1)} %get-tuple-element.52.refs_5_), channel_id=1, source_target_pairs={{0,1},{1,0},{2,3},{3,2},{4,5},{5,4},{6,7},{7,6},{8,9},{9,8},{10,11... | collective-permute-start | bytes 786440 | tf_op jit(solution)/shard_map/ppermute | solution.py:271
  51.5 18.6 %collective-permute-start.17 = (bf16[512,256]{1,0:T(8,128)(2,1)S(1)}, bf16[512,256]{1,0:T(8,128)(2,1)S(1)}, u32[]{:S(2)}, u32[]{:S(2)}) collective-permute-start(bf16[512,256]{1,0:T(8,128)(2,1)S(1)} %get-tuple-element.52.refs_5_), channel_id=1, source_target_pairs={{1,3},{2,0},{5,7},{6,4},{9,11},{10,8},{13,15},{14,12},{17,19},{18,... | collective-permute-start | bytes 786440 | tf_op jit(solution)/shard_map/ppermute | solution.py:331
  52.8 17.3 %collective-permute-start.16 = (bf16[512,256]{1,0:T(8,128)(2,1)S(1)}, bf16[512,256]{1,0:T(8,128)(2,1)S(1)}, u32[]{:S(2)}, u32[]{:S(2)}) collective-permute-start(bf16[512,256]{1,0:T(8,128)(2,1)S(1)} %get-tuple-element.52.refs_5_), channel_id=1, source_target_pairs={{1,2},{2,1},{5,6},{6,5},{9,10},{10,9},{13,14},{14,13},{17,18},{18,... | collective-permute-start | bytes 786440 | tf_op jit(solution)/shard_map/ppermute | solution.py:330
  57.6 13.8 %collective-permute-start.15 = (bf16[512,256]{1,0:T(8,128)(2,1)S(1)}, bf16[512,256]{1,0:T(8,128)(2,1)S(1)}, u32[]{:S(2)}, u32[]{:S(2)}) collective-permute-start(bf16[512,256]{1,0:T(8,128)(2,1)S(1)} %collective-permute-done.12.refs_3_), channel_id=1, source_target_pairs={{2,3},{1,0},{6,7},{5,4},{10,11},{9,8},{14,15},{13,12},{18,19},{17,... | collective-permute-start | bytes 786440 | tf_op jit(solution)/shard_map/ppermute | solution.py:334
  75.6 4.3 %collective-permute-start.19 = (bf16[2048,256]{1,0:T(8,128)(2,1)S(1)}, bf16[2048,256]{1,0:T(8,128)(2,1)S(1)}, u32[]{:S(2)}, u32[]{:S(2)}) collective-permute-start(bf16[2048,256]{1,0:T(8,128)(2,1)S(1)} %get-tuple-element.54), channel_id=1, source_target_pairs={{0,4},{4,0},{8,12},{12,8},{16,20},{20,16},{24,28},{28,24},{1,5},{5... | collective-permute-start | bytes 3145736 | tf_op jit(solution)/shard_map/ppermute | solution.py:271
  75.7 13.7 %all-to-all-start = ((bf16[4,128,256]{2,1,0:T(8,128)(2,1)}), bf16[4,128,256]{2,1,0:T(8,128)(2,1)S(1)}, u32[]{:S(2)}, u32[]{:S(2)}) async-start(bf16[4,128,256]{2,1,0:T(8,128)(2,1)} %bitcast.3), calls=%async_computation | async-start | bytes 524288 | tf_op jit(solution)/shard_map/all_to_all | solution.py:346
  80.1 10.2 %collective-permute-start.20 = (bf16[512,256]{1,0:T(8,128)(2,1)S(1)}, bf16[512,256]{1,0:T(8,128)(2,1)S(1)}, u32[]{:S(2)}, u32[]{:S(2)}) collective-permute-start(bf16[512,256]{1,0:T(8,128)(2,1)S(1)} %get-tuple-element.55), channel_id=1, source_target_pairs={{0,24},{4,28},{8,16},{12,20},{16,8},{20,12},{24,0},{28,4},{1,25},{... | collective-permute-start | bytes 786440 | tf_op jit(solution)/shard_map/ppermute | solution.py:271
  82.0 13.2 %collective-permute-start.21 = (bf16[512,256]{1,0:T(8,128)(2,1)S(1)}, bf16[512,256]{1,0:T(8,128)(2,1)S(1)}, u32[]{:S(2)}, u32[]{:S(2)}) collective-permute-start(bf16[512,256]{1,0:T(8,128)(2,1)S(1)} %get-tuple-element.56), channel_id=1, source_target_pairs={{0,16},{4,20},{8,24},{12,28},{16,0},{20,4},{24,8},{28,12},{1,17},{... | collective-permute-start | bytes 786440 | tf_op jit(solution)/shard_map/ppermute | solution.py:271
  82.9 12.2 %collective-permute-start.22 = (bf16[512,256]{1,0:T(8,128)(2,1)S(1)}, bf16[512,256]{1,0:T(8,128)(2,1)S(1)}, u32[]{:S(2)}, u32[]{:S(2)}) collective-permute-start(bf16[512,256]{1,0:T(8,128)(2,1)S(1)} %get-tuple-element.57), channel_id=1, source_target_pairs={{0,8},{4,12},{8,0},{12,4},{16,24},{20,28},{24,16},{28,20},{1,9},{5... | collective-permute-start | bytes 786440 | tf_op jit(solution)/shard_map/ppermute | solution.py:271
  89.4 6.5 %collective-permute-start.14 = (f32[128,256]{1,0:T(8,128)S(1)}, f32[128,256]{1,0:T(8,128)S(1)}, u32[]{:S(2)}, u32[]{:S(2)}) collective-permute-start(f32[128,256]{1,0:T(8,128)S(1)} %convert_reduce_fusion.own_ref), channel_id=1, source_target_pairs={{0,4},{4,0},{8,12},{12,8},{16,20},{20,16},{24,28},{28,24},{1,5},{5... | collective-permute-start | bytes 393224 | tf_op jit(solution)/shard_map/ppermute | solution.py:271

commit v12 on v11

--- a/solution.py
+++ b/solution.py
@@ -391,7 +391,6 @@
     halves = exchange(copies, "col")
     half = jnp.sum(halves.reshape(n_col, -1, halves.shape[1]).astype(F32), axis=0)
     other = swap(half, "row", n_row, 1)
-    other, feature_grad = lax.optimization_barrier((other, feature_grad))
     weight_grad = assemble(half, other, me_row, n_row // 2)
     return (activations, feature_grad, weight_grad)
 

time: 96.9 us -> 95.9 us (0.990)
    ppermute x1, waiting for transfers between devices: 5.2 us -> 2.91 us  [exchange_terms(): inward = lax.ppermute(terms[2], 'col', [(0, 2), (3, 1)])]
    ppermute x15, starting transfers between devices: 12.3 us -> 10.1 us  [swap(): return lax.ppermute(x, axis, [(i, i ^ m) for i in range(n)])]
    ppermute x1, waiting for transfers between devices: 0.29 us -> 1.97 us  [exchange_terms(): far = lax.ppermute(terms[3], 'col', [(0, 1), (3, 2)])]
    ppermute x1, starting transfers between devices: 2.9 us -> 4.45 us  [exchange_terms(): far = lax.ppermute(terms[3], 'col', [(0, 1), (3, 2)])]
  transfers between devices with their start and end apart: 24 -> 24, of which waited for: 13 -> 13; matrix products, arithmetic and copies ran while one was open for 1% -> 0% of each run, Pallas kernels for 5% -> 5%
where the time goes in v12:
time: 95.9 us; the launch traced here: 95.6 us
  waiting for transfers between devices  38.8 us (40%)
  starting transfers between devices  28.1 us (29%)
  Pallas kernels  14.5 us (15%)
  blocking collectives  10.1 us (11%)
  local copies, waits for them, and re-layouts  2.3 us (2%)
  other arithmetic  0.96 us (1%)
    ppermute x15, waiting for transfers between devices, swap(): return lax.ppermute(x, axis, [(i, i ^ m) for i in range(n)])  16.7 us
    ppermute x15, starting transfers between devices, swap(): return lax.ppermute(x, axis, [(i, i ^ m) for i in range(n)])  10.1 us
    all_gather x1, blocking collectives, on_device(): lax.all_gather(term, 'row', axis=0, axis_index_groups=cores, tiled=True)  10.1 us
    pallas_call x2, Pallas kernels, sparse_product(): pl.pallas_call(functools.partial(sparse_kernel, counts, outs, backward),...  8.12 us
    all_to_all x1, waiting for transfers between devices, exchange(): return lax.all_to_all(x, axis, 0, 0, tiled=True)  5.95 us
    ppermute x1, waiting for transfers between devices, exchange_terms(): outward = lax.ppermute(relay, 'col', [(1, 3), (2, 0)])  5.61 us
    ppermute x1, starting transfers between devices, exchange_terms(): far = lax.ppermute(terms[3], 'col', [(0, 1), (3, 2)])  4.45 us
    ppermute x1, waiting for transfers between devices, gather_parts(): inward = lax.ppermute(own, 'col', [(0, 2), (3, 1)])  3.72 us
  transfers between devices with their start and end apart: 24, of which 13 were waited for; matrix products, arithmetic and copies ran while one was open for 0% of the time, Pallas kernels for 5%

profile of v12, /device:TPU:0, one launch (start us, length us, event | category | flops | bytes accessed | tf_op | source)
XLA Modules:
  0.0 95.6 jit_solution(5256518792762155233)
XLA Ops:
  0.6 4.0 %collective-permute-start = (bf16[512,256]{1,0:T(8,128)(2,1)}, bf16[512,256]{1,0:T(8,128)(2,1)S(1)}, u32[]{:S(2)}, u32[]{:S(2)}) collective-permute-start(bf16[512,256]{1,0:T(8,128)(2,1)} %features.1), channel_id=1, source_target_pairs={{0,24},{4,28},{8,16},{12,20},{16,8},{20,12},{24,0},{28,4},{1,25},{... | collective-permute-start | bytes 786440 | tf_op jit(solution)/shard_map/ppermute | solution.py:271
  4.6 0.5 collective-permute-start.4
  5.1 0.1 collective-permute-start.2
  5.2 1.0 %copy-done = bf16[512,256]{1,0:T(8,128)(2,1)S(1)} copy-done((bf16[512,256]{1,0:T(8,128)(2,1)S(1)}, bf16[512,256]{1,0:T(8,128)(2,1)}, u32[]{:S(2)}) %copy-start) | copy-done | bytes 262168
  6.2 0.7 copy-done.3
  6.9 0.7 copy-done.4
  7.5 2.9 %shard_map.85 = (s32[129]{0:T(256)S(1)}, s32[128]{0:T(128)S(1)}, bf16[512,256]{1,0:T(8,128)(2,1)S(1)}) custom-call(s32[1,1,17]{2,1,0:T(1,128)S(1)} %copy-done.3, s32[1,1,128]{2,1,0:T(1,128)S(1)} %copy-done.4, bf16[512,256]{1,0:T(8,128)(2,1)S(1)} %copy-done), custom_call_target="tpu_custom_call" | custom-call | tf_op jit(solution)/shard_map/pallas_call | solution.py:58
  10.4 1.6 %collective-permute-done.refs_1_ = bf16[512,256]{1,0:T(8,128)(2,1)S(1)} collective-permute-done((bf16[512,256]{1,0:T(8,128)(2,1)}, bf16[512,256]{1,0:T(8,128)(2,1)S(1)}, u32[]{:S(2)}, u32[]{:S(2)}) %collective-permute-start) | collective-permute-done | bytes 262176 | tf_op jit(solution)/shard_map/ppermute | solution.py:271
  12.0 0.0 collective-permute-start.1
  12.0 0.5 collective-permute-start.6
  12.5 4.5 %collective-permute-done.4.refs_5_ = bf16[512,256]{1,0:T(8,128)(2,1)S(1)} collective-permute-done((bf16[512,256]{1,0:T(8,128)(2,1)}, bf16[512,256]{1,0:T(8,128)(2,1)S(1)}, u32[]{:S(2)}, u32[]{:S(2)}) %collective-permute-start.4) | collective-permute-done | bytes 262176 | tf_op jit(solution)/shard_map/ppermute | solution.py:271
  17.0 0.0 collective-permute-start.5
  17.0 0.0 collective-permute-done.2.refs_3_
  17.0 0.5 collective-permute-start.3
  17.5 0.0 collective-permute-done.1.refs_0_
  17.5 0.0 collective-permute-done.6.refs_6_
  17.5 1.0 %collective-permute-done.5.refs_4_ = bf16[512,256]{1,0:T(8,128)(2,1)S(1)} collective-permute-done((bf16[512,256]{1,0:T(8,128)(2,1)S(1)}, bf16[512,256]{1,0:T(8,128)(2,1)S(1)}, u32[]{:S(2)}, u32[]{:S(2)}) %collective-permute-start.5) | collective-permute-done | bytes 262176 | tf_op jit(solution)/shard_map/ppermute | solution.py:271
  18.6 0.4 collective-permute-done.3.refs_2_
  18.9 3.9 %shard_map.86 = (bf16[512,256]{1,0:T(8,128)(2,1)S(1)}, bf16[512,256]{1,0:T(8,128)(2,1)S(1)}, bf16[512,256]{1,0:T(8,128)(2,1)S(1)}, bf16[512,256]{1,0:T(8,128)(2,1)S(1)}) custom-call(s32[129]{0:T(256)S(1)} %get-tuple-element.33.row_of, s32[128]{0:T(128)S(1)} %get-tuple-element.34.col_of, s32[1]{0:T(128)} %bitcast.here_ref.me.mine_ref, ...), custom_call_target="tpu_custom_call" | custom-call | flops 1073741824 | bytes 6291456 | tf_op jit(solution)/shard_map/pallas_call | solution.py:144
  22.9 4.5 %collective-permute-start.10 = (bf16[512,256]{1,0:T(8,128)(2,1)S(1)}, bf16[512,256]{1,0:T(8,128)(2,1)S(1)}, u32[]{:S(2)}, u32[]{:S(2)}) collective-permute-start(bf16[512,256]{1,0:T(8,128)(2,1)S(1)} %get-tuple-element.37), channel_id=1, source_target_pairs={{0,1},{3,2},{4,5},{7,6},{8,9},{11,10},{12,13},{15,14},{16,17},{19,... | collective-permute-start | bytes 786440 | tf_op jit(solution)/shard_map/ppermute | solution.py:317
  27.3 0.7 collective-permute-start.7
  28.0 0.7 collective-permute-start.9
  28.7 3.4 %collective-permute-start.8 = (bf16[512,256]{1,0:T(8,128)(2,1)S(1)}, bf16[512,256]{1,0:T(8,128)(2,1)S(1)}, u32[]{:S(2)}, u32[]{:S(2)}) collective-permute-start(bf16[512,256]{1,0:T(8,128)(2,1)S(1)} %get-tuple-element.38), channel_id=1, source_target_pairs={{0,2},{3,1},{4,6},{7,5},{8,10},{11,9},{12,14},{15,13},{16,18},{19,... | collective-permute-start | bytes 786440 | tf_op jit(solution)/shard_map/ppermute | solution.py:319
  32.1 2.0 %collective-permute-done.10 = bf16[512,256]{1,0:T(8,128)(2,1)S(1)} collective-permute-done((bf16[512,256]{1,0:T(8,128)(2,1)S(1)}, bf16[512,256]{1,0:T(8,128)(2,1)S(1)}, u32[]{:S(2)}, u32[]{:S(2)}) %collective-permute-start.10) | collective-permute-done | bytes 262176 | tf_op jit(solution)/shard_map/ppermute | solution.py:317
  34.0 0.1 add_convert_fusion.1
  34.1 1.3 %collective-permute-start.11 = (bf16[512,256]{1,0:T(8,128)(2,1)S(1)}, bf16[512,256]{1,0:T(8,128)(2,1)S(1)}, u32[]{:S(2)}, u32[]{:S(2)}) collective-permute-start(bf16[512,256]{1,0:T(8,128)(2,1)S(1)} %add_convert_fusion.1), channel_id=1, source_target_pairs={{1,3},{2,0},{5,7},{6,4},{9,11},{10,8},{13,15},{14,12},{17,19},{18,... | collective-permute-start | bytes 786440 | tf_op jit(solution)/shard_map/ppermute | solution.py:322
  35.4 4.2 %collective-permute-done.9.refs_2_ = bf16[512,256]{1,0:T(8,128)(2,1)S(1)} collective-permute-done((bf16[512,256]{1,0:T(8,128)(2,1)S(1)}, bf16[512,256]{1,0:T(8,128)(2,1)S(1)}, u32[]{:S(2)}, u32[]{:S(2)}) %collective-permute-start.9) | collective-permute-done | bytes 262176 | tf_op jit(solution)/shard_map/ppermute | solution.py:271
  39.7 0.0 collective-permute-done.7.refs_0_
  39.7 2.9 %collective-permute-done.8.refs_1_ = bf16[512,256]{1,0:T(8,128)(2,1)S(1)} collective-permute-done((bf16[512,256]{1,0:T(8,128)(2,1)S(1)}, bf16[512,256]{1,0:T(8,128)(2,1)S(1)}, u32[]{:S(2)}, u32[]{:S(2)}) %collective-permute-start.8) | collective-permute-done | bytes 262176 | tf_op jit(solution)/shard_map/ppermute | solution.py:319
  42.6 0.1 shard_map.87.refs_0_
  42.7 5.6 %collective-permute-done.11.refs_1_ = bf16[512,256]{1,0:T(8,128)(2,1)S(1)} collective-permute-done((bf16[512,256]{1,0:T(8,128)(2,1)S(1)}, bf16[512,256]{1,0:T(8,128)(2,1)S(1)}, u32[]{:S(2)}, u32[]{:S(2)}) %collective-permute-start.11) | collective-permute-done | bytes 262176 | tf_op jit(solution)/shard_map/ppermute | solution.py:322
  48.3 0.0 copy-done.1
  48.3 1.2 %shard_map.88 = (bf16[512,256]{1,0:T(8,128)(2,1)}, bf16[512,256]{1,0:T(8,128)(2,1)S(1)}, f32[512,256]{1,0:T(8,128)S(1)}, f32[512,256]{1,0:T(8,128)S(1)}) custom-call(f32[512,256]{1,0:T(8,128)S(1)} %shard_map.87.refs_0_, bf16[512,256]{1,0:T(8,128)(2,1)S(1)} %collective-permute-done.11.refs_1_, bf16[256,256]{1,0:T(8,128)(2,1)S(1)} %copy-done.2, ...), custom_call_target="tpu_custom_call" | custom-call | flops 268435456 | bytes 2621440 | tf_op jit(solution)/shard_map/pallas_call | solution.py:190
  49.5 1.5 %collective-permute-start.12 = (bf16[512,256]{1,0:T(8,128)(2,1)S(1)}, bf16[512,256]{1,0:T(8,128)(2,1)S(1)}, u32[]{:S(2)}, u32[]{:S(2)}) collective-permute-start(bf16[512,256]{1,0:T(8,128)(2,1)S(1)} %get-tuple-element.49.refs_5_), channel_id=1, source_target_pairs={{0,2},{3,1},{4,6},{7,5},{8,10},{11,9},{12,14},{15,13},{16,18},{19,... | collective-permute-start | bytes 786440 | tf_op jit(solution)/shard_map/ppermute | solution.py:329
  51.0 0.5 shard_map.89
  51.4 0.1 collective-permute-start.13
  51.5 0.1 collective-permute-start.17
  51.6 1.3 %collective-permute-start.16 = (bf16[512,256]{1,0:T(8,128)(2,1)S(1)}, bf16[512,256]{1,0:T(8,128)(2,1)S(1)}, u32[]{:S(2)}, u32[]{:S(2)}) collective-permute-start(bf16[512,256]{1,0:T(8,128)(2,1)S(1)} %get-tuple-element.49.refs_5_), channel_id=1, source_target_pairs={{1,3},{2,0},{5,7},{6,4},{9,11},{10,8},{13,15},{14,12},{17,19},{18,... | collective-permute-start | bytes 786440 | tf_op jit(solution)/shard_map/ppermute | solution.py:331
  52.9 0.7 collective-permute-start.15
  53.6 0.0 collective-permute-done.13
  53.6 3.7 %collective-permute-done.12.refs_3_ = bf16[512,256]{1,0:T(8,128)(2,1)S(1)} collective-permute-done((bf16[512,256]{1,0:T(8,128)(2,1)S(1)}, bf16[512,256]{1,0:T(8,128)(2,1)S(1)}, u32[]{:S(2)}, u32[]{:S(2)}) %collective-permute-start.12) | collective-permute-done | bytes 262176 | tf_op jit(solution)/shard_map/ppermute | solution.py:329
  57.3 1.3 %collective-permute-start.14 = (bf16[512,256]{1,0:T(8,128)(2,1)S(1)}, bf16[512,256]{1,0:T(8,128)(2,1)S(1)}, u32[]{:S(2)}, u32[]{:S(2)}) collective-permute-start(bf16[512,256]{1,0:T(8,128)(2,1)S(1)} %collective-permute-done.12.refs_3_), channel_id=1, source_target_pairs={{2,3},{1,0},{6,7},{5,4},{10,11},{9,8},{14,15},{13,12},{18,19},{17,... | collective-permute-start | bytes 786440 | tf_op jit(solution)/shard_map/ppermute | solution.py:334
  58.6 10.1 %all_gather.3.in_ref = f32[512,256]{1,0:T(8,128)S(1)} all-gather(f32[128,256]{1,0:T(8,128)S(1)} %add.16), channel_id=1, replica_groups={{0,8,16,24},{4,12,20,28},{1,9,17,25},{5,13,21,29},{2,10,18,26},{6,14,22..., dimensions={0}, use_global_device_ids=true | all-gather | bytes 655360 | tf_op jit(solution)/shard_map/all_gather | solution.py:378
  68.7 0.7 shard_map.90
  69.5 0.0 collective-permute-done.17.refs_4_
  69.5 0.0 collective-permute-done.16.refs_2_
  69.5 0.0 collective-permute-done.15.refs_1_
  69.5 2.0 %collective-permute-done.14.refs_0_ = bf16[512,256]{1,0:T(8,128)(2,1)S(1)} collective-permute-done((bf16[512,256]{1,0:T(8,128)(2,1)S(1)}, bf16[512,256]{1,0:T(8,128)(2,1)S(1)}, u32[]{:S(2)}, u32[]{:S(2)}) %collective-permute-start.14) | collective-permute-done | bytes 262176 | tf_op jit(solution)/shard_map/ppermute | solution.py:334
  71.5 4.2 %shard_map.91 = (bf16[2048,256]{1,0:T(8,128)(2,1)S(1)}, bf16[2048,256]{1,0:T(8,128)(2,1)S(1)}) custom-call(s32[129]{0:T(256)S(1)} %get-tuple-element.33.row_of, s32[128]{0:T(128)S(1)} %get-tuple-element.34.col_of, s32[1]{0:T(128)} %bitcast.1.mine_ref.here_ref, s32[1]{0:T(128)} %bitcast.here_ref.me.mine_ref, ...), custom_call_target="tpu_custom_call" | custom-call | flops 1073741824 | bytes 5242880 | tf_op jit(solution)/shard_map/pallas_call | solution.py:144
  75.7 0.1 collective-permute-start.18
  75.8 3.4 %all-to-all-start = ((bf16[4,128,256]{2,1,0:T(8,128)(2,1)}), bf16[4,128,256]{2,1,0:T(8,128)(2,1)S(1)}, u32[]{:S(2)}, u32[]{:S(2)}) async-start(bf16[4,128,256]{2,1,0:T(8,128)(2,1)} %bitcast.3), calls=%async_computation | async-start | bytes 524288 | tf_op jit(solution)/shard_map/all_to_all | solution.py:346
  79.2 0.0 collective-permute-done.18.other_ref
  79.2 0.2 shard_map.92
  79.5 1.6 %collective-permute-start.19 = (bf16[512,256]{1,0:T(8,128)(2,1)S(1)}, bf16[512,256]{1,0:T(8,128)(2,1)S(1)}, u32[]{:S(2)}, u32[]{:S(2)}) collective-permute-start(bf16[512,256]{1,0:T(8,128)(2,1)S(1)} %get-tuple-element.52), channel_id=1, source_target_pairs={{0,24},{4,28},{8,16},{12,20},{16,8},{20,12},{24,0},{28,4},{1,25},{... | collective-permute-start | bytes 786440 | tf_op jit(solution)/shard_map/ppermute | solution.py:271
  81.0 0.7 collective-permute-start.20
  81.8 1.3 %collective-permute-start.21 = (bf16[512,256]{1,0:T(8,128)(2,1)S(1)}, bf16[512,256]{1,0:T(8,128)(2,1)S(1)}, u32[]{:S(2)}, u32[]{:S(2)}) collective-permute-start(bf16[512,256]{1,0:T(8,128)(2,1)S(1)} %get-tuple-element.54), channel_id=1, source_target_pairs={{0,8},{4,12},{8,0},{12,4},{16,24},{20,28},{24,16},{28,20},{1,9},{5... | collective-permute-start | bytes 786440 | tf_op jit(solution)/shard_map/ppermute | solution.py:271
  83.0 6.0 %all-to-all-done = bf16[4,128,256]{2,1,0:T(8,128)(2,1)S(1)} async-done(((bf16[4,128,256]{2,1,0:T(8,128)(2,1)}), bf16[4,128,256]{2,1,0:T(8,128)(2,1)S(1)}, u32[]{:S(2)}, u32[]{:S(2)}) %all-to-all-start) | async-done | bytes 262176 | tf_op jit(solution)/shard_map/all_to_all | solution.py:346
  89.0 0.1 collective-permute-start.22
  89.1 1.3 %collective-permute-done.22.other_ref = f32[128,256]{1,0:T(8,128)S(1)} collective-permute-done((f32[128,256]{1,0:T(8,128)S(1)}, f32[128,256]{1,0:T(8,128)S(1)}, u32[]{:S(2)}, u32[]{:S(2)}) %collective-permute-start.22) | collective-permute-done | bytes 131104 | tf_op jit(solution)/shard_map/ppermute | solution.py:271
  90.4 0.7 shard_map.93
  91.1 0.0 collective-permute-done.19
  91.1 3.6 %collective-permute-done.20 = bf16[512,256]{1,0:T(8,128)(2,1)S(1)} collective-permute-done((bf16[512,256]{1,0:T(8,128)(2,1)S(1)}, bf16[512,256]{1,0:T(8,128)(2,1)S(1)}, u32[]{:S(2)}, u32[]{:S(2)}) %collective-permute-start.20) | collective-permute-done | bytes 262176 | tf_op jit(solution)/shard_map/ppermute | solution.py:271
  94.7 0.0 collective-permute-done.21
  94.7 0.8 add_convert_fusion
  (8 shorter events, 0.1 us)
Async XLA Ops:
  0.6 11.3 %collective-permute-start = (bf16[512,256]{1,0:T(8,128)(2,1)}, bf16[512,256]{1,0:T(8,128)(2,1)S(1)}, u32[]{:S(2)}, u32[]{:S(2)}) collective-permute-start(bf16[512,256]{1,0:T(8,128)(2,1)} %features.1), channel_id=1, source_target_pairs={{0,24},{4,28},{8,16},{12,20},{16,8},{20,12},{24,0},{28,4},{1,25},{... | collective-permute-start | bytes 786440 | tf_op jit(solution)/shard_map/ppermute | solution.py:271
  4.6 12.4 %collective-permute-start.4 = (bf16[512,256]{1,0:T(8,128)(2,1)}, bf16[512,256]{1,0:T(8,128)(2,1)S(1)}, u32[]{:S(2)}, u32[]{:S(2)}) collective-permute-start(bf16[512,256]{1,0:T(8,128)(2,1)} %features.1), channel_id=1, source_target_pairs={{0,8},{4,12},{8,0},{12,4},{16,24},{20,28},{24,16},{28,20},{1,9},{5... | collective-permute-start | bytes 786440 | tf_op jit(solution)/shard_map/ppermute | solution.py:271
  5.1 11.9 %collective-permute-start.2 = (bf16[512,256]{1,0:T(8,128)(2,1)}, bf16[512,256]{1,0:T(8,128)(2,1)S(1)}, u32[]{:S(2)}, u32[]{:S(2)}) collective-permute-start(bf16[512,256]{1,0:T(8,128)(2,1)} %features.1), channel_id=1, source_target_pairs={{0,16},{4,20},{8,24},{12,28},{16,0},{20,4},{24,8},{28,12},{1,17},{... | collective-permute-start | bytes 786440 | tf_op jit(solution)/shard_map/ppermute | solution.py:271
  5.2 1.0 %copy-start = (bf16[512,256]{1,0:T(8,128)(2,1)S(1)}, bf16[512,256]{1,0:T(8,128)(2,1)}, u32[]{:S(2)}) copy-start(bf16[512,256]{1,0:T(8,128)(2,1)} %features.1) | copy-start | bytes 786436
  6.2 0.7 copy-start.3
  6.9 0.7 copy-start.4
  12.0 5.6 %collective-permute-start.1 = (bf16[512,256]{1,0:T(8,128)(2,1)S(1)}, bf16[512,256]{1,0:T(8,128)(2,1)S(1)}, u32[]{:S(2)}, u32[]{:S(2)}) collective-permute-start(bf16[512,256]{1,0:T(8,128)(2,1)S(1)} %collective-permute-done.refs_1_), channel_id=1, source_target_pairs={{0,4},{4,0},{8,12},{12,8},{16,20},{20,16},{24,28},{28,24},{1,5},{5... | collective-permute-start | bytes 786440 | tf_op jit(solution)/shard_map/ppermute | solution.py:271
  12.0 5.6 %collective-permute-start.6 = (bf16[512,256]{1,0:T(8,128)(2,1)S(1)}, bf16[512,256]{1,0:T(8,128)(2,1)S(1)}, u32[]{:S(2)}, u32[]{:S(2)}) collective-permute-start(bf16[512,256]{1,0:T(8,128)(2,1)S(1)} %get-tuple-element.36.refs_7_), channel_id=1, source_target_pairs={{0,4},{4,0},{8,12},{12,8},{16,20},{20,16},{24,28},{28,24},{1,5},{5... | collective-permute-start | bytes 786440 | tf_op jit(solution)/shard_map/ppermute | solution.py:271
  17.0 1.5 %collective-permute-start.5 = (bf16[512,256]{1,0:T(8,128)(2,1)S(1)}, bf16[512,256]{1,0:T(8,128)(2,1)S(1)}, u32[]{:S(2)}, u32[]{:S(2)}) collective-permute-start(bf16[512,256]{1,0:T(8,128)(2,1)S(1)} %collective-permute-done.4.refs_5_), channel_id=1, source_target_pairs={{0,4},{4,0},{8,12},{12,8},{16,20},{20,16},{24,28},{28,24},{1,5},{5... | collective-permute-start | bytes 786440 | tf_op jit(solution)/shard_map/ppermute | solution.py:271
  17.0 1.9 %collective-permute-start.3 = (bf16[512,256]{1,0:T(8,128)(2,1)S(1)}, bf16[512,256]{1,0:T(8,128)(2,1)S(1)}, u32[]{:S(2)}, u32[]{:S(2)}) collective-permute-start(bf16[512,256]{1,0:T(8,128)(2,1)S(1)} %collective-permute-done.2.refs_3_), channel_id=1, source_target_pairs={{0,4},{4,0},{8,12},{12,8},{16,20},{20,16},{24,28},{28,24},{1,5},{5... | collective-permute-start | bytes 786440 | tf_op jit(solution)/shard_map/ppermute | solution.py:271
  18.9 29.4 %copy-start.1 = (bf16[512,256]{1,0:T(8,128)(2,1)S(1)}, bf16[512,256]{1,0:T(8,128)(2,1)}, u32[]{:S(2)}) copy-start(bf16[512,256]{1,0:T(8,128)(2,1)} %refs_3_.1) | copy-start | bytes 786436
  18.9 29.4 %copy-start.2 = (bf16[256,256]{1,0:T(8,128)(2,1)S(1)}, bf16[256,256]{1,0:T(8,128)(2,1)}, u32[]{:S(2)}) copy-start(bf16[256,256]{1,0:T(8,128)(2,1)} %refs_2_.1) | copy-start | bytes 393220
  22.9 11.2 %collective-permute-start.10 = (bf16[512,256]{1,0:T(8,128)(2,1)S(1)}, bf16[512,256]{1,0:T(8,128)(2,1)S(1)}, u32[]{:S(2)}, u32[]{:S(2)}) collective-permute-start(bf16[512,256]{1,0:T(8,128)(2,1)S(1)} %get-tuple-element.37), channel_id=1, source_target_pairs={{0,1},{3,2},{4,5},{7,6},{8,9},{11,10},{12,13},{15,14},{16,17},{19,... | collective-permute-start | bytes 786440 | tf_op jit(solution)/shard_map/ppermute | solution.py:317
  27.3 12.4 %collective-permute-start.7 = (bf16[512,256]{1,0:T(8,128)(2,1)S(1)}, bf16[512,256]{1,0:T(8,128)(2,1)S(1)}, u32[]{:S(2)}, u32[]{:S(2)}) collective-permute-start(bf16[512,256]{1,0:T(8,128)(2,1)S(1)} %get-tuple-element.37), channel_id=1, source_target_pairs={{1,2},{2,1},{5,6},{6,5},{9,10},{10,9},{13,14},{14,13},{17,18},{18,... | collective-permute-start | bytes 786440 | tf_op jit(solution)/shard_map/ppermute | solution.py:318
  28.0 11.7 %collective-permute-start.9 = (bf16[512,256]{1,0:T(8,128)(2,1)S(1)}, bf16[512,256]{1,0:T(8,128)(2,1)S(1)}, u32[]{:S(2)}, u32[]{:S(2)}) collective-permute-start(bf16[512,256]{1,0:T(8,128)(2,1)S(1)} %get-tuple-element.39), channel_id=1, source_target_pairs={{0,1},{1,0},{2,3},{3,2},{4,5},{5,4},{6,7},{7,6},{8,9},{9,8},{10,11... | collective-permute-start | bytes 786440 | tf_op jit(solution)/shard_map/ppermute | solution.py:271
  28.7 13.9 %collective-permute-start.8 = (bf16[512,256]{1,0:T(8,128)(2,1)S(1)}, bf16[512,256]{1,0:T(8,128)(2,1)S(1)}, u32[]{:S(2)}, u32[]{:S(2)}) collective-permute-start(bf16[512,256]{1,0:T(8,128)(2,1)S(1)} %get-tuple-element.38), channel_id=1, source_target_pairs={{0,2},{3,1},{4,6},{7,5},{8,10},{11,9},{12,14},{15,13},{16,18},{19,... | collective-permute-start | bytes 786440 | tf_op jit(solution)/shard_map/ppermute | solution.py:319
  34.1 14.2 %collective-permute-start.11 = (bf16[512,256]{1,0:T(8,128)(2,1)S(1)}, bf16[512,256]{1,0:T(8,128)(2,1)S(1)}, u32[]{:S(2)}, u32[]{:S(2)}) collective-permute-start(bf16[512,256]{1,0:T(8,128)(2,1)S(1)} %add_convert_fusion.1), channel_id=1, source_target_pairs={{1,3},{2,0},{5,7},{6,4},{9,11},{10,8},{13,15},{14,12},{17,19},{18,... | collective-permute-start | bytes 786440 | tf_op jit(solution)/shard_map/ppermute | solution.py:322
  49.5 7.8 %collective-permute-start.12 = (bf16[512,256]{1,0:T(8,128)(2,1)S(1)}, bf16[512,256]{1,0:T(8,128)(2,1)S(1)}, u32[]{:S(2)}, u32[]{:S(2)}) collective-permute-start(bf16[512,256]{1,0:T(8,128)(2,1)S(1)} %get-tuple-element.49.refs_5_), channel_id=1, source_target_pairs={{0,2},{3,1},{4,6},{7,5},{8,10},{11,9},{12,14},{15,13},{16,18},{19,... | collective-permute-start | bytes 786440 | tf_op jit(solution)/shard_map/ppermute | solution.py:329
  51.4 2.1 %collective-permute-start.13 = (f32[128,256]{1,0:T(8,128)S(1)}, f32[128,256]{1,0:T(8,128)S(1)}, u32[]{:S(2)}, u32[]{:S(2)}) collective-permute-start(f32[128,256]{1,0:T(8,128)S(1)} %get-tuple-element.46), channel_id=1, source_target_pairs={{0,4},{4,0},{8,12},{12,8},{16,20},{20,16},{24,28},{28,24},{1,5},{5... | collective-permute-start | bytes 393224 | tf_op jit(solution)/shard_map/ppermute | solution.py:271
  51.5 18.0 %collective-permute-start.17 = (bf16[512,256]{1,0:T(8,128)(2,1)S(1)}, bf16[512,256]{1,0:T(8,128)(2,1)S(1)}, u32[]{:S(2)}, u32[]{:S(2)}) collective-permute-start(bf16[512,256]{1,0:T(8,128)(2,1)S(1)} %get-tuple-element.49.refs_5_), channel_id=1, source_target_pairs={{0,1},{1,0},{2,3},{3,2},{4,5},{5,4},{6,7},{7,6},{8,9},{9,8},{10,11... | collective-permute-start | bytes 786440 | tf_op jit(solution)/shard_map/ppermute | solution.py:271
  51.6 17.9 %collective-permute-start.16 = (bf16[512,256]{1,0:T(8,128)(2,1)S(1)}, bf16[512,256]{1,0:T(8,128)(2,1)S(1)}, u32[]{:S(2)}, u32[]{:S(2)}) collective-permute-start(bf16[512,256]{1,0:T(8,128)(2,1)S(1)} %get-tuple-element.49.refs_5_), channel_id=1, source_target_pairs={{1,3},{2,0},{5,7},{6,4},{9,11},{10,8},{13,15},{14,12},{17,19},{18,... | collective-permute-start | bytes 786440 | tf_op jit(solution)/shard_map/ppermute | solution.py:331
  52.9 16.6 %collective-permute-start.15 = (bf16[512,256]{1,0:T(8,128)(2,1)S(1)}, bf16[512,256]{1,0:T(8,128)(2,1)S(1)}, u32[]{:S(2)}, u32[]{:S(2)}) collective-permute-start(bf16[512,256]{1,0:T(8,128)(2,1)S(1)} %get-tuple-element.49.refs_5_), channel_id=1, source_target_pairs={{1,2},{2,1},{5,6},{6,5},{9,10},{10,9},{13,14},{14,13},{17,18},{18,... | collective-permute-start | bytes 786440 | tf_op jit(solution)/shard_map/ppermute | solution.py:330
  57.3 14.1 %collective-permute-start.14 = (bf16[512,256]{1,0:T(8,128)(2,1)S(1)}, bf16[512,256]{1,0:T(8,128)(2,1)S(1)}, u32[]{:S(2)}, u32[]{:S(2)}) collective-permute-start(bf16[512,256]{1,0:T(8,128)(2,1)S(1)} %collective-permute-done.12.refs_3_), channel_id=1, source_target_pairs={{2,3},{1,0},{6,7},{5,4},{10,11},{9,8},{14,15},{13,12},{18,19},{17,... | collective-permute-start | bytes 786440 | tf_op jit(solution)/shard_map/ppermute | solution.py:334
  75.7 3.5 %collective-permute-start.18 = (bf16[2048,256]{1,0:T(8,128)(2,1)S(1)}, bf16[2048,256]{1,0:T(8,128)(2,1)S(1)}, u32[]{:S(2)}, u32[]{:S(2)}) collective-permute-start(bf16[2048,256]{1,0:T(8,128)(2,1)S(1)} %get-tuple-element.51), channel_id=1, source_target_pairs={{0,4},{4,0},{8,12},{12,8},{16,20},{20,16},{24,28},{28,24},{1,5},{5... | collective-permute-start | bytes 3145736 | tf_op jit(solution)/shard_map/ppermute | solution.py:271
  75.8 13.2 %all-to-all-start = ((bf16[4,128,256]{2,1,0:T(8,128)(2,1)}), bf16[4,128,256]{2,1,0:T(8,128)(2,1)S(1)}, u32[]{:S(2)}, u32[]{:S(2)}) async-start(bf16[4,128,256]{2,1,0:T(8,128)(2,1)} %bitcast.3), calls=%async_computation | async-start | bytes 524288 | tf_op jit(solution)/shard_map/all_to_all | solution.py:346
  79.5 11.7 %collective-permute-start.19 = (bf16[512,256]{1,0:T(8,128)(2,1)S(1)}, bf16[512,256]{1,0:T(8,128)(2,1)S(1)}, u32[]{:S(2)}, u32[]{:S(2)}) collective-permute-start(bf16[512,256]{1,0:T(8,128)(2,1)S(1)} %get-tuple-element.52), channel_id=1, source_target_pairs={{0,24},{4,28},{8,16},{12,20},{16,8},{20,12},{24,0},{28,4},{1,25},{... | collective-permute-start | bytes 786440 | tf_op jit(solution)/shard_map/ppermute | solution.py:271
  81.0 13.7 %collective-permute-start.20 = (bf16[512,256]{1,0:T(8,128)(2,1)S(1)}, bf16[512,256]{1,0:T(8,128)(2,1)S(1)}, u32[]{:S(2)}, u32[]{:S(2)}) collective-permute-start(bf16[512,256]{1,0:T(8,128)(2,1)S(1)} %get-tuple-element.53), channel_id=1, source_target_pairs={{0,16},{4,20},{8,24},{12,28},{16,0},{20,4},{24,8},{28,12},{1,17},{... | collective-permute-start | bytes 786440 | tf_op jit(solution)/shard_map/ppermute | solution.py:271
  81.8 13.0 %collective-permute-start.21 = (bf16[512,256]{1,0:T(8,128)(2,1)S(1)}, bf16[512,256]{1,0:T(8,128)(2,1)S(1)}, u32[]{:S(2)}, u32[]{:S(2)}) collective-permute-start(bf16[512,256]{1,0:T(8,128)(2,1)S(1)} %get-tuple-element.54), channel_id=1, source_target_pairs={{0,8},{4,12},{8,0},{12,4},{16,24},{20,28},{24,16},{28,20},{1,9},{5... | collective-permute-start | bytes 786440 | tf_op jit(solution)/shard_map/ppermute | solution.py:271
  89.0 1.4 %collective-permute-start.22 = (f32[128,256]{1,0:T(8,128)S(1)}, f32[128,256]{1,0:T(8,128)S(1)}, u32[]{:S(2)}, u32[]{:S(2)}) collective-permute-start(f32[128,256]{1,0:T(8,128)S(1)} %convert_reduce_fusion.own_ref), channel_id=1, source_target_pairs={{0,4},{4,0},{8,12},{12,8},{16,20},{20,16},{24,28},{28,24},{1,5},{5... | collective-permute-start | bytes 393224 | tf_op jit(solution)/shard_map/ppermute | solution.py:271

commit v13 on v12

--- a/solution.py
+++ b/solution.py
@@ -66,6 +66,10 @@
         out_specs=[SMEM, SMEM, VMEM],
         compiler_params=params(32),
     )(starts, cols, features)
+
+
+def order(parts, backward):
+    return parts if backward else parts[::-1]
 
 
 def sparse_kernel(counts, outs, backward, row_of, col_of, here_ref, mine_ref, *refs):
@@ -88,14 +92,14 @@
     used = (live + GROUP - 1) // GROUP
     lax.fori_loop(0, used, begin, 0)
     total[...] = jnp.zeros_like(total)
-    at = parts
-    for m, count in enumerate(counts):
+    at = 0
+    for m, count in order(list(enumerate(counts)), backward):
         start = pl.multiple_of((here ^ m) * chunk, chunk)
-        part = panel_refs[at - 1][...]
-        for ref in panel_refs[at - count : at - 1]:
+        part = panel_refs[at][...]
+        for ref in panel_refs[at + 1 : at + count]:
             part += ref[...]
         panel[pl.ds(start, chunk), :] = part
-        at -= count
+        at += count
     spare = total.shape[0] // size - 1
     last = panel.shape[0] // size - 1
 
@@ -136,7 +140,7 @@
 
 def sparse_product(panel_parts, values, row_of, col_of, here, mine, blocks, outs, backward):
     counts = [len(part) for part in panel_parts]
-    operands = [operand for part in panel_parts for operand in part]
+    operands = [operand for part in order(panel_parts, backward) for operand in part]
     parts = len(counts)
     slots, size, _ = values.shape
     chunk, width = operands[0].shape
@@ -154,7 +158,7 @@
         ],
         compiler_params=params(48),
         cost_estimate=cost(flops, 2 * values.size + 2 * parts * chunk * width),
-    )(row_of, col_of, here, mine, *operands[::-1], values)
+    )(row_of, col_of, here, mine, *operands, values)
 
 
 def split(value):

time: 95.9 us -> 98.9 us (1.031)
  starting transfers between devices: 28.1 us -> 31.1 us
  Pallas kernels: 14.5 us -> 13.4 us
    ppermute x15, starting transfers between devices: 10.1 us -> 14.3 us  [swap(): return lax.ppermute(x, axis, [(i, i ^ m) for i in range(n)])]
    ppermute x1, waiting for transfers between devices: 3.72 us -> 0.01 us  [gather_parts(): inward = lax.ppermute(own, 'col', [(0, 2), (3, 1)])]
    ppermute x1, waiting for transfers between devices: 1.99 us -> 5.21 us  [gather_parts(): far = lax.ppermute(inward, 'col', [(2, 3), (1, 0)])]
    ppermute x1, waiting for transfers between devices: 2.91 us -> 4.86 us  [exchange_terms(): inward = lax.ppermute(terms[2], 'col', [(0, 2), (3, 1)])]
    pallas_call x2, Pallas kernels: 8.12 us -> 7.03 us  [sparse_product(): pl.pallas_call(functools.partial(sparse_kernel, counts, outs, backward),...]
    ppermute x1, waiting for transfers between devices: 5.61 us -> 4.61 us  [exchange_terms(): outward = lax.ppermute(relay, 'col', [(1, 3), (2, 0)])]
  transfers between devices with their start and end apart: 24 -> 24, of which waited for: 13 -> 14; matrix products, arithmetic and copies ran while one was open for 0% -> 0% of each run, Pallas kernels for 5% -> 5%
where the time goes in v13:
time: 98.9 us; the launch traced here: 97.8 us
  waiting for transfers between devices  39.6 us (40%)
  starting transfers between devices  31.1 us (31%)
  Pallas kernels  13.4 us (14%)
  blocking collectives  9.55 us (10%)
  local copies, waits for them, and re-layouts  2.3 us (2%)
    ppermute x15, waiting for transfers between devices, swap(): return lax.ppermute(x, axis, [(i, i ^ m) for i in range(n)])  17.5 us
    ppermute x15, starting transfers between devices, swap(): return lax.ppermute(x, axis, [(i, i ^ m) for i in range(n)])  14.3 us
    all_gather x1, blocking collectives, on_device(): lax.all_gather(term, 'row', axis=0, axis_index_groups=cores, tiled=True)  9.55 us
    pallas_call x2, Pallas kernels, sparse_product(): pl.pallas_call(functools.partial(sparse_kernel, counts, outs, backward),...  7.03 us
    all_to_all x1, waiting for transfers between devices, exchange(): return lax.all_to_all(x, axis, 0, 0, tiled=True)  5.95 us
    ppermute x1, waiting for transfers between devices, gather_parts(): far = lax.ppermute(inward, 'col', [(2, 3), (1, 0)])  5.21 us
    ppermute x1, waiting for transfers between devices, exchange_terms(): inward = lax.ppermute(terms[2], 'col', [(0, 2), (3, 1)])  4.86 us
    ppermute x1, waiting for transfers between devices, exchange_terms(): outward = lax.ppermute(relay, 'col', [(1, 3), (2, 0)])  4.61 us
  transfers between devices with their start and end apart: 24, of which 14 were waited for; matrix products, arithmetic and copies ran while one was open for 0% of the time, Pallas kernels for 5%

profile of v13, /device:TPU:0, one launch (start us, length us, event | category | flops | bytes accessed | tf_op | source)
XLA Modules:
  0.0 97.8 jit_solution(14717510808297557995)
XLA Ops:
  0.6 4.0 %collective-permute-start = (bf16[512,256]{1,0:T(8,128)(2,1)}, bf16[512,256]{1,0:T(8,128)(2,1)S(1)}, u32[]{:S(2)}, u32[]{:S(2)}) collective-permute-start(bf16[512,256]{1,0:T(8,128)(2,1)} %features.1), channel_id=1, source_target_pairs={{0,24},{4,28},{8,16},{12,20},{16,8},{20,12},{24,0},{28,4},{1,25},{... | collective-permute-start | bytes 786440 | tf_op jit(solution)/shard_map/ppermute | solution.py:275
  4.6 0.5 collective-permute-start.4
  5.1 0.1 collective-permute-start.2
  5.2 1.0 %copy-done = bf16[512,256]{1,0:T(8,128)(2,1)S(1)} copy-done((bf16[512,256]{1,0:T(8,128)(2,1)S(1)}, bf16[512,256]{1,0:T(8,128)(2,1)}, u32[]{:S(2)}) %copy-start) | copy-done | bytes 262168
  6.2 0.7 copy-done.3
  6.9 0.7 copy-done.4
  7.5 2.9 %shard_map.85 = (s32[129]{0:T(256)S(1)}, s32[128]{0:T(128)S(1)}, bf16[512,256]{1,0:T(8,128)(2,1)S(1)}) custom-call(s32[1,1,17]{2,1,0:T(1,128)S(1)} %copy-done.3, s32[1,1,128]{2,1,0:T(1,128)S(1)} %copy-done.4, bf16[512,256]{1,0:T(8,128)(2,1)S(1)} %copy-done), custom_call_target="tpu_custom_call" | custom-call | tf_op jit(solution)/shard_map/pallas_call | solution.py:58
  10.4 1.6 %collective-permute-done.refs_1_ = bf16[512,256]{1,0:T(8,128)(2,1)S(1)} collective-permute-done((bf16[512,256]{1,0:T(8,128)(2,1)}, bf16[512,256]{1,0:T(8,128)(2,1)S(1)}, u32[]{:S(2)}, u32[]{:S(2)}) %collective-permute-start) | collective-permute-done | bytes 262176 | tf_op jit(solution)/shard_map/ppermute | solution.py:275
  12.0 0.0 collective-permute-start.1
  12.0 0.5 collective-permute-start.6
  12.5 4.5 %collective-permute-done.4.refs_5_ = bf16[512,256]{1,0:T(8,128)(2,1)S(1)} collective-permute-done((bf16[512,256]{1,0:T(8,128)(2,1)}, bf16[512,256]{1,0:T(8,128)(2,1)S(1)}, u32[]{:S(2)}, u32[]{:S(2)}) %collective-permute-start.4) | collective-permute-done | bytes 262176 | tf_op jit(solution)/shard_map/ppermute | solution.py:275
  17.0 0.0 collective-permute-start.5
  17.0 0.0 collective-permute-done.2.refs_3_
  17.0 0.5 collective-permute-start.3
  17.5 0.0 collective-permute-done.1.refs_0_
  17.5 0.0 collective-permute-done.6.refs_6_
  17.5 1.0 %collective-permute-done.5.refs_4_ = bf16[512,256]{1,0:T(8,128)(2,1)S(1)} collective-permute-done((bf16[512,256]{1,0:T(8,128)(2,1)S(1)}, bf16[512,256]{1,0:T(8,128)(2,1)S(1)}, u32[]{:S(2)}, u32[]{:S(2)}) %collective-permute-start.5) | collective-permute-done | bytes 262176 | tf_op jit(solution)/shard_map/ppermute | solution.py:275
  18.6 0.4 collective-permute-done.3.refs_2_
  18.9 3.4 %shard_map.86 = (bf16[512,256]{1,0:T(8,128)(2,1)S(1)}, bf16[512,256]{1,0:T(8,128)(2,1)S(1)}, bf16[512,256]{1,0:T(8,128)(2,1)S(1)}, bf16[512,256]{1,0:T(8,128)(2,1)S(1)}) custom-call(s32[129]{0:T(256)S(1)} %get-tuple-element.33.row_of, s32[128]{0:T(128)S(1)} %get-tuple-element.34.col_of, s32[1]{0:T(128)} %bitcast.here_ref.me.mine_ref, ...), custom_call_target="tpu_custom_call" | custom-call | flops 1073741824 | bytes 6291456 | tf_op jit(solution)/shard_map/pallas_call | solution.py:148
  22.4 4.0 %collective-permute-start.10 = (bf16[512,256]{1,0:T(8,128)(2,1)S(1)}, bf16[512,256]{1,0:T(8,128)(2,1)S(1)}, u32[]{:S(2)}, u32[]{:S(2)}) collective-permute-start(bf16[512,256]{1,0:T(8,128)(2,1)S(1)} %get-tuple-element.37), channel_id=1, source_target_pairs={{0,1},{3,2},{4,5},{7,6},{8,9},{11,10},{12,13},{15,14},{16,17},{19,... | collective-permute-start | bytes 786440 | tf_op jit(solution)/shard_map/ppermute | solution.py:321
  26.4 0.7 collective-permute-start.7
  27.0 1.9 %collective-permute-start.9 = (bf16[512,256]{1,0:T(8,128)(2,1)S(1)}, bf16[512,256]{1,0:T(8,128)(2,1)S(1)}, u32[]{:S(2)}, u32[]{:S(2)}) collective-permute-start(bf16[512,256]{1,0:T(8,128)(2,1)S(1)} %get-tuple-element.39), channel_id=1, source_target_pairs={{0,1},{1,0},{2,3},{3,2},{4,5},{5,4},{6,7},{7,6},{8,9},{9,8},{10,11... | collective-permute-start | bytes 786440 | tf_op jit(solution)/shard_map/ppermute | solution.py:275
  29.0 2.8 %collective-permute-start.8 = (bf16[512,256]{1,0:T(8,128)(2,1)S(1)}, bf16[512,256]{1,0:T(8,128)(2,1)S(1)}, u32[]{:S(2)}, u32[]{:S(2)}) collective-permute-start(bf16[512,256]{1,0:T(8,128)(2,1)S(1)} %get-tuple-element.38), channel_id=1, source_target_pairs={{0,2},{3,1},{4,6},{7,5},{8,10},{11,9},{12,14},{15,13},{16,18},{19,... | collective-permute-start | bytes 786440 | tf_op jit(solution)/shard_map/ppermute | solution.py:323
  31.8 1.2 %collective-permute-done.10 = bf16[512,256]{1,0:T(8,128)(2,1)S(1)} collective-permute-done((bf16[512,256]{1,0:T(8,128)(2,1)S(1)}, bf16[512,256]{1,0:T(8,128)(2,1)S(1)}, u32[]{:S(2)}, u32[]{:S(2)}) %collective-permute-start.10) | collective-permute-done | bytes 262176 | tf_op jit(solution)/shard_map/ppermute | solution.py:321
  33.0 0.1 add_convert_fusion.1
  33.1 1.3 %collective-permute-start.11 = (bf16[512,256]{1,0:T(8,128)(2,1)S(1)}, bf16[512,256]{1,0:T(8,128)(2,1)S(1)}, u32[]{:S(2)}, u32[]{:S(2)}) collective-permute-start(bf16[512,256]{1,0:T(8,128)(2,1)S(1)} %add_convert_fusion.1), channel_id=1, source_target_pairs={{1,3},{2,0},{5,7},{6,4},{9,11},{10,8},{13,15},{14,12},{17,19},{18,... | collective-permute-start | bytes 786440 | tf_op jit(solution)/shard_map/ppermute | solution.py:326
  34.4 4.2 %collective-permute-done.9.refs_2_ = bf16[512,256]{1,0:T(8,128)(2,1)S(1)} collective-permute-done((bf16[512,256]{1,0:T(8,128)(2,1)S(1)}, bf16[512,256]{1,0:T(8,128)(2,1)S(1)}, u32[]{:S(2)}, u32[]{:S(2)}) %collective-permute-start.9) | collective-permute-done | bytes 262176 | tf_op jit(solution)/shard_map/ppermute | solution.py:275
  38.6 0.0 collective-permute-done.7.refs_0_
  38.6 4.9 %collective-permute-done.8.refs_1_ = bf16[512,256]{1,0:T(8,128)(2,1)S(1)} collective-permute-done((bf16[512,256]{1,0:T(8,128)(2,1)S(1)}, bf16[512,256]{1,0:T(8,128)(2,1)S(1)}, u32[]{:S(2)}, u32[]{:S(2)}) %collective-permute-start.8) | collective-permute-done | bytes 262176 | tf_op jit(solution)/shard_map/ppermute | solution.py:323
  43.5 0.1 shard_map.87.refs_0_
  43.6 4.6 %collective-permute-done.11.refs_1_ = bf16[512,256]{1,0:T(8,128)(2,1)S(1)} collective-permute-done((bf16[512,256]{1,0:T(8,128)(2,1)S(1)}, bf16[512,256]{1,0:T(8,128)(2,1)S(1)}, u32[]{:S(2)}, u32[]{:S(2)}) %collective-permute-start.11) | collective-permute-done | bytes 262176 | tf_op jit(solution)/shard_map/ppermute | solution.py:326
  48.2 0.0 copy-done.1
  48.2 1.2 %shard_map.88 = (bf16[512,256]{1,0:T(8,128)(2,1)}, bf16[512,256]{1,0:T(8,128)(2,1)S(1)}, f32[512,256]{1,0:T(8,128)S(1)}, f32[512,256]{1,0:T(8,128)S(1)}) custom-call(f32[512,256]{1,0:T(8,128)S(1)} %shard_map.87.refs_0_, bf16[512,256]{1,0:T(8,128)(2,1)S(1)} %collective-permute-done.11.refs_1_, bf16[256,256]{1,0:T(8,128)(2,1)S(1)} %copy-done.2, ...), custom_call_target="tpu_custom_call" | custom-call | flops 268435456 | bytes 2621440 | tf_op jit(solution)/shard_map/pallas_call | solution.py:194
  49.4 1.5 %collective-permute-start.12 = (bf16[512,256]{1,0:T(8,128)(2,1)S(1)}, bf16[512,256]{1,0:T(8,128)(2,1)S(1)}, u32[]{:S(2)}, u32[]{:S(2)}) collective-permute-start(bf16[512,256]{1,0:T(8,128)(2,1)S(1)} %get-tuple-element.48.refs_0_), channel_id=1, source_target_pairs={{0,2},{3,1},{4,6},{7,5},{8,10},{11,9},{12,14},{15,13},{16,18},{19,... | collective-permute-start | bytes 786440 | tf_op jit(solution)/shard_map/ppermute | solution.py:333
  50.9 0.5 shard_map.89
  51.3 0.1 collective-permute-start.13
  51.4 0.7 collective-permute-start.16
  52.1 1.3 %collective-permute-start.15 = (bf16[512,256]{1,0:T(8,128)(2,1)S(1)}, bf16[512,256]{1,0:T(8,128)(2,1)S(1)}, u32[]{:S(2)}, u32[]{:S(2)}) collective-permute-start(bf16[512,256]{1,0:T(8,128)(2,1)S(1)} %get-tuple-element.48.refs_0_), channel_id=1, source_target_pairs={{1,3},{2,0},{5,7},{6,4},{9,11},{10,8},{13,15},{14,12},{17,19},{18,... | collective-permute-start | bytes 786440 | tf_op jit(solution)/shard_map/ppermute | solution.py:335
  53.4 3.0 %collective-permute-start.14 = (bf16[512,256]{1,0:T(8,128)(2,1)S(1)}, bf16[512,256]{1,0:T(8,128)(2,1)S(1)}, u32[]{:S(2)}, u32[]{:S(2)}) collective-permute-start(bf16[512,256]{1,0:T(8,128)(2,1)S(1)} %get-tuple-element.48.refs_0_), channel_id=1, source_target_pairs={{0,1},{1,0},{2,3},{3,2},{4,5},{5,4},{6,7},{7,6},{8,9},{9,8},{10,11... | collective-permute-start | bytes 786440 | tf_op jit(solution)/shard_map/ppermute | solution.py:275
  56.4 0.0 collective-permute-done.13
  56.4 0.0 collective-permute-done.12.refs_2_
  56.4 1.3 %collective-permute-start.17 = (bf16[512,256]{1,0:T(8,128)(2,1)S(1)}, bf16[512,256]{1,0:T(8,128)(2,1)S(1)}, u32[]{:S(2)}, u32[]{:S(2)}) collective-permute-start(bf16[512,256]{1,0:T(8,128)(2,1)S(1)} %collective-permute-done.12.refs_2_), channel_id=1, source_target_pairs={{2,3},{1,0},{6,7},{5,4},{10,11},{9,8},{14,15},{13,12},{18,19},{17,... | collective-permute-start | bytes 786440 | tf_op jit(solution)/shard_map/ppermute | solution.py:338
  57.7 9.5 %all_gather.3.in_ref = f32[512,256]{1,0:T(8,128)S(1)} all-gather(f32[128,256]{1,0:T(8,128)S(1)} %add.16), channel_id=1, replica_groups={{0,8,16,24},{4,12,20,28},{1,9,17,25},{5,13,21,29},{2,10,18,26},{6,14,22..., dimensions={0}, use_global_device_ids=true | all-gather | bytes 655360 | tf_op jit(solution)/shard_map/all_gather | solution.py:382
  67.2 0.7 shard_map.90
  68.0 0.0 collective-permute-done.16.refs_4_
  68.0 0.3 collective-permute-done.15.refs_3_
  68.2 0.8 collective-permute-done.14.refs_1_
  69.1 5.2 %collective-permute-done.17.refs_5_ = bf16[512,256]{1,0:T(8,128)(2,1)S(1)} collective-permute-done((bf16[512,256]{1,0:T(8,128)(2,1)S(1)}, bf16[512,256]{1,0:T(8,128)(2,1)S(1)}, u32[]{:S(2)}, u32[]{:S(2)}) %collective-permute-start.17) | collective-permute-done | bytes 262176 | tf_op jit(solution)/shard_map/ppermute | solution.py:338
  74.3 3.6 %shard_map.91 = (bf16[2048,256]{1,0:T(8,128)(2,1)S(1)}, bf16[2048,256]{1,0:T(8,128)(2,1)S(1)}) custom-call(s32[129]{0:T(256)S(1)} %get-tuple-element.33.row_of, s32[128]{0:T(128)S(1)} %get-tuple-element.34.col_of, s32[1]{0:T(128)} %bitcast.1.mine_ref.here_ref, s32[1]{0:T(128)} %bitcast.here_ref.me.mine_ref, bf16[512,256]{1,0:T(8,128)(2,1)S(1)} %get-tuple-element.48.refs_0_, ...), custom_call_target="tpu_custom_call" | custom-call | flops 1073741824 | bytes 5242880 | tf_op jit(solution)/shard_map/pallas_call | solution.py:148
  77.9 0.1 collective-permute-start.18
  78.0 3.4 %all-to-all-start = ((bf16[4,128,256]{2,1,0:T(8,128)(2,1)}), bf16[4,128,256]{2,1,0:T(8,128)(2,1)S(1)}, u32[]{:S(2)}, u32[]{:S(2)}) async-start(bf16[4,128,256]{2,1,0:T(8,128)(2,1)} %bitcast.3), calls=%async_computation | async-start | bytes 524288 | tf_op jit(solution)/shard_map/all_to_all | solution.py:350
  81.4 0.0 collective-permute-done.18.other_ref
  81.4 0.2 shard_map.92
  81.7 1.1 %collective-permute-start.19 = (bf16[512,256]{1,0:T(8,128)(2,1)S(1)}, bf16[512,256]{1,0:T(8,128)(2,1)S(1)}, u32[]{:S(2)}, u32[]{:S(2)}) collective-permute-start(bf16[512,256]{1,0:T(8,128)(2,1)S(1)} %get-tuple-element.52), channel_id=1, source_target_pairs={{0,24},{4,28},{8,16},{12,20},{16,8},{20,12},{24,0},{28,4},{1,25},{... | collective-permute-start | bytes 786440 | tf_op jit(solution)/shard_map/ppermute | solution.py:275
  82.8 2.0 %collective-permute-start.20 = (bf16[512,256]{1,0:T(8,128)(2,1)S(1)}, bf16[512,256]{1,0:T(8,128)(2,1)S(1)}, u32[]{:S(2)}, u32[]{:S(2)}) collective-permute-start(bf16[512,256]{1,0:T(8,128)(2,1)S(1)} %get-tuple-element.53), channel_id=1, source_target_pairs={{0,16},{4,20},{8,24},{12,28},{16,0},{20,4},{24,8},{28,12},{1,17},{... | collective-permute-start | bytes 786440 | tf_op jit(solution)/shard_map/ppermute | solution.py:275
  84.8 0.4 collective-permute-start.21
  85.2 6.0 %all-to-all-done = bf16[4,128,256]{2,1,0:T(8,128)(2,1)S(1)} async-done(((bf16[4,128,256]{2,1,0:T(8,128)(2,1)}), bf16[4,128,256]{2,1,0:T(8,128)(2,1)S(1)}, u32[]{:S(2)}, u32[]{:S(2)}) %all-to-all-start) | async-done | bytes 262176 | tf_op jit(solution)/shard_map/all_to_all | solution.py:350
  91.2 0.1 collective-permute-start.22
  91.3 1.3 %collective-permute-done.22.other_ref = f32[128,256]{1,0:T(8,128)S(1)} collective-permute-done((f32[128,256]{1,0:T(8,128)S(1)}, f32[128,256]{1,0:T(8,128)S(1)}, u32[]{:S(2)}, u32[]{:S(2)}) %collective-permute-start.22) | collective-permute-done | bytes 131104 | tf_op jit(solution)/shard_map/ppermute | solution.py:275
  92.6 0.7 shard_map.93
  93.3 0.0 collective-permute-done.19
  93.3 3.6 %collective-permute-done.20 = bf16[512,256]{1,0:T(8,128)(2,1)S(1)} collective-permute-done((bf16[512,256]{1,0:T(8,128)(2,1)S(1)}, bf16[512,256]{1,0:T(8,128)(2,1)S(1)}, u32[]{:S(2)}, u32[]{:S(2)}) %collective-permute-start.20) | collective-permute-done | bytes 262176 | tf_op jit(solution)/shard_map/ppermute | solution.py:275
  96.9 0.0 collective-permute-done.21
  96.9 0.8 add_convert_fusion
  (8 shorter events, 0.1 us)
Async XLA Ops:
  0.6 11.3 %collective-permute-start = (bf16[512,256]{1,0:T(8,128)(2,1)}, bf16[512,256]{1,0:T(8,128)(2,1)S(1)}, u32[]{:S(2)}, u32[]{:S(2)}) collective-permute-start(bf16[512,256]{1,0:T(8,128)(2,1)} %features.1), channel_id=1, source_target_pairs={{0,24},{4,28},{8,16},{12,20},{16,8},{20,12},{24,0},{28,4},{1,25},{... | collective-permute-start | bytes 786440 | tf_op jit(solution)/shard_map/ppermute | solution.py:275
  4.6 12.4 %collective-permute-start.4 = (bf16[512,256]{1,0:T(8,128)(2,1)}, bf16[512,256]{1,0:T(8,128)(2,1)S(1)}, u32[]{:S(2)}, u32[]{:S(2)}) collective-permute-start(bf16[512,256]{1,0:T(8,128)(2,1)} %features.1), channel_id=1, source_target_pairs={{0,8},{4,12},{8,0},{12,4},{16,24},{20,28},{24,16},{28,20},{1,9},{5... | collective-permute-start | bytes 786440 | tf_op jit(solution)/shard_map/ppermute | solution.py:275
  5.1 11.9 %collective-permute-start.2 = (bf16[512,256]{1,0:T(8,128)(2,1)}, bf16[512,256]{1,0:T(8,128)(2,1)S(1)}, u32[]{:S(2)}, u32[]{:S(2)}) collective-permute-start(bf16[512,256]{1,0:T(8,128)(2,1)} %features.1), channel_id=1, source_target_pairs={{0,16},{4,20},{8,24},{12,28},{16,0},{20,4},{24,8},{28,12},{1,17},{... | collective-permute-start | bytes 786440 | tf_op jit(solution)/shard_map/ppermute | solution.py:275
  5.2 1.0 %copy-start = (bf16[512,256]{1,0:T(8,128)(2,1)S(1)}, bf16[512,256]{1,0:T(8,128)(2,1)}, u32[]{:S(2)}) copy-start(bf16[512,256]{1,0:T(8,128)(2,1)} %features.1) | copy-start | bytes 786436
  6.2 0.7 copy-start.3
  6.9 0.7 copy-start.4
  12.0 5.6 %collective-permute-start.1 = (bf16[512,256]{1,0:T(8,128)(2,1)S(1)}, bf16[512,256]{1,0:T(8,128)(2,1)S(1)}, u32[]{:S(2)}, u32[]{:S(2)}) collective-permute-start(bf16[512,256]{1,0:T(8,128)(2,1)S(1)} %collective-permute-done.refs_1_), channel_id=1, source_target_pairs={{0,4},{4,0},{8,12},{12,8},{16,20},{20,16},{24,28},{28,24},{1,5},{5... | collective-permute-start | bytes 786440 | tf_op jit(solution)/shard_map/ppermute | solution.py:275
  12.0 5.6 %collective-permute-start.6 = (bf16[512,256]{1,0:T(8,128)(2,1)S(1)}, bf16[512,256]{1,0:T(8,128)(2,1)S(1)}, u32[]{:S(2)}, u32[]{:S(2)}) collective-permute-start(bf16[512,256]{1,0:T(8,128)(2,1)S(1)} %get-tuple-element.36.refs_7_), channel_id=1, source_target_pairs={{0,4},{4,0},{8,12},{12,8},{16,20},{20,16},{24,28},{28,24},{1,5},{5... | collective-permute-start | bytes 786440 | tf_op jit(solution)/shard_map/ppermute | solution.py:275
  17.0 1.5 %collective-permute-start.5 = (bf16[512,256]{1,0:T(8,128)(2,1)S(1)}, bf16[512,256]{1,0:T(8,128)(2,1)S(1)}, u32[]{:S(2)}, u32[]{:S(2)}) collective-permute-start(bf16[512,256]{1,0:T(8,128)(2,1)S(1)} %collective-permute-done.4.refs_5_), channel_id=1, source_target_pairs={{0,4},{4,0},{8,12},{12,8},{16,20},{20,16},{24,28},{28,24},{1,5},{5... | collective-permute-start | bytes 786440 | tf_op jit(solution)/shard_map/ppermute | solution.py:275
  17.0 1.9 %collective-permute-start.3 = (bf16[512,256]{1,0:T(8,128)(2,1)S(1)}, bf16[512,256]{1,0:T(8,128)(2,1)S(1)}, u32[]{:S(2)}, u32[]{:S(2)}) collective-permute-start(bf16[512,256]{1,0:T(8,128)(2,1)S(1)} %collective-permute-done.2.refs_3_), channel_id=1, source_target_pairs={{0,4},{4,0},{8,12},{12,8},{16,20},{20,16},{24,28},{28,24},{1,5},{5... | collective-permute-start | bytes 786440 | tf_op jit(solution)/shard_map/ppermute | solution.py:275
  18.9 29.3 %copy-start.1 = (bf16[512,256]{1,0:T(8,128)(2,1)S(1)}, bf16[512,256]{1,0:T(8,128)(2,1)}, u32[]{:S(2)}) copy-start(bf16[512,256]{1,0:T(8,128)(2,1)} %refs_3_.1) | copy-start | bytes 786436
  18.9 29.3 %copy-start.2 = (bf16[256,256]{1,0:T(8,128)(2,1)S(1)}, bf16[256,256]{1,0:T(8,128)(2,1)}, u32[]{:S(2)}) copy-start(bf16[256,256]{1,0:T(8,128)(2,1)} %refs_2_.1) | copy-start | bytes 393220
  22.4 10.6 %collective-permute-start.10 = (bf16[512,256]{1,0:T(8,128)(2,1)S(1)}, bf16[512,256]{1,0:T(8,128)(2,1)S(1)}, u32[]{:S(2)}, u32[]{:S(2)}) collective-permute-start(bf16[512,256]{1,0:T(8,128)(2,1)S(1)} %get-tuple-element.37), channel_id=1, source_target_pairs={{0,1},{3,2},{4,5},{7,6},{8,9},{11,10},{12,13},{15,14},{16,17},{19,... | collective-permute-start | bytes 786440 | tf_op jit(solution)/shard_map/ppermute | solution.py:321
  26.4 12.3 %collective-permute-start.7 = (bf16[512,256]{1,0:T(8,128)(2,1)S(1)}, bf16[512,256]{1,0:T(8,128)(2,1)S(1)}, u32[]{:S(2)}, u32[]{:S(2)}) collective-permute-start(bf16[512,256]{1,0:T(8,128)(2,1)S(1)} %get-tuple-element.37), channel_id=1, source_target_pairs={{1,2},{2,1},{5,6},{6,5},{9,10},{10,9},{13,14},{14,13},{17,18},{18,... | collective-permute-start | bytes 786440 | tf_op jit(solution)/shard_map/ppermute | solution.py:322
  27.0 11.6 %collective-permute-start.9 = (bf16[512,256]{1,0:T(8,128)(2,1)S(1)}, bf16[512,256]{1,0:T(8,128)(2,1)S(1)}, u32[]{:S(2)}, u32[]{:S(2)}) collective-permute-start(bf16[512,256]{1,0:T(8,128)(2,1)S(1)} %get-tuple-element.39), channel_id=1, source_target_pairs={{0,1},{1,0},{2,3},{3,2},{4,5},{5,4},{6,7},{7,6},{8,9},{9,8},{10,11... | collective-permute-start | bytes 786440 | tf_op jit(solution)/shard_map/ppermute | solution.py:275
  29.0 14.5 %collective-permute-start.8 = (bf16[512,256]{1,0:T(8,128)(2,1)S(1)}, bf16[512,256]{1,0:T(8,128)(2,1)S(1)}, u32[]{:S(2)}, u32[]{:S(2)}) collective-permute-start(bf16[512,256]{1,0:T(8,128)(2,1)S(1)} %get-tuple-element.38), channel_id=1, source_target_pairs={{0,2},{3,1},{4,6},{7,5},{8,10},{11,9},{12,14},{15,13},{16,18},{19,... | collective-permute-start | bytes 786440 | tf_op jit(solution)/shard_map/ppermute | solution.py:323
  33.1 15.1 %collective-permute-start.11 = (bf16[512,256]{1,0:T(8,128)(2,1)S(1)}, bf16[512,256]{1,0:T(8,128)(2,1)S(1)}, u32[]{:S(2)}, u32[]{:S(2)}) collective-permute-start(bf16[512,256]{1,0:T(8,128)(2,1)S(1)} %add_convert_fusion.1), channel_id=1, source_target_pairs={{1,3},{2,0},{5,7},{6,4},{9,11},{10,8},{13,15},{14,12},{17,19},{18,... | collective-permute-start | bytes 786440 | tf_op jit(solution)/shard_map/ppermute | solution.py:326
  49.4 7.0 %collective-permute-start.12 = (bf16[512,256]{1,0:T(8,128)(2,1)S(1)}, bf16[512,256]{1,0:T(8,128)(2,1)S(1)}, u32[]{:S(2)}, u32[]{:S(2)}) collective-permute-start(bf16[512,256]{1,0:T(8,128)(2,1)S(1)} %get-tuple-element.48.refs_0_), channel_id=1, source_target_pairs={{0,2},{3,1},{4,6},{7,5},{8,10},{11,9},{12,14},{15,13},{16,18},{19,... | collective-permute-start | bytes 786440 | tf_op jit(solution)/shard_map/ppermute | solution.py:333
  51.3 5.0 %collective-permute-start.13 = (f32[128,256]{1,0:T(8,128)S(1)}, f32[128,256]{1,0:T(8,128)S(1)}, u32[]{:S(2)}, u32[]{:S(2)}) collective-permute-start(f32[128,256]{1,0:T(8,128)S(1)} %get-tuple-element.46), channel_id=1, source_target_pairs={{0,4},{4,0},{8,12},{12,8},{16,20},{20,16},{24,28},{28,24},{1,5},{5... | collective-permute-start | bytes 393224 | tf_op jit(solution)/shard_map/ppermute | solution.py:275
  51.4 16.6 %collective-permute-start.16 = (bf16[512,256]{1,0:T(8,128)(2,1)S(1)}, bf16[512,256]{1,0:T(8,128)(2,1)S(1)}, u32[]{:S(2)}, u32[]{:S(2)}) collective-permute-start(bf16[512,256]{1,0:T(8,128)(2,1)S(1)} %get-tuple-element.48.refs_0_), channel_id=1, source_target_pairs={{1,2},{2,1},{5,6},{6,5},{9,10},{10,9},{13,14},{14,13},{17,18},{18,... | collective-permute-start | bytes 786440 | tf_op jit(solution)/shard_map/ppermute | solution.py:334
  52.1 16.1 %collective-permute-start.15 = (bf16[512,256]{1,0:T(8,128)(2,1)S(1)}, bf16[512,256]{1,0:T(8,128)(2,1)S(1)}, u32[]{:S(2)}, u32[]{:S(2)}) collective-permute-start(bf16[512,256]{1,0:T(8,128)(2,1)S(1)} %get-tuple-element.48.refs_0_), channel_id=1, source_target_pairs={{1,3},{2,0},{5,7},{6,4},{9,11},{10,8},{13,15},{14,12},{17,19},{18,... | collective-permute-start | bytes 786440 | tf_op jit(solution)/shard_map/ppermute | solution.py:335
  53.4 15.7 %collective-permute-start.14 = (bf16[512,256]{1,0:T(8,128)(2,1)S(1)}, bf16[512,256]{1,0:T(8,128)(2,1)S(1)}, u32[]{:S(2)}, u32[]{:S(2)}) collective-permute-start(bf16[512,256]{1,0:T(8,128)(2,1)S(1)} %get-tuple-element.48.refs_0_), channel_id=1, source_target_pairs={{0,1},{1,0},{2,3},{3,2},{4,5},{5,4},{6,7},{7,6},{8,9},{9,8},{10,11... | collective-permute-start | bytes 786440 | tf_op jit(solution)/shard_map/ppermute | solution.py:275
  56.4 17.9 %collective-permute-start.17 = (bf16[512,256]{1,0:T(8,128)(2,1)S(1)}, bf16[512,256]{1,0:T(8,128)(2,1)S(1)}, u32[]{:S(2)}, u32[]{:S(2)}) collective-permute-start(bf16[512,256]{1,0:T(8,128)(2,1)S(1)} %collective-permute-done.12.refs_2_), channel_id=1, source_target_pairs={{2,3},{1,0},{6,7},{5,4},{10,11},{9,8},{14,15},{13,12},{18,19},{17,... | collective-permute-start | bytes 786440 | tf_op jit(solution)/shard_map/ppermute | solution.py:338
  77.9 3.5 %collective-permute-start.18 = (bf16[2048,256]{1,0:T(8,128)(2,1)S(1)}, bf16[2048,256]{1,0:T(8,128)(2,1)S(1)}, u32[]{:S(2)}, u32[]{:S(2)}) collective-permute-start(bf16[2048,256]{1,0:T(8,128)(2,1)S(1)} %get-tuple-element.51), channel_id=1, source_target_pairs={{0,4},{4,0},{8,12},{12,8},{16,20},{20,16},{24,28},{28,24},{1,5},{5... | collective-permute-start | bytes 3145736 | tf_op jit(solution)/shard_map/ppermute | solution.py:275
  78.0 13.2 %all-to-all-start = ((bf16[4,128,256]{2,1,0:T(8,128)(2,1)}), bf16[4,128,256]{2,1,0:T(8,128)(2,1)S(1)}, u32[]{:S(2)}, u32[]{:S(2)}) async-start(bf16[4,128,256]{2,1,0:T(8,128)(2,1)} %bitcast.3), calls=%async_computation | async-start | bytes 524288 | tf_op jit(solution)/shard_map/all_to_all | solution.py:350
  81.7 11.7 %collective-permute-start.19 = (bf16[512,256]{1,0:T(8,128)(2,1)S(1)}, bf16[512,256]{1,0:T(8,128)(2,1)S(1)}, u32[]{:S(2)}, u32[]{:S(2)}) collective-permute-start(bf16[512,256]{1,0:T(8,128)(2,1)S(1)} %get-tuple-element.52), channel_id=1, source_target_pairs={{0,24},{4,28},{8,16},{12,20},{16,8},{20,12},{24,0},{28,4},{1,25},{... | collective-permute-start | bytes 786440 | tf_op jit(solution)/shard_map/ppermute | solution.py:275
  82.8 14.1 %collective-permute-start.20 = (bf16[512,256]{1,0:T(8,128)(2,1)S(1)}, bf16[512,256]{1,0:T(8,128)(2,1)S(1)}, u32[]{:S(2)}, u32[]{:S(2)}) collective-permute-start(bf16[512,256]{1,0:T(8,128)(2,1)S(1)} %get-tuple-element.53), channel_id=1, source_target_pairs={{0,16},{4,20},{8,24},{12,28},{16,0},{20,4},{24,8},{28,12},{1,17},{... | collective-permute-start | bytes 786440 | tf_op jit(solution)/shard_map/ppermute | solution.py:275
  84.8 12.1 %collective-permute-start.21 = (bf16[512,256]{1,0:T(8,128)(2,1)S(1)}, bf16[512,256]{1,0:T(8,128)(2,1)S(1)}, u32[]{:S(2)}, u32[]{:S(2)}) collective-permute-start(bf16[512,256]{1,0:T(8,128)(2,1)S(1)} %get-tuple-element.54), channel_id=1, source_target_pairs={{0,8},{4,12},{8,0},{12,4},{16,24},{20,28},{24,16},{28,20},{1,9},{5... | collective-permute-start | bytes 786440 | tf_op jit(solution)/shard_map/ppermute | solution.py:275
  91.2 1.4 %collective-permute-start.22 = (f32[128,256]{1,0:T(8,128)S(1)}, f32[128,256]{1,0:T(8,128)S(1)}, u32[]{:S(2)}, u32[]{:S(2)}) collective-permute-start(f32[128,256]{1,0:T(8,128)S(1)} %convert_reduce_fusion.own_ref), channel_id=1, source_target_pairs={{0,4},{4,0},{8,12},{12,8},{16,20},{20,16},{24,28},{28,24},{1,5},{5... | collective-permute-start | bytes 393224 | tf_op jit(solution)/shard_map/ppermute | solution.py:275

commit v14 on v12

--- a/solution.py
+++ b/solution.py
@@ -122,8 +122,9 @@
 
         return step
 
-    long = live // LONG
-    lax.fori_loop(0, long, steps(LONG), 0)
+    longest, long = live // (2 * LONG), live // LONG
+    lax.fori_loop(0, longest, steps(2 * LONG), 0)
+    lax.fori_loop(longest * 2, long, steps(LONG), 0)
     lax.fori_loop(long * (LONG // GROUP), used, steps(GROUP), 0)
     for out_ref, members in zip(out_refs, outs):
         rows = out_ref.shape[0] // len(members)

time: 95.9 us -> 96.4 us (level)
  Pallas kernels: 14.5 us -> 16.2 us
  starting transfers between devices: 28.1 us -> 27.1 us
    ppermute x1, starting transfers between devices: 4.45 us -> 1.95 us  [exchange_terms(): far = lax.ppermute(terms[3], 'col', [(0, 1), (3, 2)])]
    ppermute x1, waiting for transfers between devices: 2.91 us -> 5.2 us  [exchange_terms(): inward = lax.ppermute(terms[2], 'col', [(0, 2), (3, 1)])]
    ppermute x15, starting transfers between devices: 10.1 us -> 12.3 us  [swap(): return lax.ppermute(x, axis, [(i, i ^ m) for i in range(n)])]
    pallas_call x2, Pallas kernels: 8.12 us -> 9.89 us  [sparse_product(): pl.pallas_call(functools.partial(sparse_kernel, counts, outs, backward),...]
    ppermute x1, waiting for transfers between devices: 1.97 us -> 0.29 us  [exchange_terms(): far = lax.ppermute(terms[3], 'col', [(0, 1), (3, 2)])]
where the time goes in v14:
time: 96.4 us; the launch traced here: 96 us
  waiting for transfers between devices  38.8 us (40%)
  starting transfers between devices  27.1 us (28%)
  Pallas kernels  16.2 us (17%)
  blocking collectives  9.86 us (10%)
  local copies, waits for them, and re-layouts  2.3 us (2%)
    ppermute x15, waiting for transfers between devices, swap(): return lax.ppermute(x, axis, [(i, i ^ m) for i in range(n)])  16.2 us
    ppermute x15, starting transfers between devices, swap(): return lax.ppermute(x, axis, [(i, i ^ m) for i in range(n)])  12.3 us
    pallas_call x2, Pallas kernels, sparse_product(): pl.pallas_call(functools.partial(sparse_kernel, counts, outs, backward),...  9.89 us
    all_gather x1, blocking collectives, on_device(): lax.all_gather(term, 'row', axis=0, axis_index_groups=cores, tiled=True)  9.86 us
    all_to_all x1, waiting for transfers between devices, exchange(): return lax.all_to_all(x, axis, 0, 0, tiled=True)  5.95 us
    ppermute x1, waiting for transfers between devices, exchange_terms(): inward = lax.ppermute(terms[2], 'col', [(0, 2), (3, 1)])  5.2 us
    ppermute x1, waiting for transfers between devices, exchange_terms(): outward = lax.ppermute(relay, 'col', [(1, 3), (2, 0)])  5.14 us
    ppermute x1, waiting for transfers between devices, gather_parts(): inward = lax.ppermute(own, 'col', [(0, 2), (3, 1)])  4.06 us
  transfers between devices with their start and end apart: 24, of which 13 were waited for; matrix products, arithmetic and copies ran while one was open for 0% of the time, Pallas kernels for 5%

profile of v14, /device:TPU:0, one launch (start us, length us, event | category | flops | bytes accessed | tf_op | source)
XLA Modules:
  0.0 96.0 jit_solution(18115137937241570309)
XLA Ops:
  0.6 4.0 %collective-permute-start = (bf16[512,256]{1,0:T(8,128)(2,1)}, bf16[512,256]{1,0:T(8,128)(2,1)S(1)}, u32[]{:S(2)}, u32[]{:S(2)}) collective-permute-start(bf16[512,256]{1,0:T(8,128)(2,1)} %features.1), channel_id=1, source_target_pairs={{0,24},{4,28},{8,16},{12,20},{16,8},{20,12},{24,0},{28,4},{1,25},{... | collective-permute-start | bytes 786440 | tf_op jit(solution)/shard_map/ppermute | solution.py:272
  4.6 0.5 collective-permute-start.4
  5.1 0.1 collective-permute-start.2
  5.2 1.0 %copy-done = bf16[512,256]{1,0:T(8,128)(2,1)S(1)} copy-done((bf16[512,256]{1,0:T(8,128)(2,1)S(1)}, bf16[512,256]{1,0:T(8,128)(2,1)}, u32[]{:S(2)}) %copy-start) | copy-done | bytes 262168
  6.2 0.7 copy-done.3
  6.9 0.7 copy-done.4
  7.5 2.8 %shard_map.85 = (s32[129]{0:T(256)S(1)}, s32[128]{0:T(128)S(1)}, bf16[512,256]{1,0:T(8,128)(2,1)S(1)}) custom-call(s32[1,1,17]{2,1,0:T(1,128)S(1)} %copy-done.3, s32[1,1,128]{2,1,0:T(1,128)S(1)} %copy-done.4, bf16[512,256]{1,0:T(8,128)(2,1)S(1)} %copy-done), custom_call_target="tpu_custom_call" | custom-call | tf_op jit(solution)/shard_map/pallas_call | solution.py:58
  10.3 1.6 %collective-permute-done.refs_1_ = bf16[512,256]{1,0:T(8,128)(2,1)S(1)} collective-permute-done((bf16[512,256]{1,0:T(8,128)(2,1)}, bf16[512,256]{1,0:T(8,128)(2,1)S(1)}, u32[]{:S(2)}, u32[]{:S(2)}) %collective-permute-start) | collective-permute-done | bytes 262176 | tf_op jit(solution)/shard_map/ppermute | solution.py:272
  12.0 0.0 collective-permute-start.1
  12.0 0.5 collective-permute-start.6
  12.5 4.5 %collective-permute-done.4.refs_5_ = bf16[512,256]{1,0:T(8,128)(2,1)S(1)} collective-permute-done((bf16[512,256]{1,0:T(8,128)(2,1)}, bf16[512,256]{1,0:T(8,128)(2,1)S(1)}, u32[]{:S(2)}, u32[]{:S(2)}) %collective-permute-start.4) | collective-permute-done | bytes 262176 | tf_op jit(solution)/shard_map/ppermute | solution.py:272
  17.0 0.0 collective-permute-start.5
  17.0 0.0 collective-permute-done.2.refs_3_
  17.0 0.5 collective-permute-start.3
  17.5 0.0 collective-permute-done.1.refs_0_
  17.5 0.0 collective-permute-done.6.refs_6_
  17.5 1.0 %collective-permute-done.5.refs_4_ = bf16[512,256]{1,0:T(8,128)(2,1)S(1)} collective-permute-done((bf16[512,256]{1,0:T(8,128)(2,1)S(1)}, bf16[512,256]{1,0:T(8,128)(2,1)S(1)}, u32[]{:S(2)}, u32[]{:S(2)}) %collective-permute-start.5) | collective-permute-done | bytes 262176 | tf_op jit(solution)/shard_map/ppermute | solution.py:272
  18.6 0.4 collective-permute-done.3.refs_2_
  18.9 4.9 %shard_map.86 = (bf16[512,256]{1,0:T(8,128)(2,1)S(1)}, bf16[512,256]{1,0:T(8,128)(2,1)S(1)}, bf16[512,256]{1,0:T(8,128)(2,1)S(1)}, bf16[512,256]{1,0:T(8,128)(2,1)S(1)}) custom-call(s32[129]{0:T(256)S(1)} %get-tuple-element.33.row_of, s32[128]{0:T(128)S(1)} %get-tuple-element.34.col_of, s32[1]{0:T(128)} %bitcast.here_ref.me.mine_ref, ...), custom_call_target="tpu_custom_call" | custom-call | flops 1073741824 | bytes 6291456 | tf_op jit(solution)/shard_map/pallas_call | solution.py:145
  23.8 1.9 %collective-permute-start.10 = (bf16[512,256]{1,0:T(8,128)(2,1)S(1)}, bf16[512,256]{1,0:T(8,128)(2,1)S(1)}, u32[]{:S(2)}, u32[]{:S(2)}) collective-permute-start(bf16[512,256]{1,0:T(8,128)(2,1)S(1)} %get-tuple-element.37), channel_id=1, source_target_pairs={{0,1},{3,2},{4,5},{7,6},{8,9},{11,10},{12,13},{15,14},{16,17},{19,... | collective-permute-start | bytes 786440 | tf_op jit(solution)/shard_map/ppermute | solution.py:318
  25.8 0.7 collective-permute-start.7
  26.4 2.8 %collective-permute-start.9 = (bf16[512,256]{1,0:T(8,128)(2,1)S(1)}, bf16[512,256]{1,0:T(8,128)(2,1)S(1)}, u32[]{:S(2)}, u32[]{:S(2)}) collective-permute-start(bf16[512,256]{1,0:T(8,128)(2,1)S(1)} %get-tuple-element.39), channel_id=1, source_target_pairs={{0,1},{1,0},{2,3},{3,2},{4,5},{5,4},{6,7},{7,6},{8,9},{9,8},{10,11... | collective-permute-start | bytes 786440 | tf_op jit(solution)/shard_map/ppermute | solution.py:272
  29.3 2.8 %collective-permute-start.8 = (bf16[512,256]{1,0:T(8,128)(2,1)S(1)}, bf16[512,256]{1,0:T(8,128)(2,1)S(1)}, u32[]{:S(2)}, u32[]{:S(2)}) collective-permute-start(bf16[512,256]{1,0:T(8,128)(2,1)S(1)} %get-tuple-element.38), channel_id=1, source_target_pairs={{0,2},{3,1},{4,6},{7,5},{8,10},{11,9},{12,14},{15,13},{16,18},{19,... | collective-permute-start | bytes 786440 | tf_op jit(solution)/shard_map/ppermute | solution.py:320
  32.1 0.3 collective-permute-done.10
  32.4 0.1 add_convert_fusion.1
  32.4 1.3 %collective-permute-start.11 = (bf16[512,256]{1,0:T(8,128)(2,1)S(1)}, bf16[512,256]{1,0:T(8,128)(2,1)S(1)}, u32[]{:S(2)}, u32[]{:S(2)}) collective-permute-start(bf16[512,256]{1,0:T(8,128)(2,1)S(1)} %add_convert_fusion.1), channel_id=1, source_target_pairs={{1,3},{2,0},{5,7},{6,4},{9,11},{10,8},{13,15},{14,12},{17,19},{18,... | collective-permute-start | bytes 786440 | tf_op jit(solution)/shard_map/ppermute | solution.py:323
  33.7 4.2 %collective-permute-done.9.refs_2_ = bf16[512,256]{1,0:T(8,128)(2,1)S(1)} collective-permute-done((bf16[512,256]{1,0:T(8,128)(2,1)S(1)}, bf16[512,256]{1,0:T(8,128)(2,1)S(1)}, u32[]{:S(2)}, u32[]{:S(2)}) %collective-permute-start.9) | collective-permute-done | bytes 262176 | tf_op jit(solution)/shard_map/ppermute | solution.py:272
  38.0 0.0 collective-permute-done.7.refs_0_
  38.0 5.2 %collective-permute-done.8.refs_1_ = bf16[512,256]{1,0:T(8,128)(2,1)S(1)} collective-permute-done((bf16[512,256]{1,0:T(8,128)(2,1)S(1)}, bf16[512,256]{1,0:T(8,128)(2,1)S(1)}, u32[]{:S(2)}, u32[]{:S(2)}) %collective-permute-start.8) | collective-permute-done | bytes 262176 | tf_op jit(solution)/shard_map/ppermute | solution.py:320
  43.2 0.1 shard_map.87.refs_0_
  43.3 5.1 %collective-permute-done.11.refs_1_ = bf16[512,256]{1,0:T(8,128)(2,1)S(1)} collective-permute-done((bf16[512,256]{1,0:T(8,128)(2,1)S(1)}, bf16[512,256]{1,0:T(8,128)(2,1)S(1)}, u32[]{:S(2)}, u32[]{:S(2)}) %collective-permute-start.11) | collective-permute-done | bytes 262176 | tf_op jit(solution)/shard_map/ppermute | solution.py:323
  48.4 0.0 copy-done.1
  48.4 1.2 %shard_map.88 = (bf16[512,256]{1,0:T(8,128)(2,1)}, bf16[512,256]{1,0:T(8,128)(2,1)S(1)}, f32[512,256]{1,0:T(8,128)S(1)}, f32[512,256]{1,0:T(8,128)S(1)}) custom-call(f32[512,256]{1,0:T(8,128)S(1)} %shard_map.87.refs_0_, bf16[512,256]{1,0:T(8,128)(2,1)S(1)} %collective-permute-done.11.refs_1_, bf16[256,256]{1,0:T(8,128)(2,1)S(1)} %copy-done.2, ...), custom_call_target="tpu_custom_call" | custom-call | flops 268435456 | bytes 2621440 | tf_op jit(solution)/shard_map/pallas_call | solution.py:191
  49.6 1.5 %collective-permute-start.12 = (bf16[512,256]{1,0:T(8,128)(2,1)S(1)}, bf16[512,256]{1,0:T(8,128)(2,1)S(1)}, u32[]{:S(2)}, u32[]{:S(2)}) collective-permute-start(bf16[512,256]{1,0:T(8,128)(2,1)S(1)} %get-tuple-element.49.refs_5_), channel_id=1, source_target_pairs={{0,2},{3,1},{4,6},{7,5},{8,10},{11,9},{12,14},{15,13},{16,18},{19,... | collective-permute-start | bytes 786440 | tf_op jit(solution)/shard_map/ppermute | solution.py:330
  51.1 0.5 shard_map.89
  51.6 0.1 collective-permute-start.13
  51.7 0.1 collective-permute-start.17
  51.7 1.3 %collective-permute-start.16 = (bf16[512,256]{1,0:T(8,128)(2,1)S(1)}, bf16[512,256]{1,0:T(8,128)(2,1)S(1)}, u32[]{:S(2)}, u32[]{:S(2)}) collective-permute-start(bf16[512,256]{1,0:T(8,128)(2,1)S(1)} %get-tuple-element.49.refs_5_), channel_id=1, source_target_pairs={{1,3},{2,0},{5,7},{6,4},{9,11},{10,8},{13,15},{14,12},{17,19},{18,... | collective-permute-start | bytes 786440 | tf_op jit(solution)/shard_map/ppermute | solution.py:332
  53.0 0.7 collective-permute-start.15
  53.7 0.0 collective-permute-done.13
  53.8 4.1 %collective-permute-done.12.refs_3_ = bf16[512,256]{1,0:T(8,128)(2,1)S(1)} collective-permute-done((bf16[512,256]{1,0:T(8,128)(2,1)S(1)}, bf16[512,256]{1,0:T(8,128)(2,1)S(1)}, u32[]{:S(2)}, u32[]{:S(2)}) %collective-permute-start.12) | collective-permute-done | bytes 262176 | tf_op jit(solution)/shard_map/ppermute | solution.py:330
  57.8 1.3 %collective-permute-start.14 = (bf16[512,256]{1,0:T(8,128)(2,1)S(1)}, bf16[512,256]{1,0:T(8,128)(2,1)S(1)}, u32[]{:S(2)}, u32[]{:S(2)}) collective-permute-start(bf16[512,256]{1,0:T(8,128)(2,1)S(1)} %collective-permute-done.12.refs_3_), channel_id=1, source_target_pairs={{2,3},{1,0},{6,7},{5,4},{10,11},{9,8},{14,15},{13,12},{18,19},{17,... | collective-permute-start | bytes 786440 | tf_op jit(solution)/shard_map/ppermute | solution.py:335
  59.1 9.9 %all_gather.3.in_ref = f32[512,256]{1,0:T(8,128)S(1)} all-gather(f32[128,256]{1,0:T(8,128)S(1)} %add.16), channel_id=1, replica_groups={{0,8,16,24},{4,12,20,28},{1,9,17,25},{5,13,21,29},{2,10,18,26},{6,14,22..., dimensions={0}, use_global_device_ids=true | all-gather | bytes 655360 | tf_op jit(solution)/shard_map/all_gather | solution.py:379
  69.0 0.7 shard_map.90
  69.7 0.0 collective-permute-done.17.refs_4_
  69.7 0.0 collective-permute-done.16.refs_2_
  69.7 0.0 collective-permute-done.15.refs_1_
  69.7 1.9 %collective-permute-done.14.refs_0_ = bf16[512,256]{1,0:T(8,128)(2,1)S(1)} collective-permute-done((bf16[512,256]{1,0:T(8,128)(2,1)S(1)}, bf16[512,256]{1,0:T(8,128)(2,1)S(1)}, u32[]{:S(2)}, u32[]{:S(2)}) %collective-permute-start.14) | collective-permute-done | bytes 262176 | tf_op jit(solution)/shard_map/ppermute | solution.py:335
  71.6 5.0 %shard_map.91 = (bf16[2048,256]{1,0:T(8,128)(2,1)S(1)}, bf16[2048,256]{1,0:T(8,128)(2,1)S(1)}) custom-call(s32[129]{0:T(256)S(1)} %get-tuple-element.33.row_of, s32[128]{0:T(128)S(1)} %get-tuple-element.34.col_of, s32[1]{0:T(128)} %bitcast.1.mine_ref.here_ref, s32[1]{0:T(128)} %bitcast.here_ref.me.mine_ref, ...), custom_call_target="tpu_custom_call" | custom-call | flops 1073741824 | bytes 5242880 | tf_op jit(solution)/shard_map/pallas_call | solution.py:145
  76.6 0.1 collective-permute-start.18
  76.7 3.4 %all-to-all-start = ((bf16[4,128,256]{2,1,0:T(8,128)(2,1)}), bf16[4,128,256]{2,1,0:T(8,128)(2,1)S(1)}, u32[]{:S(2)}, u32[]{:S(2)}) async-start(bf16[4,128,256]{2,1,0:T(8,128)(2,1)} %bitcast.3), calls=%async_computation | async-start | bytes 524288 | tf_op jit(solution)/shard_map/all_to_all | solution.py:347
  80.2 0.0 collective-permute-done.18.other_ref
  80.2 0.2 shard_map.92
  80.4 1.0 %collective-permute-start.19 = (bf16[512,256]{1,0:T(8,128)(2,1)S(1)}, bf16[512,256]{1,0:T(8,128)(2,1)S(1)}, u32[]{:S(2)}, u32[]{:S(2)}) collective-permute-start(bf16[512,256]{1,0:T(8,128)(2,1)S(1)} %get-tuple-element.52), channel_id=1, source_target_pairs={{0,24},{4,28},{8,16},{12,20},{16,8},{20,12},{24,0},{28,4},{1,25},{... | collective-permute-start | bytes 786440 | tf_op jit(solution)/shard_map/ppermute | solution.py:272
  81.4 0.8 collective-permute-start.20
  82.2 1.8 %collective-permute-start.21 = (bf16[512,256]{1,0:T(8,128)(2,1)S(1)}, bf16[512,256]{1,0:T(8,128)(2,1)S(1)}, u32[]{:S(2)}, u32[]{:S(2)}) collective-permute-start(bf16[512,256]{1,0:T(8,128)(2,1)S(1)} %get-tuple-element.54), channel_id=1, source_target_pairs={{0,8},{4,12},{8,0},{12,4},{16,24},{20,28},{24,16},{28,20},{1,9},{5... | collective-permute-start | bytes 786440 | tf_op jit(solution)/shard_map/ppermute | solution.py:272
  84.0 6.0 %all-to-all-done = bf16[4,128,256]{2,1,0:T(8,128)(2,1)S(1)} async-done(((bf16[4,128,256]{2,1,0:T(8,128)(2,1)}), bf16[4,128,256]{2,1,0:T(8,128)(2,1)S(1)}, u32[]{:S(2)}, u32[]{:S(2)}) %all-to-all-start) | async-done | bytes 262176 | tf_op jit(solution)/shard_map/all_to_all | solution.py:347
  90.0 0.1 collective-permute-start.22
  90.0 1.3 %collective-permute-done.22.other_ref = f32[128,256]{1,0:T(8,128)S(1)} collective-permute-done((f32[128,256]{1,0:T(8,128)S(1)}, f32[128,256]{1,0:T(8,128)S(1)}, u32[]{:S(2)}, u32[]{:S(2)}) %collective-permute-start.22) | collective-permute-done | bytes 131104 | tf_op jit(solution)/shard_map/ppermute | solution.py:272
  91.4 0.7 shard_map.93
  92.1 0.0 collective-permute-done.19
  92.1 3.1 %collective-permute-done.20 = bf16[512,256]{1,0:T(8,128)(2,1)S(1)} collective-permute-done((bf16[512,256]{1,0:T(8,128)(2,1)S(1)}, bf16[512,256]{1,0:T(8,128)(2,1)S(1)}, u32[]{:S(2)}, u32[]{:S(2)}) %collective-permute-start.20) | collective-permute-done | bytes 262176 | tf_op jit(solution)/shard_map/ppermute | solution.py:272
  95.2 0.0 collective-permute-done.21
  95.2 0.8 add_convert_fusion
  (8 shorter events, 0.1 us)
Async XLA Ops:
  0.6 11.3 %collective-permute-start = (bf16[512,256]{1,0:T(8,128)(2,1)}, bf16[512,256]{1,0:T(8,128)(2,1)S(1)}, u32[]{:S(2)}, u32[]{:S(2)}) collective-permute-start(bf16[512,256]{1,0:T(8,128)(2,1)} %features.1), channel_id=1, source_target_pairs={{0,24},{4,28},{8,16},{12,20},{16,8},{20,12},{24,0},{28,4},{1,25},{... | collective-permute-start | bytes 786440 | tf_op jit(solution)/shard_map/ppermute | solution.py:272
  4.6 12.4 %collective-permute-start.4 = (bf16[512,256]{1,0:T(8,128)(2,1)}, bf16[512,256]{1,0:T(8,128)(2,1)S(1)}, u32[]{:S(2)}, u32[]{:S(2)}) collective-permute-start(bf16[512,256]{1,0:T(8,128)(2,1)} %features.1), channel_id=1, source_target_pairs={{0,8},{4,12},{8,0},{12,4},{16,24},{20,28},{24,16},{28,20},{1,9},{5... | collective-permute-start | bytes 786440 | tf_op jit(solution)/shard_map/ppermute | solution.py:272
  5.1 11.9 %collective-permute-start.2 = (bf16[512,256]{1,0:T(8,128)(2,1)}, bf16[512,256]{1,0:T(8,128)(2,1)S(1)}, u32[]{:S(2)}, u32[]{:S(2)}) collective-permute-start(bf16[512,256]{1,0:T(8,128)(2,1)} %features.1), channel_id=1, source_target_pairs={{0,16},{4,20},{8,24},{12,28},{16,0},{20,4},{24,8},{28,12},{1,17},{... | collective-permute-start | bytes 786440 | tf_op jit(solution)/shard_map/ppermute | solution.py:272
  5.2 1.0 %copy-start = (bf16[512,256]{1,0:T(8,128)(2,1)S(1)}, bf16[512,256]{1,0:T(8,128)(2,1)}, u32[]{:S(2)}) copy-start(bf16[512,256]{1,0:T(8,128)(2,1)} %features.1) | copy-start | bytes 786436
  6.2 0.7 copy-start.3
  6.9 0.7 copy-start.4
  12.0 5.6 %collective-permute-start.1 = (bf16[512,256]{1,0:T(8,128)(2,1)S(1)}, bf16[512,256]{1,0:T(8,128)(2,1)S(1)}, u32[]{:S(2)}, u32[]{:S(2)}) collective-permute-start(bf16[512,256]{1,0:T(8,128)(2,1)S(1)} %collective-permute-done.refs_1_), channel_id=1, source_target_pairs={{0,4},{4,0},{8,12},{12,8},{16,20},{20,16},{24,28},{28,24},{1,5},{5... | collective-permute-start | bytes 786440 | tf_op jit(solution)/shard_map/ppermute | solution.py:272
  12.0 5.6 %collective-permute-start.6 = (bf16[512,256]{1,0:T(8,128)(2,1)S(1)}, bf16[512,256]{1,0:T(8,128)(2,1)S(1)}, u32[]{:S(2)}, u32[]{:S(2)}) collective-permute-start(bf16[512,256]{1,0:T(8,128)(2,1)S(1)} %get-tuple-element.36.refs_7_), channel_id=1, source_target_pairs={{0,4},{4,0},{8,12},{12,8},{16,20},{20,16},{24,28},{28,24},{1,5},{5... | collective-permute-start | bytes 786440 | tf_op jit(solution)/shard_map/ppermute | solution.py:272
  17.0 1.5 %collective-permute-start.5 = (bf16[512,256]{1,0:T(8,128)(2,1)S(1)}, bf16[512,256]{1,0:T(8,128)(2,1)S(1)}, u32[]{:S(2)}, u32[]{:S(2)}) collective-permute-start(bf16[512,256]{1,0:T(8,128)(2,1)S(1)} %collective-permute-done.4.refs_5_), channel_id=1, source_target_pairs={{0,4},{4,0},{8,12},{12,8},{16,20},{20,16},{24,28},{28,24},{1,5},{5... | collective-permute-start | bytes 786440 | tf_op jit(solution)/shard_map/ppermute | solution.py:272
  17.0 1.9 %collective-permute-start.3 = (bf16[512,256]{1,0:T(8,128)(2,1)S(1)}, bf16[512,256]{1,0:T(8,128)(2,1)S(1)}, u32[]{:S(2)}, u32[]{:S(2)}) collective-permute-start(bf16[512,256]{1,0:T(8,128)(2,1)S(1)} %collective-permute-done.2.refs_3_), channel_id=1, source_target_pairs={{0,4},{4,0},{8,12},{12,8},{16,20},{20,16},{24,28},{28,24},{1,5},{5... | collective-permute-start | bytes 786440 | tf_op jit(solution)/shard_map/ppermute | solution.py:272
  18.9 29.5 %copy-start.1 = (bf16[512,256]{1,0:T(8,128)(2,1)S(1)}, bf16[512,256]{1,0:T(8,128)(2,1)}, u32[]{:S(2)}) copy-start(bf16[512,256]{1,0:T(8,128)(2,1)} %refs_3_.1) | copy-start | bytes 786436
  18.9 29.5 %copy-start.2 = (bf16[256,256]{1,0:T(8,128)(2,1)S(1)}, bf16[256,256]{1,0:T(8,128)(2,1)}, u32[]{:S(2)}) copy-start(bf16[256,256]{1,0:T(8,128)(2,1)} %refs_2_.1) | copy-start | bytes 393220
  23.8 8.6 %collective-permute-start.10 = (bf16[512,256]{1,0:T(8,128)(2,1)S(1)}, bf16[512,256]{1,0:T(8,128)(2,1)S(1)}, u32[]{:S(2)}, u32[]{:S(2)}) collective-permute-start(bf16[512,256]{1,0:T(8,128)(2,1)S(1)} %get-tuple-element.37), channel_id=1, source_target_pairs={{0,1},{3,2},{4,5},{7,6},{8,9},{11,10},{12,13},{15,14},{16,17},{19,... | collective-permute-start | bytes 786440 | tf_op jit(solution)/shard_map/ppermute | solution.py:318
  25.8 12.2 %collective-permute-start.7 = (bf16[512,256]{1,0:T(8,128)(2,1)S(1)}, bf16[512,256]{1,0:T(8,128)(2,1)S(1)}, u32[]{:S(2)}, u32[]{:S(2)}) collective-permute-start(bf16[512,256]{1,0:T(8,128)(2,1)S(1)} %get-tuple-element.37), channel_id=1, source_target_pairs={{1,2},{2,1},{5,6},{6,5},{9,10},{10,9},{13,14},{14,13},{17,18},{18,... | collective-permute-start | bytes 786440 | tf_op jit(solution)/shard_map/ppermute | solution.py:319
  26.4 11.5 %collective-permute-start.9 = (bf16[512,256]{1,0:T(8,128)(2,1)S(1)}, bf16[512,256]{1,0:T(8,128)(2,1)S(1)}, u32[]{:S(2)}, u32[]{:S(2)}) collective-permute-start(bf16[512,256]{1,0:T(8,128)(2,1)S(1)} %get-tuple-element.39), channel_id=1, source_target_pairs={{0,1},{1,0},{2,3},{3,2},{4,5},{5,4},{6,7},{7,6},{8,9},{9,8},{10,11... | collective-permute-start | bytes 786440 | tf_op jit(solution)/shard_map/ppermute | solution.py:272
  29.3 13.9 %collective-permute-start.8 = (bf16[512,256]{1,0:T(8,128)(2,1)S(1)}, bf16[512,256]{1,0:T(8,128)(2,1)S(1)}, u32[]{:S(2)}, u32[]{:S(2)}) collective-permute-start(bf16[512,256]{1,0:T(8,128)(2,1)S(1)} %get-tuple-element.38), channel_id=1, source_target_pairs={{0,2},{3,1},{4,6},{7,5},{8,10},{11,9},{12,14},{15,13},{16,18},{19,... | collective-permute-start | bytes 786440 | tf_op jit(solution)/shard_map/ppermute | solution.py:320
  32.4 16.0 %collective-permute-start.11 = (bf16[512,256]{1,0:T(8,128)(2,1)S(1)}, bf16[512,256]{1,0:T(8,128)(2,1)S(1)}, u32[]{:S(2)}, u32[]{:S(2)}) collective-permute-start(bf16[512,256]{1,0:T(8,128)(2,1)S(1)} %add_convert_fusion.1), channel_id=1, source_target_pairs={{1,3},{2,0},{5,7},{6,4},{9,11},{10,8},{13,15},{14,12},{17,19},{18,... | collective-permute-start | bytes 786440 | tf_op jit(solution)/shard_map/ppermute | solution.py:323
  49.6 8.2 %collective-permute-start.12 = (bf16[512,256]{1,0:T(8,128)(2,1)S(1)}, bf16[512,256]{1,0:T(8,128)(2,1)S(1)}, u32[]{:S(2)}, u32[]{:S(2)}) collective-permute-start(bf16[512,256]{1,0:T(8,128)(2,1)S(1)} %get-tuple-element.49.refs_5_), channel_id=1, source_target_pairs={{0,2},{3,1},{4,6},{7,5},{8,10},{11,9},{12,14},{15,13},{16,18},{19,... | collective-permute-start | bytes 786440 | tf_op jit(solution)/shard_map/ppermute | solution.py:330
  51.6 2.1 %collective-permute-start.13 = (f32[128,256]{1,0:T(8,128)S(1)}, f32[128,256]{1,0:T(8,128)S(1)}, u32[]{:S(2)}, u32[]{:S(2)}) collective-permute-start(f32[128,256]{1,0:T(8,128)S(1)} %get-tuple-element.46), channel_id=1, source_target_pairs={{0,4},{4,0},{8,12},{12,8},{16,20},{20,16},{24,28},{28,24},{1,5},{5... | collective-permute-start | bytes 393224 | tf_op jit(solution)/shard_map/ppermute | solution.py:272
  51.7 18.0 %collective-permute-start.17 = (bf16[512,256]{1,0:T(8,128)(2,1)S(1)}, bf16[512,256]{1,0:T(8,128)(2,1)S(1)}, u32[]{:S(2)}, u32[]{:S(2)}) collective-permute-start(bf16[512,256]{1,0:T(8,128)(2,1)S(1)} %get-tuple-element.49.refs_5_), channel_id=1, source_target_pairs={{0,1},{1,0},{2,3},{3,2},{4,5},{5,4},{6,7},{7,6},{8,9},{9,8},{10,11... | collective-permute-start | bytes 786440 | tf_op jit(solution)/shard_map/ppermute | solution.py:272
  51.7 18.0 %collective-permute-start.16 = (bf16[512,256]{1,0:T(8,128)(2,1)S(1)}, bf16[512,256]{1,0:T(8,128)(2,1)S(1)}, u32[]{:S(2)}, u32[]{:S(2)}) collective-permute-start(bf16[512,256]{1,0:T(8,128)(2,1)S(1)} %get-tuple-element.49.refs_5_), channel_id=1, source_target_pairs={{1,3},{2,0},{5,7},{6,4},{9,11},{10,8},{13,15},{14,12},{17,19},{18,... | collective-permute-start | bytes 786440 | tf_op jit(solution)/shard_map/ppermute | solution.py:332
  53.0 16.7 %collective-permute-start.15 = (bf16[512,256]{1,0:T(8,128)(2,1)S(1)}, bf16[512,256]{1,0:T(8,128)(2,1)S(1)}, u32[]{:S(2)}, u32[]{:S(2)}) collective-permute-start(bf16[512,256]{1,0:T(8,128)(2,1)S(1)} %get-tuple-element.49.refs_5_), channel_id=1, source_target_pairs={{1,2},{2,1},{5,6},{6,5},{9,10},{10,9},{13,14},{14,13},{17,18},{18,... | collective-permute-start | bytes 786440 | tf_op jit(solution)/shard_map/ppermute | solution.py:331
  57.8 13.8 %collective-permute-start.14 = (bf16[512,256]{1,0:T(8,128)(2,1)S(1)}, bf16[512,256]{1,0:T(8,128)(2,1)S(1)}, u32[]{:S(2)}, u32[]{:S(2)}) collective-permute-start(bf16[512,256]{1,0:T(8,128)(2,1)S(1)} %collective-permute-done.12.refs_3_), channel_id=1, source_target_pairs={{2,3},{1,0},{6,7},{5,4},{10,11},{9,8},{14,15},{13,12},{18,19},{17,... | collective-permute-start | bytes 786440 | tf_op jit(solution)/shard_map/ppermute | solution.py:335
  76.6 3.5 %collective-permute-start.18 = (bf16[2048,256]{1,0:T(8,128)(2,1)S(1)}, bf16[2048,256]{1,0:T(8,128)(2,1)S(1)}, u32[]{:S(2)}, u32[]{:S(2)}) collective-permute-start(bf16[2048,256]{1,0:T(8,128)(2,1)S(1)} %get-tuple-element.51), channel_id=1, source_target_pairs={{0,4},{4,0},{8,12},{12,8},{16,20},{20,16},{24,28},{28,24},{1,5},{5... | collective-permute-start | bytes 3145736 | tf_op jit(solution)/shard_map/ppermute | solution.py:272
  76.7 13.2 %all-to-all-start = ((bf16[4,128,256]{2,1,0:T(8,128)(2,1)}), bf16[4,128,256]{2,1,0:T(8,128)(2,1)S(1)}, u32[]{:S(2)}, u32[]{:S(2)}) async-start(bf16[4,128,256]{2,1,0:T(8,128)(2,1)} %bitcast.3), calls=%async_computation | async-start | bytes 524288 | tf_op jit(solution)/shard_map/all_to_all | solution.py:347
  80.4 11.7 %collective-permute-start.19 = (bf16[512,256]{1,0:T(8,128)(2,1)S(1)}, bf16[512,256]{1,0:T(8,128)(2,1)S(1)}, u32[]{:S(2)}, u32[]{:S(2)}) collective-permute-start(bf16[512,256]{1,0:T(8,128)(2,1)S(1)} %get-tuple-element.52), channel_id=1, source_target_pairs={{0,24},{4,28},{8,16},{12,20},{16,8},{20,12},{24,0},{28,4},{1,25},{... | collective-permute-start | bytes 786440 | tf_op jit(solution)/shard_map/ppermute | solution.py:272
  81.4 13.8 %collective-permute-start.20 = (bf16[512,256]{1,0:T(8,128)(2,1)S(1)}, bf16[512,256]{1,0:T(8,128)(2,1)S(1)}, u32[]{:S(2)}, u32[]{:S(2)}) collective-permute-start(bf16[512,256]{1,0:T(8,128)(2,1)S(1)} %get-tuple-element.53), channel_id=1, source_target_pairs={{0,16},{4,20},{8,24},{12,28},{16,0},{20,4},{24,8},{28,12},{1,17},{... | collective-permute-start | bytes 786440 | tf_op jit(solution)/shard_map/ppermute | solution.py:272
  82.2 13.0 %collective-permute-start.21 = (bf16[512,256]{1,0:T(8,128)(2,1)S(1)}, bf16[512,256]{1,0:T(8,128)(2,1)S(1)}, u32[]{:S(2)}, u32[]{:S(2)}) collective-permute-start(bf16[512,256]{1,0:T(8,128)(2,1)S(1)} %get-tuple-element.54), channel_id=1, source_target_pairs={{0,8},{4,12},{8,0},{12,4},{16,24},{20,28},{24,16},{28,20},{1,9},{5... | collective-permute-start | bytes 786440 | tf_op jit(solution)/shard_map/ppermute | solution.py:272
  90.0 1.4 %collective-permute-start.22 = (f32[128,256]{1,0:T(8,128)S(1)}, f32[128,256]{1,0:T(8,128)S(1)}, u32[]{:S(2)}, u32[]{:S(2)}) collective-permute-start(f32[128,256]{1,0:T(8,128)S(1)} %convert_reduce_fusion.own_ref), channel_id=1, source_target_pairs={{0,4},{4,0},{8,12},{12,8},{16,20},{20,16},{24,28},{28,24},{1,5},{5... | collective-permute-start | bytes 393224 | tf_op jit(solution)/shard_map/ppermute | solution.py:272
